TPU v7x, 512 devices: a whole 4x4x16 slice. The times are simulated.
512 devices in a mesh: ha: 8 (over y_hi, x), sa: 64 (over z, y_lo, core).
Axes of the slice: x: 4, y: 4 (y_hi: 2, y_lo: 2; y = y_hi * 2 + y_lo), z: 16, core: 2. Of those that a mesh axis runs over, the one named last changes fastest.
Arguments:
- enc_query: bfloat16 [131072, 1024], P(('ha', 'sa'))
- enc_key: bfloat16 [131072, 1024], P(('ha', 'sa')), may hold values from -6 to 6
- enc_value: bfloat16 [131072, 1024], P(('ha', 'sa')), may hold values from -6 to 6
- enc_resid: bfloat16 [131072, 1024], P(('ha', 'sa')), may hold values from -24 to 24
- out_weight: bfloat16 [1024, 1024], P('sa'), may hold values from -0.1875 to 0.1875
- norm_gain: float32 [1024], replicated, may hold values from 0.25 to 1.75
- kv_weight: bfloat16 [1024, 8, 256], P(None, 'ha'), may hold values from -0.1875 to 0.1875
- cross_query: bfloat16 [64, 8, 1024], P(None, 'ha')
- span_ids: int32 [512], replicated, may hold values from 0 to 511, each once
- seg_lengths: int32 [512], replicated, may hold values from 1 to 256, as said below
Outputs:
- cross_out: float32 [64, 8, 1024], P('sa', 'ha')
Inputs may be any that keep to these rules, and one draw needn't show every extreme that they name: `seg_lengths`: valid tokens of each segment; some segment is full.
All inputs are finite; a program needn't handle non-finite values.
Results may differ from a plain program's by a relative error of at most 0.015.
Values may be sent and summed in bfloat16 or wider, within the bound.
No kernel may reach another device: no remote copies, remote signals or barrier semaphores. Data moves between devices by JAX's collectives and lax.ppermute only.
A program may use at most 128 MiB of HBM per device.

v0:
```python
import math

import jax
import jax.numpy as jnp
from jax import lax
from jax.sharding import PartitionSpec as P

D_ENC = 1024
ENC_HEADS = 16
GROUP = 8
HEAD = 128
SEG_LEN = 256
QTAIL = 64


masked_value = -1e30
query_block = 64


def joined_2(value, axis, join):
    pieces = jax.tree.map(lambda part: lax.all_gather(part, axis), value)
    head = jax.tree.map(lambda part: part[0], pieces)
    tail = jax.tree.map(lambda part: part[1:], pieces)
    subtotal, _ = lax.scan(lambda subtotal, share: (join(subtotal, share), None), head, tail)
    return subtotal


def slot_lengths(slots, span_ids, seg_lengths):
    table_index = jnp.arange(span_ids.shape[0])
    flat_slots = slots.reshape(-1)
    picked = jnp.sum(
        jnp.where(table_index[None, :] == flat_slots[:, None], span_ids[None, :], 0), axis=1
    )
    found = jnp.sum(
        jnp.where(table_index[None, :] == picked[:, None], seg_lengths[None, :], 0), axis=1
    )
    return found.reshape(slots.shape)


def merge_partials(first, second):
    top_first, total_first, summed_first = first
    top_second, total_second, summed_second = second
    highest = jnp.maximum(top_first, top_second)
    scale_first = jnp.exp(top_first - highest)
    scale_second = jnp.exp(top_second - highest)
    total = total_first * scale_first + total_second * scale_second
    summed = summed_first * scale_first[..., None] + summed_second * scale_second[..., None]
    return (highest, total, summed)


def local(
    enc_query,
    enc_key,
    enc_value,
    enc_resid,
    out_weight,
    norm_gain,
    kv_weight,
    cross_query,
    span_ids,
    seg_lengths,
):
    ha_count = lax.axis_size("ha")
    sa_count = lax.axis_size("sa")
    row_count = enc_query.shape[0]
    seg_count = row_count // SEG_LEN
    head_dim = D_ENC // ENC_HEADS
    device_slot = lax.axis_index("ha") * sa_count + lax.axis_index("sa")
    own_slots = device_slot * seg_count + jnp.arange(seg_count)
    own_valid = slot_lengths(own_slots, span_ids, seg_lengths)
    query_heads = enc_query.reshape(seg_count, SEG_LEN, ENC_HEADS, head_dim)
    key_heads = enc_key.reshape(seg_count, SEG_LEN, ENC_HEADS, head_dim)
    value_heads = enc_value.reshape(seg_count, SEG_LEN, ENC_HEADS, head_dim)
    scores = jnp.einsum(
        "cqhd,ckhd->chqk", query_heads, key_heads, preferred_element_type=jnp.float32
    ) / math.sqrt(head_dim)
    keep = jnp.arange(SEG_LEN)[None, :] < own_valid[:, None]
    scores = jnp.where(keep[:, None, None, :], scores, masked_value)
    highest = jnp.max(scores, axis=-1, keepdims=True)
    expo = jnp.exp(scores - highest)
    probs = (expo / jnp.sum(expo, axis=-1, keepdims=True)).astype(jnp.bfloat16)
    context = jnp.einsum("chqk,ckhd->cqhd", probs, value_heads, preferred_element_type=jnp.float32)
    context = context.astype(jnp.bfloat16).reshape(row_count, D_ENC)
    attended = jnp.dot(
        context,
        lax.all_gather(out_weight, "sa", axis=0, tiled=True),
        preferred_element_type=jnp.float32,
    )
    hidden = enc_resid.astype(jnp.float32) + attended
    factor = lax.rsqrt(jnp.mean(hidden * hidden, axis=-1, keepdims=True) + 1e-05)
    encoded = (hidden * factor * norm_gain).astype(jnp.bfloat16)
    heads_here = kv_weight.shape[1]
    own_weight = kv_weight.reshape(D_ENC, heads_here * 2 * HEAD)
    keyval = jnp.dot(
        lax.all_gather(encoded, "ha", axis=0, tiled=True),
        own_weight,
        preferred_element_type=jnp.float32,
    ).astype(jnp.bfloat16)
    keyval = keyval.reshape(ha_count * row_count, heads_here, 2 * HEAD)
    holder = jnp.arange(ha_count) * sa_count + lax.axis_index("sa")
    column_slots = holder[:, None] * seg_count + jnp.arange(seg_count)[None, :]
    column_valid = slot_lengths(column_slots, span_ids, seg_lengths)
    keep_keys = (jnp.arange(SEG_LEN)[None, None, :] < column_valid[:, :, None]).reshape(-1)
    keys = keyval[:, :, :HEAD]
    values = keyval[:, :, HEAD:]
    query_count = cross_query.shape[0]
    blocks = cross_query.reshape(query_count // query_block, query_block, heads_here, GROUP, HEAD)

    def attend_block(query_rows):
        block_scores = jnp.einsum(
            "qhgd,rhd->qhgr", query_rows, keys, preferred_element_type=jnp.float32
        ) / math.sqrt(HEAD)
        block_scores = jnp.where(keep_keys[None, None, None, :], block_scores, masked_value)
        block_top = jnp.max(block_scores, axis=-1)
        block_expo = jnp.exp(block_scores - block_top[..., None])
        block_total = jnp.sum(block_expo, axis=-1)
        block_sum = jnp.einsum(
            "qhgr,rhd->qhgd",
            block_expo.astype(jnp.bfloat16),
            values,
            preferred_element_type=jnp.float32,
        )
        return (block_top, block_total, block_sum)

    tops, totals, sums = lax.map(attend_block, blocks)
    local_top = tops.reshape(query_count, heads_here, GROUP)
    local_total = totals.reshape(query_count, heads_here, GROUP)
    local_sum = sums.reshape(query_count, heads_here, GROUP, HEAD)
    out_count = QTAIL // sa_count
    joined = joined_2((local_top, local_total, local_sum), "sa", merge_partials)
    whole = joined[2] / joined[1][..., None]
    result = lax.dynamic_slice_in_dim(whole, lax.axis_index("sa") * out_count, out_count, 0)
    return result.reshape(out_count, heads_here, GROUP * HEAD).astype(jnp.float32)


def solution(mesh):
    placed = (
        P(("ha", "sa"), None),
        P(("ha", "sa"), None),
        P(("ha", "sa"), None),
        P(("ha", "sa"), None),
        P("sa", None),
        P(),
        P(None, "ha", None),
        P(None, "ha", None),
        P(),
        P(),
    )
    return jax.shard_map(
        local, mesh=mesh, in_specs=placed, out_specs=P("sa", "ha", None), check_vma=False
    )
```

profile of v0, /device:TPU:1, one launch (start us, length us, event | category | flops | bytes accessed | tf_op | source)
XLA Modules:
  0.0 485.2 jit_solution(8386391322221486120)
XLA Ops:
  7.3 1.2 copy.45
  8.6 1.2 copy.46
  9.8 1.2 copy.47
  11.1 1.3 select_reduce_fusion.3
  12.4 2.0 select_reduce_fusion.2
  15.1 3.6 fusion.33
  18.7 2.7 fusion.20
  21.5 115.9 %all-gather.9.cloned.1.call-done = bf16[1024,1024]{1,0:T(8,128)(2,1)} async-done(((bf16[16,1024]{1,0:T(8,128)(2,1)}), bf16[1024,1024]{1,0:T(8,128)(2,1)}) %all-gather.9.cloned.1.call-update) | async-done | bytes 2097168 | tf_op jit(solution)/shard_map/all_gather | solution.py:86
  137.4 2.4 multiply_reduce_fusion
  141.4 82.0 %all-gather.11.cloned.1.call-done = bf16[2048,1024]{1,0:T(8,128)(2,1)} async-done(((bf16[256,1024]{1,0:T(8,128)(2,1)}), bf16[2048,1024]{1,0:T(8,128)(2,1)}) %all-gather.11.cloned.1.call-update) | async-done | bytes 4194320 | tf_op jit(solution)/shard_map/all_gather | solution.py:95
  223.4 3.4 fusion.11
  227.7 1.9 copy-done.1
  229.6 1.6 fusion.21
  231.2 66.0 %all-gather.3 = f32[64,64,8]{1,2,0:T(8,128)S(1)} all-gather(f32[1,64,8]{1,2,0:T(8,128)S(1)} %bitcast.136), channel_id=2, replica_groups=mesh['ha'=8,'sa'=64] {'sa'}, dimensions={0}, use_global_device_ids=true | all-gather | bytes 133120 | tf_op jit(solution)/shard_map/all_gather | solution.py:21
  297.2 3.2 fusion.10
  300.4 61.4 %all-gather.4 = f32[64,64,8]{1,2,0:T(8,128)S(1)} all-gather(f32[1,64,8]{1,2,0:T(8,128)S(1)} %bitcast.137), channel_id=3, replica_groups=mesh['ha'=8,'sa'=64] {'sa'}, dimensions={0}, use_global_device_ids=true | all-gather | bytes 133120 | tf_op jit(solution)/shard_map/all_gather | solution.py:21
  361.8 8.3 %all-gather.13.cloned.1.call-done = f32[4096,1,8,128]{3,0,2,1:T(8,128)} async-done(((f32[64,1,8,128]{3,0,2,1:T(8,128)}), f32[4096,1,8,128]{3,0,2,1:T(8,128)}) %all-gather.13.cloned.1.call-update) | async-done | bytes 16777232 | tf_op jit(solution)/shard_map/all_gather | solution.py:21
  371.3 11.3 %slice.49 = f32[4032,1,8,128]{3,0,2,1:T(8,128)} slice(f32[4096,1,8,128]{3,0,2,1:T(8,128)} %all-gather.13.cloned.1.call-done), slice={[64:4096], [0:1], [0:8], [0:128]} | slice | bytes 33030144 | tf_op jit(solution)/shard_map/slice | solution.py:23
  382.6 95.3 %while.2 = (s32[]{:T(128)}, f32[64,1,8]{0,2,1:T(8,128)S(1)}, f32[64,1,8]{0,2,1:T(8,128)S(1)}, f32[64,1,8,128]{3,2,1,0:T(8,128)S(1)}, f32[63,64,1,8]{1,3,2,0:T(8,...) while((s32[]{:T(128)}, f32[64,1,8]{0,2,1:T(8,128)S(1)}, ...), condition=%wide.region_10.11_spmd, body=%wide.region_9.10_spmd.sunk | while | flops 200194 | bytes 1349737 | solution.py:24
  384.3 1.0 constant_dynamic-slice_fusion.3
  385.8 1.0 constant_dynamic-slice_fusion.3
  387.3 1.0 constant_dynamic-slice_fusion.3
  388.8 1.0 constant_dynamic-slice_fusion.3
  399.4 1.0 constant_dynamic-slice_fusion.3
  (474 shorter events, 93.5 us)
Async XLA Ops:
  6.5 216.9 %copy-start = (bf16[1024,1,256]{2,0,1:T(8,128)(2,1)S(1)}, bf16[1024,1,256]{2,0,1:T(8,128)(2,1)}, u32[]{:S(2)}) copy-start(bf16[1024,1,256]{2,0,1:T(8,128)(2,1)} %param.18) | copy-start | bytes 1572868
  6.5 130.9 %all-gather.9.cloned.1.call-start = ((), (), s32[]{:S(2)}) async-start(), calls=%async_computation | async-start | bytes 2129920 | tf_op jit(solution)/shard_map/all_gather | solution.py:86
  7.3 216.1 %all-gather.11.cloned.1.call-start = ((), (), s32[]{:S(2)}) async-start(), calls=%async_computation.1 | async-start | bytes 4718592 | tf_op jit(solution)/shard_map/all_gather | solution.py:95
  18.7 118.7 %copy-start.2 = (bf16[256,1024]{1,0:T(8,128)(2,1)S(1)}, bf16[256,1024]{1,0:T(8,128)(2,1)}, u32[]{:S(2)}) copy-start(bf16[256,1024]{1,0:T(8,128)(2,1)} %param.15) | copy-start | bytes 1572868
  21.4 118.4 %copy-start.6 = (f32[1024]{0:T(1024)S(1)}, f32[1024]{0:T(1024)}, u32[]{:S(2)}) copy-start(f32[1024]{0:T(1024)} %param.17) | copy-start | bytes 12292
  21.4 119.4 %copy-start.4 = (s32[512]{0:T(512)S(1)}, s32[512]{0:T(512)}, u32[]{:S(2)}) copy-start(s32[512]{0:T(512)} %param.20) | copy-start | bytes 6148
  21.5 119.6 %copy-start.5 = (s32[512]{0:T(512)S(1)}, s32[512]{0:T(512)}, u32[]{:S(2)}) copy-start(s32[512]{0:T(512)} %param.21) | copy-start | bytes 6148
  21.5 119.9 %copy-start.3 = (bf16[64,1,1024]{2,0,1:T(8,128)(2,1)S(1)}, bf16[64,1,1024]{2,0,1:T(8,128)(2,1)}, u32[]{:S(2)}) copy-start(bf16[64,1,1024]{2,0,1:T(8,128)(2,1)} %param.19) | copy-start | bytes 393220
  140.8 229.4 %all-gather.13.cloned.1.call-start = ((), (), s32[]{:S(2)}) async-start(), calls=%async_computation.2 | async-start | bytes 17039360 | tf_op jit(solution)/shard_map/all_gather | solution.py:21
  227.7 1.9 copy-start.1
Sparse Core Ops, SparseCore 0:
  9.5 127.8 all-gather.8
  140.9 82.4 all-gather.10
  231.4 138.7 all-gather.12
where the time goes:
time: 488 us; the launch traced here: 485 us
  waiting for transfers between devices  207 us (42%)
  blocking collectives  127 us (26%)
  local copies, waits for them, and re-layouts  90.1 us (18%)
  other arithmetic  30.1 us (6%)
  matrix products  14.6 us (3%)
  between operations  13.3 us (3%)
    all_gather x2, blocking collectives, joined_2(): pieces = jax.tree.map(lambda part: lax.all_gather(part, axis), value)  127 us
    all_gather x1, waiting for transfers between devices, local(): lax.all_gather(out_weight, 'sa', axis=0, tiled=True)  116 us
    all_gather x1, waiting for transfers between devices, local(): lax.all_gather(encoded, 'ha', axis=0, tiled=True)  82 us
    dynamic_slice x63, local copies, waits for them, and re-layouts, joined_2(): lax.scan(lambda subtotal, share: (join(subtotal, share), None), head, tail)  61 us
    add x63, other arithmetic, merge_partials(): summed_first * scale_first[..., None]  18.9 us
    slice x1, local copies, waits for them, and re-layouts, joined_2(): tail = jax.tree.map(lambda part: part[1:], pieces)  11.3 us
  transfers between devices with their start and end apart: 3, of which 3 were waited for; matrix products, arithmetic and copies ran while one was open for 4% of the time, Pallas kernels for 0%

commit v1 on v0

v1 whole, which is shorter than its diff:
```python
import functools
import math

import jax
import jax.numpy as jnp
import numpy as np
from jax import lax
from jax.experimental import pallas as pl
from jax.experimental.pallas import tpu as pltpu
from jax.sharding import Mesh, PartitionSpec as P

D_ENC = 1024
ENC_HEADS = 16
ENC_HEAD = D_ENC // ENC_HEADS
KV_HEADS = 8
GROUP = 8
HEAD = 128
SEG_LEN = 256
QTAIL = 64
MASKED = -1e30

PARTS = ("yh", "x", "z", "yl", "c")
HA = ("yh", "x")
SA = ("z", "yl", "c")
PLANE = ("yh", "x", "yl")


def params(**kw):
    return pltpu.CompilerParams(vmem_limit_bytes=48 * 1024 * 1024, **kw)


def dot(a, b):
    return jnp.dot(a, b, preferred_element_type=jnp.float32)


def dot_t(a, b):
    return lax.dot_general(a, b, (((1,), (1,)), ((), ())), preferred_element_type=jnp.float32)


def encoder_attention_kernel(slot_ref, span_ref, len_ref, q_ref, k_ref, v_ref, o_ref):
    valid = len_ref[span_ref[slot_ref[0]]]
    keep = lax.broadcasted_iota(jnp.int32, (1, SEG_LEN), 1) < valid
    bias = jnp.where(keep, 0.0, MASKED).astype(jnp.float32)
    low = lax.broadcasted_iota(jnp.int32, (SEG_LEN, 2 * ENC_HEAD), 1) < ENC_HEAD
    for pair in range(ENC_HEADS // 2):
        cols = slice(pair * 2 * ENC_HEAD, (pair + 1) * 2 * ENC_HEAD)
        q, k, v = q_ref[:, cols], k_ref[:, cols], v_ref[:, cols]
        zero = jnp.zeros_like(k)
        parts = []
        for mine in (low, jnp.logical_not(low)):
            scores = dot_t(q, jnp.where(mine, k, zero)) * (1.0 / math.sqrt(ENC_HEAD)) + bias
            expo = jnp.exp(scores - jnp.max(scores, axis=-1, keepdims=True))
            probs = (expo * (1.0 / jnp.sum(expo, axis=-1, keepdims=True))).astype(jnp.bfloat16)
            parts.append(dot(probs, v))
        o_ref[:, cols] = jnp.where(low, parts[0], parts[1]).astype(jnp.bfloat16)


def encoder_attention(slot, span_ids, seg_lengths, q, k, v):
    smem = pl.BlockSpec(memory_space=pltpu.SMEM)
    vmem = pl.BlockSpec(memory_space=pltpu.VMEM)
    return pl.pallas_call(
        encoder_attention_kernel,
        out_shape=jax.ShapeDtypeStruct((SEG_LEN, D_ENC), jnp.bfloat16),
        in_specs=[smem, smem, smem, vmem, vmem, vmem],
        out_specs=vmem,
        compiler_params=params(),
        cost_estimate=pl.CostEstimate(
            flops=8 * SEG_LEN * SEG_LEN * D_ENC, bytes_accessed=8 * SEG_LEN * D_ENC,
            transcendentals=SEG_LEN * SEG_LEN * ENC_HEADS),
        name="encoder_attention",
    )(slot, span_ids, seg_lengths, q, k, v)


def encode_kernel(core_ref, ctx_ref, w_mine_ref, w_other_ref, resid_ref, gain_ref, kv_mine_ref,
                  kv_other_ref, o_ref, w_ref, enc_ref):
    core = core_ref[0]
    for part_ref, at in ((w_mine_ref, core), (w_other_ref, 1 - core)):
        for yh in range(2):
            for x in range(4):
                for yl in range(2):
                    ha = yh * 4 + x
                    row = pl.multiple_of(32 * yl + 16 * at, 16)
                    w_ref[:, pl.ds(row, 16), HEAD * ha:HEAD * (ha + 1)] = part_ref[ha * 2 + yl]
    weight = w_ref[...].reshape(D_ENC, D_ENC)
    hidden = resid_ref[...].astype(jnp.float32) + dot(ctx_ref[...], weight)
    factor = lax.rsqrt(jnp.mean(hidden * hidden, axis=-1, keepdims=True) + 1e-05)
    encoded = (hidden * factor * gain_ref[...]).astype(jnp.bfloat16)
    half = D_ENC // 2
    enc_ref[0] = encoded[:, :half]
    enc_ref[1] = encoded[:, half:]
    mine, other = enc_ref[core], enc_ref[1 - core]
    for h in range(KV_HEADS):
        o_ref[h] = (dot(mine, kv_mine_ref[h]) + dot(other, kv_other_ref[h])).astype(jnp.bfloat16)


def encode(core, ctx, w_mine, w_other, resid, gain, kv_mine, kv_other):
    smem = pl.BlockSpec(memory_space=pltpu.SMEM)
    vmem = pl.BlockSpec(memory_space=pltpu.VMEM)
    return pl.pallas_call(
        encode_kernel,
        out_shape=jax.ShapeDtypeStruct((KV_HEADS, SEG_LEN, 2 * HEAD), jnp.bfloat16),
        in_specs=[smem] + [vmem] * 7,
        out_specs=vmem,
        scratch_shapes=[pltpu.VMEM((16, 64, D_ENC), jnp.bfloat16),
                        pltpu.VMEM((2, SEG_LEN, D_ENC // 2), jnp.bfloat16)],
        compiler_params=params(),
        cost_estimate=pl.CostEstimate(
            flops=6 * SEG_LEN * D_ENC * D_ENC, bytes_accessed=8 * D_ENC * D_ENC, transcendentals=SEG_LEN),
        name="encode_keyval",
    )(core, ctx, w_mine, w_other, resid, gain, kv_mine, kv_other)


def cross_kernel(slots, first_ref, span_ref, len_ref, q_ref, kv_ref, o_ref):
    scale = 1.0 / math.sqrt(HEAD)
    lane = lax.broadcasted_iota(jnp.int32, (1, SEG_LEN), 1)
    bias = []
    for s in range(slots):
        valid = len_ref[span_ref[first_ref[0] + s * first_ref[1]]]
        bias.append(jnp.where(lane < valid, 0.0, MASKED).astype(jnp.float32))
    bias = jnp.concatenate(bias, axis=1)
    keys = kv_ref[:, :, :HEAD].reshape(slots * SEG_LEN, HEAD)
    values = kv_ref[:, :, HEAD:].reshape(slots * SEG_LEN, HEAD)
    rows = 128
    queries = rows // GROUP
    column = lax.broadcasted_iota(jnp.int32, (rows, HEAD), 1)
    for b in range(QTAIL // queries):
        q = q_ref[b * rows:(b + 1) * rows]
        scores = dot_t(q, keys) + bias
        top = jnp.max(scores, axis=-1, keepdims=True)
        expo = jnp.exp((scores - top) * scale)
        total = jnp.sum(expo, axis=-1, keepdims=True)
        average = dot(expo.astype(jnp.bfloat16), values) / total
        level = jnp.broadcast_to(top * scale + jnp.log(total), (rows, HEAD))
        high = level.astype(jnp.bfloat16).astype(jnp.float32)
        middle = (level - high).astype(jnp.bfloat16).astype(jnp.float32)
        rest = level - high - middle
        split = jnp.where(column == 0, high, jnp.where(column == 1, middle, rest))
        o_ref[b * queries:(b + 1) * queries, :GROUP] = average.reshape(queries, GROUP, HEAD).astype(jnp.bfloat16)
        o_ref[b * queries:(b + 1) * queries, GROUP:] = split.reshape(queries, GROUP, HEAD).astype(jnp.bfloat16)


def cross_attention(first, span_ids, seg_lengths, q, kv):
    smem = pl.BlockSpec(memory_space=pltpu.SMEM)
    vmem = pl.BlockSpec(memory_space=pltpu.VMEM)
    slots = kv.shape[0]
    return pl.pallas_call(
        functools.partial(cross_kernel, slots),
        out_shape=jax.ShapeDtypeStruct((QTAIL, 2 * GROUP, HEAD), jnp.bfloat16),
        in_specs=[smem, smem, smem, vmem, vmem],
        out_specs=vmem,
        compiler_params=params(),
        name="cross_attention",
    )(first, span_ids, seg_lengths, q, kv)


def merge_kernel(part_ref, o_ref):
    average = part_ref[:, :GROUP].astype(jnp.float32)
    pieces = part_ref[:, GROUP:, :3].astype(jnp.float32)
    level = jnp.sum(pieces, axis=-1, keepdims=True)
    weight = jnp.exp(level - jnp.max(level, axis=0, keepdims=True))
    o_ref[...] = jnp.sum(average * weight, axis=0) / jnp.sum(weight, axis=0)


def merge(parts):
    vmem = pl.BlockSpec(memory_space=pltpu.VMEM)
    return pl.pallas_call(
        merge_kernel,
        out_shape=jax.ShapeDtypeStruct((GROUP, HEAD), jnp.float32),
        in_specs=[vmem],
        out_specs=vmem,
        name="merge_partials",
    )(parts)


def spread(block, axes):
    count = lax.axis_size(axes)
    copies = jnp.broadcast_to(block[None], (count,) + block.shape)
    return lax.all_to_all(copies, axes, 0, 0, tiled=True)


def local(enc_query, enc_key, enc_value, enc_resid, out_weight, norm_gain, kv_weight, cross_query,
          span_ids, seg_lengths):
    ha = lax.axis_index(HA)
    sa = lax.axis_index(SA)
    sa_count = lax.axis_size(SA)
    core = lax.axis_index("c")

    swap = functools.partial(lax.ppermute, axis_name="c", perm=[(0, 1), (1, 0)])

    with jax.named_scope("gather_kv_weight"):
        half = D_ENC // 2
        kv_half = lax.dynamic_slice_in_dim(kv_weight.reshape(D_ENC, 2 * HEAD), core * half, half, 0)
        kv_mine = lax.all_gather(kv_half, HA)
        kv_other = swap(kv_mine)

    with jax.named_scope("gather_out_weight"):
        mine = lax.dynamic_slice_in_dim(out_weight, ha * HEAD, HEAD, 1)
        w_mine = spread(spread(mine, "z"), PLANE).reshape(16, 16, 16, HEAD)
        w_other = swap(w_mine)

    slot = (ha * sa_count + sa).reshape(1).astype(jnp.int32)
    context = encoder_attention(slot, span_ids, seg_lengths, enc_query, enc_key, enc_value)
    keyval = encode(core.reshape(1).astype(jnp.int32), context, w_mine, w_other, enc_resid,
                    norm_gain.reshape(1, D_ENC), kv_mine, kv_other)
    with jax.named_scope("exchange_keyval"):
        keyval = lax.all_to_all(keyval, HA, 0, 0, tiled=True)
    first = jnp.stack([sa, sa_count]).astype(jnp.int32)
    parts = cross_attention(first, span_ids, seg_lengths, cross_query.reshape(QTAIL * GROUP, HEAD), keyval)
    with jax.named_scope("exchange_partials"):
        parts = lax.all_to_all(parts, SA, 0, 0, tiled=True)
    return merge(parts).reshape(1, 1, GROUP * HEAD)


def solution(mesh):
    fine = Mesh(mesh.devices.reshape(2, 4, 16, 2, 2), PARTS)
    rows = P(PARTS, None)
    heads = P(None, HA, None)
    placed = (rows, rows, rows, rows, P(SA, None), P(), heads, heads, P(), P())
    return jax.shard_map(
        local, mesh=fine, in_specs=placed, out_specs=P(SA, HA, None), check_vma=False
    )
```

time: 488 us -> 193 us (0.40)
  waiting for transfers between devices: 207 us -> 76.8 us
  local copies, waits for them, and re-layouts: 90.1 us -> 5.45 us
  blocking collectives: 127 us -> 56.3 us
  other arithmetic: 30.1 us -> 0.08 us
  starting transfers between devices: 0.08 us -> 26.6 us
  matrix products: 14.6 us -> 0 us
  Pallas kernels: 0 us -> 13.8 us
    all_gather x3 -> x1, waiting for transfers between devices: 206 us -> 59.5 us  [local(): kv_mine = lax.all_gather(kv_half, HA)]
    all_gather x2 -> x0, blocking collectives: 127 us -> none  [joined_2(): pieces = jax.tree.map(lambda part: lax.all_gather(part, axis), value)]
    dynamic_slice x64 -> x2, local copies, waits for them, and re-layouts: 61 us -> 1.42 us  [the longest x1 0.73 us: local(): lax.dynamic_slice_in_dim(kv_weight.reshape(D_ENC, 2 * HEAD), core * half,...]
    all_to_all x0 -> x2, blocking collectives: none -> 56.3 us  [the longest x1 35.6 us: local(): parts = lax.all_to_all(parts, SA, 0, 0, tiled=True)]
    all_to_all x0 -> x2, starting transfers between devices: none -> 19.4 us  [the longest x1 15.7 us: spread(): return lax.all_to_all(copies, axes, 0, 0, tiled=True)]
    add x64 -> x0, other arithmetic: 18.9 us -> none  [the longest x63 18.9 us: merge_partials(): summed_first * scale_first[..., None]]
    all_to_all x0 -> x2, waiting for transfers between devices: none -> 17.2 us  [the longest x1 17.2 us: local(): keyval = lax.all_to_all(keyval, HA, 0, 0, tiled=True)]
    pallas_call x0 -> x4, Pallas kernels: none -> 13.8 us  [the longest x1 5.92 us: encode(): pl.pallas_call(encode_kernel, out_shape=jax.ShapeDtypeStruct((KV_HEADS, S...]
  transfers between devices with their start and end apart: 3 -> 5, of which waited for: 3 -> 2; matrix products, arithmetic and copies ran while one was open for 4% -> 1% of each run, Pallas kernels for 0% -> 2%
where the time goes in v1:
time: 193 us
  waiting for transfers between devices  76.8 us (40%)
  blocking collectives  56.3 us (29%)
  starting transfers between devices  26.6 us (14%)
  Pallas kernels  13.8 us (7%)
  between operations  13.6 us (7%)
  local copies, waits for them, and re-layouts  5.45 us (3%)
    all_gather x1, waiting for transfers between devices, local(): kv_mine = lax.all_gather(kv_half, HA)  59.5 us
    all_to_all x1, blocking collectives, local(): parts = lax.all_to_all(parts, SA, 0, 0, tiled=True)  35.6 us
    all_to_all x1, blocking collectives, spread(): return lax.all_to_all(copies, axes, 0, 0, tiled=True)  20.7 us
    all_to_all x1, waiting for transfers between devices, local(): keyval = lax.all_to_all(keyval, HA, 0, 0, tiled=True)  17.2 us
    all_to_all x1, starting transfers between devices, spread(): return lax.all_to_all(copies, axes, 0, 0, tiled=True)  15.7 us
    pallas_call x1, Pallas kernels, encode(): pl.pallas_call(encode_kernel, out_shape=jax.ShapeDtypeStruct((KV_HEADS, S...  5.92 us
    ppermute x1, starting transfers between devices, local(): kv_other = swap(kv_mine)  3.88 us
  transfers between devices with their start and end apart: 5, of which 2 were waited for; matrix products, arithmetic and copies ran while one was open for 1% of the time, Pallas kernels for 2%

profile of v1, /device:TPU:1, one launch (start us, length us, event | category | flops | bytes accessed | tf_op | source)
XLA Modules:
  0.0 192.6 jit_solution(12009090989282826430)
XLA Ops:
  6.5 1.0 copy-done
  7.6 0.7 constant_dynamic-slice_fusion
  8.3 0.0 all-gather.3.cloned.1.call-update
  8.3 0.7 constant_dynamic-slice_fusion.1
  9.0 0.6 broadcast_in_dim.4
  9.7 15.7 %all-to-all-start = ((bf16[16,16,128]{2,1,0:T(8,128)(2,1)}), bf16[16,16,128]{2,1,0:T(8,128)(2,1)S(1)}, u32[]{:S(2)}, u32[]{:S(2)}) async-start(bf16[16,16,128]{2,1,0:T(8,128)(2,1)} %broadcast_in_dim.4), calls=%async_computation | async-start | bytes 131072 | tf_op jit(solution)/shard_map/gather_out_weight/all_to_all | solution.py:178
  25.4 59.5 %all-gather.3.cloned.1.call-done = bf16[4096,1,256]{2,0,1:T(8,128)(2,1)} async-done(((bf16[512,1,256]{2,0,1:T(8,128)(2,1)}), bf16[4096,1,256]{2,0,1:T(8,128)(2,1)}) %all-gather.3.cloned.1.call-update) | async-done | bytes 2097168 | tf_op jit(solution)/shard_map/gather_kv_weight/all_gather | solution.py:193
  84.9 3.9 %collective-permute-start.1 = (bf16[8,512,256]{2,1,0:T(8,128)(2,1)}, bf16[8,512,256]{2,1,0:T(8,128)(2,1)}, u32[]{:S(2)}, u32[]{:S(2)}) collective-permute-start(bf16[8,512,256]{2,1,0:T(8,128)(2,1)} %bitcast.9), channel_id=1, source_target_pairs={{0,1},{1,0},{2,3},{3,2},{4,5},{5,4},{6,7},{7,6},{8,9},{9,8},{10,11... | collective-permute-start | bytes 6291464 | tf_op jit(solution)/shard_map/gather_kv_weight/ppermute | solution.py:194
  88.8 0.2 broadcast_in_dim.5
  89.0 0.0 copy-start.7
  89.0 20.7 %all_to_all.20.w_mine_ref = bf16[16,16,16,128]{3,2,1,0:T(8,128)(2,1)S(1)} all-to-all(bf16[16,16,16,128]{3,2,1,0:T(8,128)(2,1)S(1)} %broadcast_in_dim.5), channel_id=1, replica_groups=mesh['yh'=2,'x'=4,'z'=16,'yl'=2,'c'=2] {'yh','x','yl'}, dimensions={0} | all-to-all | bytes 2097152 | tf_op jit(solution)/shard_map/gather_out_weight/all_to_all | solution.py:178
  109.7 3.3 %collective-permute-start = (bf16[16,16,16,128]{3,2,1,0:T(8,128)(2,1)S(1)}, bf16[16,16,16,128]{3,2,1,0:T(8,128)(2,1)S(1)}, u32[]{:S(2)}, u32[]{:S(2)}) collective-permute-start(bf16[16,16,16,128]{3,2,1,0:T(8,128)(2,1)S(1)} %all_to_all.20.w_mine_ref), channel_id=1, source_target_pairs={{0,1},{1,0},{2,3},{3,2},{4,5},{5,4},{6,7},{7,6},{8,9},{9,8},{10,11... | collective-permute-start | bytes 3145736 | tf_op jit(solution)/shard_map/gather_out_weight/ppermute | solution.py:199
  113.1 0.0 copy-start.2
  113.1 1.0 copy-done.2
  114.1 1.0 copy-done.3
  115.2 3.1 %encoder_attention.1.ctx_ref = bf16[256,1024]{1,0:T(8,128)(2,1)S(1)} custom-call(s32[1]{0:T(128)} %bitcast.2.slot_ref, s32[512]{0:T(512)S(1)} %copy-done.5, s32[512]{0:T(512)S(1)} %copy-done.6, bf16[256,1024]{1,0:T(8,128)(2,1)S(1)} %copy-done.1, bf16[256,1024]{1,0:T(8,128)(2,1)S(1)} %copy-done.2, bf16[256,1024]{1,0:T(8,128)(2,1)S(1)} %copy-done.3), custom_call_target="tpu_custom_call" | custom-call | flops 536870912 | bytes 2097152 | tf_op jit(solution)/shard_map/encoder_attention/pallas_call | solution.py:61
  118.3 5.9 %encode_keyval.1 = bf16[8,256,256]{2,1,0:T(8,128)(2,1)} custom-call(s32[1]{0:T(128)} %bitcast.1.core_ref, bf16[256,1024]{1,0:T(8,128)(2,1)S(1)} %encoder_attention.1.ctx_ref, bf16[16,16,16,128]{3,2,1,0:T(8,128)(2,1)S(1)} %all_to_all.20.w_mine_ref, bf16[16,16,16,128]{3,2,1,0:T(8,128)(2,1)S(1)} %collective-permute-done.w_other_ref, ...), custom_call_target="tpu_custom_call" | custom-call | flops 1610612736 | bytes 8388608 | tf_op jit(solution)/shard_map/encode_keyval/pallas_call | solution.py:99
  124.2 3.7 %all-to-all-start.2 = ((bf16[8,256,256]{2,1,0:T(8,128)(2,1)}), bf16[8,256,256]{2,1,0:T(8,128)(2,1)S(1)}, u32[]{:S(2)}, u32[]{:S(2)}) async-start(bf16[8,256,256]{2,1,0:T(8,128)(2,1)} %encode_keyval.1), calls=%async_computation.2 | async-start | bytes 2097152 | tf_op jit(solution)/shard_map/exchange_keyval/all_to_all | solution.py:206
  127.9 0.1 reshape.20.q_ref
  128.0 0.1 pad_add_fusion.first_ref
  128.1 17.2 %all-to-all-done.2.kv_ref = bf16[8,256,256]{2,1,0:T(8,128)(2,1)S(1)} async-done(((bf16[8,256,256]{2,1,0:T(8,128)(2,1)}), bf16[8,256,256]{2,1,0:T(8,128)(2,1)S(1)}, u32[]{:S(2)}, u32[]{:S(2)}) %all-to-all-start.2) | async-done | bytes 1048608 | tf_op jit(solution)/shard_map/exchange_keyval/all_to_all | solution.py:206
  145.3 3.0 %cross_attention.1 = bf16[64,16,128]{2,1,0:T(8,128)(2,1)S(1)} custom-call(s32[2]{0:T(128)S(1)} %pad_add_fusion.first_ref, s32[512]{0:T(512)S(1)} %copy-done.5, s32[512]{0:T(512)S(1)} %copy-done.6, bf16[512,128]{1,0:T(8,128)(2,1)S(1)} %reshape.20.q_ref, bf16[8,256,256]{2,1,0:T(8,128)(2,1)S(1)} %all-to-all-done.2.kv_ref), custom_call_target="tpu_custom_call" | custom-call | tf_op jit(solution)/shard_map/cross_attention/pallas_call | solution.py:146
  148.3 35.6 %all_to_all.21.part_ref = bf16[64,16,128]{2,1,0:T(8,128)(2,1)} all-to-all(bf16[64,16,128]{2,1,0:T(8,128)(2,1)S(1)} %cross_attention.1), channel_id=1, replica_groups=mesh['yh'=2,'x'=4,'z'=16,'yl'=2,'c'=2] {'z','yl','c'}, dimensions={0} | all-to-all | bytes 524288 | tf_op jit(solution)/shard_map/exchange_partials/all_to_all | solution.py:210
  184.0 1.8 merge_partials.1
  (17 shorter events, 0.0 us)
Async XLA Ops:
  6.5 1.0 copy-start
  6.5 78.4 %all-gather.3.cloned.1.call-start = ((), (), s32[]{:S(2)}) async-start(), calls=%async_computation.4 | async-start | bytes 2359296 | tf_op jit(solution)/shard_map/gather_kv_weight/all_gather | solution.py:193
  7.6 105.5 %copy-start.1 = (bf16[256,1024]{1,0:T(8,128)(2,1)S(1)}, bf16[256,1024]{1,0:T(8,128)(2,1)}, u32[]{:S(2)}) copy-start(bf16[256,1024]{1,0:T(8,128)(2,1)} %q_ref.1) | copy-start | bytes 1572868
  7.6 105.5 %copy-start.5 = (s32[512]{0:T(512)S(1)}, s32[512]{0:T(512)}, u32[]{:S(2)}) copy-start(s32[512]{0:T(512)} %span_ref.3) | copy-start | bytes 6148
  7.6 105.5 %copy-start.6 = (s32[512]{0:T(512)S(1)}, s32[512]{0:T(512)}, u32[]{:S(2)}) copy-start(s32[512]{0:T(512)} %len_ref.3) | copy-start | bytes 6148
  9.7 79.2 %all-to-all-start = ((bf16[16,16,128]{2,1,0:T(8,128)(2,1)}), bf16[16,16,128]{2,1,0:T(8,128)(2,1)S(1)}, u32[]{:S(2)}, u32[]{:S(2)}) async-start(bf16[16,16,128]{2,1,0:T(8,128)(2,1)} %broadcast_in_dim.4), calls=%async_computation | async-start | bytes 131072 | tf_op jit(solution)/shard_map/gather_out_weight/all_to_all | solution.py:178
  84.9 33.3 %collective-permute-start.1 = (bf16[8,512,256]{2,1,0:T(8,128)(2,1)}, bf16[8,512,256]{2,1,0:T(8,128)(2,1)}, u32[]{:S(2)}, u32[]{:S(2)}) collective-permute-start(bf16[8,512,256]{2,1,0:T(8,128)(2,1)} %bitcast.9), channel_id=1, source_target_pairs={{0,1},{1,0},{2,3},{3,2},{4,5},{5,4},{6,7},{7,6},{8,9},{9,8},{10,11... | collective-permute-start | bytes 6291464 | tf_op jit(solution)/shard_map/gather_kv_weight/ppermute | solution.py:194
  89.0 29.2 %copy-start.7 = (f32[1024]{0:T(1024)S(1)}, f32[1024]{0:T(1024)}, u32[]{:S(2)}) copy-start(f32[1024]{0:T(1024)} %param.15) | copy-start | bytes 12292
  109.7 8.5 %collective-permute-start = (bf16[16,16,16,128]{3,2,1,0:T(8,128)(2,1)S(1)}, bf16[16,16,16,128]{3,2,1,0:T(8,128)(2,1)S(1)}, u32[]{:S(2)}, u32[]{:S(2)}) collective-permute-start(bf16[16,16,16,128]{3,2,1,0:T(8,128)(2,1)S(1)} %all_to_all.20.w_mine_ref), channel_id=1, source_target_pairs={{0,1},{1,0},{2,3},{3,2},{4,5},{5,4},{6,7},{7,6},{8,9},{9,8},{10,11... | collective-permute-start | bytes 3145736 | tf_op jit(solution)/shard_map/gather_out_weight/ppermute | solution.py:199
  113.1 1.0 copy-start.2
  114.1 1.0 copy-start.3
  115.2 3.1 %copy-start.4 = (bf16[256,1024]{1,0:T(8,128)(2,1)S(1)}, bf16[256,1024]{1,0:T(8,128)(2,1)}, u32[]{:S(2)}) copy-start(bf16[256,1024]{1,0:T(8,128)(2,1)} %resid_ref.1) | copy-start | bytes 1572868
  124.2 3.7 %copy-start.8 = (bf16[64,1,1024]{2,0,1:T(8,128)(2,1)S(1)}, bf16[64,1,1024]{2,0,1:T(8,128)(2,1)}, u32[]{:S(2)}) copy-start(bf16[64,1,1024]{2,0,1:T(8,128)(2,1)} %param.17) | copy-start | bytes 393220
  124.2 21.1 %all-to-all-start.2 = ((bf16[8,256,256]{2,1,0:T(8,128)(2,1)}), bf16[8,256,256]{2,1,0:T(8,128)(2,1)S(1)}, u32[]{:S(2)}, u32[]{:S(2)}) async-start(bf16[8,256,256]{2,1,0:T(8,128)(2,1)} %encode_keyval.1), calls=%async_computation.2 | async-start | bytes 2097152 | tf_op jit(solution)/shard_map/exchange_keyval/all_to_all | solution.py:206
Sparse Core Ops, SparseCore 0:
  10.6 74.3 all-gather.2

commit v2 on v1

--- a/solution.py
+++ b/solution.py
@@ -71,29 +71,36 @@
     )(slot, span_ids, seg_lengths, q, k, v)
 
 
-def encode_kernel(core_ref, ctx_ref, w_mine_ref, w_other_ref, resid_ref, gain_ref, kv_mine_ref,
+def encode_kernel(core_ref, ctx_ref, mine_ref, other_ref, resid_ref, gain_ref, kv_mine_ref,
                   kv_other_ref, o_ref, w_ref, enc_ref):
     core = core_ref[0]
-    for part_ref, at in ((w_mine_ref, core), (w_other_ref, 1 - core)):
-        for yh in range(2):
-            for x in range(4):
-                for yl in range(2):
-                    ha = yh * 4 + x
-                    row = pl.multiple_of(32 * yl + 16 * at, 16)
-                    w_ref[:, pl.ds(row, 16), HEAD * ha:HEAD * (ha + 1)] = part_ref[ha * 2 + yl]
+    for part_ref, at in ((mine_ref, core), (other_ref, 1 - core)):
+        for ha in range(KV_HEADS):
+            for yl in range(2):
+                row = pl.multiple_of(32 * yl + 16 * at, 16)
+                w_ref[:, pl.ds(row, 16), HEAD * ha:HEAD * (ha + 1)] = (
+                    part_ref[ha * 2 + yl, :256].reshape(16, 16, HEAD))
     weight = w_ref[...].reshape(D_ENC, D_ENC)
     hidden = resid_ref[...].astype(jnp.float32) + dot(ctx_ref[...], weight)
     factor = lax.rsqrt(jnp.mean(hidden * hidden, axis=-1, keepdims=True) + 1e-05)
     encoded = (hidden * factor * gain_ref[...]).astype(jnp.bfloat16)
-    half = D_ENC // 2
-    enc_ref[0] = encoded[:, :half]
-    enc_ref[1] = encoded[:, half:]
-    mine, other = enc_ref[core], enc_ref[1 - core]
+    for piece in range(4):
+        enc_ref[piece] = encoded[:, piece * 256:(piece + 1) * 256]
+    near, far = enc_ref[core], enc_ref[1 - core]
+    near_last, far_last = enc_ref[2 + core], enc_ref[3 - core]
+
+    def first_rows(ref, h):
+        return jnp.concatenate(
+            [jnp.concatenate([ref[2 * h + yl, 256:384], ref[2 * h + yl, 384:]], axis=1) for yl in range(2)],
+            axis=0)
+
     for h in range(KV_HEADS):
-        o_ref[h] = (dot(mine, kv_mine_ref[h]) + dot(other, kv_other_ref[h])).astype(jnp.bfloat16)
-
-
-def encode(core, ctx, w_mine, w_other, resid, gain, kv_mine, kv_other):
+        total = dot(near, first_rows(mine_ref, h)) + dot(far, first_rows(other_ref, h))
+        total += dot(near_last, kv_mine_ref[h]) + dot(far_last, kv_other_ref[h])
+        o_ref[h] = total.astype(jnp.bfloat16)
+
+
+def encode(core, ctx, mine, other, resid, gain, kv_mine, kv_other):
     smem = pl.BlockSpec(memory_space=pltpu.SMEM)
     vmem = pl.BlockSpec(memory_space=pltpu.VMEM)
     return pl.pallas_call(
@@ -102,12 +109,12 @@
         in_specs=[smem] + [vmem] * 7,
         out_specs=vmem,
         scratch_shapes=[pltpu.VMEM((16, 64, D_ENC), jnp.bfloat16),
-                        pltpu.VMEM((2, SEG_LEN, D_ENC // 2), jnp.bfloat16)],
+                        pltpu.VMEM((4, SEG_LEN, 256), jnp.bfloat16)],
         compiler_params=params(),
         cost_estimate=pl.CostEstimate(
             flops=6 * SEG_LEN * D_ENC * D_ENC, bytes_accessed=8 * D_ENC * D_ENC, transcendentals=SEG_LEN),
         name="encode_keyval",
-    )(core, ctx, w_mine, w_other, resid, gain, kv_mine, kv_other)
+    )(core, ctx, mine, other, resid, gain, kv_mine, kv_other)
 
 
 def cross_kernel(slots, first_ref, span_ref, len_ref, q_ref, kv_ref, o_ref):
@@ -120,23 +127,28 @@
     bias = jnp.concatenate(bias, axis=1)
     keys = kv_ref[:, :, :HEAD].reshape(slots * SEG_LEN, HEAD)
     values = kv_ref[:, :, HEAD:].reshape(slots * SEG_LEN, HEAD)
-    rows = 128
-    queries = rows // GROUP
+    rows = 2 * QTAIL
     column = lax.broadcasted_iota(jnp.int32, (rows, HEAD), 1)
-    for b in range(QTAIL // queries):
+    levels = jnp.zeros((rows, HEAD), jnp.float32)
+
+    def put(at, block):
+        block = block.reshape(2, QTAIL, HEAD)
+        o_ref[:, :, at * HEAD:(at + 1) * HEAD] = jnp.stack([block[0], block[1]], axis=1).astype(jnp.bfloat16)
+
+    for b in range(GROUP // 2):
         q = q_ref[b * rows:(b + 1) * rows]
         scores = dot_t(q, keys) + bias
         top = jnp.max(scores, axis=-1, keepdims=True)
         expo = jnp.exp((scores - top) * scale)
         total = jnp.sum(expo, axis=-1, keepdims=True)
-        average = dot(expo.astype(jnp.bfloat16), values) / total
+        put(b, dot(expo.astype(jnp.bfloat16), values) / total)
         level = jnp.broadcast_to(top * scale + jnp.log(total), (rows, HEAD))
         high = level.astype(jnp.bfloat16).astype(jnp.float32)
         middle = (level - high).astype(jnp.bfloat16).astype(jnp.float32)
         rest = level - high - middle
-        split = jnp.where(column == 0, high, jnp.where(column == 1, middle, rest))
-        o_ref[b * queries:(b + 1) * queries, :GROUP] = average.reshape(queries, GROUP, HEAD).astype(jnp.bfloat16)
-        o_ref[b * queries:(b + 1) * queries, GROUP:] = split.reshape(queries, GROUP, HEAD).astype(jnp.bfloat16)
+        for k, part in enumerate((high, middle, rest)):
+            levels = jnp.where(column == 3 * b + k, part, levels)
+    put(GROUP // 2, levels)
 
 
 def cross_attention(first, span_ids, seg_lengths, q, kv):
@@ -145,7 +157,7 @@
     slots = kv.shape[0]
     return pl.pallas_call(
         functools.partial(cross_kernel, slots),
-        out_shape=jax.ShapeDtypeStruct((QTAIL, 2 * GROUP, HEAD), jnp.bfloat16),
+        out_shape=jax.ShapeDtypeStruct((QTAIL, 2, 640), jnp.bfloat16),
         in_specs=[smem, smem, smem, vmem, vmem],
         out_specs=vmem,
         compiler_params=params(),
@@ -154,11 +166,11 @@
 
 
 def merge_kernel(part_ref, o_ref):
-    average = part_ref[:, :GROUP].astype(jnp.float32)
-    pieces = part_ref[:, GROUP:, :3].astype(jnp.float32)
-    level = jnp.sum(pieces, axis=-1, keepdims=True)
-    weight = jnp.exp(level - jnp.max(level, axis=0, keepdims=True))
-    o_ref[...] = jnp.sum(average * weight, axis=0) / jnp.sum(weight, axis=0)
+    for b in range(GROUP // 2):
+        level = jnp.sum(part_ref[:, :, 512 + 3 * b:515 + 3 * b].astype(jnp.float32), axis=-1, keepdims=True)
+        weight = jnp.exp(level - jnp.max(level, axis=0, keepdims=True))
+        average = part_ref[:, :, HEAD * b:HEAD * (b + 1)].astype(jnp.float32)
+        o_ref[2 * b:2 * b + 2] = jnp.sum(average * weight, axis=0) / jnp.sum(weight, axis=0)
 
 
 def merge(parts):
@@ -187,25 +199,29 @@
 
     swap = functools.partial(lax.ppermute, axis_name="c", perm=[(0, 1), (1, 0)])
 
-    with jax.named_scope("gather_kv_weight"):
-        half = D_ENC // 2
-        kv_half = lax.dynamic_slice_in_dim(kv_weight.reshape(D_ENC, 2 * HEAD), core * half, half, 0)
-        kv_mine = lax.all_gather(kv_half, HA)
+    yl = lax.axis_index("yl")
+
+    with jax.named_scope("gather_weights"):
+        over_z = spread(lax.dynamic_slice_in_dim(out_weight, ha * HEAD, HEAD, 1), "z")
+        own = kv_weight.reshape(D_ENC, 2 * HEAD)
+        first = lax.dynamic_slice_in_dim(own, core * 256 + yl * 128, 128, 0)
+        last = lax.dynamic_slice_in_dim(own, 512 + core * 256, 256, 0)
+        kv_mine = lax.all_gather(last, HA)
+        block = jnp.concatenate([over_z.reshape(256, HEAD), first[:, :HEAD], first[:, HEAD:]], axis=0)
+        mine = spread(block, PLANE)
+        kv_mine, mine, enc_query = lax.optimization_barrier((kv_mine, mine, enc_query))
+        other = swap(mine)
         kv_other = swap(kv_mine)
-
-    with jax.named_scope("gather_out_weight"):
-        mine = lax.dynamic_slice_in_dim(out_weight, ha * HEAD, HEAD, 1)
-        w_mine = spread(spread(mine, "z"), PLANE).reshape(16, 16, 16, HEAD)
-        w_other = swap(w_mine)
 
     slot = (ha * sa_count + sa).reshape(1).astype(jnp.int32)
     context = encoder_attention(slot, span_ids, seg_lengths, enc_query, enc_key, enc_value)
-    keyval = encode(core.reshape(1).astype(jnp.int32), context, w_mine, w_other, enc_resid,
+    keyval = encode(core.reshape(1).astype(jnp.int32), context, mine, other, enc_resid,
                     norm_gain.reshape(1, D_ENC), kv_mine, kv_other)
     with jax.named_scope("exchange_keyval"):
         keyval = lax.all_to_all(keyval, HA, 0, 0, tiled=True)
     first = jnp.stack([sa, sa_count]).astype(jnp.int32)
-    parts = cross_attention(first, span_ids, seg_lengths, cross_query.reshape(QTAIL * GROUP, HEAD), keyval)
+    query = cross_query.reshape(QTAIL, GROUP, HEAD).transpose(1, 0, 2).reshape(GROUP * QTAIL, HEAD)
+    parts = cross_attention(first, span_ids, seg_lengths, query, keyval)
     with jax.named_scope("exchange_partials"):
         parts = lax.all_to_all(parts, SA, 0, 0, tiled=True)
     return merge(parts).reshape(1, 1, GROUP * HEAD)

time: 193 us -> 188 us (0.974)
  blocking collectives: 56.3 us -> 32.5 us
  waiting for transfers between devices: 76.8 us -> 88.9 us
  starting transfers between devices: 26.6 us -> 31.9 us
    all_to_all x1 -> x0, blocking collectives: 20.7 us -> none  [spread(): return lax.all_to_all(copies, axes, 0, 0, tiled=True)]
    all_to_all x1 -> x2, waiting for transfers between devices: 0.01 us -> 11.5 us  [spread(): return lax.all_to_all(copies, axes, 0, 0, tiled=True)]
    all_to_all x1 -> x2, starting transfers between devices: 15.7 us -> 22.7 us  [spread(): return lax.all_to_all(copies, axes, 0, 0, tiled=True)]
    all_to_all x1, blocking collectives: 35.6 us -> 32.5 us  [local(): parts = lax.all_to_all(parts, SA, 0, 0, tiled=True)]
    ppermute x1, starting transfers between devices: 3.88 us -> 1.92 us  [local(): kv_other = swap(kv_mine)]
  transfers between devices with their start and end apart: 5 -> 6, of which waited for: 2 -> 3; matrix products, arithmetic and copies ran while one was open for 1% -> 0% of each run, Pallas kernels for 2% -> 2%
where the time goes in v2:
time: 188 us
  waiting for transfers between devices  88.9 us (47%)
  blocking collectives  32.5 us (17%)
  starting transfers between devices  31.9 us (17%)
  Pallas kernels  14.6 us (8%)
  between operations  13.6 us (7%)
  local copies, waits for them, and re-layouts  5.93 us (3%)
    all_gather x1, waiting for transfers between devices, local(): kv_mine = lax.all_gather(last, HA)  60.3 us
    all_to_all x1, blocking collectives, local(): parts = lax.all_to_all(parts, SA, 0, 0, tiled=True)  32.5 us
    all_to_all x2, starting transfers between devices, spread(): return lax.all_to_all(copies, axes, 0, 0, tiled=True)  22.7 us
    all_to_all x1, waiting for transfers between devices, local(): keyval = lax.all_to_all(keyval, HA, 0, 0, tiled=True)  17.1 us
    all_to_all x2, waiting for transfers between devices, spread(): return lax.all_to_all(copies, axes, 0, 0, tiled=True)  11.5 us
    pallas_call x1, Pallas kernels, encode(): pl.pallas_call(encode_kernel, out_shape=jax.ShapeDtypeStruct((KV_HEADS, S...  5.92 us
  transfers between devices with their start and end apart: 6, of which 3 were waited for; matrix products, arithmetic and copies ran while one was open for 0% of the time, Pallas kernels for 2%

profile of v2, /device:TPU:1, one launch (start us, length us, event | category | flops | bytes accessed | tf_op | source)
XLA Modules:
  0.0 187.6 jit_solution(806381625486438092)
XLA Ops:
  6.5 0.7 constant_dynamic-slice_fusion
  7.3 0.6 broadcast_in_dim.4
  7.9 15.7 %all-to-all-start = ((bf16[16,16,128]{2,1,0:T(8,128)(2,1)}), bf16[16,16,128]{2,1,0:T(8,128)(2,1)S(1)}, u32[]{:S(2)}, u32[]{:S(2)}) async-start(bf16[16,16,128]{2,1,0:T(8,128)(2,1)} %broadcast_in_dim.4), calls=%async_computation | async-start | bytes 131072 | tf_op jit(solution)/shard_map/gather_weights/all_to_all | solution.py:190
  23.7 11.5 %all-to-all-done = bf16[16,16,128]{2,1,0:T(8,128)(2,1)S(1)} async-done(((bf16[16,16,128]{2,1,0:T(8,128)(2,1)}), bf16[16,16,128]{2,1,0:T(8,128)(2,1)S(1)}, u32[]{:S(2)}, u32[]{:S(2)}) %all-to-all-start) | async-done | bytes 65568 | tf_op jit(solution)/shard_map/gather_weights/all_to_all | solution.py:190
  35.3 1.7 broadcast_in_dim.5
  37.0 6.9 %all-to-all-start.1 = ((bf16[16,512,128]{2,1,0:T(8,128)(2,1)}), bf16[16,512,128]{2,1,0:T(8,128)(2,1)}, u32[]{:S(2)}, u32[]{:S(2)}) async-start(bf16[16,512,128]{2,1,0:T(8,128)(2,1)} %broadcast_in_dim.5), calls=%async_computation.1 | async-start | bytes 4194304 | tf_op jit(solution)/shard_map/gather_weights/all_to_all | solution.py:190
  43.9 0.0 copy-start.8
  43.9 0.0 all-gather.3.cloned.1.call-start
  44.0 0.7 constant_dynamic-slice_fusion.1
  44.6 0.0 all-gather.3.cloned.1.call-update
  44.7 60.3 %all-gather.3.cloned.1.call-done = bf16[2048,1,256]{2,0,1:T(8,128)(2,1)} async-done(((bf16[256,1,256]{2,0,1:T(8,128)(2,1)}), bf16[2048,1,256]{2,0,1:T(8,128)(2,1)}) %all-gather.3.cloned.1.call-update) | async-done | bytes 1048592 | tf_op jit(solution)/shard_map/gather_weights/all_gather | solution.py:209
  104.9 3.6 %collective-permute-start = (bf16[16,512,128]{2,1,0:T(8,128)(2,1)}, bf16[16,512,128]{2,1,0:T(8,128)(2,1)}, u32[]{:S(2)}, u32[]{:S(2)}) collective-permute-start(bf16[16,512,128]{2,1,0:T(8,128)(2,1)} %all-to-all-done.1.mine_ref), channel_id=1, source_target_pairs={{0,1},{1,0},{2,3},{3,2},{4,5},{5,4},{6,7},{7,6},{8,9},{9,8},{10,11... | collective-permute-start | bytes 6291464 | tf_op jit(solution)/shard_map/gather_weights/ppermute | solution.py:213
  108.6 1.9 %collective-permute-start.1 = (bf16[8,256,256]{2,1,0:T(8,128)(2,1)}, bf16[8,256,256]{2,1,0:T(8,128)(2,1)S(1)}, u32[]{:S(2)}, u32[]{:S(2)}) collective-permute-start(bf16[8,256,256]{2,1,0:T(8,128)(2,1)} %bitcast.16), channel_id=1, source_target_pairs={{0,1},{1,0},{2,3},{3,2},{4,5},{5,4},{6,7},{7,6},{8,9},{9,8},{10,11... | collective-permute-start | bytes 3145736 | tf_op jit(solution)/shard_map/gather_weights/ppermute | solution.py:214
  110.5 0.0 copy-start.3
  110.5 1.0 copy-done.3
  111.6 1.0 copy-done.4
  112.6 3.1 %encoder_attention.1.ctx_ref = bf16[256,1024]{1,0:T(8,128)(2,1)S(1)} custom-call(s32[1]{0:T(128)} %bitcast.4.slot_ref, s32[512]{0:T(512)S(1)} %copy-done.6, s32[512]{0:T(512)S(1)} %copy-done.7, bf16[256,1024]{1,0:T(8,128)(2,1)S(1)} %copy-done.2, bf16[256,1024]{1,0:T(8,128)(2,1)S(1)} %copy-done.3, bf16[256,1024]{1,0:T(8,128)(2,1)S(1)} %copy-done.4), custom_call_target="tpu_custom_call" | custom-call | flops 536870912 | bytes 2097152 | tf_op jit(solution)/shard_map/encoder_attention/pallas_call | solution.py:61
  115.7 5.9 %encode_keyval.1 = bf16[8,256,256]{2,1,0:T(8,128)(2,1)} custom-call(s32[1]{0:T(128)} %bitcast.3.core_ref, bf16[256,1024]{1,0:T(8,128)(2,1)S(1)} %encoder_attention.1.ctx_ref, bf16[16,512,128]{2,1,0:T(8,128)(2,1)} %all-to-all-done.1.mine_ref, bf16[16,512,128]{2,1,0:T(8,128)(2,1)} %collective-permute-done.other_ref, bf16[256,1024]{1,0:T(8,128)(2,1)S(1)} %copy-done.5, ...), custom_call_target="tpu_custom_call" | custom-call | flops 1610612736 | bytes 8388608 | tf_op jit(solution)/shard_map/encode_keyval/pallas_call | solution.py:106
  121.7 3.7 %all-to-all-start.2 = ((bf16[8,256,256]{2,1,0:T(8,128)(2,1)}), bf16[8,256,256]{2,1,0:T(8,128)(2,1)S(1)}, u32[]{:S(2)}, u32[]{:S(2)}) async-start(bf16[8,256,256]{2,1,0:T(8,128)(2,1)} %encode_keyval.1), calls=%async_computation.2 | async-start | bytes 2097152 | tf_op jit(solution)/shard_map/exchange_keyval/all_to_all | solution.py:221
  125.4 0.1 pad_add_fusion.first_ref
  125.5 17.1 %all-to-all-done.2.kv_ref = bf16[8,256,256]{2,1,0:T(8,128)(2,1)S(1)} async-done(((bf16[8,256,256]{2,1,0:T(8,128)(2,1)}), bf16[8,256,256]{2,1,0:T(8,128)(2,1)S(1)}, u32[]{:S(2)}, u32[]{:S(2)}) %all-to-all-start.2) | async-done | bytes 1048608 | tf_op jit(solution)/shard_map/exchange_keyval/all_to_all | solution.py:221
  142.6 3.3 %cross_attention.1 = bf16[64,2,640]{2,1,0:T(2,128)(2,1)S(1)} custom-call(s32[2]{0:T(128)S(1)} %pad_add_fusion.first_ref, s32[512]{0:T(512)S(1)} %copy-done.6, s32[512]{0:T(512)S(1)} %copy-done.7, bf16[512,128]{1,0:T(8,128)(2,1)S(1)} %bitcast.18, bf16[8,256,256]{2,1,0:T(8,128)(2,1)S(1)} %all-to-all-done.2.kv_ref), custom_call_target="tpu_custom_call" | custom-call | tf_op jit(solution)/shard_map/cross_attention/pallas_call | solution.py:158
  145.9 32.5 %all_to_all.20.part_ref = bf16[64,2,640]{2,1,0:T(2,128)(2,1)} all-to-all(bf16[64,2,640]{2,1,0:T(2,128)(2,1)S(1)} %cross_attention.1), channel_id=1, replica_groups=mesh['yh'=2,'x'=4,'z'=16,'yl'=2,'c'=2] {'z','yl','c'}, dimensions={0} | all-to-all | bytes 327680 | tf_op jit(solution)/shard_map/exchange_partials/all_to_all | solution.py:226
  178.4 2.3 %merge_partials.1 = f32[8,128]{1,0:T(8,128)} custom-call(bf16[64,2,640]{2,1,0:T(2,128)(2,1)} %all_to_all.20.part_ref), custom_call_target="tpu_custom_call" | custom-call | tf_op jit(solution)/shard_map/merge_partials/pallas_call | solution.py:178
  (24 shorter events, 0.1 us)
Async XLA Ops:
  6.5 17.1 %copy-start = (bf16[1024,1,256]{2,0,1:T(8,128)(2,1)S(1)}, bf16[1024,1,256]{2,0,1:T(8,128)(2,1)}, u32[]{:S(2)}) copy-start(bf16[1024,1,256]{2,0,1:T(8,128)(2,1)} %param.16) | copy-start | bytes 1572868
  7.9 27.3 %all-to-all-start = ((bf16[16,16,128]{2,1,0:T(8,128)(2,1)}), bf16[16,16,128]{2,1,0:T(8,128)(2,1)S(1)}, u32[]{:S(2)}, u32[]{:S(2)}) async-start(bf16[16,16,128]{2,1,0:T(8,128)(2,1)} %broadcast_in_dim.4), calls=%async_computation | async-start | bytes 131072 | tf_op jit(solution)/shard_map/gather_weights/all_to_all | solution.py:190
  37.0 73.5 %copy-start.2 = (bf16[256,1024]{1,0:T(8,128)(2,1)S(1)}, bf16[256,1024]{1,0:T(8,128)(2,1)}, u32[]{:S(2)}) copy-start(bf16[256,1024]{1,0:T(8,128)(2,1)} %q_ref) | copy-start | bytes 1572868
  37.0 73.5 %copy-start.6 = (s32[512]{0:T(512)S(1)}, s32[512]{0:T(512)}, u32[]{:S(2)}) copy-start(s32[512]{0:T(512)} %span_ref.3) | copy-start | bytes 6148
  37.0 73.6 %copy-start.7 = (s32[512]{0:T(512)S(1)}, s32[512]{0:T(512)}, u32[]{:S(2)}) copy-start(s32[512]{0:T(512)} %len_ref.3) | copy-start | bytes 6148
  37.0 68.0 %all-to-all-start.1 = ((bf16[16,512,128]{2,1,0:T(8,128)(2,1)}), bf16[16,512,128]{2,1,0:T(8,128)(2,1)}, u32[]{:S(2)}, u32[]{:S(2)}) async-start(bf16[16,512,128]{2,1,0:T(8,128)(2,1)} %broadcast_in_dim.5), calls=%async_computation.1 | async-start | bytes 4194304 | tf_op jit(solution)/shard_map/gather_weights/all_to_all | solution.py:190
  43.9 71.8 %copy-start.8 = (f32[1024]{0:T(1024)S(1)}, f32[1024]{0:T(1024)}, u32[]{:S(2)}) copy-start(f32[1024]{0:T(1024)} %param.15) | copy-start | bytes 12292
  43.9 61.0 %all-gather.3.cloned.1.call-start = ((), (), s32[]{:S(2)}) async-start(), calls=%async_computation.4 | async-start | bytes 1179648 | tf_op jit(solution)/shard_map/gather_weights/all_gather | solution.py:209
  104.9 10.8 %copy-start.1 = (bf16[2048,1,256]{2,0,1:T(8,128)(2,1)S(1)}, bf16[2048,1,256]{2,0,1:T(8,128)(2,1)}, u32[]{:S(2)}) copy-start(bf16[2048,1,256]{2,0,1:T(8,128)(2,1)} %all-gather.3.cloned.1.call-done) | copy-start | bytes 3145732
  104.9 10.8 %collective-permute-start = (bf16[16,512,128]{2,1,0:T(8,128)(2,1)}, bf16[16,512,128]{2,1,0:T(8,128)(2,1)}, u32[]{:S(2)}, u32[]{:S(2)}) collective-permute-start(bf16[16,512,128]{2,1,0:T(8,128)(2,1)} %all-to-all-done.1.mine_ref), channel_id=1, source_target_pairs={{0,1},{1,0},{2,3},{3,2},{4,5},{5,4},{6,7},{7,6},{8,9},{9,8},{10,11... | collective-permute-start | bytes 6291464 | tf_op jit(solution)/shard_map/gather_weights/ppermute | solution.py:213
  108.6 7.1 %collective-permute-start.1 = (bf16[8,256,256]{2,1,0:T(8,128)(2,1)}, bf16[8,256,256]{2,1,0:T(8,128)(2,1)S(1)}, u32[]{:S(2)}, u32[]{:S(2)}) collective-permute-start(bf16[8,256,256]{2,1,0:T(8,128)(2,1)} %bitcast.16), channel_id=1, source_target_pairs={{0,1},{1,0},{2,3},{3,2},{4,5},{5,4},{6,7},{7,6},{8,9},{9,8},{10,11... | collective-permute-start | bytes 3145736 | tf_op jit(solution)/shard_map/gather_weights/ppermute | solution.py:214
  110.5 1.0 copy-start.3
  111.6 1.0 copy-start.4
  112.6 3.1 %copy-start.5 = (bf16[256,1024]{1,0:T(8,128)(2,1)S(1)}, bf16[256,1024]{1,0:T(8,128)(2,1)}, u32[]{:S(2)}) copy-start(bf16[256,1024]{1,0:T(8,128)(2,1)} %resid_ref.1) | copy-start | bytes 1572868
  121.6 3.7 %copy-start.9 = (bf16[64,1,1024]{2,0,1:T(8,128)(2,1)S(1)}, bf16[64,1,1024]{2,0,1:T(8,128)(2,1)}, u32[]{:S(2)}) copy-start(bf16[64,1,1024]{2,0,1:T(8,128)(2,1)} %param.17) | copy-start | bytes 393220
  121.7 21.0 %all-to-all-start.2 = ((bf16[8,256,256]{2,1,0:T(8,128)(2,1)}), bf16[8,256,256]{2,1,0:T(8,128)(2,1)S(1)}, u32[]{:S(2)}, u32[]{:S(2)}) async-start(bf16[8,256,256]{2,1,0:T(8,128)(2,1)} %encode_keyval.1), calls=%async_computation.2 | async-start | bytes 2097152 | tf_op jit(solution)/shard_map/exchange_keyval/all_to_all | solution.py:221
Sparse Core Ops, SparseCore 0:
  48.0 56.9 all-gather.2

commit v3 on v2

--- a/solution.py
+++ b/solution.py
@@ -71,36 +71,26 @@
     )(slot, span_ids, seg_lengths, q, k, v)
 
 
-def encode_kernel(core_ref, ctx_ref, mine_ref, other_ref, resid_ref, gain_ref, kv_mine_ref,
+def encode_kernel(place_ref, ctx_ref, mine_ref, other_ref, resid_ref, gain_ref, kv_mine_ref,
                   kv_other_ref, o_ref, w_ref, enc_ref):
-    core = core_ref[0]
+    z, core = place_ref[0], place_ref[1]
     for part_ref, at in ((mine_ref, core), (other_ref, 1 - core)):
         for ha in range(KV_HEADS):
+            plane = lax.rem(z + 32 - 2 * ha - at, 16)
             for yl in range(2):
-                row = pl.multiple_of(32 * yl + 16 * at, 16)
-                w_ref[:, pl.ds(row, 16), HEAD * ha:HEAD * (ha + 1)] = (
-                    part_ref[ha * 2 + yl, :256].reshape(16, 16, HEAD))
-    weight = w_ref[...].reshape(D_ENC, D_ENC)
-    hidden = resid_ref[...].astype(jnp.float32) + dot(ctx_ref[...], weight)
+                w_ref[pl.ds(pl.multiple_of(64 * plane + 32 * yl, 32), 32), :] = part_ref[ha * 2 + yl]
+    hidden = resid_ref[...].astype(jnp.float32) + dot(ctx_ref[...], w_ref[...])
     factor = lax.rsqrt(jnp.mean(hidden * hidden, axis=-1, keepdims=True) + 1e-05)
     encoded = (hidden * factor * gain_ref[...]).astype(jnp.bfloat16)
-    for piece in range(4):
-        enc_ref[piece] = encoded[:, piece * 256:(piece + 1) * 256]
+    half = D_ENC // 2
+    enc_ref[0] = encoded[:, :half]
+    enc_ref[1] = encoded[:, half:]
     near, far = enc_ref[core], enc_ref[1 - core]
-    near_last, far_last = enc_ref[2 + core], enc_ref[3 - core]
-
-    def first_rows(ref, h):
-        return jnp.concatenate(
-            [jnp.concatenate([ref[2 * h + yl, 256:384], ref[2 * h + yl, 384:]], axis=1) for yl in range(2)],
-            axis=0)
-
     for h in range(KV_HEADS):
-        total = dot(near, first_rows(mine_ref, h)) + dot(far, first_rows(other_ref, h))
-        total += dot(near_last, kv_mine_ref[h]) + dot(far_last, kv_other_ref[h])
-        o_ref[h] = total.astype(jnp.bfloat16)
-
-
-def encode(core, ctx, mine, other, resid, gain, kv_mine, kv_other):
+        o_ref[h] = (dot(near, kv_mine_ref[h]) + dot(far, kv_other_ref[h])).astype(jnp.bfloat16)
+
+
+def encode(place, ctx, mine, other, resid, gain, kv_mine, kv_other):
     smem = pl.BlockSpec(memory_space=pltpu.SMEM)
     vmem = pl.BlockSpec(memory_space=pltpu.VMEM)
     return pl.pallas_call(
@@ -108,13 +98,13 @@
         out_shape=jax.ShapeDtypeStruct((KV_HEADS, SEG_LEN, 2 * HEAD), jnp.bfloat16),
         in_specs=[smem] + [vmem] * 7,
         out_specs=vmem,
-        scratch_shapes=[pltpu.VMEM((16, 64, D_ENC), jnp.bfloat16),
-                        pltpu.VMEM((4, SEG_LEN, 256), jnp.bfloat16)],
+        scratch_shapes=[pltpu.VMEM((D_ENC, D_ENC), jnp.bfloat16),
+                        pltpu.VMEM((2, SEG_LEN, D_ENC // 2), jnp.bfloat16)],
         compiler_params=params(),
         cost_estimate=pl.CostEstimate(
             flops=6 * SEG_LEN * D_ENC * D_ENC, bytes_accessed=8 * D_ENC * D_ENC, transcendentals=SEG_LEN),
         name="encode_keyval",
-    )(core, ctx, mine, other, resid, gain, kv_mine, kv_other)
+    )(place, ctx, mine, other, resid, gain, kv_mine, kv_other)
 
 
 def cross_kernel(slots, first_ref, span_ref, len_ref, q_ref, kv_ref, o_ref):
@@ -197,26 +187,36 @@
     sa_count = lax.axis_size(SA)
     core = lax.axis_index("c")
 
+    yl, z = lax.axis_index("yl"), lax.axis_index("z")
     swap = functools.partial(lax.ppermute, axis_name="c", perm=[(0, 1), (1, 0)])
 
-    yl = lax.axis_index("yl")
-
-    with jax.named_scope("gather_weights"):
-        over_z = spread(lax.dynamic_slice_in_dim(out_weight, ha * HEAD, HEAD, 1), "z")
-        own = kv_weight.reshape(D_ENC, 2 * HEAD)
-        first = lax.dynamic_slice_in_dim(own, core * 256 + yl * 128, 128, 0)
-        last = lax.dynamic_slice_in_dim(own, 512 + core * 256, 256, 0)
-        kv_mine = lax.all_gather(last, HA)
-        block = jnp.concatenate([over_z.reshape(256, HEAD), first[:, :HEAD], first[:, HEAD:]], axis=0)
-        mine = spread(block, PLANE)
-        kv_mine, mine, enc_query = lax.optimization_barrier((kv_mine, mine, enc_query))
-        other = swap(mine)
+    with jax.named_scope("gather_kv_weight"):
+        quarter = lax.dynamic_slice_in_dim(
+            kv_weight.reshape(D_ENC, 2 * HEAD), core * 512 + yl * 256, 256, 0)
+        kv_mine = spread(quarter, PLANE)
+    with jax.named_scope("out_weight_over_z"):
+        pair = lax.all_gather(out_weight, "c", axis=0, tiled=True)
+        hops = []
+        for ha_at in range(8):
+            for z_at in range(16):
+                for c_at in range(2):
+                    there = (z_at + 2 * ha_at + c_at) % 16
+                    hops.append(((ha_at * 16 + z_at) * 2 + c_at, (ha_at * 16 + there) * 2 + c_at))
+        pair = lax.ppermute(pair, ("yh", "x", "z", "c"), hops)
+    kv_mine, pair, enc_query = lax.optimization_barrier((kv_mine, pair, enc_query))
+    with jax.named_scope("out_weight_over_plane"):
+        w_mine = spread(pair, PLANE)
+    kv_mine = kv_mine.reshape(KV_HEADS, D_ENC // 2, 2 * HEAD)
+    with jax.named_scope("swap_kv_weight"):
         kv_other = swap(kv_mine)
-
     slot = (ha * sa_count + sa).reshape(1).astype(jnp.int32)
     context = encoder_attention(slot, span_ids, seg_lengths, enc_query, enc_key, enc_value)
-    keyval = encode(core.reshape(1).astype(jnp.int32), context, mine, other, enc_resid,
-                    norm_gain.reshape(1, D_ENC), kv_mine, kv_other)
+    w_mine, kv_other, context = lax.optimization_barrier((w_mine, kv_other, context))
+    with jax.named_scope("swap_out_weight"):
+        w_other = swap(w_mine)
+    place = jnp.stack([z, core]).astype(jnp.int32)
+    keyval = encode(place, context, w_mine, w_other, enc_resid, norm_gain.reshape(1, D_ENC),
+                    kv_mine, kv_other)
     with jax.named_scope("exchange_keyval"):
         keyval = lax.all_to_all(keyval, HA, 0, 0, tiled=True)
     first = jnp.stack([sa, sa_count]).astype(jnp.int32)

time: 188 us -> 141 us (0.75)
  waiting for transfers between devices: 88.9 us -> 52.2 us
  between operations: 13.6 us -> 0.2 us
  blocking collectives: 32.5 us -> 41.3 us
  starting transfers between devices: 31.9 us -> 26.8 us
    all_gather x1 -> x0, waiting for transfers between devices: 60.3 us -> none  [local(): kv_mine = lax.all_gather(last, HA)]
    all_to_all x2, waiting for transfers between devices: 11.5 us -> 24.3 us  [spread(): return lax.all_to_all(copies, axes, 0, 0, tiled=True)]
    all_to_all x2, starting transfers between devices: 22.7 us -> 11.6 us  [spread(): return lax.all_to_all(copies, axes, 0, 0, tiled=True)]
    ppermute x1 -> x2, waiting for transfers between devices: 0.01 us -> 10.7 us  [the longest x1 8.5 us: local(): pair = lax.ppermute(pair, ('yh', 'x', 'z', 'c'), hops)]
    all_gather x0 -> x1, blocking collectives: none -> 5.34 us  [local(): pair = lax.all_gather(out_weight, 'c', axis=0, tiled=True)]
    ppermute x1, starting transfers between devices: 1.92 us -> 6.8 us  [local(): kv_other = swap(kv_mine)]
    all_to_all x1, blocking collectives: 32.5 us -> 36 us  [local(): parts = lax.all_to_all(parts, SA, 0, 0, tiled=True)]
    ppermute x1 -> x2, starting transfers between devices: 3.61 us -> 4.8 us  [the longest x1 2.89 us: local(): w_other = swap(w_mine)]
  transfers between devices with their start and end apart: 6 -> 6, of which waited for: 3 -> 5; matrix products, arithmetic and copies ran while one was open for 0% -> 1% of each run, Pallas kernels for 2% -> 2%
where the time goes in v3:
time: 141 us
  waiting for transfers between devices  52.2 us (37%)
  blocking collectives  41.3 us (29%)
  starting transfers between devices  26.8 us (19%)
  Pallas kernels  14.2 us (10%)
  local copies, waits for them, and re-layouts  5.83 us (4%)
    all_to_all x1, blocking collectives, local(): parts = lax.all_to_all(parts, SA, 0, 0, tiled=True)  36 us
    all_to_all x2, waiting for transfers between devices, spread(): return lax.all_to_all(copies, axes, 0, 0, tiled=True)  24.3 us
    all_to_all x1, waiting for transfers between devices, local(): keyval = lax.all_to_all(keyval, HA, 0, 0, tiled=True)  17.2 us
    all_to_all x2, starting transfers between devices, spread(): return lax.all_to_all(copies, axes, 0, 0, tiled=True)  11.6 us
    ppermute x1, waiting for transfers between devices, local(): pair = lax.ppermute(pair, ('yh', 'x', 'z', 'c'), hops)  8.5 us
    ppermute x1, starting transfers between devices, local(): kv_other = swap(kv_mine)  6.8 us
    pallas_call x1, Pallas kernels, encode(): pl.pallas_call(encode_kernel, out_shape=jax.ShapeDtypeStruct((KV_HEADS, S...  5.46 us
    all_gather x1, blocking collectives, local(): pair = lax.all_gather(out_weight, 'c', axis=0, tiled=True)  5.34 us
  transfers between devices with their start and end apart: 6, of which 5 were waited for; matrix products, arithmetic and copies ran while one was open for 1% of the time, Pallas kernels for 2%

profile of v3, /device:TPU:1, one launch (start us, length us, event | category | flops | bytes accessed | tf_op | source)
XLA Modules:
  0.0 140.7 jit_solution(9300656885398138583)
XLA Ops:
  0.0 1.0 copy-done
  1.1 1.5 %broadcast_in_dim.7 = bf16[16,256,256]{2,1,0:T(8,128)(2,1)} broadcast(bf16[256,256]{1,0:T(8,128)(2,1)S(1)} %dynamic-slice_bitcast_fusion), dimensions={1,2} | broadcast | bytes 2228224 | tf_op jit(solution)/shard_map/gather_kv_weight/broadcast_in_dim | solution.py:179
  2.6 7.8 %all-to-all-start = ((bf16[16,256,256]{2,1,0:T(8,128)(2,1)}), bf16[16,256,256]{2,1,0:T(8,128)(2,1)}, u32[]{:S(2)}, u32[]{:S(2)}) async-start(bf16[16,256,256]{2,1,0:T(8,128)(2,1)} %broadcast_in_dim.7), calls=%async_computation | async-start | bytes 4194304 | tf_op jit(solution)/shard_map/gather_kv_weight/all_to_all | solution.py:180
  10.4 5.3 %all_gather.3 = bf16[32,1024]{1,0:T(8,128)(2,1)S(1)} all-gather(bf16[16,1024]{1,0:T(8,128)(2,1)S(1)} %copy-done.9), channel_id=1, replica_groups=mesh['yh'=2,'x'=4,'z'=16,'yl'=2,'c'=2] {'c'}, dimensions={0}, use_global_device_ids=true | all-gather | bytes 98304 | tf_op jit(solution)/shard_map/out_weight_over_z/all_gather | solution.py:198
  15.8 1.9 %collective-permute-start = (bf16[32,1024]{1,0:T(8,128)(2,1)S(1)}, bf16[32,1024]{1,0:T(8,128)(2,1)S(1)}, u32[]{:S(2)}, u32[]{:S(2)}) collective-permute-start(bf16[32,1024]{1,0:T(8,128)(2,1)S(1)} %all_gather.3), channel_id=1, source_target_pairs={{0,0},{1,5},{4,4},{5,9},{8,8},{9,13},{12,12},{13,17},{16,16},{17,2... | collective-permute-start | bytes 196616 | tf_op jit(solution)/shard_map/out_weight_over_z/ppermute | solution.py:205
  17.7 8.5 %collective-permute-done = bf16[32,1024]{1,0:T(8,128)(2,1)S(1)} collective-permute-done((bf16[32,1024]{1,0:T(8,128)(2,1)S(1)}, bf16[32,1024]{1,0:T(8,128)(2,1)S(1)}, u32[]{:S(2)}, u32[]{:S(2)}) %collective-permute-start) | collective-permute-done | bytes 65568 | tf_op jit(solution)/shard_map/out_weight_over_z/ppermute | solution.py:205
  26.2 10.0 %all-to-all-done = bf16[16,256,256]{2,1,0:T(8,128)(2,1)} async-done(((bf16[16,256,256]{2,1,0:T(8,128)(2,1)}), bf16[16,256,256]{2,1,0:T(8,128)(2,1)}, u32[]{:S(2)}, u32[]{:S(2)}) %all-to-all-start) | async-done | bytes 2097184 | tf_op jit(solution)/shard_map/gather_kv_weight/all_to_all | solution.py:180
  36.2 6.8 %collective-permute-start.1 = (bf16[8,512,256]{2,1,0:T(8,128)(2,1)}, bf16[8,512,256]{2,1,0:T(8,128)(2,1)}, u32[]{:S(2)}, u32[]{:S(2)}) collective-permute-start(bf16[8,512,256]{2,1,0:T(8,128)(2,1)} %bitcast.6.kv_mine_ref), channel_id=1, source_target_pairs={{0,1},{1,0},{2,3},{3,2},{4,5},{5,4},{6,7},{7,6},{8,9},{9,8},{10,11... | collective-permute-start | bytes 6291464 | tf_op jit(solution)/shard_map/swap_kv_weight/ppermute | solution.py:211
  43.0 1.1 broadcast_in_dim.16
  44.1 3.8 %all-to-all-start.1 = ((bf16[16,32,1024]{2,1,0:T(8,128)(2,1)}), bf16[16,32,1024]{2,1,0:T(8,128)(2,1)S(1)}, u32[]{:S(2)}, u32[]{:S(2)}) async-start(bf16[16,32,1024]{2,1,0:T(8,128)(2,1)} %broadcast_in_dim.16), calls=%async_computation.1 | async-start | bytes 2097152 | tf_op jit(solution)/shard_map/out_weight_over_plane/all_to_all | solution.py:180
  48.0 1.0 copy-done.3
  49.0 3.1 %encoder_attention.1.ctx_ref = bf16[256,1024]{1,0:T(8,128)(2,1)S(1)} custom-call(s32[1]{0:T(128)} %bitcast.7.slot_ref, s32[512]{0:T(512)S(1)} %copy-done.5, s32[512]{0:T(512)S(1)} %copy-done.6, bf16[256,1024]{1,0:T(8,128)(2,1)S(1)} %copy-done.1, bf16[256,1024]{1,0:T(8,128)(2,1)S(1)} %copy-done.2, bf16[256,1024]{1,0:T(8,128)(2,1)S(1)} %copy-done.3), custom_call_target="tpu_custom_call" | custom-call | flops 536870912 | bytes 2097152 | tf_op jit(solution)/shard_map/encoder_attention/pallas_call | solution.py:61
  52.1 14.2 %all-to-all-done.1.mine_ref = bf16[16,32,1024]{2,1,0:T(8,128)(2,1)S(1)} async-done(((bf16[16,32,1024]{2,1,0:T(8,128)(2,1)}), bf16[16,32,1024]{2,1,0:T(8,128)(2,1)S(1)}, u32[]{:S(2)}, u32[]{:S(2)}) %all-to-all-start.1) | async-done | bytes 1048608 | tf_op jit(solution)/shard_map/out_weight_over_plane/all_to_all | solution.py:180
  66.4 2.9 %collective-permute-start.2 = (bf16[16,32,1024]{2,1,0:T(8,128)(2,1)S(1)}, bf16[16,32,1024]{2,1,0:T(8,128)(2,1)S(1)}, u32[]{:S(2)}, u32[]{:S(2)}) collective-permute-start(bf16[16,32,1024]{2,1,0:T(8,128)(2,1)S(1)} %all-to-all-done.1.mine_ref), channel_id=1, source_target_pairs={{0,1},{1,0},{2,3},{3,2},{4,5},{5,4},{6,7},{7,6},{8,9},{9,8},{10,11... | collective-permute-start | bytes 3145736 | tf_op jit(solution)/shard_map/swap_out_weight/ppermute | solution.py:216
  69.3 0.1 pad_add_fusion.1.place_ref
  69.3 2.2 %collective-permute-done.2.other_ref = bf16[16,32,1024]{2,1,0:T(8,128)(2,1)S(1)} collective-permute-done((bf16[16,32,1024]{2,1,0:T(8,128)(2,1)S(1)}, bf16[16,32,1024]{2,1,0:T(8,128)(2,1)S(1)}, u32[]{:S(2)}, u32[]{:S(2)}) %collective-permute-start.2) | collective-permute-done | bytes 1048608 | tf_op jit(solution)/shard_map/swap_out_weight/ppermute | solution.py:216
  71.5 1.0 copy-done.4
  72.6 5.5 %encode_keyval.1 = bf16[8,256,256]{2,1,0:T(8,128)(2,1)} custom-call(s32[2]{0:T(128)S(1)} %pad_add_fusion.1.place_ref, bf16[256,1024]{1,0:T(8,128)(2,1)S(1)} %encoder_attention.1.ctx_ref, bf16[16,32,1024]{2,1,0:T(8,128)(2,1)S(1)} %all-to-all-done.1.mine_ref, bf16[16,32,1024]{2,1,0:T(8,128)(2,1)S(1)} %collective-permute-done.2.other_ref, ...), custom_call_target="tpu_custom_call" | custom-call | flops 1610612736 | bytes 8388608 | tf_op jit(solution)/shard_map/encode_keyval/pallas_call | solution.py:96
  78.0 3.7 %all-to-all-start.2 = ((bf16[8,256,256]{2,1,0:T(8,128)(2,1)}), bf16[8,256,256]{2,1,0:T(8,128)(2,1)S(1)}, u32[]{:S(2)}, u32[]{:S(2)}) async-start(bf16[8,256,256]{2,1,0:T(8,128)(2,1)} %encode_keyval.1), calls=%async_computation.2 | async-start | bytes 2097152 | tf_op jit(solution)/shard_map/exchange_keyval/all_to_all | solution.py:221
  81.8 0.1 pad_add_fusion.first_ref
  81.9 17.2 %all-to-all-done.2.kv_ref = bf16[8,256,256]{2,1,0:T(8,128)(2,1)S(1)} async-done(((bf16[8,256,256]{2,1,0:T(8,128)(2,1)}), bf16[8,256,256]{2,1,0:T(8,128)(2,1)S(1)}, u32[]{:S(2)}, u32[]{:S(2)}) %all-to-all-start.2) | async-done | bytes 1048608 | tf_op jit(solution)/shard_map/exchange_keyval/all_to_all | solution.py:221
  99.1 3.3 %cross_attention.1 = bf16[64,2,640]{2,1,0:T(2,128)(2,1)S(1)} custom-call(s32[2]{0:T(128)S(1)} %pad_add_fusion.first_ref, s32[512]{0:T(512)S(1)} %copy-done.5, s32[512]{0:T(512)S(1)} %copy-done.6, bf16[512,128]{1,0:T(8,128)(2,1)S(1)} %bitcast.16, bf16[8,256,256]{2,1,0:T(8,128)(2,1)S(1)} %all-to-all-done.2.kv_ref), custom_call_target="tpu_custom_call" | custom-call | tf_op jit(solution)/shard_map/cross_attention/pallas_call | solution.py:148
  102.4 36.0 %all_to_all.20.part_ref = bf16[64,2,640]{2,1,0:T(2,128)(2,1)} all-to-all(bf16[64,2,640]{2,1,0:T(2,128)(2,1)S(1)} %cross_attention.1), channel_id=1, replica_groups=mesh['yh'=2,'x'=4,'z'=16,'yl'=2,'c'=2] {'z','yl','c'}, dimensions={0} | all-to-all | bytes 327680 | tf_op jit(solution)/shard_map/exchange_partials/all_to_all | solution.py:226
  138.4 2.3 %merge_partials.1 = f32[8,128]{1,0:T(8,128)} custom-call(bf16[64,2,640]{2,1,0:T(2,128)(2,1)} %all_to_all.20.part_ref), custom_call_target="tpu_custom_call" | custom-call | tf_op jit(solution)/shard_map/merge_partials/pallas_call | solution.py:168
  (21 shorter events, 0.1 us)
Async XLA Ops:
  0.0 1.0 copy-start
  2.6 7.8 %copy-start.9 = (bf16[16,1024]{1,0:T(8,128)(2,1)S(1)}, bf16[16,1024]{1,0:T(8,128)(2,1)}, u32[]{:S(2)}) copy-start(bf16[16,1024]{1,0:T(8,128)(2,1)} %param.14) | copy-start | bytes 98308
  2.6 33.6 %all-to-all-start = ((bf16[16,256,256]{2,1,0:T(8,128)(2,1)}), bf16[16,256,256]{2,1,0:T(8,128)(2,1)}, u32[]{:S(2)}, u32[]{:S(2)}) async-start(bf16[16,256,256]{2,1,0:T(8,128)(2,1)} %broadcast_in_dim.7), calls=%async_computation | async-start | bytes 4194304 | tf_op jit(solution)/shard_map/gather_kv_weight/all_to_all | solution.py:180
  10.4 37.6 %copy-start.1 = (bf16[256,1024]{1,0:T(8,128)(2,1)S(1)}, bf16[256,1024]{1,0:T(8,128)(2,1)}, u32[]{:S(2)}) copy-start(bf16[256,1024]{1,0:T(8,128)(2,1)} %q_ref) | copy-start | bytes 1572868
  10.4 37.6 %copy-start.2 = (bf16[256,1024]{1,0:T(8,128)(2,1)S(1)}, bf16[256,1024]{1,0:T(8,128)(2,1)}, u32[]{:S(2)}) copy-start(bf16[256,1024]{1,0:T(8,128)(2,1)} %k_ref.1) | copy-start | bytes 1572868
  10.4 37.6 %copy-start.5 = (s32[512]{0:T(512)S(1)}, s32[512]{0:T(512)}, u32[]{:S(2)}) copy-start(s32[512]{0:T(512)} %span_ref.3) | copy-start | bytes 6148
  10.4 37.6 %copy-start.6 = (s32[512]{0:T(512)S(1)}, s32[512]{0:T(512)}, u32[]{:S(2)}) copy-start(s32[512]{0:T(512)} %len_ref.3) | copy-start | bytes 6148
  15.8 10.4 %collective-permute-start = (bf16[32,1024]{1,0:T(8,128)(2,1)S(1)}, bf16[32,1024]{1,0:T(8,128)(2,1)S(1)}, u32[]{:S(2)}, u32[]{:S(2)}) collective-permute-start(bf16[32,1024]{1,0:T(8,128)(2,1)S(1)} %all_gather.3), channel_id=1, source_target_pairs={{0,0},{1,5},{4,4},{5,9},{8,8},{9,13},{12,12},{13,17},{16,16},{17,2... | collective-permute-start | bytes 196616 | tf_op jit(solution)/shard_map/out_weight_over_z/ppermute | solution.py:205
  36.2 30.1 %collective-permute-start.1 = (bf16[8,512,256]{2,1,0:T(8,128)(2,1)}, bf16[8,512,256]{2,1,0:T(8,128)(2,1)}, u32[]{:S(2)}, u32[]{:S(2)}) collective-permute-start(bf16[8,512,256]{2,1,0:T(8,128)(2,1)} %bitcast.6.kv_mine_ref), channel_id=1, source_target_pairs={{0,1},{1,0},{2,3},{3,2},{4,5},{5,4},{6,7},{7,6},{8,9},{9,8},{10,11... | collective-permute-start | bytes 6291464 | tf_op jit(solution)/shard_map/swap_kv_weight/ppermute | solution.py:211
  44.1 27.4 %copy-start.7 = (f32[1024]{0:T(1024)S(1)}, f32[1024]{0:T(1024)}, u32[]{:S(2)}) copy-start(f32[1024]{0:T(1024)} %param.15) | copy-start | bytes 12292
  44.1 22.2 %all-to-all-start.1 = ((bf16[16,32,1024]{2,1,0:T(8,128)(2,1)}), bf16[16,32,1024]{2,1,0:T(8,128)(2,1)S(1)}, u32[]{:S(2)}, u32[]{:S(2)}) async-start(bf16[16,32,1024]{2,1,0:T(8,128)(2,1)} %broadcast_in_dim.16), calls=%async_computation.1 | async-start | bytes 2097152 | tf_op jit(solution)/shard_map/out_weight_over_plane/all_to_all | solution.py:180
  48.0 1.0 copy-start.3
  66.4 5.2 %collective-permute-start.2 = (bf16[16,32,1024]{2,1,0:T(8,128)(2,1)S(1)}, bf16[16,32,1024]{2,1,0:T(8,128)(2,1)S(1)}, u32[]{:S(2)}, u32[]{:S(2)}) collective-permute-start(bf16[16,32,1024]{2,1,0:T(8,128)(2,1)S(1)} %all-to-all-done.1.mine_ref), channel_id=1, source_target_pairs={{0,1},{1,0},{2,3},{3,2},{4,5},{5,4},{6,7},{7,6},{8,9},{9,8},{10,11... | collective-permute-start | bytes 3145736 | tf_op jit(solution)/shard_map/swap_out_weight/ppermute | solution.py:216
  71.5 1.0 copy-start.4
  78.0 3.7 %copy-start.8 = (bf16[64,1,1024]{2,0,1:T(8,128)(2,1)S(1)}, bf16[64,1,1024]{2,0,1:T(8,128)(2,1)}, u32[]{:S(2)}) copy-start(bf16[64,1,1024]{2,0,1:T(8,128)(2,1)} %param.17) | copy-start | bytes 393220
  78.0 21.0 %all-to-all-start.2 = ((bf16[8,256,256]{2,1,0:T(8,128)(2,1)}), bf16[8,256,256]{2,1,0:T(8,128)(2,1)S(1)}, u32[]{:S(2)}, u32[]{:S(2)}) async-start(bf16[8,256,256]{2,1,0:T(8,128)(2,1)} %encode_keyval.1), calls=%async_computation.2 | async-start | bytes 2097152 | tf_op jit(solution)/shard_map/exchange_keyval/all_to_all | solution.py:221

commit v4 on v3

--- a/solution.py
+++ b/solution.py
@@ -25,8 +25,8 @@
 PLANE = ("yh", "x", "yl")
 
 
-def params(**kw):
-    return pltpu.CompilerParams(vmem_limit_bytes=48 * 1024 * 1024, **kw)
+def params(mebibytes=20):
+    return pltpu.CompilerParams(vmem_limit_bytes=mebibytes * 1024 * 1024)
 
 
 def dot(a, b):
@@ -71,40 +71,79 @@
     )(slot, span_ids, seg_lengths, q, k, v)
 
 
-def encode_kernel(place_ref, ctx_ref, mine_ref, other_ref, resid_ref, gain_ref, kv_mine_ref,
-                  kv_other_ref, o_ref, w_ref, enc_ref):
-    z, core = place_ref[0], place_ref[1]
-    for part_ref, at in ((mine_ref, core), (other_ref, 1 - core)):
+def encode_kernel(place_ref, gain_ref, ctx_ref, resid_ref, mine_ref, other_ref, *refs):
+    kv_refs, o_ref = refs[:6], refs[6]
+    w_ref, enc_ref, done_ref, hold_ref = refs[7:11]
+    kv_bufs, w_sems, kv_sems, o_sems = refs[11:17], refs[17], refs[18], refs[19]
+    z, core, odd = place_ref[0], place_ref[1], place_ref[2]
+
+    copies = []
+    for which, part_ref, at in ((0, mine_ref, core), (1, other_ref, 1 - core)):
         for ha in range(KV_HEADS):
             plane = lax.rem(z + 32 - 2 * ha - at, 16)
             for yl in range(2):
-                w_ref[pl.ds(pl.multiple_of(64 * plane + 32 * yl, 32), 32), :] = part_ref[ha * 2 + yl]
-    hidden = resid_ref[...].astype(jnp.float32) + dot(ctx_ref[...], w_ref[...])
+                for c in range(2):
+                    row = pl.multiple_of(64 * plane + 32 * yl + 16 * c, 16)
+                    copies.append(pltpu.make_async_copy(
+                        part_ref.at[ha * 2 + yl, c], w_ref.at[:, pl.ds(row, 16)], w_sems.at[len(copies)]))
+    copies.append(pltpu.make_async_copy(ctx_ref, hold_ref.at[0], w_sems.at[64]))
+    copies.append(pltpu.make_async_copy(resid_ref, hold_ref.at[1], w_sems.at[65]))
+    kv_copies = [pltpu.make_async_copy(kv_refs[i], kv_bufs[i], kv_sems.at[i]) for i in range(6)]
+    for copy in copies + kv_copies:
+        copy.start()
+    for copy in copies:
+        copy.wait()
+
+    ctx = hold_ref[0]
+    hidden = jnp.concatenate(
+        [dot(ctx, jnp.concatenate([w_ref[2 * j], w_ref[2 * j + 1]], axis=1)) for j in range(4)], axis=1)
+    hidden = hidden + hold_ref[1].astype(jnp.float32)
     factor = lax.rsqrt(jnp.mean(hidden * hidden, axis=-1, keepdims=True) + 1e-05)
     encoded = (hidden * factor * gain_ref[...]).astype(jnp.bfloat16)
-    half = D_ENC // 2
-    enc_ref[0] = encoded[:, :half]
-    enc_ref[1] = encoded[:, half:]
-    near, far = enc_ref[core], enc_ref[1 - core]
+    for piece in range(4):
+        enc_ref[piece] = encoded[:, piece * 256:(piece + 1) * 256]
+    near, far = 2 * core, 2 - 2 * core
+    pieces = [enc_ref[near + odd], enc_ref[near + 1 - odd], enc_ref[far + odd], enc_ref[far + 1 - odd]]
+    for copy in kv_copies:
+        copy.wait()
+
+    def rows(buf, h):
+        return jnp.concatenate(
+            [jnp.concatenate([buf[2 * h + yl, :128], buf[2 * h + yl, 128:]], axis=1) for yl in range(2)], axis=0)
+
+    out_copies = []
     for h in range(KV_HEADS):
-        o_ref[h] = (dot(near, kv_mine_ref[h]) + dot(far, kv_other_ref[h])).astype(jnp.bfloat16)
-
-
-def encode(place, ctx, mine, other, resid, gain, kv_mine, kv_other):
+        side, at = divmod(h, KV_HEADS // 2)
+        total = dot(pieces[0], rows(kv_bufs[0], h)) + dot(pieces[1], rows(kv_bufs[1 + side], at))
+        total += dot(pieces[2], rows(kv_bufs[3], h)) + dot(pieces[3], rows(kv_bufs[4 + side], at))
+        done_ref[h, :SEG_LEN] = total[:, :HEAD].astype(jnp.bfloat16)
+        done_ref[h, SEG_LEN:] = total[:, HEAD:].astype(jnp.bfloat16)
+        out_copies.append(pltpu.make_async_copy(done_ref.at[h], o_ref.at[h], o_sems.at[h]))
+        out_copies[h].start()
+    for copy in out_copies:
+        copy.wait()
+
+
+def encode(place, gain, ctx, resid, mine, other, kvs):
     smem = pl.BlockSpec(memory_space=pltpu.SMEM)
     vmem = pl.BlockSpec(memory_space=pltpu.VMEM)
+    hbm = pl.BlockSpec(memory_space=pltpu.HBM)
     return pl.pallas_call(
         encode_kernel,
-        out_shape=jax.ShapeDtypeStruct((KV_HEADS, SEG_LEN, 2 * HEAD), jnp.bfloat16),
-        in_specs=[smem] + [vmem] * 7,
-        out_specs=vmem,
-        scratch_shapes=[pltpu.VMEM((D_ENC, D_ENC), jnp.bfloat16),
-                        pltpu.VMEM((2, SEG_LEN, D_ENC // 2), jnp.bfloat16)],
-        compiler_params=params(),
+        out_shape=jax.ShapeDtypeStruct((KV_HEADS, 2 * SEG_LEN, HEAD), jnp.bfloat16),
+        in_specs=[smem, vmem] + [hbm] * 10,
+        out_specs=hbm,
+        scratch_shapes=[pltpu.VMEM((8, D_ENC, HEAD), jnp.bfloat16),
+                        pltpu.VMEM((4, SEG_LEN, 256), jnp.bfloat16),
+                        pltpu.VMEM((KV_HEADS, 2 * SEG_LEN, HEAD), jnp.bfloat16),
+                        pltpu.VMEM((2, SEG_LEN, D_ENC), jnp.bfloat16)]
+        + [pltpu.VMEM(kv.shape, kv.dtype) for kv in kvs]
+        + [pltpu.SemaphoreType.DMA((66,)), pltpu.SemaphoreType.DMA((6,)), pltpu.SemaphoreType.DMA((KV_HEADS,))],
+        compiler_params=params(47),
         cost_estimate=pl.CostEstimate(
             flops=6 * SEG_LEN * D_ENC * D_ENC, bytes_accessed=8 * D_ENC * D_ENC, transcendentals=SEG_LEN),
         name="encode_keyval",
-    )(place, ctx, mine, other, resid, gain, kv_mine, kv_other)
+    )(place, gain, ctx, resid, mine, other, *kvs)
 
 
 def cross_kernel(slots, first_ref, span_ref, len_ref, q_ref, kv_ref, o_ref):
@@ -115,8 +154,8 @@
         valid = len_ref[span_ref[first_ref[0] + s * first_ref[1]]]
         bias.append(jnp.where(lane < valid, 0.0, MASKED).astype(jnp.float32))
     bias = jnp.concatenate(bias, axis=1)
-    keys = kv_ref[:, :, :HEAD].reshape(slots * SEG_LEN, HEAD)
-    values = kv_ref[:, :, HEAD:].reshape(slots * SEG_LEN, HEAD)
+    keys = kv_ref[:, :SEG_LEN].reshape(slots * SEG_LEN, HEAD)
+    values = kv_ref[:, SEG_LEN:].reshape(slots * SEG_LEN, HEAD)
     rows = 2 * QTAIL
     column = lax.broadcasted_iota(jnp.int32, (rows, HEAD), 1)
     levels = jnp.zeros((rows, HEAD), jnp.float32)
@@ -190,12 +229,14 @@
     yl, z = lax.axis_index("yl"), lax.axis_index("z")
     swap = functools.partial(lax.ppermute, axis_name="c", perm=[(0, 1), (1, 0)])
 
+    odd = lax.rem(z, 2)
+
     with jax.named_scope("gather_kv_weight"):
-        quarter = lax.dynamic_slice_in_dim(
-            kv_weight.reshape(D_ENC, 2 * HEAD), core * 512 + yl * 256, 256, 0)
-        kv_mine = spread(quarter, PLANE)
+        eighth = lax.dynamic_slice_in_dim(
+            kv_weight.reshape(D_ENC, 2 * HEAD), core * 512 + odd * 256 + yl * 128, 128, 0)
+        kv_mine = spread(jnp.concatenate([eighth[:, :HEAD], eighth[:, HEAD:]], axis=0), PLANE)
     with jax.named_scope("out_weight_over_z"):
-        pair = lax.all_gather(out_weight, "c", axis=0, tiled=True)
+        pair = lax.all_gather(out_weight.reshape(16, 8, HEAD).transpose(1, 0, 2), "c")
         hops = []
         for ha_at in range(8):
             for z_at in range(16):
@@ -206,17 +247,22 @@
     kv_mine, pair, enc_query = lax.optimization_barrier((kv_mine, pair, enc_query))
     with jax.named_scope("out_weight_over_plane"):
         w_mine = spread(pair, PLANE)
-    kv_mine = kv_mine.reshape(KV_HEADS, D_ENC // 2, 2 * HEAD)
+    with jax.named_scope("kv_weight_over_z"):
+        some = 8
+        up = [(i, (i + 1) % 16) for i in range(16)]
+        down = [(i, (i + 15) % 16) for i in range(16)]
+        kv_first = lax.ppermute(kv_mine[:some], "z", down)
+        kv_last = lax.ppermute(kv_mine[some:], "z", up)
     with jax.named_scope("swap_kv_weight"):
-        kv_other = swap(kv_mine)
+        kvs = [kv_mine, kv_first, kv_last]
+        kvs = kvs + [swap(kv) for kv in kvs]
     slot = (ha * sa_count + sa).reshape(1).astype(jnp.int32)
     context = encoder_attention(slot, span_ids, seg_lengths, enc_query, enc_key, enc_value)
-    w_mine, kv_other, context = lax.optimization_barrier((w_mine, kv_other, context))
+    w_mine, kvs, context = lax.optimization_barrier((w_mine, kvs, context))
     with jax.named_scope("swap_out_weight"):
         w_other = swap(w_mine)
-    place = jnp.stack([z, core]).astype(jnp.int32)
-    keyval = encode(place, context, w_mine, w_other, enc_resid, norm_gain.reshape(1, D_ENC),
-                    kv_mine, kv_other)
+    place = jnp.stack([z, core, odd]).astype(jnp.int32)
+    keyval = encode(place, norm_gain.reshape(1, D_ENC), context, enc_resid, w_mine, w_other, kvs)
     with jax.named_scope("exchange_keyval"):
         keyval = lax.all_to_all(keyval, HA, 0, 0, tiled=True)
     first = jnp.stack([sa, sa_count]).astype(jnp.int32)

time: 141 us -> 142 us (level)
  starting transfers between devices: 26.8 us -> 46.3 us
  waiting for transfers between devices: 52.2 us -> 36 us
  blocking collectives: 41.3 us -> 35.8 us
  local copies, waits for them, and re-layouts: 5.83 us -> 8.36 us
    ppermute x1 -> x5, starting transfers between devices: 6.8 us -> 23.9 us  [the longest x1 11.8 us: local(): kv_first = lax.ppermute(kv_mine[:some], 'z', down)]
    all_to_all x2, waiting for transfers between devices: 24.3 us -> 7.95 us  [spread(): return lax.all_to_all(copies, axes, 0, 0, tiled=True)]
    all_to_all x1, blocking collectives: 36 us -> 30.7 us  [local(): parts = lax.all_to_all(parts, SA, 0, 0, tiled=True)]
    all_to_all x2, starting transfers between devices: 11.6 us -> 13.8 us  [spread(): return lax.all_to_all(copies, axes, 0, 0, tiled=True)]
    slice x0 -> x2, local copies, waits for them, and re-layouts: none -> 2.07 us  [the longest x1 2.07 us: local(): kv_last = lax.ppermute(kv_mine[some:], 'z', up)]
    unnamed x21 -> x22, local copies, waits for them, and re-layouts: 3.18 us -> 3.84 us
  transfers between devices with their start and end apart: 6 -> 10, of which waited for: 5 -> 4; matrix products, arithmetic and copies ran while one was open for 1% -> 1% of each run, Pallas kernels for 2% -> 2%
where the time goes in v4:
time: 142 us; the launch traced here: 141 us
  starting transfers between devices  46.3 us (33%)
  waiting for transfers between devices  36 us (25%)
  blocking collectives  35.8 us (25%)
  Pallas kernels  14.5 us (10%)
  local copies, waits for them, and re-layouts  8.36 us (6%)
    all_to_all x1, blocking collectives, local(): parts = lax.all_to_all(parts, SA, 0, 0, tiled=True)  30.7 us
    all_to_all x1, waiting for transfers between devices, local(): keyval = lax.all_to_all(keyval, HA, 0, 0, tiled=True)  17.2 us
    all_to_all x2, starting transfers between devices, spread(): return lax.all_to_all(copies, axes, 0, 0, tiled=True)  13.8 us
    ppermute x1, starting transfers between devices, local(): kv_first = lax.ppermute(kv_mine[:some], 'z', down)  11.8 us
    ppermute x3, starting transfers between devices, local(): kvs = kvs + [swap(kv) for kv in kvs]  10.2 us
    ppermute x1, waiting for transfers between devices, local(): pair = lax.ppermute(pair, ('yh', 'x', 'z', 'c'), hops)  8.61 us
    all_to_all x2, waiting for transfers between devices, spread(): return lax.all_to_all(copies, axes, 0, 0, tiled=True)  7.95 us
    pallas_call x1, Pallas kernels, encode(): pl.pallas_call(encode_kernel, out_shape=jax.ShapeDtypeStruct((KV_HEADS, 2...  5.93 us
  transfers between devices with their start and end apart: 10, of which 4 were waited for; matrix products, arithmetic and copies ran while one was open for 1% of the time, Pallas kernels for 2%

profile of v4, /device:TPU:1, one launch (start us, length us, event | category | flops | bytes accessed | tf_op | source)
XLA Modules:
  0.0 141.3 jit_solution(9159322248078435201)
XLA Ops:
  1.1 1.2 broadcast_in_dim.4
  2.3 7.8 %all-to-all-start = ((bf16[16,256,128]{2,1,0:T(8,128)(2,1)}), bf16[16,256,128]{2,1,0:T(8,128)(2,1)}, u32[]{:S(2)}, u32[]{:S(2)}) async-start(bf16[16,256,128]{2,1,0:T(8,128)(2,1)} %broadcast_in_dim.4), calls=%async_computation | async-start | bytes 2097152 | tf_op jit(solution)/shard_map/gather_kv_weight/all_to_all | solution.py:219
  10.1 5.1 %all-gather = bf16[16,16,128]{2,0,1:T(8,128)(2,1)S(1)} all-gather(bf16[8,16,128]{2,0,1:T(8,128)(2,1)S(1)} %bitcast.24), channel_id=2, replica_groups=mesh['yh'=2,'x'=4,'z'=16,'yl'=2,'c'=2] {'c'}, dimensions={0}, use_global_device_ids=true | all-gather | bytes 98304 | tf_op jit(solution)/shard_map/out_weight_over_z/all_gather | solution.py:239
  15.2 1.9 %collective-permute-start = (bf16[2,8,16,128]{3,2,1,0:T(8,128)(2,1)S(1)}, bf16[2,8,16,128]{3,2,1,0:T(8,128)(2,1)S(1)}, u32[]{:S(2)}, u32[]{:S(2)}) collective-permute-start(bf16[2,8,16,128]{3,2,1,0:T(8,128)(2,1)S(1)} %bitcast.26), channel_id=1, source_target_pairs={{0,0},{1,5},{4,4},{5,9},{8,8},{9,13},{12,12},{13,17},{16,16},{17,2... | collective-permute-start | bytes 196616 | tf_op jit(solution)/shard_map/out_weight_over_z/ppermute | solution.py:246
  17.1 8.6 %collective-permute-done = bf16[2,8,16,128]{3,2,1,0:T(8,128)(2,1)S(1)} collective-permute-done((bf16[2,8,16,128]{3,2,1,0:T(8,128)(2,1)S(1)}, bf16[2,8,16,128]{3,2,1,0:T(8,128)(2,1)S(1)}, u32[]{:S(2)}, u32[]{:S(2)}) %collective-permute-start) | collective-permute-done | bytes 65568 | tf_op jit(solution)/shard_map/out_weight_over_z/ppermute | solution.py:246
  25.7 2.1 %fusion = (bf16[8,256,128]{2,1,0:T(8,128)(2,1)S(1)}, bf16[8,256,128]{2,1,0:T(8,128)(2,1)}) fusion(bf16[16,256,128]{2,1,0:T(8,128)(2,1)} %all-to-all-done.refs_0_), kind=kLoop, calls=%fused_computation.4 | loop fusion | bytes 2097152 | tf_op jit(solution)/shard_map/kv_weight_over_z/slice | solution.py:255
  27.8 11.8 %collective-permute-start.1 = (bf16[8,256,128]{2,1,0:T(8,128)(2,1)}, bf16[8,256,128]{2,1,0:T(8,128)(2,1)}, u32[]{:S(2)}, u32[]{:S(2)}) collective-permute-start(bf16[8,256,128]{2,1,0:T(8,128)(2,1)} %get-tuple-element.28), channel_id=1, source_target_pairs={{0,60},{4,0},{8,4},{12,8},{16,12},{20,16},{24,20},{28,24},{32,28},... | collective-permute-start | bytes 1572872 | tf_op jit(solution)/shard_map/kv_weight_over_z/ppermute | solution.py:254
  39.6 1.9 %collective-permute-start.2 = (bf16[8,256,128]{2,1,0:T(8,128)(2,1)S(1)}, bf16[8,256,128]{2,1,0:T(8,128)(2,1)}, u32[]{:S(2)}, u32[]{:S(2)}) collective-permute-start(bf16[8,256,128]{2,1,0:T(8,128)(2,1)S(1)} %get-tuple-element.27), channel_id=1, source_target_pairs={{0,4},{4,8},{8,12},{12,16},{16,20},{20,24},{24,28},{28,32},{32,36}... | collective-permute-start | bytes 1572872 | tf_op jit(solution)/shard_map/kv_weight_over_z/ppermute | solution.py:255
  41.5 4.7 %collective-permute-start.3 = (bf16[16,256,128]{2,1,0:T(8,128)(2,1)}, bf16[16,256,128]{2,1,0:T(8,128)(2,1)}, u32[]{:S(2)}, u32[]{:S(2)}) collective-permute-start(bf16[16,256,128]{2,1,0:T(8,128)(2,1)} %all-to-all-done.refs_0_), channel_id=1, source_target_pairs={{0,1},{1,0},{2,3},{3,2},{4,5},{5,4},{6,7},{7,6},{8,9},{9,8},{10,11... | collective-permute-start | bytes 3145736 | tf_op jit(solution)/shard_map/swap_kv_weight/ppermute | solution.py:258
  46.2 1.2 broadcast_in_dim.5
  47.4 6.0 %all-to-all-start.1 = ((bf16[16,2,8,16,128]{4,3,2,1,0:T(8,128)(2,1)}), bf16[16,2,8,16,128]{4,3,2,1,0:T(8,128)(2,1)S(1)}, u32[]{:S(2)}, u32[]{:S(2)}) async-start(bf16[16,2,8,16,128]{4,3,2,1,0:T(8,128)(2,1)} %broadcast_in_dim.5), calls=%async_computation.1 | async-start | bytes 2097152 | tf_op jit(solution)/shard_map/out_weight_over_plane/all_to_all | solution.py:219
  53.5 2.2 %collective-permute-start.4 = (bf16[8,256,128]{2,1,0:T(8,128)(2,1)}, bf16[8,256,128]{2,1,0:T(8,128)(2,1)}, u32[]{:S(2)}, u32[]{:S(2)}) collective-permute-start(bf16[8,256,128]{2,1,0:T(8,128)(2,1)} %collective-permute-done.1.refs_1_), channel_id=1, source_target_pairs={{0,1},{1,0},{2,3},{3,2},{4,5},{5,4},{6,7},{7,6},{8,9},{9,8},{10,11... | collective-permute-start | bytes 1572872 | tf_op jit(solution)/shard_map/swap_kv_weight/ppermute | solution.py:258
  55.7 3.3 %collective-permute-start.5 = (bf16[8,256,128]{2,1,0:T(8,128)(2,1)}, bf16[8,256,128]{2,1,0:T(8,128)(2,1)}, u32[]{:S(2)}, u32[]{:S(2)}) collective-permute-start(bf16[8,256,128]{2,1,0:T(8,128)(2,1)} %collective-permute-done.2.refs_2_), channel_id=1, source_target_pairs={{0,1},{1,0},{2,3},{3,2},{4,5},{5,4},{6,7},{7,6},{8,9},{9,8},{10,11... | collective-permute-start | bytes 1572872 | tf_op jit(solution)/shard_map/swap_kv_weight/ppermute | solution.py:258
  60.8 3.1 %encoder_attention.1.ctx_ref = bf16[256,1024]{1,0:T(8,128)(2,1)S(1)} custom-call(s32[1]{0:T(128)} %bitcast.10.slot_ref, s32[512]{0:T(512)S(1)} %copy-done.5, s32[512]{0:T(512)S(1)} %copy-done.6, bf16[256,1024]{1,0:T(8,128)(2,1)S(1)} %copy-done.1, bf16[256,1024]{1,0:T(8,128)(2,1)S(1)} %copy-done.2, bf16[256,1024]{1,0:T(8,128)(2,1)S(1)} %copy-done.3), custom_call_target="tpu_custom_call" | custom-call | flops 536870912 | bytes 2097152 | tf_op jit(solution)/shard_map/encoder_attention/pallas_call | solution.py:61
  63.8 8.0 %all-to-all-done.1.mine_ref = bf16[16,2,8,16,128]{4,3,2,1,0:T(8,128)(2,1)S(1)} async-done(((bf16[16,2,8,16,128]{4,3,2,1,0:T(8,128)(2,1)}), bf16[16,2,8,16,128]{4,3,2,1,0:T(8,128)(2,1)S(1)}, u32[]{:S(2)}, u32[]{:S(2)}) %all-to-all-start.1) | async-done | bytes 1048608 | tf_op jit(solution)/shard_map/out_weight_over_plane/all_to_all | solution.py:219
  71.8 3.0 %collective-permute-start.6 = (bf16[16,2,8,16,128]{4,3,2,1,0:T(8,128)(2,1)S(1)}, bf16[16,2,8,16,128]{4,3,2,1,0:T(8,128)(2,1)S(1)}, u32[]{:S(2)}, u32[]{:S(2)}) collective-permute-start(bf16[16,2,8,16,128]{4,3,2,1,0:T(8,128)(2,1)S(1)} %all-to-all-done.1.mine_ref), channel_id=1, source_target_pairs={{0,1},{1,0},{2,3},{3,2},{4,5},{5,4},{6,7},{7,6},{8,9},{9,8},{10,11... | collective-permute-start | bytes 3145736 | tf_op jit(solution)/shard_map/swap_out_weight/ppermute | solution.py:263
  74.9 2.2 %collective-permute-done.6.other_ref = bf16[16,2,8,16,128]{4,3,2,1,0:T(8,128)(2,1)S(1)} collective-permute-done((bf16[16,2,8,16,128]{4,3,2,1,0:T(8,128)(2,1)S(1)}, bf16[16,2,8,16,128]{4,3,2,1,0:T(8,128)(2,1)S(1)}, u32[]{:S(2)}, u32[]{:S(2)}) %collective-permute-start.6) | collective-permute-done | bytes 1048608 | tf_op jit(solution)/shard_map/swap_out_weight/ppermute | solution.py:263
  77.0 1.0 copy-done.4
  78.1 5.9 %encode_keyval.1 = bf16[8,512,128]{2,1,0:T(8,128)(2,1)} custom-call(s32[3]{0:T(128)S(1)} %pad_add_fusion.1.place_ref, f32[1,1024]{1,0:T(1,128)S(1)} %bitcast.22, bf16[256,1024]{1,0:T(8,128)(2,1)S(1)} %encoder_attention.1.ctx_ref, bf16[256,1024]{1,0:T(8,128)(2,1)S(1)} %copy-done.4, bf16[16,2,8,16,128]{4,3,2,1,0:T(8,128)(2,1)S(1)} %all-to-all-done.1.mine_ref, ...), custom_call_target="tpu_custom_call" | custom-call | flops 1610612736 | bytes 8388608 | tf_op jit(solution)/shard_map/encode_keyval/pallas_call | solution.py:131
  84.0 3.7 %all-to-all-start.2 = ((bf16[8,512,128]{2,1,0:T(8,128)(2,1)}), bf16[8,512,128]{2,1,0:T(8,128)(2,1)S(1)}, u32[]{:S(2)}, u32[]{:S(2)}) async-start(bf16[8,512,128]{2,1,0:T(8,128)(2,1)} %encode_keyval.1), calls=%async_computation.2 | async-start | bytes 2097152 | tf_op jit(solution)/shard_map/exchange_keyval/all_to_all | solution.py:267
  87.9 17.2 %all-to-all-done.2.kv_ref = bf16[8,512,128]{2,1,0:T(8,128)(2,1)S(1)} async-done(((bf16[8,512,128]{2,1,0:T(8,128)(2,1)}), bf16[8,512,128]{2,1,0:T(8,128)(2,1)S(1)}, u32[]{:S(2)}, u32[]{:S(2)}) %all-to-all-start.2) | async-done | bytes 1048608 | tf_op jit(solution)/shard_map/exchange_keyval/all_to_all | solution.py:267
  105.1 3.2 %cross_attention.1 = bf16[64,2,640]{2,1,0:T(2,128)(2,1)S(1)} custom-call(s32[2]{0:T(128)S(1)} %pad_add_fusion.first_ref, s32[512]{0:T(512)S(1)} %copy-done.5, s32[512]{0:T(512)S(1)} %copy-done.6, bf16[512,128]{1,0:T(8,128)(2,1)S(1)} %bitcast.21, bf16[8,512,128]{2,1,0:T(8,128)(2,1)S(1)} %all-to-all-done.2.kv_ref), custom_call_target="tpu_custom_call" | custom-call | tf_op jit(solution)/shard_map/cross_attention/pallas_call | solution.py:187
  108.3 30.7 %all_to_all.20.part_ref = bf16[64,2,640]{2,1,0:T(2,128)(2,1)} all-to-all(bf16[64,2,640]{2,1,0:T(2,128)(2,1)S(1)} %cross_attention.1), channel_id=1, replica_groups=mesh['yh'=2,'x'=4,'z'=16,'yl'=2,'c'=2] {'z','yl','c'}, dimensions={0} | all-to-all | bytes 327680 | tf_op jit(solution)/shard_map/exchange_partials/all_to_all | solution.py:272
  139.0 2.3 %merge_partials.1 = f32[8,128]{1,0:T(8,128)} custom-call(bf16[64,2,640]{2,1,0:T(2,128)(2,1)} %all_to_all.20.part_ref), custom_call_target="tpu_custom_call" | custom-call | tf_op jit(solution)/shard_map/merge_partials/pallas_call | solution.py:207
  (34 shorter events, 3.0 us)
Async XLA Ops:
  0.0 1.0 copy-start
  2.2 7.8 %copy-start.9 = (bf16[16,1024]{1,0:T(8,128)(2,1)S(1)}, bf16[16,1024]{1,0:T(8,128)(2,1)}, u32[]{:S(2)}) copy-start(bf16[16,1024]{1,0:T(8,128)(2,1)} %param.14) | copy-start | bytes 98308
  2.3 23.5 %all-to-all-start = ((bf16[16,256,128]{2,1,0:T(8,128)(2,1)}), bf16[16,256,128]{2,1,0:T(8,128)(2,1)}, u32[]{:S(2)}, u32[]{:S(2)}) async-start(bf16[16,256,128]{2,1,0:T(8,128)(2,1)} %broadcast_in_dim.4), calls=%async_computation | async-start | bytes 2097152 | tf_op jit(solution)/shard_map/gather_kv_weight/all_to_all | solution.py:219
  15.2 10.5 %collective-permute-start = (bf16[2,8,16,128]{3,2,1,0:T(8,128)(2,1)S(1)}, bf16[2,8,16,128]{3,2,1,0:T(8,128)(2,1)S(1)}, u32[]{:S(2)}, u32[]{:S(2)}) collective-permute-start(bf16[2,8,16,128]{3,2,1,0:T(8,128)(2,1)S(1)} %bitcast.26), channel_id=1, source_target_pairs={{0,0},{1,5},{4,4},{5,9},{8,8},{9,13},{12,12},{13,17},{16,16},{17,2... | collective-permute-start | bytes 196616 | tf_op jit(solution)/shard_map/out_weight_over_z/ppermute | solution.py:246
  27.8 25.7 %collective-permute-start.1 = (bf16[8,256,128]{2,1,0:T(8,128)(2,1)}, bf16[8,256,128]{2,1,0:T(8,128)(2,1)}, u32[]{:S(2)}, u32[]{:S(2)}) collective-permute-start(bf16[8,256,128]{2,1,0:T(8,128)(2,1)} %get-tuple-element.28), channel_id=1, source_target_pairs={{0,60},{4,0},{8,4},{12,8},{16,12},{20,16},{24,20},{28,24},{32,28},... | collective-permute-start | bytes 1572872 | tf_op jit(solution)/shard_map/kv_weight_over_z/ppermute | solution.py:254
  39.6 16.1 %collective-permute-start.2 = (bf16[8,256,128]{2,1,0:T(8,128)(2,1)S(1)}, bf16[8,256,128]{2,1,0:T(8,128)(2,1)}, u32[]{:S(2)}, u32[]{:S(2)}) collective-permute-start(bf16[8,256,128]{2,1,0:T(8,128)(2,1)S(1)} %get-tuple-element.27), channel_id=1, source_target_pairs={{0,4},{4,8},{8,12},{12,16},{16,20},{20,24},{24,28},{28,32},{32,36}... | collective-permute-start | bytes 1572872 | tf_op jit(solution)/shard_map/kv_weight_over_z/ppermute | solution.py:255
  41.5 30.3 %collective-permute-start.3 = (bf16[16,256,128]{2,1,0:T(8,128)(2,1)}, bf16[16,256,128]{2,1,0:T(8,128)(2,1)}, u32[]{:S(2)}, u32[]{:S(2)}) collective-permute-start(bf16[16,256,128]{2,1,0:T(8,128)(2,1)} %all-to-all-done.refs_0_), channel_id=1, source_target_pairs={{0,1},{1,0},{2,3},{3,2},{4,5},{5,4},{6,7},{7,6},{8,9},{9,8},{10,11... | collective-permute-start | bytes 3145736 | tf_op jit(solution)/shard_map/swap_kv_weight/ppermute | solution.py:258
  47.4 11.7 %copy-start.1 = (bf16[256,1024]{1,0:T(8,128)(2,1)S(1)}, bf16[256,1024]{1,0:T(8,128)(2,1)}, u32[]{:S(2)}) copy-start(bf16[256,1024]{1,0:T(8,128)(2,1)} %q_ref) | copy-start | bytes 1572868
  47.4 11.7 %copy-start.2 = (bf16[256,1024]{1,0:T(8,128)(2,1)S(1)}, bf16[256,1024]{1,0:T(8,128)(2,1)}, u32[]{:S(2)}) copy-start(bf16[256,1024]{1,0:T(8,128)(2,1)} %k_ref.1) | copy-start | bytes 1572868
  47.4 24.4 %all-to-all-start.1 = ((bf16[16,2,8,16,128]{4,3,2,1,0:T(8,128)(2,1)}), bf16[16,2,8,16,128]{4,3,2,1,0:T(8,128)(2,1)S(1)}, u32[]{:S(2)}, u32[]{:S(2)}) async-start(bf16[16,2,8,16,128]{4,3,2,1,0:T(8,128)(2,1)} %broadcast_in_dim.5), calls=%async_computation.1 | async-start | bytes 2097152 | tf_op jit(solution)/shard_map/out_weight_over_plane/all_to_all | solution.py:219
  53.5 18.3 %collective-permute-start.4 = (bf16[8,256,128]{2,1,0:T(8,128)(2,1)}, bf16[8,256,128]{2,1,0:T(8,128)(2,1)}, u32[]{:S(2)}, u32[]{:S(2)}) collective-permute-start(bf16[8,256,128]{2,1,0:T(8,128)(2,1)} %collective-permute-done.1.refs_1_), channel_id=1, source_target_pairs={{0,1},{1,0},{2,3},{3,2},{4,5},{5,4},{6,7},{7,6},{8,9},{9,8},{10,11... | collective-permute-start | bytes 1572872 | tf_op jit(solution)/shard_map/swap_kv_weight/ppermute | solution.py:258
  55.7 16.1 %collective-permute-start.5 = (bf16[8,256,128]{2,1,0:T(8,128)(2,1)}, bf16[8,256,128]{2,1,0:T(8,128)(2,1)}, u32[]{:S(2)}, u32[]{:S(2)}) collective-permute-start(bf16[8,256,128]{2,1,0:T(8,128)(2,1)} %collective-permute-done.2.refs_2_), channel_id=1, source_target_pairs={{0,1},{1,0},{2,3},{3,2},{4,5},{5,4},{6,7},{7,6},{8,9},{9,8},{10,11... | collective-permute-start | bytes 1572872 | tf_op jit(solution)/shard_map/swap_kv_weight/ppermute | solution.py:258
  59.0 0.7 copy-start.6
  59.1 0.7 copy-start.5
  59.7 1.0 copy-start.3
  71.8 5.2 %collective-permute-start.6 = (bf16[16,2,8,16,128]{4,3,2,1,0:T(8,128)(2,1)S(1)}, bf16[16,2,8,16,128]{4,3,2,1,0:T(8,128)(2,1)S(1)}, u32[]{:S(2)}, u32[]{:S(2)}) collective-permute-start(bf16[16,2,8,16,128]{4,3,2,1,0:T(8,128)(2,1)S(1)} %all-to-all-done.1.mine_ref), channel_id=1, source_target_pairs={{0,1},{1,0},{2,3},{3,2},{4,5},{5,4},{6,7},{7,6},{8,9},{9,8},{10,11... | collective-permute-start | bytes 3145736 | tf_op jit(solution)/shard_map/swap_out_weight/ppermute | solution.py:263
  74.8 2.3 %copy-start.7 = (f32[1024]{0:T(1024)S(1)}, f32[1024]{0:T(1024)}, u32[]{:S(2)}) copy-start(f32[1024]{0:T(1024)} %param.15) | copy-start | bytes 12292
  77.0 1.0 copy-start.4
  84.0 3.7 %copy-start.8 = (bf16[64,1,1024]{2,0,1:T(8,128)(2,1)S(1)}, bf16[64,1,1024]{2,0,1:T(8,128)(2,1)}, u32[]{:S(2)}) copy-start(bf16[64,1,1024]{2,0,1:T(8,128)(2,1)} %param.17) | copy-start | bytes 393220
  84.0 21.0 %all-to-all-start.2 = ((bf16[8,512,128]{2,1,0:T(8,128)(2,1)}), bf16[8,512,128]{2,1,0:T(8,128)(2,1)S(1)}, u32[]{:S(2)}, u32[]{:S(2)}) async-start(bf16[8,512,128]{2,1,0:T(8,128)(2,1)} %encode_keyval.1), calls=%async_computation.2 | async-start | bytes 2097152 | tf_op jit(solution)/shard_map/exchange_keyval/all_to_all | solution.py:267

commit v5 on v3

--- a/solution.py
+++ b/solution.py
@@ -25,8 +25,8 @@
 PLANE = ("yh", "x", "yl")
 
 
-def params(**kw):
-    return pltpu.CompilerParams(vmem_limit_bytes=48 * 1024 * 1024, **kw)
+def params(mebibytes=20):
+    return pltpu.CompilerParams(vmem_limit_bytes=mebibytes * 1024 * 1024)
 
 
 def dot(a, b):
@@ -37,7 +37,8 @@
     return lax.dot_general(a, b, (((1,), (1,)), ((), ())), preferred_element_type=jnp.float32)
 
 
-def encoder_attention_kernel(slot_ref, span_ref, len_ref, q_ref, k_ref, v_ref, o_ref):
+def encoder_attention_kernel(slot_ref, span_ref, len_ref, q_ref, k_ref, v_ref, resid_ref, o_ref):
+    o_ref[1] = resid_ref[...]
     valid = len_ref[span_ref[slot_ref[0]]]
     keep = lax.broadcasted_iota(jnp.int32, (1, SEG_LEN), 1) < valid
     bias = jnp.where(keep, 0.0, MASKED).astype(jnp.float32)
@@ -52,59 +53,91 @@
             expo = jnp.exp(scores - jnp.max(scores, axis=-1, keepdims=True))
             probs = (expo * (1.0 / jnp.sum(expo, axis=-1, keepdims=True))).astype(jnp.bfloat16)
             parts.append(dot(probs, v))
-        o_ref[:, cols] = jnp.where(low, parts[0], parts[1]).astype(jnp.bfloat16)
-
-
-def encoder_attention(slot, span_ids, seg_lengths, q, k, v):
+        o_ref[0, :, cols] = jnp.where(low, parts[0], parts[1]).astype(jnp.bfloat16)
+
+
+def encoder_attention(slot, span_ids, seg_lengths, q, k, v, resid):
     smem = pl.BlockSpec(memory_space=pltpu.SMEM)
     vmem = pl.BlockSpec(memory_space=pltpu.VMEM)
     return pl.pallas_call(
         encoder_attention_kernel,
-        out_shape=jax.ShapeDtypeStruct((SEG_LEN, D_ENC), jnp.bfloat16),
-        in_specs=[smem, smem, smem, vmem, vmem, vmem],
+        out_shape=jax.ShapeDtypeStruct((2, SEG_LEN, D_ENC), jnp.bfloat16),
+        in_specs=[smem, smem, smem, vmem, vmem, vmem, vmem],
         out_specs=vmem,
         compiler_params=params(),
         cost_estimate=pl.CostEstimate(
             flops=8 * SEG_LEN * SEG_LEN * D_ENC, bytes_accessed=8 * SEG_LEN * D_ENC,
             transcendentals=SEG_LEN * SEG_LEN * ENC_HEADS),
         name="encoder_attention",
-    )(slot, span_ids, seg_lengths, q, k, v)
-
-
-def encode_kernel(place_ref, ctx_ref, mine_ref, other_ref, resid_ref, gain_ref, kv_mine_ref,
-                  kv_other_ref, o_ref, w_ref, enc_ref):
+    )(slot, span_ids, seg_lengths, q, k, v, resid)
+
+
+def project_kernel(place_ref, gain_ref, ctx_ref, mine_ref, other_ref, o_ref, w_ref):
     z, core = place_ref[0], place_ref[1]
     for part_ref, at in ((mine_ref, core), (other_ref, 1 - core)):
         for ha in range(KV_HEADS):
             plane = lax.rem(z + 32 - 2 * ha - at, 16)
             for yl in range(2):
-                w_ref[pl.ds(pl.multiple_of(64 * plane + 32 * yl, 32), 32), :] = part_ref[ha * 2 + yl]
-    hidden = resid_ref[...].astype(jnp.float32) + dot(ctx_ref[...], w_ref[...])
+                for c in range(2):
+                    row = pl.multiple_of(64 * plane + 32 * yl + 16 * c, 16)
+                    w_ref[:, pl.ds(row, 16), :] = part_ref[ha * 2 + yl, c]
+    ctx = ctx_ref[0]
+    hidden = jnp.concatenate(
+        [dot(ctx, jnp.concatenate([w_ref[2 * j], w_ref[2 * j + 1]], axis=1)) for j in range(4)], axis=1)
+    hidden = hidden + ctx_ref[1].astype(jnp.float32)
     factor = lax.rsqrt(jnp.mean(hidden * hidden, axis=-1, keepdims=True) + 1e-05)
     encoded = (hidden * factor * gain_ref[...]).astype(jnp.bfloat16)
-    half = D_ENC // 2
-    enc_ref[0] = encoded[:, :half]
-    enc_ref[1] = encoded[:, half:]
-    near, far = enc_ref[core], enc_ref[1 - core]
+    for piece in range(4):
+        o_ref[piece] = encoded[:, piece * 256:(piece + 1) * 256]
+
+
+def project(place, gain, ctx, mine, other):
+    smem = pl.BlockSpec(memory_space=pltpu.SMEM)
+    vmem = pl.BlockSpec(memory_space=pltpu.VMEM)
+    return pl.pallas_call(
+        project_kernel,
+        out_shape=jax.ShapeDtypeStruct((4, SEG_LEN, 256), jnp.bfloat16),
+        in_specs=[smem] + [vmem] * 4,
+        out_specs=vmem,
+        scratch_shapes=[pltpu.VMEM((8, D_ENC, HEAD), jnp.bfloat16)],
+        compiler_params=params(),
+        cost_estimate=pl.CostEstimate(
+            flops=2 * SEG_LEN * D_ENC * D_ENC, bytes_accessed=6 * D_ENC * D_ENC, transcendentals=SEG_LEN),
+        name="project",
+    )(place, gain, ctx, mine, other)
+
+
+def keyval_kernel(place_ref, enc_ref, *refs):
+    kv_refs, o_ref = refs[:8], refs[-1]
+    core, odd = place_ref[1], place_ref[2]
+    near, far = 2 * core, 2 - 2 * core
+    pieces = [enc_ref[near + odd], enc_ref[near + 1 - odd], enc_ref[far + odd], enc_ref[far + 1 - odd]]
+
+    def rows(ref, h):
+        return jnp.concatenate(
+            [jnp.concatenate([ref[2 * h + yl, :128], ref[2 * h + yl, 128:]], axis=1) for yl in range(2)], axis=0)
+
     for h in range(KV_HEADS):
-        o_ref[h] = (dot(near, kv_mine_ref[h]) + dot(far, kv_other_ref[h])).astype(jnp.bfloat16)
-
-
-def encode(place, ctx, mine, other, resid, gain, kv_mine, kv_other):
-    smem = pl.BlockSpec(memory_space=pltpu.SMEM)
-    vmem = pl.BlockSpec(memory_space=pltpu.VMEM)
-    return pl.pallas_call(
-        encode_kernel,
-        out_shape=jax.ShapeDtypeStruct((KV_HEADS, SEG_LEN, 2 * HEAD), jnp.bfloat16),
-        in_specs=[smem] + [vmem] * 7,
-        out_specs=vmem,
-        scratch_shapes=[pltpu.VMEM((D_ENC, D_ENC), jnp.bfloat16),
-                        pltpu.VMEM((2, SEG_LEN, D_ENC // 2), jnp.bfloat16)],
+        side, at = divmod(h, KV_HEADS // 2)
+        total = dot(pieces[0], rows(kv_refs[side], at)) + dot(pieces[1], rows(kv_refs[2 + side], at))
+        total += dot(pieces[2], rows(kv_refs[4 + side], at)) + dot(pieces[3], rows(kv_refs[6 + side], at))
+        o_ref[h, :SEG_LEN] = total[:, :HEAD].astype(jnp.bfloat16)
+        o_ref[h, SEG_LEN:] = total[:, HEAD:].astype(jnp.bfloat16)
+
+
+def keys_and_values(place, encoded, kvs):
+    smem = pl.BlockSpec(memory_space=pltpu.SMEM)
+    vmem = pl.BlockSpec(memory_space=pltpu.VMEM)
+    return pl.pallas_call(
+        keyval_kernel,
+        out_shape=jax.ShapeDtypeStruct((KV_HEADS, 2 * SEG_LEN, HEAD), jnp.bfloat16),
+        in_specs=[smem] + [vmem] * 9,
+        out_specs=vmem,
         compiler_params=params(),
         cost_estimate=pl.CostEstimate(
-            flops=6 * SEG_LEN * D_ENC * D_ENC, bytes_accessed=8 * D_ENC * D_ENC, transcendentals=SEG_LEN),
-        name="encode_keyval",
-    )(place, ctx, mine, other, resid, gain, kv_mine, kv_other)
+            flops=4 * SEG_LEN * D_ENC * D_ENC, bytes_accessed=5 * D_ENC * D_ENC, transcendentals=0),
+        name="keys_and_values",
+    )(place, encoded, *kvs)
 
 
 def cross_kernel(slots, first_ref, span_ref, len_ref, q_ref, kv_ref, o_ref):
@@ -115,8 +148,8 @@
         valid = len_ref[span_ref[first_ref[0] + s * first_ref[1]]]
         bias.append(jnp.where(lane < valid, 0.0, MASKED).astype(jnp.float32))
     bias = jnp.concatenate(bias, axis=1)
-    keys = kv_ref[:, :, :HEAD].reshape(slots * SEG_LEN, HEAD)
-    values = kv_ref[:, :, HEAD:].reshape(slots * SEG_LEN, HEAD)
+    keys = kv_ref[:, :SEG_LEN].reshape(slots * SEG_LEN, HEAD)
+    values = kv_ref[:, SEG_LEN:].reshape(slots * SEG_LEN, HEAD)
     rows = 2 * QTAIL
     column = lax.broadcasted_iota(jnp.int32, (rows, HEAD), 1)
     levels = jnp.zeros((rows, HEAD), jnp.float32)
@@ -190,12 +223,14 @@
     yl, z = lax.axis_index("yl"), lax.axis_index("z")
     swap = functools.partial(lax.ppermute, axis_name="c", perm=[(0, 1), (1, 0)])
 
+    odd = lax.rem(z, 2)
+
     with jax.named_scope("gather_kv_weight"):
-        quarter = lax.dynamic_slice_in_dim(
-            kv_weight.reshape(D_ENC, 2 * HEAD), core * 512 + yl * 256, 256, 0)
-        kv_mine = spread(quarter, PLANE)
+        eighth = lax.dynamic_slice_in_dim(
+            kv_weight.reshape(D_ENC, 2 * HEAD), core * 512 + odd * 256 + yl * 128, 128, 0)
+        kv_mine = spread(jnp.concatenate([eighth[:, :HEAD], eighth[:, HEAD:]], axis=0), PLANE)
     with jax.named_scope("out_weight_over_z"):
-        pair = lax.all_gather(out_weight, "c", axis=0, tiled=True)
+        pair = lax.all_gather(out_weight.reshape(16, 8, HEAD).transpose(1, 0, 2), "c")
         hops = []
         for ha_at in range(8):
             for z_at in range(16):
@@ -203,20 +238,24 @@
                     there = (z_at + 2 * ha_at + c_at) % 16
                     hops.append(((ha_at * 16 + z_at) * 2 + c_at, (ha_at * 16 + there) * 2 + c_at))
         pair = lax.ppermute(pair, ("yh", "x", "z", "c"), hops)
-    kv_mine, pair, enc_query = lax.optimization_barrier((kv_mine, pair, enc_query))
+    slot = (ha * sa_count + sa).reshape(1).astype(jnp.int32)
+    context = encoder_attention(slot, span_ids, seg_lengths, enc_query, enc_key, enc_value, enc_resid)
+    kv_mine, pair, context = lax.optimization_barrier((kv_mine, pair, context))
     with jax.named_scope("out_weight_over_plane"):
         w_mine = spread(pair, PLANE)
-    kv_mine = kv_mine.reshape(KV_HEADS, D_ENC // 2, 2 * HEAD)
-    with jax.named_scope("swap_kv_weight"):
-        kv_other = swap(kv_mine)
-    slot = (ha * sa_count + sa).reshape(1).astype(jnp.int32)
-    context = encoder_attention(slot, span_ids, seg_lengths, enc_query, enc_key, enc_value)
-    w_mine, kv_other, context = lax.optimization_barrier((w_mine, kv_other, context))
-    with jax.named_scope("swap_out_weight"):
+    with jax.named_scope("kv_weight_over_z"):
+        up = [(i, (i + 1) % 16) for i in range(16)]
+        down = [(i, (i + 15) % 16) for i in range(16)]
+        halves = kv_mine[:8], kv_mine[8:]
+        near = list(halves) + [lax.ppermute(halves[0], "z", down), lax.ppermute(halves[1], "z", up)]
+    with jax.named_scope("swap_weights"):
+        far = [swap(half) for half in halves]
+        w_mine, near, far = lax.optimization_barrier((w_mine, near, far))
         w_other = swap(w_mine)
-    place = jnp.stack([z, core]).astype(jnp.int32)
-    keyval = encode(place, context, w_mine, w_other, enc_resid, norm_gain.reshape(1, D_ENC),
-                    kv_mine, kv_other)
+        far = far + [swap(half) for half in near[2:]]
+    place = jnp.stack([z, core, odd]).astype(jnp.int32)
+    encoded = project(place, norm_gain.reshape(1, D_ENC), context, w_mine, w_other)
+    keyval = keys_and_values(place, encoded, near + far)
     with jax.named_scope("exchange_keyval"):
         keyval = lax.all_to_all(keyval, HA, 0, 0, tiled=True)
     first = jnp.stack([sa, sa_count]).astype(jnp.int32)

time: 141 us -> 137 us (0.972)
  waiting for transfers between devices: 52.2 us -> 26.5 us
  starting transfers between devices: 26.8 us -> 52.3 us
  blocking collectives: 41.3 us -> 33.8 us
  local copies, waits for them, and re-layouts: 5.83 us -> 10.3 us
    all_to_all x2, waiting for transfers between devices: 24.3 us -> 0.01 us  [spread(): return lax.all_to_all(copies, axes, 0, 0, tiled=True)]
    all_to_all x2, starting transfers between devices: 11.6 us -> 22.3 us  [spread(): return lax.all_to_all(copies, axes, 0, 0, tiled=True)]
    ppermute x1 -> x6, starting transfers between devices: 6.8 us -> 16.3 us  [the longest x2 6.09 us: local(): far = [swap(half) for half in halves]]
    all_to_all x1, blocking collectives: 36 us -> 28.7 us  [local(): parts = lax.all_to_all(parts, SA, 0, 0, tiled=True)]
    ppermute x1 -> x6, waiting for transfers between devices: 0.01 us -> 5.46 us  [the longest x1 2.75 us: local(): lax.ppermute(halves[1], 'z', up)]
    ppermute x1, waiting for transfers between devices: 8.5 us -> 3.76 us  [local(): pair = lax.ppermute(pair, ('yh', 'x', 'z', 'c'), hops)]
    unnamed x21 -> x42, local copies, waits for them, and re-layouts: 3.18 us -> 6.59 us
    all_to_all x1, starting transfers between devices: 3.69 us -> 6.69 us  [local(): keyval = lax.all_to_all(keyval, HA, 0, 0, tiled=True)]
  transfers between devices with their start and end apart: 6 -> 11, of which waited for: 5 -> 4; matrix products, arithmetic and copies ran while one was open for 1% -> 1% of each run, Pallas kernels for 2% -> 3%
where the time goes in v5:
time: 137 us; the launch traced here: 136 us
  starting transfers between devices  52.3 us (38%)
  blocking collectives  33.8 us (25%)
  waiting for transfers between devices  26.5 us (19%)
  Pallas kernels  13 us (9%)
  local copies, waits for them, and re-layouts  10.3 us (8%)
    all_to_all x1, blocking collectives, local(): parts = lax.all_to_all(parts, SA, 0, 0, tiled=True)  28.7 us
    all_to_all x2, starting transfers between devices, spread(): return lax.all_to_all(copies, axes, 0, 0, tiled=True)  22.3 us
    all_to_all x1, waiting for transfers between devices, local(): keyval = lax.all_to_all(keyval, HA, 0, 0, tiled=True)  17.3 us
    all_to_all x1, starting transfers between devices, local(): keyval = lax.all_to_all(keyval, HA, 0, 0, tiled=True)  6.69 us
    unnamed x42, local copies, waits for them, and re-layouts  6.59 us
    ppermute x2, starting transfers between devices, local(): far = [swap(half) for half in halves]  6.09 us
    all_gather x1, blocking collectives, local(): lax.all_gather(out_weight.reshape(16, 8, HEAD).transpose(1, 0, 2), 'c')  5.09 us
    ppermute x1, starting transfers between devices, local(): w_other = swap(w_mine)  5.08 us
  transfers between devices with their start and end apart: 11, of which 4 were waited for; matrix products, arithmetic and copies ran while one was open for 1% of the time, Pallas kernels for 3%

profile of v5, /device:TPU:1, one launch (start us, length us, event | category | flops | bytes accessed | tf_op | source)
XLA Modules:
  0.0 136.4 jit_solution(10663702131612027205)
XLA Ops:
  2.3 7.8 %all-to-all-start = ((bf16[16,256,128]{2,1,0:T(8,128)(2,1)}), bf16[16,256,128]{2,1,0:T(8,128)(2,1)}, u32[]{:S(2)}, u32[]{:S(2)}) async-start(bf16[16,256,128]{2,1,0:T(8,128)(2,1)} %broadcast_in_dim.4), calls=%async_computation | async-start | bytes 2097152 | tf_op jit(solution)/shard_map/gather_kv_weight/all_to_all | solution.py:213
  10.1 5.1 %all-gather = bf16[16,16,128]{2,0,1:T(8,128)(2,1)S(1)} all-gather(bf16[8,16,128]{2,0,1:T(8,128)(2,1)S(1)} %bitcast.24), channel_id=2, replica_groups=mesh['yh'=2,'x'=4,'z'=16,'yl'=2,'c'=2] {'c'}, dimensions={0}, use_global_device_ids=true | all-gather | bytes 98304 | tf_op jit(solution)/shard_map/out_weight_over_z/all_gather | solution.py:233
  15.2 1.9 %collective-permute-start = (bf16[2,8,16,128]{3,2,1,0:T(8,128)(2,1)S(1)}, bf16[2,8,16,128]{3,2,1,0:T(8,128)(2,1)S(1)}, u32[]{:S(2)}, u32[]{:S(2)}) collective-permute-start(bf16[2,8,16,128]{3,2,1,0:T(8,128)(2,1)S(1)} %bitcast.26), channel_id=1, source_target_pairs={{0,0},{1,5},{4,4},{5,9},{8,8},{9,13},{12,12},{13,17},{16,16},{17,2... | collective-permute-start | bytes 196616 | tf_op jit(solution)/shard_map/out_weight_over_z/ppermute | solution.py:240
  18.9 3.1 %encoder_attention.1.ctx_ref = bf16[2,256,1024]{2,1,0:T(8,128)(2,1)S(1)} custom-call(s32[1]{0:T(128)} %bitcast.10.slot_ref, s32[512]{0:T(512)S(1)} %copy-done.15, s32[512]{0:T(512)S(1)} %copy-done.16, bf16[256,1024]{1,0:T(8,128)(2,1)S(1)} %copy-done.11, bf16[256,1024]{1,0:T(8,128)(2,1)S(1)} %copy-done.12, bf16[256,1024]{1,0:T(8,128)(2,1)S(1)} %copy-done.13, ...), custom_call_target="tpu_custom_call" | custom-call | flops 536870912 | bytes 2097152 | tf_op jit(solution)/shard_map/encoder_attention/pallas_call | solution.py:62
  22.0 3.8 %collective-permute-done = bf16[2,8,16,128]{3,2,1,0:T(8,128)(2,1)S(1)} collective-permute-done((bf16[2,8,16,128]{3,2,1,0:T(8,128)(2,1)S(1)}, bf16[2,8,16,128]{3,2,1,0:T(8,128)(2,1)S(1)}, u32[]{:S(2)}, u32[]{:S(2)}) %collective-permute-start) | collective-permute-done | bytes 65568 | tf_op jit(solution)/shard_map/out_weight_over_z/ppermute | solution.py:240
  25.7 1.2 broadcast_in_dim.5
  27.0 14.5 %all-to-all-start.1 = ((bf16[16,2,8,16,128]{4,3,2,1,0:T(8,128)(2,1)}), bf16[16,2,8,16,128]{4,3,2,1,0:T(8,128)(2,1)S(1)}, u32[]{:S(2)}, u32[]{:S(2)}) async-start(bf16[16,2,8,16,128]{4,3,2,1,0:T(8,128)(2,1)} %broadcast_in_dim.5), calls=%async_computation.1 | async-start | bytes 2097152 | tf_op jit(solution)/shard_map/out_weight_over_plane/all_to_all | solution.py:213
  41.5 1.3 fusion
  42.8 3.9 %collective-permute-start.1 = (bf16[8,256,128]{2,1,0:T(8,128)(2,1)S(1)}, bf16[8,256,128]{2,1,0:T(8,128)(2,1)S(1)}, u32[]{:S(2)}, u32[]{:S(2)}) collective-permute-start(bf16[8,256,128]{2,1,0:T(8,128)(2,1)S(1)} %get-tuple-element.19.refs_0_), channel_id=1, source_target_pairs={{0,60},{4,0},{8,4},{12,8},{16,12},{20,16},{24,20},{28,24},{32,28},... | collective-permute-start | bytes 1572872 | tf_op jit(solution)/shard_map/kv_weight_over_z/ppermute | solution.py:250
  46.7 1.9 %collective-permute-start.2 = (bf16[8,256,128]{2,1,0:T(8,128)(2,1)S(1)}, bf16[8,256,128]{2,1,0:T(8,128)(2,1)S(1)}, u32[]{:S(2)}, u32[]{:S(2)}) collective-permute-start(bf16[8,256,128]{2,1,0:T(8,128)(2,1)S(1)} %get-tuple-element.20.refs_1_), channel_id=1, source_target_pairs={{0,4},{4,8},{8,12},{12,16},{16,20},{20,24},{24,28},{28,32},{32,36}... | collective-permute-start | bytes 1572872 | tf_op jit(solution)/shard_map/kv_weight_over_z/ppermute | solution.py:250
  48.6 4.2 %collective-permute-start.3 = (bf16[8,256,128]{2,1,0:T(8,128)(2,1)S(1)}, bf16[8,256,128]{2,1,0:T(8,128)(2,1)S(1)}, u32[]{:S(2)}, u32[]{:S(2)}) collective-permute-start(bf16[8,256,128]{2,1,0:T(8,128)(2,1)S(1)} %get-tuple-element.19.refs_0_), channel_id=1, source_target_pairs={{0,1},{1,0},{2,3},{3,2},{4,5},{5,4},{6,7},{7,6},{8,9},{9,8},{10,11... | collective-permute-start | bytes 1572872 | tf_op jit(solution)/shard_map/swap_weights/ppermute | solution.py:252
  53.6 1.9 %collective-permute-start.4 = (bf16[8,256,128]{2,1,0:T(8,128)(2,1)S(1)}, bf16[8,256,128]{2,1,0:T(8,128)(2,1)S(1)}, u32[]{:S(2)}, u32[]{:S(2)}) collective-permute-start(bf16[8,256,128]{2,1,0:T(8,128)(2,1)S(1)} %get-tuple-element.20.refs_1_), channel_id=1, source_target_pairs={{0,1},{1,0},{2,3},{3,2},{4,5},{5,4},{6,7},{7,6},{8,9},{9,8},{10,11... | collective-permute-start | bytes 1572872 | tf_op jit(solution)/shard_map/swap_weights/ppermute | solution.py:252
  55.5 2.7 %collective-permute-done.1.refs_2_ = bf16[8,256,128]{2,1,0:T(8,128)(2,1)S(1)} collective-permute-done((bf16[8,256,128]{2,1,0:T(8,128)(2,1)S(1)}, bf16[8,256,128]{2,1,0:T(8,128)(2,1)S(1)}, u32[]{:S(2)}, u32[]{:S(2)}) %collective-permute-start.1) | collective-permute-done | bytes 524320 | tf_op jit(solution)/shard_map/kv_weight_over_z/ppermute | solution.py:250
  58.2 2.7 %collective-permute-done.2.refs_3_ = bf16[8,256,128]{2,1,0:T(8,128)(2,1)S(1)} collective-permute-done((bf16[8,256,128]{2,1,0:T(8,128)(2,1)S(1)}, bf16[8,256,128]{2,1,0:T(8,128)(2,1)S(1)}, u32[]{:S(2)}, u32[]{:S(2)}) %collective-permute-start.2) | collective-permute-done | bytes 524320 | tf_op jit(solution)/shard_map/kv_weight_over_z/ppermute | solution.py:250
  63.4 5.1 %collective-permute-start.5 = (bf16[16,2,8,16,128]{4,3,2,1,0:T(8,128)(2,1)S(1)}, bf16[16,2,8,16,128]{4,3,2,1,0:T(8,128)(2,1)S(1)}, u32[]{:S(2)}, u32[]{:S(2)}) collective-permute-start(bf16[16,2,8,16,128]{4,3,2,1,0:T(8,128)(2,1)S(1)} %all-to-all-done.1.mine_ref), channel_id=1, source_target_pairs={{0,1},{1,0},{2,3},{3,2},{4,5},{5,4},{6,7},{7,6},{8,9},{9,8},{10,11... | collective-permute-start | bytes 3145736 | tf_op jit(solution)/shard_map/swap_weights/ppermute | solution.py:254
  68.5 1.9 %collective-permute-start.6 = (bf16[8,256,128]{2,1,0:T(8,128)(2,1)}, bf16[8,256,128]{2,1,0:T(8,128)(2,1)S(1)}, u32[]{:S(2)}, u32[]{:S(2)}) collective-permute-start(bf16[8,256,128]{2,1,0:T(8,128)(2,1)} %copy-done.3), channel_id=1, source_target_pairs={{0,1},{1,0},{2,3},{3,2},{4,5},{5,4},{6,7},{7,6},{8,9},{9,8},{10,11... | collective-permute-start | bytes 1572872 | tf_op jit(solution)/shard_map/swap_weights/ppermute | solution.py:255
  70.4 2.4 %collective-permute-start.7 = (bf16[8,256,128]{2,1,0:T(8,128)(2,1)}, bf16[8,256,128]{2,1,0:T(8,128)(2,1)S(1)}, u32[]{:S(2)}, u32[]{:S(2)}) collective-permute-start(bf16[8,256,128]{2,1,0:T(8,128)(2,1)} %copy-done.5), channel_id=1, source_target_pairs={{0,1},{1,0},{2,3},{3,2},{4,5},{5,4},{6,7},{7,6},{8,9},{9,8},{10,11... | collective-permute-start | bytes 1572872 | tf_op jit(solution)/shard_map/swap_weights/ppermute | solution.py:255
  73.5 1.5 %project.1.enc_ref = bf16[4,256,256]{2,1,0:T(8,128)(2,1)S(1)} custom-call(s32[3]{0:T(128)S(1)} %pad_add_fusion.1.place_ref, f32[1,1024]{1,0:T(1,128)S(1)} %bitcast.22, bf16[2,256,1024]{2,1,0:T(8,128)(2,1)S(1)} %encoder_attention.1.ctx_ref, bf16[16,2,8,16,128]{4,3,2,1,0:T(8,128)(2,1)S(1)} %all-to-all-done.1.mine_ref, ...), custom_call_target="tpu_custom_call" | custom-call | flops 536870912 | bytes 6291456 | tf_op jit(solution)/shard_map/project/pallas_call | solution.py:97
  75.2 2.8 %keys_and_values.1 = bf16[8,512,128]{2,1,0:T(8,128)(2,1)} custom-call(s32[3]{0:T(128)S(1)} %pad_add_fusion.1.place_ref, bf16[4,256,256]{2,1,0:T(8,128)(2,1)S(1)} %project.1.enc_ref, bf16[8,256,128]{2,1,0:T(8,128)(2,1)S(1)} %copy-done.2, bf16[8,256,128]{2,1,0:T(8,128)(2,1)S(1)} %get-tuple-element.20.refs_1_, bf16[8,256,128]{2,1,0:T(8,128)(2,1)S(1)} %copy-done.4, ...), custom_call_target="tpu_custom_call" | custom-call | flops 1073741824 | bytes 5242880 | tf_op jit(solution)/shard_map/keys_and_values/pallas_call | solution.py:131
  78.0 6.7 %all-to-all-start.2 = ((bf16[8,512,128]{2,1,0:T(8,128)(2,1)}), bf16[8,512,128]{2,1,0:T(8,128)(2,1)S(1)}, u32[]{:S(2)}, u32[]{:S(2)}) async-start(bf16[8,512,128]{2,1,0:T(8,128)(2,1)} %keys_and_values.1), calls=%async_computation.2 | async-start | bytes 2097152 | tf_op jit(solution)/shard_map/exchange_keyval/all_to_all | solution.py:260
  84.8 17.3 %all-to-all-done.2.kv_ref = bf16[8,512,128]{2,1,0:T(8,128)(2,1)S(1)} async-done(((bf16[8,512,128]{2,1,0:T(8,128)(2,1)}), bf16[8,512,128]{2,1,0:T(8,128)(2,1)S(1)}, u32[]{:S(2)}, u32[]{:S(2)}) %all-to-all-start.2) | async-done | bytes 1048608 | tf_op jit(solution)/shard_map/exchange_keyval/all_to_all | solution.py:260
  102.1 3.3 %cross_attention.1 = bf16[64,2,640]{2,1,0:T(2,128)(2,1)S(1)} custom-call(s32[2]{0:T(128)S(1)} %pad_add_fusion.first_ref, s32[512]{0:T(512)S(1)} %copy-done.15, s32[512]{0:T(512)S(1)} %copy-done.16, bf16[512,128]{1,0:T(8,128)(2,1)S(1)} %bitcast.21, bf16[8,512,128]{2,1,0:T(8,128)(2,1)S(1)} %all-to-all-done.2.kv_ref), custom_call_target="tpu_custom_call" | custom-call | tf_op jit(solution)/shard_map/cross_attention/pallas_call | solution.py:181
  105.3 28.7 %all_to_all.20.part_ref = bf16[64,2,640]{2,1,0:T(2,128)(2,1)} all-to-all(bf16[64,2,640]{2,1,0:T(2,128)(2,1)S(1)} %cross_attention.1), channel_id=1, replica_groups=mesh['yh'=2,'x'=4,'z'=16,'yl'=2,'c'=2] {'z','yl','c'}, dimensions={0} | all-to-all | bytes 327680 | tf_op jit(solution)/shard_map/exchange_partials/all_to_all | solution.py:265
  134.1 2.3 %merge_partials.1 = f32[8,128]{1,0:T(8,128)} custom-call(bf16[64,2,640]{2,1,0:T(2,128)(2,1)} %all_to_all.20.part_ref), custom_call_target="tpu_custom_call" | custom-call | tf_op jit(solution)/shard_map/merge_partials/pallas_call | solution.py:201
  (57 shorter events, 8.0 us)
Async XLA Ops:
  0.0 1.0 copy-start
  2.3 7.8 %copy-start.19 = (bf16[16,1024]{1,0:T(8,128)(2,1)S(1)}, bf16[16,1024]{1,0:T(8,128)(2,1)}, u32[]{:S(2)}) copy-start(bf16[16,1024]{1,0:T(8,128)(2,1)} %param.14) | copy-start | bytes 98308
  2.3 14.9 %copy-start.11 = (bf16[256,1024]{1,0:T(8,128)(2,1)S(1)}, bf16[256,1024]{1,0:T(8,128)(2,1)}, u32[]{:S(2)}) copy-start(bf16[256,1024]{1,0:T(8,128)(2,1)} %q_ref.1) | copy-start | bytes 1572868
  2.3 14.9 %copy-start.12 = (bf16[256,1024]{1,0:T(8,128)(2,1)S(1)}, bf16[256,1024]{1,0:T(8,128)(2,1)}, u32[]{:S(2)}) copy-start(bf16[256,1024]{1,0:T(8,128)(2,1)} %k_ref.1) | copy-start | bytes 1572868
  2.3 14.9 %copy-start.13 = (bf16[256,1024]{1,0:T(8,128)(2,1)S(1)}, bf16[256,1024]{1,0:T(8,128)(2,1)}, u32[]{:S(2)}) copy-start(bf16[256,1024]{1,0:T(8,128)(2,1)} %v_ref.1) | copy-start | bytes 1572868
  2.3 23.5 %all-to-all-start = ((bf16[16,256,128]{2,1,0:T(8,128)(2,1)}), bf16[16,256,128]{2,1,0:T(8,128)(2,1)}, u32[]{:S(2)}, u32[]{:S(2)}) async-start(bf16[16,256,128]{2,1,0:T(8,128)(2,1)} %broadcast_in_dim.4), calls=%async_computation | async-start | bytes 2097152 | tf_op jit(solution)/shard_map/gather_kv_weight/all_to_all | solution.py:213
  15.2 10.5 %collective-permute-start = (bf16[2,8,16,128]{3,2,1,0:T(8,128)(2,1)S(1)}, bf16[2,8,16,128]{3,2,1,0:T(8,128)(2,1)S(1)}, u32[]{:S(2)}, u32[]{:S(2)}) collective-permute-start(bf16[2,8,16,128]{3,2,1,0:T(8,128)(2,1)S(1)} %bitcast.26), channel_id=1, source_target_pairs={{0,0},{1,5},{4,4},{5,9},{8,8},{9,13},{12,12},{13,17},{16,16},{17,2... | collective-permute-start | bytes 196616 | tf_op jit(solution)/shard_map/out_weight_over_z/ppermute | solution.py:240
  17.8 1.0 copy-start.14
  27.0 36.4 %all-to-all-start.1 = ((bf16[16,2,8,16,128]{4,3,2,1,0:T(8,128)(2,1)}), bf16[16,2,8,16,128]{4,3,2,1,0:T(8,128)(2,1)S(1)}, u32[]{:S(2)}, u32[]{:S(2)}) async-start(bf16[16,2,8,16,128]{4,3,2,1,0:T(8,128)(2,1)} %broadcast_in_dim.5), calls=%async_computation.1 | async-start | bytes 2097152 | tf_op jit(solution)/shard_map/out_weight_over_plane/all_to_all | solution.py:213
  42.8 15.5 %collective-permute-start.1 = (bf16[8,256,128]{2,1,0:T(8,128)(2,1)S(1)}, bf16[8,256,128]{2,1,0:T(8,128)(2,1)S(1)}, u32[]{:S(2)}, u32[]{:S(2)}) collective-permute-start(bf16[8,256,128]{2,1,0:T(8,128)(2,1)S(1)} %get-tuple-element.19.refs_0_), channel_id=1, source_target_pairs={{0,60},{4,0},{8,4},{12,8},{16,12},{20,16},{24,20},{28,24},{32,28},... | collective-permute-start | bytes 1572872 | tf_op jit(solution)/shard_map/kv_weight_over_z/ppermute | solution.py:250
  46.7 14.3 %collective-permute-start.2 = (bf16[8,256,128]{2,1,0:T(8,128)(2,1)S(1)}, bf16[8,256,128]{2,1,0:T(8,128)(2,1)S(1)}, u32[]{:S(2)}, u32[]{:S(2)}) collective-permute-start(bf16[8,256,128]{2,1,0:T(8,128)(2,1)S(1)} %get-tuple-element.20.refs_1_), channel_id=1, source_target_pairs={{0,4},{4,8},{8,12},{12,16},{16,20},{20,24},{24,28},{28,32},{32,36}... | collective-permute-start | bytes 1572872 | tf_op jit(solution)/shard_map/kv_weight_over_z/ppermute | solution.py:250
  48.6 12.4 %collective-permute-start.3 = (bf16[8,256,128]{2,1,0:T(8,128)(2,1)S(1)}, bf16[8,256,128]{2,1,0:T(8,128)(2,1)S(1)}, u32[]{:S(2)}, u32[]{:S(2)}) collective-permute-start(bf16[8,256,128]{2,1,0:T(8,128)(2,1)S(1)} %get-tuple-element.19.refs_0_), channel_id=1, source_target_pairs={{0,1},{1,0},{2,3},{3,2},{4,5},{5,4},{6,7},{7,6},{8,9},{9,8},{10,11... | collective-permute-start | bytes 1572872 | tf_op jit(solution)/shard_map/swap_weights/ppermute | solution.py:252
  53.6 9.0 %collective-permute-start.4 = (bf16[8,256,128]{2,1,0:T(8,128)(2,1)S(1)}, bf16[8,256,128]{2,1,0:T(8,128)(2,1)S(1)}, u32[]{:S(2)}, u32[]{:S(2)}) collective-permute-start(bf16[8,256,128]{2,1,0:T(8,128)(2,1)S(1)} %get-tuple-element.20.refs_1_), channel_id=1, source_target_pairs={{0,1},{1,0},{2,3},{3,2},{4,5},{5,4},{6,7},{7,6},{8,9},{9,8},{10,11... | collective-permute-start | bytes 1572872 | tf_op jit(solution)/shard_map/swap_weights/ppermute | solution.py:252
  58.2 2.8 %copy-start.3 = (bf16[8,256,128]{2,1,0:T(8,128)(2,1)}, bf16[8,256,128]{2,1,0:T(8,128)(2,1)S(1)}, u32[]{:S(2)}) copy-start(bf16[8,256,128]{2,1,0:T(8,128)(2,1)S(1)} %collective-permute-done.1.refs_2_) | copy-start | bytes 1572868
  63.4 9.5 %collective-permute-start.5 = (bf16[16,2,8,16,128]{4,3,2,1,0:T(8,128)(2,1)S(1)}, bf16[16,2,8,16,128]{4,3,2,1,0:T(8,128)(2,1)S(1)}, u32[]{:S(2)}, u32[]{:S(2)}) collective-permute-start(bf16[16,2,8,16,128]{4,3,2,1,0:T(8,128)(2,1)S(1)} %all-to-all-done.1.mine_ref), channel_id=1, source_target_pairs={{0,1},{1,0},{2,3},{3,2},{4,5},{5,4},{6,7},{7,6},{8,9},{9,8},{10,11... | collective-permute-start | bytes 3145736 | tf_op jit(solution)/shard_map/swap_weights/ppermute | solution.py:254
  68.5 6.6 %collective-permute-start.6 = (bf16[8,256,128]{2,1,0:T(8,128)(2,1)}, bf16[8,256,128]{2,1,0:T(8,128)(2,1)S(1)}, u32[]{:S(2)}, u32[]{:S(2)}) collective-permute-start(bf16[8,256,128]{2,1,0:T(8,128)(2,1)} %copy-done.3), channel_id=1, source_target_pairs={{0,1},{1,0},{2,3},{3,2},{4,5},{5,4},{6,7},{7,6},{8,9},{9,8},{10,11... | collective-permute-start | bytes 1572872 | tf_op jit(solution)/shard_map/swap_weights/ppermute | solution.py:255
  70.4 4.7 %collective-permute-start.7 = (bf16[8,256,128]{2,1,0:T(8,128)(2,1)}, bf16[8,256,128]{2,1,0:T(8,128)(2,1)S(1)}, u32[]{:S(2)}, u32[]{:S(2)}) collective-permute-start(bf16[8,256,128]{2,1,0:T(8,128)(2,1)} %copy-done.5), channel_id=1, source_target_pairs={{0,1},{1,0},{2,3},{3,2},{4,5},{5,4},{6,7},{7,6},{8,9},{9,8},{10,11... | collective-permute-start | bytes 1572872 | tf_op jit(solution)/shard_map/swap_weights/ppermute | solution.py:255
  73.5 1.6 %copy-start.2 = (bf16[8,256,128]{2,1,0:T(8,128)(2,1)S(1)}, bf16[8,256,128]{2,1,0:T(8,128)(2,1)}, u32[]{:S(2)}) copy-start(bf16[8,256,128]{2,1,0:T(8,128)(2,1)} %copy-done.1) | copy-start | bytes 1572868
  73.5 1.6 %copy-start.4 = (bf16[8,256,128]{2,1,0:T(8,128)(2,1)S(1)}, bf16[8,256,128]{2,1,0:T(8,128)(2,1)}, u32[]{:S(2)}) copy-start(bf16[8,256,128]{2,1,0:T(8,128)(2,1)} %copy-done.3) | copy-start | bytes 1572868
  73.5 1.6 %copy-start.6 = (bf16[8,256,128]{2,1,0:T(8,128)(2,1)S(1)}, bf16[8,256,128]{2,1,0:T(8,128)(2,1)}, u32[]{:S(2)}) copy-start(bf16[8,256,128]{2,1,0:T(8,128)(2,1)} %copy-done.5) | copy-start | bytes 1572868
  73.5 1.6 %copy-start.8 = (bf16[8,256,128]{2,1,0:T(8,128)(2,1)S(1)}, bf16[8,256,128]{2,1,0:T(8,128)(2,1)}, u32[]{:S(2)}) copy-start(bf16[8,256,128]{2,1,0:T(8,128)(2,1)} %copy-done.7) | copy-start | bytes 1572868
  73.5 1.7 %copy-start.10 = (bf16[8,256,128]{2,1,0:T(8,128)(2,1)S(1)}, bf16[8,256,128]{2,1,0:T(8,128)(2,1)}, u32[]{:S(2)}) copy-start(bf16[8,256,128]{2,1,0:T(8,128)(2,1)} %copy-done.9) | copy-start | bytes 1572868
  78.0 6.7 %copy-start.18 = (bf16[64,1,1024]{2,0,1:T(8,128)(2,1)S(1)}, bf16[64,1,1024]{2,0,1:T(8,128)(2,1)}, u32[]{:S(2)}) copy-start(bf16[64,1,1024]{2,0,1:T(8,128)(2,1)} %param.17) | copy-start | bytes 393220
  78.0 24.1 %all-to-all-start.2 = ((bf16[8,512,128]{2,1,0:T(8,128)(2,1)}), bf16[8,512,128]{2,1,0:T(8,128)(2,1)S(1)}, u32[]{:S(2)}, u32[]{:S(2)}) async-start(bf16[8,512,128]{2,1,0:T(8,128)(2,1)} %keys_and_values.1), calls=%async_computation.2 | async-start | bytes 2097152 | tf_op jit(solution)/shard_map/exchange_keyval/all_to_all | solution.py:260
  (7 other events, 5.2 us)

commit v6 on v5

--- a/solution.py
+++ b/solution.py
@@ -108,8 +108,18 @@
 
 
 def keyval_kernel(place_ref, enc_ref, *refs):
-    kv_refs, o_ref = refs[:8], refs[-1]
+    kv_refs, o_ref, kv_bufs, done_ref, in_sems, out_sems = refs[:8], refs[8], refs[9:17], refs[17], refs[18], refs[19]
     core, odd = place_ref[1], place_ref[2]
+    copies = []
+    for h in range(KV_HEADS):
+        side, at = divmod(h, KV_HEADS // 2)
+        copies.append([
+            pltpu.make_async_copy(
+                kv_refs[side + 2 * i].at[pl.ds(2 * at, 2)], kv_bufs[side + 2 * i].at[pl.ds(2 * at, 2)],
+                in_sems.at[4 * h + i])
+            for i in range(4)])
+        for copy in copies[h]:
+            copy.start()
     near, far = 2 * core, 2 - 2 * core
     pieces = [enc_ref[near + odd], enc_ref[near + 1 - odd], enc_ref[far + odd], enc_ref[far + 1 - odd]]
 
@@ -117,23 +127,35 @@
         return jnp.concatenate(
             [jnp.concatenate([ref[2 * h + yl, :128], ref[2 * h + yl, 128:]], axis=1) for yl in range(2)], axis=0)
 
+    sends = []
     for h in range(KV_HEADS):
         side, at = divmod(h, KV_HEADS // 2)
-        total = dot(pieces[0], rows(kv_refs[side], at)) + dot(pieces[1], rows(kv_refs[2 + side], at))
-        total += dot(pieces[2], rows(kv_refs[4 + side], at)) + dot(pieces[3], rows(kv_refs[6 + side], at))
-        o_ref[h, :SEG_LEN] = total[:, :HEAD].astype(jnp.bfloat16)
-        o_ref[h, SEG_LEN:] = total[:, HEAD:].astype(jnp.bfloat16)
+        total = 0.0
+        for i in range(4):
+            copies[h][i].wait()
+            total += dot(pieces[i], rows(kv_bufs[side + 2 * i], at))
+        done_ref[h, :SEG_LEN] = total[:, :HEAD].astype(jnp.bfloat16)
+        done_ref[h, SEG_LEN:] = total[:, HEAD:].astype(jnp.bfloat16)
+        sends.append(pltpu.make_async_copy(done_ref.at[h], o_ref.at[h], out_sems.at[h]))
+        sends[h].start()
+    for send in sends:
+        send.wait()
 
 
 def keys_and_values(place, encoded, kvs):
     smem = pl.BlockSpec(memory_space=pltpu.SMEM)
     vmem = pl.BlockSpec(memory_space=pltpu.VMEM)
+    hbm = pl.BlockSpec(memory_space=pltpu.HBM)
+    shape = jax.ShapeDtypeStruct((KV_HEADS, 2 * SEG_LEN, HEAD), jnp.bfloat16)
     return pl.pallas_call(
         keyval_kernel,
-        out_shape=jax.ShapeDtypeStruct((KV_HEADS, 2 * SEG_LEN, HEAD), jnp.bfloat16),
-        in_specs=[smem] + [vmem] * 9,
-        out_specs=vmem,
-        compiler_params=params(),
+        out_shape=shape,
+        in_specs=[smem, vmem] + [hbm] * 8,
+        out_specs=hbm,
+        scratch_shapes=[pltpu.VMEM(kv.shape, kv.dtype) for kv in kvs]
+        + [pltpu.VMEM(shape.shape, shape.dtype), pltpu.SemaphoreType.DMA((4 * KV_HEADS,)),
+           pltpu.SemaphoreType.DMA((KV_HEADS,))],
+        compiler_params=params(47),
         cost_estimate=pl.CostEstimate(
             flops=4 * SEG_LEN * D_ENC * D_ENC, bytes_accessed=5 * D_ENC * D_ENC, transcendentals=0),
         name="keys_and_values",
@@ -225,12 +247,14 @@
 
     odd = lax.rem(z, 2)
 
+    with jax.named_scope("pair_out_weight"):
+        pair = lax.all_gather(out_weight.reshape(16, 8, HEAD).transpose(1, 0, 2), "c")
     with jax.named_scope("gather_kv_weight"):
         eighth = lax.dynamic_slice_in_dim(
             kv_weight.reshape(D_ENC, 2 * HEAD), core * 512 + odd * 256 + yl * 128, 128, 0)
+        pair, eighth = lax.optimization_barrier((pair, eighth))
         kv_mine = spread(jnp.concatenate([eighth[:, :HEAD], eighth[:, HEAD:]], axis=0), PLANE)
     with jax.named_scope("out_weight_over_z"):
-        pair = lax.all_gather(out_weight.reshape(16, 8, HEAD).transpose(1, 0, 2), "c")
         hops = []
         for ha_at in range(8):
             for z_at in range(16):
@@ -240,7 +264,7 @@
         pair = lax.ppermute(pair, ("yh", "x", "z", "c"), hops)
     slot = (ha * sa_count + sa).reshape(1).astype(jnp.int32)
     context = encoder_attention(slot, span_ids, seg_lengths, enc_query, enc_key, enc_value, enc_resid)
-    kv_mine, pair, context = lax.optimization_barrier((kv_mine, pair, context))
+    kv_mine, context = lax.optimization_barrier((kv_mine, context))
     with jax.named_scope("out_weight_over_plane"):
         w_mine = spread(pair, PLANE)
     with jax.named_scope("kv_weight_over_z"):
@@ -249,10 +273,9 @@
         halves = kv_mine[:8], kv_mine[8:]
         near = list(halves) + [lax.ppermute(halves[0], "z", down), lax.ppermute(halves[1], "z", up)]
     with jax.named_scope("swap_weights"):
-        far = [swap(half) for half in halves]
+        far = [swap(half) for half in near]
         w_mine, near, far = lax.optimization_barrier((w_mine, near, far))
         w_other = swap(w_mine)
-        far = far + [swap(half) for half in near[2:]]
     place = jnp.stack([z, core, odd]).astype(jnp.int32)
     encoded = project(place, norm_gain.reshape(1, D_ENC), context, w_mine, w_other)
     keyval = keys_and_values(place, encoded, near + far)

time: 137 us -> 135 us (0.985)
  starting transfers between devices: 52.3 us -> 40.5 us
  waiting for transfers between devices: 26.5 us -> 34.1 us
  Pallas kernels: 13 us -> 16.7 us
  local copies, waits for them, and re-layouts: 10.3 us -> 7.1 us
  blocking collectives: 33.8 us -> 35.2 us
    all_to_all x2, waiting for transfers between devices: 0.01 us -> 14.7 us  [spread(): return lax.all_to_all(copies, axes, 0, 0, tiled=True)]
    all_to_all x2, starting transfers between devices: 22.3 us -> 8.12 us  [spread(): return lax.all_to_all(copies, axes, 0, 0, tiled=True)]
    unnamed x42 -> x22, local copies, waits for them, and re-layouts: 6.59 us -> 2.56 us
    ppermute x1, waiting for transfers between devices: 3.76 us -> 0.01 us  [local(): pair = lax.ppermute(pair, ('yh', 'x', 'z', 'c'), hops)]
    pallas_call x1, Pallas kernels: 2.79 us -> 6.47 us  [keys_and_values(): pl.pallas_call(keyval_kernel, out_shape=shape, in_specs=[smem, vmem] + [h...]
    ppermute x1, starting transfers between devices: 3.93 us -> 7.49 us  [local(): lax.ppermute(halves[0], 'z', down)]
    all_gather x1, blocking collectives: 5.09 us -> 8.37 us  [local(): lax.all_gather(out_weight.reshape(16, 8, HEAD).transpose(1, 0, 2), 'c')]
    all_to_all x1, starting transfers between devices: 6.69 us -> 3.7 us  [local(): keyval = lax.all_to_all(keyval, HA, 0, 0, tiled=True)]
  transfers between devices with their start and end apart: 11 -> 11, of which waited for: 4 -> 4; matrix products, arithmetic and copies ran while one was open for 1% -> 3% of each run, Pallas kernels for 3% -> 2%
where the time goes in v6:
time: 135 us; the launch traced here: 134 us
  starting transfers between devices  40.5 us (30%)
  blocking collectives  35.2 us (26%)
  waiting for transfers between devices  34.1 us (25%)
  Pallas kernels  16.7 us (12%)
  local copies, waits for them, and re-layouts  7.1 us (5%)
    all_to_all x1, blocking collectives, local(): parts = lax.all_to_all(parts, SA, 0, 0, tiled=True)  26.8 us
    all_to_all x1, waiting for transfers between devices, local(): keyval = lax.all_to_all(keyval, HA, 0, 0, tiled=True)  17.2 us
    all_to_all x2, waiting for transfers between devices, spread(): return lax.all_to_all(copies, axes, 0, 0, tiled=True)  14.7 us
    ppermute x4, starting transfers between devices, local(): far = [swap(half) for half in near]  12.6 us
    all_gather x1, blocking collectives, local(): lax.all_gather(out_weight.reshape(16, 8, HEAD).transpose(1, 0, 2), 'c')  8.37 us
    all_to_all x2, starting transfers between devices, spread(): return lax.all_to_all(copies, axes, 0, 0, tiled=True)  8.12 us
    ppermute x1, starting transfers between devices, local(): lax.ppermute(halves[0], 'z', down)  7.49 us
    pallas_call x1, Pallas kernels, keys_and_values(): pl.pallas_call(keyval_kernel, out_shape=shape, in_specs=[smem, vmem] + [h...  6.47 us
  transfers between devices with their start and end apart: 11, of which 4 were waited for; matrix products, arithmetic and copies ran while one was open for 3% of the time, Pallas kernels for 2%

profile of v6, /device:TPU:1, one launch (start us, length us, event | category | flops | bytes accessed | tf_op | source)
XLA Modules:
  0.0 134.0 jit_solution(7181999487993167965)
XLA Ops:
  0.8 8.4 %all-gather = bf16[16,16,128]{2,0,1:T(8,128)(2,1)S(1)} all-gather(bf16[8,16,128]{2,0,1:T(8,128)(2,1)S(1)} %bitcast.24), channel_id=2, replica_groups=mesh['yh'=2,'x'=4,'z'=16,'yl'=2,'c'=2] {'c'}, dimensions={0}, use_global_device_ids=true | all-gather | bytes 98304 | tf_op jit(solution)/shard_map/pair_out_weight/all_gather | solution.py:251
  10.5 4.5 %all-to-all-start = ((bf16[16,256,128]{2,1,0:T(8,128)(2,1)}), bf16[16,256,128]{2,1,0:T(8,128)(2,1)}, u32[]{:S(2)}, u32[]{:S(2)}) async-start(bf16[16,256,128]{2,1,0:T(8,128)(2,1)} %broadcast_in_dim.4), calls=%async_computation | async-start | bytes 2097152 | tf_op jit(solution)/shard_map/gather_kv_weight/all_to_all | solution.py:235
  14.9 1.9 %collective-permute-start = (bf16[2,8,16,128]{3,2,1,0:T(8,128)(2,1)S(1)}, bf16[2,8,16,128]{3,2,1,0:T(8,128)(2,1)S(1)}, u32[]{:S(2)}, u32[]{:S(2)}) collective-permute-start(bf16[2,8,16,128]{3,2,1,0:T(8,128)(2,1)S(1)} %bitcast.26), channel_id=1, source_target_pairs={{0,0},{1,5},{4,4},{5,9},{8,8},{9,13},{12,12},{13,17},{16,16},{17,2... | collective-permute-start | bytes 196616 | tf_op jit(solution)/shard_map/out_weight_over_z/ppermute | solution.py:264
  18.6 3.1 %encoder_attention.1.ctx_ref = bf16[2,256,1024]{2,1,0:T(8,128)(2,1)S(1)} custom-call(s32[1]{0:T(128)} %bitcast.10.slot_ref, s32[512]{0:T(512)S(1)} %copy-done.5, s32[512]{0:T(512)S(1)} %copy-done.6, bf16[256,1024]{1,0:T(8,128)(2,1)S(1)} %copy-done.1, bf16[256,1024]{1,0:T(8,128)(2,1)S(1)} %copy-done.2, bf16[256,1024]{1,0:T(8,128)(2,1)S(1)} %copy-done.3, ...), custom_call_target="tpu_custom_call" | custom-call | flops 536870912 | bytes 2097152 | tf_op jit(solution)/shard_map/encoder_attention/pallas_call | solution.py:62
  21.7 11.5 %all-to-all-done = bf16[16,256,128]{2,1,0:T(8,128)(2,1)} async-done(((bf16[16,256,128]{2,1,0:T(8,128)(2,1)}), bf16[16,256,128]{2,1,0:T(8,128)(2,1)}, u32[]{:S(2)}, u32[]{:S(2)}) %all-to-all-start) | async-done | bytes 1048608 | tf_op jit(solution)/shard_map/gather_kv_weight/all_to_all | solution.py:235
  33.2 2.1 %fusion = (bf16[8,256,128]{2,1,0:T(8,128)(2,1)S(1)}, bf16[8,256,128]{2,1,0:T(8,128)(2,1)}) fusion(bf16[16,256,128]{2,1,0:T(8,128)(2,1)} %all-to-all-done), kind=kLoop, calls=%fused_computation.4 | loop fusion | bytes 2097152 | tf_op jit(solution)/shard_map/kv_weight_over_z/slice | solution.py:273
  35.3 7.5 %collective-permute-start.1 = (bf16[8,256,128]{2,1,0:T(8,128)(2,1)}, bf16[8,256,128]{2,1,0:T(8,128)(2,1)}, u32[]{:S(2)}, u32[]{:S(2)}) collective-permute-start(bf16[8,256,128]{2,1,0:T(8,128)(2,1)} %get-tuple-element.23.refs_0_), channel_id=1, source_target_pairs={{0,60},{4,0},{8,4},{12,8},{16,12},{20,16},{24,20},{28,24},{32,28},... | collective-permute-start | bytes 1572872 | tf_op jit(solution)/shard_map/kv_weight_over_z/ppermute | solution.py:274
  42.8 1.9 %collective-permute-start.2 = (bf16[8,256,128]{2,1,0:T(8,128)(2,1)S(1)}, bf16[8,256,128]{2,1,0:T(8,128)(2,1)}, u32[]{:S(2)}, u32[]{:S(2)}) collective-permute-start(bf16[8,256,128]{2,1,0:T(8,128)(2,1)S(1)} %get-tuple-element.24.refs_1_), channel_id=1, source_target_pairs={{0,4},{4,8},{8,12},{12,16},{16,20},{20,24},{24,28},{28,32},{32,36}... | collective-permute-start | bytes 1572872 | tf_op jit(solution)/shard_map/kv_weight_over_z/ppermute | solution.py:274
  44.7 1.2 broadcast_in_dim.5
  46.0 3.7 %all-to-all-start.1 = ((bf16[16,2,8,16,128]{4,3,2,1,0:T(8,128)(2,1)}), bf16[16,2,8,16,128]{4,3,2,1,0:T(8,128)(2,1)S(1)}, u32[]{:S(2)}, u32[]{:S(2)}) async-start(bf16[16,2,8,16,128]{4,3,2,1,0:T(8,128)(2,1)} %broadcast_in_dim.5), calls=%async_computation.1 | async-start | bytes 2097152 | tf_op jit(solution)/shard_map/out_weight_over_plane/all_to_all | solution.py:235
  49.6 3.7 %collective-permute-start.3 = (bf16[8,256,128]{2,1,0:T(8,128)(2,1)}, bf16[8,256,128]{2,1,0:T(8,128)(2,1)}, u32[]{:S(2)}, u32[]{:S(2)}) collective-permute-start(bf16[8,256,128]{2,1,0:T(8,128)(2,1)} %get-tuple-element.23.refs_0_), channel_id=1, source_target_pairs={{0,1},{1,0},{2,3},{3,2},{4,5},{5,4},{6,7},{7,6},{8,9},{9,8},{10,11... | collective-permute-start | bytes 1572872 | tf_op jit(solution)/shard_map/swap_weights/ppermute | solution.py:276
  53.3 1.9 %collective-permute-start.4 = (bf16[8,256,128]{2,1,0:T(8,128)(2,1)S(1)}, bf16[8,256,128]{2,1,0:T(8,128)(2,1)}, u32[]{:S(2)}, u32[]{:S(2)}) collective-permute-start(bf16[8,256,128]{2,1,0:T(8,128)(2,1)S(1)} %get-tuple-element.24.refs_1_), channel_id=1, source_target_pairs={{0,1},{1,0},{2,3},{3,2},{4,5},{5,4},{6,7},{7,6},{8,9},{9,8},{10,11... | collective-permute-start | bytes 1572872 | tf_op jit(solution)/shard_map/swap_weights/ppermute | solution.py:276
  55.3 2.4 %collective-permute-start.5 = (bf16[8,256,128]{2,1,0:T(8,128)(2,1)}, bf16[8,256,128]{2,1,0:T(8,128)(2,1)}, u32[]{:S(2)}, u32[]{:S(2)}) collective-permute-start(bf16[8,256,128]{2,1,0:T(8,128)(2,1)} %collective-permute-done.1.refs_2_), channel_id=1, source_target_pairs={{0,1},{1,0},{2,3},{3,2},{4,5},{5,4},{6,7},{7,6},{8,9},{9,8},{10,11... | collective-permute-start | bytes 1572872 | tf_op jit(solution)/shard_map/swap_weights/ppermute | solution.py:276
  57.7 4.5 %collective-permute-start.6 = (bf16[8,256,128]{2,1,0:T(8,128)(2,1)}, bf16[8,256,128]{2,1,0:T(8,128)(2,1)}, u32[]{:S(2)}, u32[]{:S(2)}) collective-permute-start(bf16[8,256,128]{2,1,0:T(8,128)(2,1)} %collective-permute-done.2.refs_3_), channel_id=1, source_target_pairs={{0,1},{1,0},{2,3},{3,2},{4,5},{5,4},{6,7},{7,6},{8,9},{9,8},{10,11... | collective-permute-start | bytes 1572872 | tf_op jit(solution)/shard_map/swap_weights/ppermute | solution.py:276
  62.3 3.2 %all-to-all-done.1.mine_ref = bf16[16,2,8,16,128]{4,3,2,1,0:T(8,128)(2,1)S(1)} async-done(((bf16[16,2,8,16,128]{4,3,2,1,0:T(8,128)(2,1)}), bf16[16,2,8,16,128]{4,3,2,1,0:T(8,128)(2,1)S(1)}, u32[]{:S(2)}, u32[]{:S(2)}) %all-to-all-start.1) | async-done | bytes 1048608 | tf_op jit(solution)/shard_map/out_weight_over_plane/all_to_all | solution.py:235
  65.4 4.7 %collective-permute-start.7 = (bf16[16,2,8,16,128]{4,3,2,1,0:T(8,128)(2,1)S(1)}, bf16[16,2,8,16,128]{4,3,2,1,0:T(8,128)(2,1)S(1)}, u32[]{:S(2)}, u32[]{:S(2)}) collective-permute-start(bf16[16,2,8,16,128]{4,3,2,1,0:T(8,128)(2,1)S(1)} %all-to-all-done.1.mine_ref), channel_id=1, source_target_pairs={{0,1},{1,0},{2,3},{3,2},{4,5},{5,4},{6,7},{7,6},{8,9},{9,8},{10,11... | collective-permute-start | bytes 3145736 | tf_op jit(solution)/shard_map/swap_weights/ppermute | solution.py:278
  70.3 2.2 %collective-permute-done.7.other_ref = bf16[16,2,8,16,128]{4,3,2,1,0:T(8,128)(2,1)S(1)} collective-permute-done((bf16[16,2,8,16,128]{4,3,2,1,0:T(8,128)(2,1)S(1)}, bf16[16,2,8,16,128]{4,3,2,1,0:T(8,128)(2,1)S(1)}, u32[]{:S(2)}, u32[]{:S(2)}) %collective-permute-start.7) | collective-permute-done | bytes 1048608 | tf_op jit(solution)/shard_map/swap_weights/ppermute | solution.py:278
  72.5 1.5 %project.1.enc_ref = bf16[4,256,256]{2,1,0:T(8,128)(2,1)S(1)} custom-call(s32[3]{0:T(128)S(1)} %pad_add_fusion.1.place_ref, f32[1,1024]{1,0:T(1,128)S(1)} %bitcast.22, bf16[2,256,1024]{2,1,0:T(8,128)(2,1)S(1)} %encoder_attention.1.ctx_ref, bf16[16,2,8,16,128]{4,3,2,1,0:T(8,128)(2,1)S(1)} %all-to-all-done.1.mine_ref, ...), custom_call_target="tpu_custom_call" | custom-call | flops 536870912 | bytes 6291456 | tf_op jit(solution)/shard_map/project/pallas_call | solution.py:97
  74.0 6.5 %keys_and_values.1 = bf16[8,512,128]{2,1,0:T(8,128)(2,1)} custom-call(s32[3]{0:T(128)S(1)} %pad_add_fusion.1.place_ref, bf16[4,256,256]{2,1,0:T(8,128)(2,1)S(1)} %project.1.enc_ref, bf16[8,256,128]{2,1,0:T(8,128)(2,1)} %get-tuple-element.23.refs_0_, bf16[8,256,128]{2,1,0:T(8,128)(2,1)S(1)} %get-tuple-element.24.refs_1_, ...), custom_call_target="tpu_custom_call" | custom-call | flops 1073741824 | bytes 5242880 | tf_op jit(solution)/shard_map/keys_and_values/pallas_call | solution.py:150
  80.5 3.7 %all-to-all-start.2 = ((bf16[8,512,128]{2,1,0:T(8,128)(2,1)}), bf16[8,512,128]{2,1,0:T(8,128)(2,1)S(1)}, u32[]{:S(2)}, u32[]{:S(2)}) async-start(bf16[8,512,128]{2,1,0:T(8,128)(2,1)} %keys_and_values.1), calls=%async_computation.2 | async-start | bytes 2097152 | tf_op jit(solution)/shard_map/exchange_keyval/all_to_all | solution.py:283
  84.4 17.2 %all-to-all-done.2.kv_ref = bf16[8,512,128]{2,1,0:T(8,128)(2,1)S(1)} async-done(((bf16[8,512,128]{2,1,0:T(8,128)(2,1)}), bf16[8,512,128]{2,1,0:T(8,128)(2,1)S(1)}, u32[]{:S(2)}, u32[]{:S(2)}) %all-to-all-start.2) | async-done | bytes 1048608 | tf_op jit(solution)/shard_map/exchange_keyval/all_to_all | solution.py:283
  101.6 3.3 %cross_attention.1 = bf16[64,2,640]{2,1,0:T(2,128)(2,1)S(1)} custom-call(s32[2]{0:T(128)S(1)} %pad_add_fusion.first_ref, s32[512]{0:T(512)S(1)} %copy-done.5, s32[512]{0:T(512)S(1)} %copy-done.6, bf16[512,128]{1,0:T(8,128)(2,1)S(1)} %bitcast.21, bf16[8,512,128]{2,1,0:T(8,128)(2,1)S(1)} %all-to-all-done.2.kv_ref), custom_call_target="tpu_custom_call" | custom-call | tf_op jit(solution)/shard_map/cross_attention/pallas_call | solution.py:203
  104.8 26.8 %all_to_all.20.part_ref = bf16[64,2,640]{2,1,0:T(2,128)(2,1)} all-to-all(bf16[64,2,640]{2,1,0:T(2,128)(2,1)S(1)} %cross_attention.1), channel_id=1, replica_groups=mesh['yh'=2,'x'=4,'z'=16,'yl'=2,'c'=2] {'z','yl','c'}, dimensions={0} | all-to-all | bytes 327680 | tf_op jit(solution)/shard_map/exchange_partials/all_to_all | solution.py:288
  131.6 2.3 %merge_partials.1 = f32[8,128]{1,0:T(8,128)} custom-call(bf16[64,2,640]{2,1,0:T(2,128)(2,1)} %all_to_all.20.part_ref), custom_call_target="tpu_custom_call" | custom-call | tf_op jit(solution)/shard_map/merge_partials/pallas_call | solution.py:223
  (37 shorter events, 4.0 us)
Async XLA Ops:
  0.0 9.2 %copy-start = (bf16[1024,1,256]{2,0,1:T(8,128)(2,1)S(1)}, bf16[1024,1,256]{2,0,1:T(8,128)(2,1)}, u32[]{:S(2)}) copy-start(bf16[1024,1,256]{2,0,1:T(8,128)(2,1)} %param.16) | copy-start | bytes 1572868
  0.0 0.8 copy-start.9
  10.5 6.5 %copy-start.1 = (bf16[256,1024]{1,0:T(8,128)(2,1)S(1)}, bf16[256,1024]{1,0:T(8,128)(2,1)}, u32[]{:S(2)}) copy-start(bf16[256,1024]{1,0:T(8,128)(2,1)} %q_ref.1) | copy-start | bytes 1572868
  10.5 6.5 %copy-start.2 = (bf16[256,1024]{1,0:T(8,128)(2,1)S(1)}, bf16[256,1024]{1,0:T(8,128)(2,1)}, u32[]{:S(2)}) copy-start(bf16[256,1024]{1,0:T(8,128)(2,1)} %k_ref.1) | copy-start | bytes 1572868
  10.5 6.5 %copy-start.3 = (bf16[256,1024]{1,0:T(8,128)(2,1)S(1)}, bf16[256,1024]{1,0:T(8,128)(2,1)}, u32[]{:S(2)}) copy-start(bf16[256,1024]{1,0:T(8,128)(2,1)} %v_ref.1) | copy-start | bytes 1572868
  10.5 22.8 %all-to-all-start = ((bf16[16,256,128]{2,1,0:T(8,128)(2,1)}), bf16[16,256,128]{2,1,0:T(8,128)(2,1)}, u32[]{:S(2)}, u32[]{:S(2)}) async-start(bf16[16,256,128]{2,1,0:T(8,128)(2,1)} %broadcast_in_dim.4), calls=%async_computation | async-start | bytes 2097152 | tf_op jit(solution)/shard_map/gather_kv_weight/all_to_all | solution.py:235
  14.9 29.8 %collective-permute-start = (bf16[2,8,16,128]{3,2,1,0:T(8,128)(2,1)S(1)}, bf16[2,8,16,128]{3,2,1,0:T(8,128)(2,1)S(1)}, u32[]{:S(2)}, u32[]{:S(2)}) collective-permute-start(bf16[2,8,16,128]{3,2,1,0:T(8,128)(2,1)S(1)} %bitcast.26), channel_id=1, source_target_pairs={{0,0},{1,5},{4,4},{5,9},{8,8},{9,13},{12,12},{13,17},{16,16},{17,2... | collective-permute-start | bytes 196616 | tf_op jit(solution)/shard_map/out_weight_over_z/ppermute | solution.py:264
  16.9 0.7 copy-start.6
  16.9 0.7 copy-start.5
  17.6 1.0 copy-start.4
  35.3 20.0 %collective-permute-start.1 = (bf16[8,256,128]{2,1,0:T(8,128)(2,1)}, bf16[8,256,128]{2,1,0:T(8,128)(2,1)}, u32[]{:S(2)}, u32[]{:S(2)}) collective-permute-start(bf16[8,256,128]{2,1,0:T(8,128)(2,1)} %get-tuple-element.23.refs_0_), channel_id=1, source_target_pairs={{0,60},{4,0},{8,4},{12,8},{16,12},{20,16},{24,20},{28,24},{32,28},... | collective-permute-start | bytes 1572872 | tf_op jit(solution)/shard_map/kv_weight_over_z/ppermute | solution.py:274
  42.8 14.9 %collective-permute-start.2 = (bf16[8,256,128]{2,1,0:T(8,128)(2,1)S(1)}, bf16[8,256,128]{2,1,0:T(8,128)(2,1)}, u32[]{:S(2)}, u32[]{:S(2)}) collective-permute-start(bf16[8,256,128]{2,1,0:T(8,128)(2,1)S(1)} %get-tuple-element.24.refs_1_), channel_id=1, source_target_pairs={{0,4},{4,8},{8,12},{12,16},{16,20},{20,24},{24,28},{28,32},{32,36}... | collective-permute-start | bytes 1572872 | tf_op jit(solution)/shard_map/kv_weight_over_z/ppermute | solution.py:274
  46.0 19.4 %all-to-all-start.1 = ((bf16[16,2,8,16,128]{4,3,2,1,0:T(8,128)(2,1)}), bf16[16,2,8,16,128]{4,3,2,1,0:T(8,128)(2,1)S(1)}, u32[]{:S(2)}, u32[]{:S(2)}) async-start(bf16[16,2,8,16,128]{4,3,2,1,0:T(8,128)(2,1)} %broadcast_in_dim.5), calls=%async_computation.1 | async-start | bytes 2097152 | tf_op jit(solution)/shard_map/out_weight_over_plane/all_to_all | solution.py:235
  49.6 15.8 %collective-permute-start.3 = (bf16[8,256,128]{2,1,0:T(8,128)(2,1)}, bf16[8,256,128]{2,1,0:T(8,128)(2,1)}, u32[]{:S(2)}, u32[]{:S(2)}) collective-permute-start(bf16[8,256,128]{2,1,0:T(8,128)(2,1)} %get-tuple-element.23.refs_0_), channel_id=1, source_target_pairs={{0,1},{1,0},{2,3},{3,2},{4,5},{5,4},{6,7},{7,6},{8,9},{9,8},{10,11... | collective-permute-start | bytes 1572872 | tf_op jit(solution)/shard_map/swap_weights/ppermute | solution.py:276
  53.3 12.1 %collective-permute-start.4 = (bf16[8,256,128]{2,1,0:T(8,128)(2,1)S(1)}, bf16[8,256,128]{2,1,0:T(8,128)(2,1)}, u32[]{:S(2)}, u32[]{:S(2)}) collective-permute-start(bf16[8,256,128]{2,1,0:T(8,128)(2,1)S(1)} %get-tuple-element.24.refs_1_), channel_id=1, source_target_pairs={{0,1},{1,0},{2,3},{3,2},{4,5},{5,4},{6,7},{7,6},{8,9},{9,8},{10,11... | collective-permute-start | bytes 1572872 | tf_op jit(solution)/shard_map/swap_weights/ppermute | solution.py:276
  55.3 10.2 %collective-permute-start.5 = (bf16[8,256,128]{2,1,0:T(8,128)(2,1)}, bf16[8,256,128]{2,1,0:T(8,128)(2,1)}, u32[]{:S(2)}, u32[]{:S(2)}) collective-permute-start(bf16[8,256,128]{2,1,0:T(8,128)(2,1)} %collective-permute-done.1.refs_2_), channel_id=1, source_target_pairs={{0,1},{1,0},{2,3},{3,2},{4,5},{5,4},{6,7},{7,6},{8,9},{9,8},{10,11... | collective-permute-start | bytes 1572872 | tf_op jit(solution)/shard_map/swap_weights/ppermute | solution.py:276
  57.7 7.7 %collective-permute-start.6 = (bf16[8,256,128]{2,1,0:T(8,128)(2,1)}, bf16[8,256,128]{2,1,0:T(8,128)(2,1)}, u32[]{:S(2)}, u32[]{:S(2)}) collective-permute-start(bf16[8,256,128]{2,1,0:T(8,128)(2,1)} %collective-permute-done.2.refs_3_), channel_id=1, source_target_pairs={{0,1},{1,0},{2,3},{3,2},{4,5},{5,4},{6,7},{7,6},{8,9},{9,8},{10,11... | collective-permute-start | bytes 1572872 | tf_op jit(solution)/shard_map/swap_weights/ppermute | solution.py:276
  65.4 7.0 %collective-permute-start.7 = (bf16[16,2,8,16,128]{4,3,2,1,0:T(8,128)(2,1)S(1)}, bf16[16,2,8,16,128]{4,3,2,1,0:T(8,128)(2,1)S(1)}, u32[]{:S(2)}, u32[]{:S(2)}) collective-permute-start(bf16[16,2,8,16,128]{4,3,2,1,0:T(8,128)(2,1)S(1)} %all-to-all-done.1.mine_ref), channel_id=1, source_target_pairs={{0,1},{1,0},{2,3},{3,2},{4,5},{5,4},{6,7},{7,6},{8,9},{9,8},{10,11... | collective-permute-start | bytes 3145736 | tf_op jit(solution)/shard_map/swap_weights/ppermute | solution.py:278
  70.2 2.3 %copy-start.7 = (f32[1024]{0:T(1024)S(1)}, f32[1024]{0:T(1024)}, u32[]{:S(2)}) copy-start(f32[1024]{0:T(1024)} %param.15) | copy-start | bytes 12292
  80.5 3.7 %copy-start.8 = (bf16[64,1,1024]{2,0,1:T(8,128)(2,1)S(1)}, bf16[64,1,1024]{2,0,1:T(8,128)(2,1)}, u32[]{:S(2)}) copy-start(bf16[64,1,1024]{2,0,1:T(8,128)(2,1)} %param.17) | copy-start | bytes 393220
  80.5 21.0 %all-to-all-start.2 = ((bf16[8,512,128]{2,1,0:T(8,128)(2,1)}), bf16[8,512,128]{2,1,0:T(8,128)(2,1)S(1)}, u32[]{:S(2)}, u32[]{:S(2)}) async-start(bf16[8,512,128]{2,1,0:T(8,128)(2,1)} %keys_and_values.1), calls=%async_computation.2 | async-start | bytes 2097152 | tf_op jit(solution)/shard_map/exchange_keyval/all_to_all | solution.py:283

commit v7 on v6

--- a/solution.py
+++ b/solution.py
@@ -72,8 +72,21 @@
     )(slot, span_ids, seg_lengths, q, k, v, resid)
 
 
-def project_kernel(place_ref, gain_ref, ctx_ref, mine_ref, other_ref, o_ref, w_ref):
-    z, core = place_ref[0], place_ref[1]
+def encode_kernel(place_ref, gain_ref, ctx_ref, mine_ref, other_ref, *refs):
+    kv_refs, o_ref = refs[:6], refs[6]
+    w_ref, enc_ref, done_ref = refs[7:10]
+    kv_bufs, in_sems, out_sems = refs[10:14], refs[14], refs[15]
+    z, core, odd = place_ref[0], place_ref[1], place_ref[2]
+    copies = []
+    for side in range(2):
+        some = pl.ds(8 * side, 8)
+        sources = [kv_refs[0].at[some], kv_refs[1].at[some], kv_refs[2 + side], kv_refs[4 + side]]
+        copies.append([pltpu.make_async_copy(source, kv_bufs[i].at[some], in_sems.at[4 * side + i])
+                       for i, source in enumerate(sources)])
+    for side in range(2):
+        for copy in copies[side]:
+            copy.start()
+
     for part_ref, at in ((mine_ref, core), (other_ref, 1 - core)):
         for ha in range(KV_HEADS):
             plane = lax.rem(z + 32 - 2 * ha - at, 16)
@@ -88,38 +101,7 @@
     factor = lax.rsqrt(jnp.mean(hidden * hidden, axis=-1, keepdims=True) + 1e-05)
     encoded = (hidden * factor * gain_ref[...]).astype(jnp.bfloat16)
     for piece in range(4):
-        o_ref[piece] = encoded[:, piece * 256:(piece + 1) * 256]
-
-
-def project(place, gain, ctx, mine, other):
-    smem = pl.BlockSpec(memory_space=pltpu.SMEM)
-    vmem = pl.BlockSpec(memory_space=pltpu.VMEM)
-    return pl.pallas_call(
-        project_kernel,
-        out_shape=jax.ShapeDtypeStruct((4, SEG_LEN, 256), jnp.bfloat16),
-        in_specs=[smem] + [vmem] * 4,
-        out_specs=vmem,
-        scratch_shapes=[pltpu.VMEM((8, D_ENC, HEAD), jnp.bfloat16)],
-        compiler_params=params(),
-        cost_estimate=pl.CostEstimate(
-            flops=2 * SEG_LEN * D_ENC * D_ENC, bytes_accessed=6 * D_ENC * D_ENC, transcendentals=SEG_LEN),
-        name="project",
-    )(place, gain, ctx, mine, other)
-
-
-def keyval_kernel(place_ref, enc_ref, *refs):
-    kv_refs, o_ref, kv_bufs, done_ref, in_sems, out_sems = refs[:8], refs[8], refs[9:17], refs[17], refs[18], refs[19]
-    core, odd = place_ref[1], place_ref[2]
-    copies = []
-    for h in range(KV_HEADS):
-        side, at = divmod(h, KV_HEADS // 2)
-        copies.append([
-            pltpu.make_async_copy(
-                kv_refs[side + 2 * i].at[pl.ds(2 * at, 2)], kv_bufs[side + 2 * i].at[pl.ds(2 * at, 2)],
-                in_sems.at[4 * h + i])
-            for i in range(4)])
-        for copy in copies[h]:
-            copy.start()
+        enc_ref[piece] = encoded[:, piece * 256:(piece + 1) * 256]
     near, far = 2 * core, 2 - 2 * core
     pieces = [enc_ref[near + odd], enc_ref[near + 1 - odd], enc_ref[far + odd], enc_ref[far + 1 - odd]]
 
@@ -129,11 +111,12 @@
 
     sends = []
     for h in range(KV_HEADS):
-        side, at = divmod(h, KV_HEADS // 2)
-        total = 0.0
-        for i in range(4):
-            copies[h][i].wait()
-            total += dot(pieces[i], rows(kv_bufs[side + 2 * i], at))
+        if h % 4 == 0:
+            for copy in copies[h // 4]:
+                copy.wait()
+        total = dot(pieces[0], rows(kv_bufs[0], h))
+        for i in range(1, 4):
+            total += dot(pieces[i], rows(kv_bufs[i], h))
         done_ref[h, :SEG_LEN] = total[:, :HEAD].astype(jnp.bfloat16)
         done_ref[h, SEG_LEN:] = total[:, HEAD:].astype(jnp.bfloat16)
         sends.append(pltpu.make_async_copy(done_ref.at[h], o_ref.at[h], out_sems.at[h]))
@@ -142,24 +125,26 @@
         send.wait()
 
 
-def keys_and_values(place, encoded, kvs):
+def encode(place, gain, ctx, mine, other, kvs):
     smem = pl.BlockSpec(memory_space=pltpu.SMEM)
     vmem = pl.BlockSpec(memory_space=pltpu.VMEM)
     hbm = pl.BlockSpec(memory_space=pltpu.HBM)
     shape = jax.ShapeDtypeStruct((KV_HEADS, 2 * SEG_LEN, HEAD), jnp.bfloat16)
     return pl.pallas_call(
-        keyval_kernel,
+        encode_kernel,
         out_shape=shape,
-        in_specs=[smem, vmem] + [hbm] * 8,
+        in_specs=[smem] + [vmem] * 4 + [hbm] * 6,
         out_specs=hbm,
-        scratch_shapes=[pltpu.VMEM(kv.shape, kv.dtype) for kv in kvs]
-        + [pltpu.VMEM(shape.shape, shape.dtype), pltpu.SemaphoreType.DMA((4 * KV_HEADS,)),
-           pltpu.SemaphoreType.DMA((KV_HEADS,))],
+        scratch_shapes=[pltpu.VMEM((8, D_ENC, HEAD), jnp.bfloat16),
+                        pltpu.VMEM((4, SEG_LEN, 256), jnp.bfloat16),
+                        pltpu.VMEM(shape.shape, shape.dtype)]
+        + [pltpu.VMEM(kvs[0].shape, kvs[0].dtype)] * 4
+        + [pltpu.SemaphoreType.DMA((8,)), pltpu.SemaphoreType.DMA((KV_HEADS,))],
         compiler_params=params(47),
         cost_estimate=pl.CostEstimate(
-            flops=4 * SEG_LEN * D_ENC * D_ENC, bytes_accessed=5 * D_ENC * D_ENC, transcendentals=0),
-        name="keys_and_values",
-    )(place, encoded, *kvs)
+            flops=6 * SEG_LEN * D_ENC * D_ENC, bytes_accessed=8 * D_ENC * D_ENC, transcendentals=SEG_LEN),
+        name="encode_keyval",
+    )(place, gain, ctx, mine, other, *kvs)
 
 
 def cross_kernel(slots, first_ref, span_ref, len_ref, q_ref, kv_ref, o_ref):
@@ -264,21 +249,23 @@
         pair = lax.ppermute(pair, ("yh", "x", "z", "c"), hops)
     slot = (ha * sa_count + sa).reshape(1).astype(jnp.int32)
     context = encoder_attention(slot, span_ids, seg_lengths, enc_query, enc_key, enc_value, enc_resid)
-    kv_mine, context = lax.optimization_barrier((kv_mine, context))
+    kv_mine, pair, context = lax.optimization_barrier((kv_mine, pair, context))
     with jax.named_scope("out_weight_over_plane"):
         w_mine = spread(pair, PLANE)
     with jax.named_scope("kv_weight_over_z"):
-        up = [(i, (i + 1) % 16) for i in range(16)]
-        down = [(i, (i + 15) % 16) for i in range(16)]
-        halves = kv_mine[:8], kv_mine[8:]
-        near = list(halves) + [lax.ppermute(halves[0], "z", down), lax.ppermute(halves[1], "z", up)]
+        pairs = []
+        for z_at in range(16):
+            for c_at in range(2):
+                there = (z_at + (1 if (z_at + c_at) % 2 == 0 else 15)) % 16
+                pairs.append((2 * z_at + c_at, 2 * there + c_at))
+        kv_next = lax.ppermute(kv_mine, ("z", "c"), pairs)
     with jax.named_scope("swap_weights"):
-        far = [swap(half) for half in near]
-        w_mine, near, far = lax.optimization_barrier((w_mine, near, far))
+        kvs = [kv_mine, kv_next]
+        kvs = kvs + [swap(part) for kv in kvs for part in (kv[:8], kv[8:])]
+        w_mine, kvs = lax.optimization_barrier((w_mine, kvs))
         w_other = swap(w_mine)
     place = jnp.stack([z, core, odd]).astype(jnp.int32)
-    encoded = project(place, norm_gain.reshape(1, D_ENC), context, w_mine, w_other)
-    keyval = keys_and_values(place, encoded, near + far)
+    keyval = encode(place, norm_gain.reshape(1, D_ENC), context, w_mine, w_other, kvs)
     with jax.named_scope("exchange_keyval"):
         keyval = lax.all_to_all(keyval, HA, 0, 0, tiled=True)
     first = jnp.stack([sa, sa_count]).astype(jnp.int32)

time: 135 us -> 132 us (0.978)
  starting transfers between devices: 40.5 us -> 32.9 us
  blocking collectives: 35.2 us -> 40.2 us
  Pallas kernels: 16.7 us -> 13 us
  local copies, waits for them, and re-layouts: 7.1 us -> 10.4 us
    all_to_all x2, waiting for transfers between devices: 14.7 us -> 8.49 us  [spread(): return lax.all_to_all(copies, axes, 0, 0, tiled=True)]
    ppermute x6 -> x5, starting transfers between devices: 22 us -> 16.1 us  [the longest x4 8.64 us: local(): kvs = kvs + [swap(part) for kv in kvs for part in (kv[:8], kv[8:])]]
    all_to_all x1, blocking collectives: 26.8 us -> 31.9 us  [local(): parts = lax.all_to_all(parts, SA, 0, 0, tiled=True)]
    pallas_call x2 -> x1, Pallas kernels: 8.02 us -> 4.34 us  [encode(): pl.pallas_call(encode_kernel, out_shape=shape, in_specs=[smem] + [vmem] *...]
    ppermute x1, waiting for transfers between devices: 0.01 us -> 3.48 us  [local(): pair = lax.ppermute(pair, ('yh', 'x', 'z', 'c'), hops)]
    ppermute x6 -> x5, waiting for transfers between devices: 0.02 us -> 2.74 us  [the longest x1 2.16 us: local(): kv_next = lax.ppermute(kv_mine, ('z', 'c'), pairs)]
    ppermute x1, starting transfers between devices: 4.74 us -> 2.27 us  [local(): w_other = swap(w_mine)]
    unnamed x22 -> x26, local copies, waits for them, and re-layouts: 2.56 us -> 4.4 us
  transfers between devices with their start and end apart: 11 -> 10, of which waited for: 4 -> 7; matrix products, arithmetic and copies ran while one was open for 3% -> 4% of each run, Pallas kernels for 2% -> 2%
where the time goes in v7:
time: 132 us; the launch traced here: 131 us
  blocking collectives  40.2 us (30%)
  waiting for transfers between devices  34.1 us (26%)
  starting transfers between devices  32.9 us (25%)
  Pallas kernels  13 us (10%)
  local copies, waits for them, and re-layouts  10.4 us (8%)
    all_to_all x1, blocking collectives, local(): parts = lax.all_to_all(parts, SA, 0, 0, tiled=True)  31.9 us
    all_to_all x1, waiting for transfers between devices, local(): keyval = lax.all_to_all(keyval, HA, 0, 0, tiled=True)  17.2 us
    ppermute x4, starting transfers between devices, local(): kvs = kvs + [swap(part) for kv in kvs for part in (kv[:8], kv[8:])]  8.64 us
    all_to_all x2, waiting for transfers between devices, spread(): return lax.all_to_all(copies, axes, 0, 0, tiled=True)  8.49 us
    all_gather x1, blocking collectives, local(): lax.all_gather(out_weight.reshape(16, 8, HEAD).transpose(1, 0, 2), 'c')  8.37 us
    all_to_all x2, starting transfers between devices, spread(): return lax.all_to_all(copies, axes, 0, 0, tiled=True)  8.12 us
    ppermute x1, starting transfers between devices, local(): kv_next = lax.ppermute(kv_mine, ('z', 'c'), pairs)  7.49 us
    all_to_all x1, starting transfers between devices, local(): keyval = lax.all_to_all(keyval, HA, 0, 0, tiled=True)  4.49 us
  transfers between devices with their start and end apart: 10, of which 7 were waited for; matrix products, arithmetic and copies ran while one was open for 4% of the time, Pallas kernels for 2%

profile of v7, /device:TPU:1, one launch (start us, length us, event | category | flops | bytes accessed | tf_op | source)
XLA Modules:
  0.0 131.2 jit_solution(16462094400734320421)
XLA Ops:
  0.8 8.4 %all-gather = bf16[16,16,128]{2,0,1:T(8,128)(2,1)S(1)} all-gather(bf16[8,16,128]{2,0,1:T(8,128)(2,1)S(1)} %bitcast.24), channel_id=2, replica_groups=mesh['yh'=2,'x'=4,'z'=16,'yl'=2,'c'=2] {'c'}, dimensions={0}, use_global_device_ids=true | all-gather | bytes 98304 | tf_op jit(solution)/shard_map/pair_out_weight/all_gather | solution.py:236
  10.4 4.5 %all-to-all-start = ((bf16[16,256,128]{2,1,0:T(8,128)(2,1)}), bf16[16,256,128]{2,1,0:T(8,128)(2,1)}, u32[]{:S(2)}, u32[]{:S(2)}) async-start(bf16[16,256,128]{2,1,0:T(8,128)(2,1)} %broadcast_in_dim.4), calls=%async_computation | async-start | bytes 2097152 | tf_op jit(solution)/shard_map/gather_kv_weight/all_to_all | solution.py:220
  14.9 1.9 %collective-permute-start = (bf16[2,8,16,128]{3,2,1,0:T(8,128)(2,1)S(1)}, bf16[2,8,16,128]{3,2,1,0:T(8,128)(2,1)S(1)}, u32[]{:S(2)}, u32[]{:S(2)}) collective-permute-start(bf16[2,8,16,128]{3,2,1,0:T(8,128)(2,1)S(1)} %bitcast.26), channel_id=1, source_target_pairs={{0,0},{1,5},{4,4},{5,9},{8,8},{9,13},{12,12},{13,17},{16,16},{17,2... | collective-permute-start | bytes 196616 | tf_op jit(solution)/shard_map/out_weight_over_z/ppermute | solution.py:249
  18.6 3.1 %encoder_attention.1.ctx_ref = bf16[2,256,1024]{2,1,0:T(8,128)(2,1)S(1)} custom-call(s32[1]{0:T(128)} %bitcast.10.slot_ref, s32[512]{0:T(512)S(1)} %copy-done.7, s32[512]{0:T(512)S(1)} %copy-done.8, bf16[256,1024]{1,0:T(8,128)(2,1)S(1)} %copy-done.1, bf16[256,1024]{1,0:T(8,128)(2,1)S(1)} %copy-done.2, bf16[256,1024]{1,0:T(8,128)(2,1)S(1)} %copy-done.3, ...), custom_call_target="tpu_custom_call" | custom-call | flops 536870912 | bytes 2097152 | tf_op jit(solution)/shard_map/encoder_attention/pallas_call | solution.py:62
  21.7 3.5 %collective-permute-done = bf16[2,8,16,128]{3,2,1,0:T(8,128)(2,1)S(1)} collective-permute-done((bf16[2,8,16,128]{3,2,1,0:T(8,128)(2,1)S(1)}, bf16[2,8,16,128]{3,2,1,0:T(8,128)(2,1)S(1)}, u32[]{:S(2)}, u32[]{:S(2)}) %collective-permute-start) | collective-permute-done | bytes 65568 | tf_op jit(solution)/shard_map/out_weight_over_z/ppermute | solution.py:249
  25.2 8.0 %all-to-all-done.refs_0_ = bf16[16,256,128]{2,1,0:T(8,128)(2,1)} async-done(((bf16[16,256,128]{2,1,0:T(8,128)(2,1)}), bf16[16,256,128]{2,1,0:T(8,128)(2,1)}, u32[]{:S(2)}, u32[]{:S(2)}) %all-to-all-start) | async-done | bytes 1048608 | tf_op jit(solution)/shard_map/gather_kv_weight/all_to_all | solution.py:220
  33.2 7.5 %collective-permute-start.1 = (bf16[16,256,128]{2,1,0:T(8,128)(2,1)}, bf16[16,256,128]{2,1,0:T(8,128)(2,1)}, u32[]{:S(2)}, u32[]{:S(2)}) collective-permute-start(bf16[16,256,128]{2,1,0:T(8,128)(2,1)} %all-to-all-done.refs_0_), channel_id=1, source_target_pairs={{0,4},{1,61},{4,0},{5,9},{8,12},{9,5},{12,8},{13,17},{16,20},{17,1... | collective-permute-start | bytes 3145736 | tf_op jit(solution)/shard_map/kv_weight_over_z/ppermute | solution.py:261
  40.7 1.2 broadcast_in_dim.5
  41.9 3.7 %all-to-all-start.1 = ((bf16[16,2,8,16,128]{4,3,2,1,0:T(8,128)(2,1)}), bf16[16,2,8,16,128]{4,3,2,1,0:T(8,128)(2,1)S(1)}, u32[]{:S(2)}, u32[]{:S(2)}) async-start(bf16[16,2,8,16,128]{4,3,2,1,0:T(8,128)(2,1)} %broadcast_in_dim.5), calls=%async_computation.1 | async-start | bytes 2097152 | tf_op jit(solution)/shard_map/out_weight_over_plane/all_to_all | solution.py:220
  45.6 1.3 fusion.1
  46.9 1.9 %collective-permute-start.2 = (bf16[8,256,128]{2,1,0:T(8,128)(2,1)S(1)}, bf16[8,256,128]{2,1,0:T(8,128)(2,1)S(1)}, u32[]{:S(2)}, u32[]{:S(2)}) collective-permute-start(bf16[8,256,128]{2,1,0:T(8,128)(2,1)S(1)} %get-tuple-element.32), channel_id=1, source_target_pairs={{0,1},{1,0},{2,3},{3,2},{4,5},{5,4},{6,7},{7,6},{8,9},{9,8},{10,11... | collective-permute-start | bytes 1572872 | tf_op jit(solution)/shard_map/swap_weights/ppermute | solution.py:264
  48.8 2.4 %collective-permute-start.3 = (bf16[8,256,128]{2,1,0:T(8,128)(2,1)S(1)}, bf16[8,256,128]{2,1,0:T(8,128)(2,1)S(1)}, u32[]{:S(2)}, u32[]{:S(2)}) collective-permute-start(bf16[8,256,128]{2,1,0:T(8,128)(2,1)S(1)} %get-tuple-element.31), channel_id=1, source_target_pairs={{0,1},{1,0},{2,3},{3,2},{4,5},{5,4},{6,7},{7,6},{8,9},{9,8},{10,11... | collective-permute-start | bytes 1572872 | tf_op jit(solution)/shard_map/swap_weights/ppermute | solution.py:264
  51.2 2.2 %collective-permute-done.1.refs_1_ = bf16[16,256,128]{2,1,0:T(8,128)(2,1)} collective-permute-done((bf16[16,256,128]{2,1,0:T(8,128)(2,1)}, bf16[16,256,128]{2,1,0:T(8,128)(2,1)}, u32[]{:S(2)}, u32[]{:S(2)}) %collective-permute-start.1) | collective-permute-done | bytes 1048608 | tf_op jit(solution)/shard_map/kv_weight_over_z/ppermute | solution.py:261
  53.4 2.3 %fusion = (bf16[8,256,128]{2,1,0:T(8,128)(2,1)}, bf16[8,256,128]{2,1,0:T(8,128)(2,1)}) fusion(bf16[16,256,128]{2,1,0:T(8,128)(2,1)} %collective-permute-done.1.refs_1_), kind=kLoop, calls=%fused_computation.4 | loop fusion | bytes 2097152 | tf_op jit(solution)/shard_map/swap_weights/slice | solution.py:264
  55.7 1.9 %collective-permute-start.4 = (bf16[8,256,128]{2,1,0:T(8,128)(2,1)}, bf16[8,256,128]{2,1,0:T(8,128)(2,1)}, u32[]{:S(2)}, u32[]{:S(2)}) collective-permute-start(bf16[8,256,128]{2,1,0:T(8,128)(2,1)} %get-tuple-element.30), channel_id=1, source_target_pairs={{0,1},{1,0},{2,3},{3,2},{4,5},{5,4},{6,7},{7,6},{8,9},{9,8},{10,11... | collective-permute-start | bytes 1572872 | tf_op jit(solution)/shard_map/swap_weights/ppermute | solution.py:264
  57.6 2.4 %collective-permute-start.5 = (bf16[8,256,128]{2,1,0:T(8,128)(2,1)}, bf16[8,256,128]{2,1,0:T(8,128)(2,1)}, u32[]{:S(2)}, u32[]{:S(2)}) collective-permute-start(bf16[8,256,128]{2,1,0:T(8,128)(2,1)} %get-tuple-element.29), channel_id=1, source_target_pairs={{0,1},{1,0},{2,3},{3,2},{4,5},{5,4},{6,7},{7,6},{8,9},{9,8},{10,11... | collective-permute-start | bytes 1572872 | tf_op jit(solution)/shard_map/swap_weights/ppermute | solution.py:264
  61.9 2.3 %collective-permute-start.6 = (bf16[16,2,8,16,128]{4,3,2,1,0:T(8,128)(2,1)S(1)}, bf16[16,2,8,16,128]{4,3,2,1,0:T(8,128)(2,1)S(1)}, u32[]{:S(2)}, u32[]{:S(2)}) collective-permute-start(bf16[16,2,8,16,128]{4,3,2,1,0:T(8,128)(2,1)S(1)} %all-to-all-done.1.mine_ref), channel_id=1, source_target_pairs={{0,1},{1,0},{2,3},{3,2},{4,5},{5,4},{6,7},{7,6},{8,9},{9,8},{10,11... | collective-permute-start | bytes 3145736 | tf_op jit(solution)/shard_map/swap_weights/ppermute | solution.py:266
  64.3 2.2 %collective-permute-done.6.other_ref = bf16[16,2,8,16,128]{4,3,2,1,0:T(8,128)(2,1)S(1)} collective-permute-done((bf16[16,2,8,16,128]{4,3,2,1,0:T(8,128)(2,1)S(1)}, bf16[16,2,8,16,128]{4,3,2,1,0:T(8,128)(2,1)S(1)}, u32[]{:S(2)}, u32[]{:S(2)}) %collective-permute-start.6) | collective-permute-done | bytes 1048608 | tf_op jit(solution)/shard_map/swap_weights/ppermute | solution.py:266
  67.5 4.3 %encode_keyval.1 = bf16[8,512,128]{2,1,0:T(8,128)(2,1)} custom-call(s32[3]{0:T(128)S(1)} %pad_add_fusion.1.place_ref, f32[1,1024]{1,0:T(1,128)S(1)} %bitcast.22, bf16[2,256,1024]{2,1,0:T(8,128)(2,1)S(1)} %encoder_attention.1.ctx_ref, bf16[16,2,8,16,128]{4,3,2,1,0:T(8,128)(2,1)S(1)} %all-to-all-done.1.mine_ref, ...), custom_call_target="tpu_custom_call" | custom-call | flops 1610612736 | bytes 8388608 | tf_op jit(solution)/shard_map/encode_keyval/pallas_call | solution.py:133
  71.8 4.5 %all-to-all-start.2 = ((bf16[8,512,128]{2,1,0:T(8,128)(2,1)}), bf16[8,512,128]{2,1,0:T(8,128)(2,1)S(1)}, u32[]{:S(2)}, u32[]{:S(2)}) async-start(bf16[8,512,128]{2,1,0:T(8,128)(2,1)} %encode_keyval.1), calls=%async_computation.2 | async-start | bytes 2097152 | tf_op jit(solution)/shard_map/exchange_keyval/all_to_all | solution.py:270
  76.5 17.2 %all-to-all-done.2.kv_ref = bf16[8,512,128]{2,1,0:T(8,128)(2,1)S(1)} async-done(((bf16[8,512,128]{2,1,0:T(8,128)(2,1)}), bf16[8,512,128]{2,1,0:T(8,128)(2,1)S(1)}, u32[]{:S(2)}, u32[]{:S(2)}) %all-to-all-start.2) | async-done | bytes 1048608 | tf_op jit(solution)/shard_map/exchange_keyval/all_to_all | solution.py:270
  93.7 3.3 %cross_attention.1 = bf16[64,2,640]{2,1,0:T(2,128)(2,1)S(1)} custom-call(s32[2]{0:T(128)S(1)} %pad_add_fusion.first_ref, s32[512]{0:T(512)S(1)} %copy-done.7, s32[512]{0:T(512)S(1)} %copy-done.8, bf16[512,128]{1,0:T(8,128)(2,1)S(1)} %bitcast.21, bf16[8,512,128]{2,1,0:T(8,128)(2,1)S(1)} %all-to-all-done.2.kv_ref), custom_call_target="tpu_custom_call" | custom-call | tf_op jit(solution)/shard_map/cross_attention/pallas_call | solution.py:188
  97.0 31.9 %all_to_all.20.part_ref = bf16[64,2,640]{2,1,0:T(2,128)(2,1)} all-to-all(bf16[64,2,640]{2,1,0:T(2,128)(2,1)S(1)} %cross_attention.1), channel_id=1, replica_groups=mesh['yh'=2,'x'=4,'z'=16,'yl'=2,'c'=2] {'z','yl','c'}, dimensions={0} | all-to-all | bytes 327680 | tf_op jit(solution)/shard_map/exchange_partials/all_to_all | solution.py:275
  128.8 2.3 %merge_partials.1 = f32[8,128]{1,0:T(8,128)} custom-call(bf16[64,2,640]{2,1,0:T(2,128)(2,1)} %all_to_all.20.part_ref), custom_call_target="tpu_custom_call" | custom-call | tf_op jit(solution)/shard_map/merge_partials/pallas_call | solution.py:208
  (39 shorter events, 6.8 us)
Async XLA Ops:
  0.0 9.2 %copy-start = (bf16[1024,1,256]{2,0,1:T(8,128)(2,1)S(1)}, bf16[1024,1,256]{2,0,1:T(8,128)(2,1)}, u32[]{:S(2)}) copy-start(bf16[1024,1,256]{2,0,1:T(8,128)(2,1)} %param.16) | copy-start | bytes 1572868
  0.0 0.8 copy-start.11
  10.4 6.5 %copy-start.1 = (bf16[256,1024]{1,0:T(8,128)(2,1)S(1)}, bf16[256,1024]{1,0:T(8,128)(2,1)}, u32[]{:S(2)}) copy-start(bf16[256,1024]{1,0:T(8,128)(2,1)} %q_ref.1) | copy-start | bytes 1572868
  10.4 6.5 %copy-start.2 = (bf16[256,1024]{1,0:T(8,128)(2,1)S(1)}, bf16[256,1024]{1,0:T(8,128)(2,1)}, u32[]{:S(2)}) copy-start(bf16[256,1024]{1,0:T(8,128)(2,1)} %k_ref.1) | copy-start | bytes 1572868
  10.4 6.5 %copy-start.3 = (bf16[256,1024]{1,0:T(8,128)(2,1)S(1)}, bf16[256,1024]{1,0:T(8,128)(2,1)}, u32[]{:S(2)}) copy-start(bf16[256,1024]{1,0:T(8,128)(2,1)} %v_ref.1) | copy-start | bytes 1572868
  10.4 22.8 %all-to-all-start = ((bf16[16,256,128]{2,1,0:T(8,128)(2,1)}), bf16[16,256,128]{2,1,0:T(8,128)(2,1)}, u32[]{:S(2)}, u32[]{:S(2)}) async-start(bf16[16,256,128]{2,1,0:T(8,128)(2,1)} %broadcast_in_dim.4), calls=%async_computation | async-start | bytes 2097152 | tf_op jit(solution)/shard_map/gather_kv_weight/all_to_all | solution.py:220
  14.9 10.3 %collective-permute-start = (bf16[2,8,16,128]{3,2,1,0:T(8,128)(2,1)S(1)}, bf16[2,8,16,128]{3,2,1,0:T(8,128)(2,1)S(1)}, u32[]{:S(2)}, u32[]{:S(2)}) collective-permute-start(bf16[2,8,16,128]{3,2,1,0:T(8,128)(2,1)S(1)} %bitcast.26), channel_id=1, source_target_pairs={{0,0},{1,5},{4,4},{5,9},{8,8},{9,13},{12,12},{13,17},{16,16},{17,2... | collective-permute-start | bytes 196616 | tf_op jit(solution)/shard_map/out_weight_over_z/ppermute | solution.py:249
  16.9 0.7 copy-start.8
  16.9 0.7 copy-start.7
  17.6 1.0 copy-start.4
  33.2 20.2 %collective-permute-start.1 = (bf16[16,256,128]{2,1,0:T(8,128)(2,1)}, bf16[16,256,128]{2,1,0:T(8,128)(2,1)}, u32[]{:S(2)}, u32[]{:S(2)}) collective-permute-start(bf16[16,256,128]{2,1,0:T(8,128)(2,1)} %all-to-all-done.refs_0_), channel_id=1, source_target_pairs={{0,4},{1,61},{4,0},{5,9},{8,12},{9,5},{12,8},{13,17},{16,20},{17,1... | collective-permute-start | bytes 3145736 | tf_op jit(solution)/shard_map/kv_weight_over_z/ppermute | solution.py:261
  41.9 19.4 %all-to-all-start.1 = ((bf16[16,2,8,16,128]{4,3,2,1,0:T(8,128)(2,1)}), bf16[16,2,8,16,128]{4,3,2,1,0:T(8,128)(2,1)S(1)}, u32[]{:S(2)}, u32[]{:S(2)}) async-start(bf16[16,2,8,16,128]{4,3,2,1,0:T(8,128)(2,1)} %broadcast_in_dim.5), calls=%async_computation.1 | async-start | bytes 2097152 | tf_op jit(solution)/shard_map/out_weight_over_plane/all_to_all | solution.py:220
  46.9 13.1 %collective-permute-start.2 = (bf16[8,256,128]{2,1,0:T(8,128)(2,1)S(1)}, bf16[8,256,128]{2,1,0:T(8,128)(2,1)S(1)}, u32[]{:S(2)}, u32[]{:S(2)}) collective-permute-start(bf16[8,256,128]{2,1,0:T(8,128)(2,1)S(1)} %get-tuple-element.32), channel_id=1, source_target_pairs={{0,1},{1,0},{2,3},{3,2},{4,5},{5,4},{6,7},{7,6},{8,9},{9,8},{10,11... | collective-permute-start | bytes 1572872 | tf_op jit(solution)/shard_map/swap_weights/ppermute | solution.py:264
  48.8 11.2 %collective-permute-start.3 = (bf16[8,256,128]{2,1,0:T(8,128)(2,1)S(1)}, bf16[8,256,128]{2,1,0:T(8,128)(2,1)S(1)}, u32[]{:S(2)}, u32[]{:S(2)}) collective-permute-start(bf16[8,256,128]{2,1,0:T(8,128)(2,1)S(1)} %get-tuple-element.31), channel_id=1, source_target_pairs={{0,1},{1,0},{2,3},{3,2},{4,5},{5,4},{6,7},{7,6},{8,9},{9,8},{10,11... | collective-permute-start | bytes 1572872 | tf_op jit(solution)/shard_map/swap_weights/ppermute | solution.py:264
  55.7 5.6 %collective-permute-start.4 = (bf16[8,256,128]{2,1,0:T(8,128)(2,1)}, bf16[8,256,128]{2,1,0:T(8,128)(2,1)}, u32[]{:S(2)}, u32[]{:S(2)}) collective-permute-start(bf16[8,256,128]{2,1,0:T(8,128)(2,1)} %get-tuple-element.30), channel_id=1, source_target_pairs={{0,1},{1,0},{2,3},{3,2},{4,5},{5,4},{6,7},{7,6},{8,9},{9,8},{10,11... | collective-permute-start | bytes 1572872 | tf_op jit(solution)/shard_map/swap_weights/ppermute | solution.py:264
  57.6 4.3 %collective-permute-start.5 = (bf16[8,256,128]{2,1,0:T(8,128)(2,1)}, bf16[8,256,128]{2,1,0:T(8,128)(2,1)}, u32[]{:S(2)}, u32[]{:S(2)}) collective-permute-start(bf16[8,256,128]{2,1,0:T(8,128)(2,1)} %get-tuple-element.29), channel_id=1, source_target_pairs={{0,1},{1,0},{2,3},{3,2},{4,5},{5,4},{6,7},{7,6},{8,9},{9,8},{10,11... | collective-permute-start | bytes 1572872 | tf_op jit(solution)/shard_map/swap_weights/ppermute | solution.py:264
  60.0 0.8 copy-start.5
  61.9 4.5 %collective-permute-start.6 = (bf16[16,2,8,16,128]{4,3,2,1,0:T(8,128)(2,1)S(1)}, bf16[16,2,8,16,128]{4,3,2,1,0:T(8,128)(2,1)S(1)}, u32[]{:S(2)}, u32[]{:S(2)}) collective-permute-start(bf16[16,2,8,16,128]{4,3,2,1,0:T(8,128)(2,1)S(1)} %all-to-all-done.1.mine_ref), channel_id=1, source_target_pairs={{0,1},{1,0},{2,3},{3,2},{4,5},{5,4},{6,7},{7,6},{8,9},{9,8},{10,11... | collective-permute-start | bytes 3145736 | tf_op jit(solution)/shard_map/swap_weights/ppermute | solution.py:266
  64.2 2.3 %copy-start.9 = (f32[1024]{0:T(1024)S(1)}, f32[1024]{0:T(1024)}, u32[]{:S(2)}) copy-start(f32[1024]{0:T(1024)} %param.15) | copy-start | bytes 12292
  66.4 1.0 copy-start.6
  71.8 4.5 %copy-start.10 = (bf16[64,1,1024]{2,0,1:T(8,128)(2,1)S(1)}, bf16[64,1,1024]{2,0,1:T(8,128)(2,1)}, u32[]{:S(2)}) copy-start(bf16[64,1,1024]{2,0,1:T(8,128)(2,1)} %param.17) | copy-start | bytes 393220
  71.8 21.9 %all-to-all-start.2 = ((bf16[8,512,128]{2,1,0:T(8,128)(2,1)}), bf16[8,512,128]{2,1,0:T(8,128)(2,1)S(1)}, u32[]{:S(2)}, u32[]{:S(2)}) async-start(bf16[8,512,128]{2,1,0:T(8,128)(2,1)} %encode_keyval.1), calls=%async_computation.2 | async-start | bytes 2097152 | tf_op jit(solution)/shard_map/exchange_keyval/all_to_all | solution.py:270

commit v8 on v7

--- a/solution.py
+++ b/solution.py
@@ -37,42 +37,42 @@
     return lax.dot_general(a, b, (((1,), (1,)), ((), ())), preferred_element_type=jnp.float32)
 
 
-def encoder_attention_kernel(slot_ref, span_ref, len_ref, q_ref, k_ref, v_ref, resid_ref, o_ref):
-    o_ref[1] = resid_ref[...]
+def encoder_attention_kernel(slot_ref, span_ref, len_ref, q_ref, k_ref, v_ref, o_ref):
     valid = len_ref[span_ref[slot_ref[0]]]
     keep = lax.broadcasted_iota(jnp.int32, (1, SEG_LEN), 1) < valid
     bias = jnp.where(keep, 0.0, MASKED).astype(jnp.float32)
     low = lax.broadcasted_iota(jnp.int32, (SEG_LEN, 2 * ENC_HEAD), 1) < ENC_HEAD
+    scale = math.log2(math.e) / math.sqrt(ENC_HEAD)
     for pair in range(ENC_HEADS // 2):
         cols = slice(pair * 2 * ENC_HEAD, (pair + 1) * 2 * ENC_HEAD)
         q, k, v = q_ref[:, cols], k_ref[:, cols], v_ref[:, cols]
         zero = jnp.zeros_like(k)
         parts = []
         for mine in (low, jnp.logical_not(low)):
-            scores = dot_t(q, jnp.where(mine, k, zero)) * (1.0 / math.sqrt(ENC_HEAD)) + bias
-            expo = jnp.exp(scores - jnp.max(scores, axis=-1, keepdims=True))
+            scores = dot_t(q, jnp.where(mine, k, zero)) + bias
+            expo = jnp.exp2((scores - jnp.max(scores, axis=-1, keepdims=True)) * scale)
             probs = (expo * (1.0 / jnp.sum(expo, axis=-1, keepdims=True))).astype(jnp.bfloat16)
             parts.append(dot(probs, v))
-        o_ref[0, :, cols] = jnp.where(low, parts[0], parts[1]).astype(jnp.bfloat16)
-
-
-def encoder_attention(slot, span_ids, seg_lengths, q, k, v, resid):
+        o_ref[:, cols] = jnp.where(low, parts[0], parts[1]).astype(jnp.bfloat16)
+
+
+def encoder_attention(slot, span_ids, seg_lengths, q, k, v):
     smem = pl.BlockSpec(memory_space=pltpu.SMEM)
     vmem = pl.BlockSpec(memory_space=pltpu.VMEM)
     return pl.pallas_call(
         encoder_attention_kernel,
-        out_shape=jax.ShapeDtypeStruct((2, SEG_LEN, D_ENC), jnp.bfloat16),
-        in_specs=[smem, smem, smem, vmem, vmem, vmem, vmem],
+        out_shape=jax.ShapeDtypeStruct((SEG_LEN, D_ENC), jnp.bfloat16),
+        in_specs=[smem, smem, smem, vmem, vmem, vmem],
         out_specs=vmem,
         compiler_params=params(),
         cost_estimate=pl.CostEstimate(
             flops=8 * SEG_LEN * SEG_LEN * D_ENC, bytes_accessed=8 * SEG_LEN * D_ENC,
             transcendentals=SEG_LEN * SEG_LEN * ENC_HEADS),
         name="encoder_attention",
-    )(slot, span_ids, seg_lengths, q, k, v, resid)
-
-
-def encode_kernel(place_ref, gain_ref, ctx_ref, mine_ref, other_ref, *refs):
+    )(slot, span_ids, seg_lengths, q, k, v)
+
+
+def encode_kernel(place_ref, gain_ref, ctx_ref, resid_ref, mine_ref, other_ref, *refs):
     kv_refs, o_ref = refs[:6], refs[6]
     w_ref, enc_ref, done_ref = refs[7:10]
     kv_bufs, in_sems, out_sems = refs[10:14], refs[14], refs[15]
@@ -94,10 +94,10 @@
                 for c in range(2):
                     row = pl.multiple_of(64 * plane + 32 * yl + 16 * c, 16)
                     w_ref[:, pl.ds(row, 16), :] = part_ref[ha * 2 + yl, c]
-    ctx = ctx_ref[0]
+    ctx = ctx_ref[...]
     hidden = jnp.concatenate(
         [dot(ctx, jnp.concatenate([w_ref[2 * j], w_ref[2 * j + 1]], axis=1)) for j in range(4)], axis=1)
-    hidden = hidden + ctx_ref[1].astype(jnp.float32)
+    hidden = hidden + resid_ref[...].astype(jnp.float32)
     factor = lax.rsqrt(jnp.mean(hidden * hidden, axis=-1, keepdims=True) + 1e-05)
     encoded = (hidden * factor * gain_ref[...]).astype(jnp.bfloat16)
     for piece in range(4):
@@ -125,7 +125,7 @@
         send.wait()
 
 
-def encode(place, gain, ctx, mine, other, kvs):
+def encode(place, gain, ctx, resid, mine, other, kvs):
     smem = pl.BlockSpec(memory_space=pltpu.SMEM)
     vmem = pl.BlockSpec(memory_space=pltpu.VMEM)
     hbm = pl.BlockSpec(memory_space=pltpu.HBM)
@@ -133,7 +133,7 @@
     return pl.pallas_call(
         encode_kernel,
         out_shape=shape,
-        in_specs=[smem] + [vmem] * 4 + [hbm] * 6,
+        in_specs=[smem] + [vmem] * 5 + [hbm] * 6,
         out_specs=hbm,
         scratch_shapes=[pltpu.VMEM((8, D_ENC, HEAD), jnp.bfloat16),
                         pltpu.VMEM((4, SEG_LEN, 256), jnp.bfloat16),
@@ -144,7 +144,7 @@
         cost_estimate=pl.CostEstimate(
             flops=6 * SEG_LEN * D_ENC * D_ENC, bytes_accessed=8 * D_ENC * D_ENC, transcendentals=SEG_LEN),
         name="encode_keyval",
-    )(place, gain, ctx, mine, other, *kvs)
+    )(place, gain, ctx, resid, mine, other, *kvs)
 
 
 def cross_kernel(slots, first_ref, span_ref, len_ref, q_ref, kv_ref, o_ref):
@@ -169,7 +169,7 @@
         q = q_ref[b * rows:(b + 1) * rows]
         scores = dot_t(q, keys) + bias
         top = jnp.max(scores, axis=-1, keepdims=True)
-        expo = jnp.exp((scores - top) * scale)
+        expo = jnp.exp2((scores - top) * (scale * math.log2(math.e)))
         total = jnp.sum(expo, axis=-1, keepdims=True)
         put(b, dot(expo.astype(jnp.bfloat16), values) / total)
         level = jnp.broadcast_to(top * scale + jnp.log(total), (rows, HEAD))
@@ -196,11 +196,14 @@
 
 
 def merge_kernel(part_ref, o_ref):
+    pieces = part_ref[:, :, 4 * HEAD:].astype(jnp.float32)
+    level = pieces + pltpu.roll(pieces, HEAD - 1, 2) + pltpu.roll(pieces, HEAD - 2, 2)
+    weight = jnp.exp(level - jnp.max(level, axis=0, keepdims=True))
+    total = jnp.sum(weight, axis=0)
     for b in range(GROUP // 2):
-        level = jnp.sum(part_ref[:, :, 512 + 3 * b:515 + 3 * b].astype(jnp.float32), axis=-1, keepdims=True)
-        weight = jnp.exp(level - jnp.max(level, axis=0, keepdims=True))
         average = part_ref[:, :, HEAD * b:HEAD * (b + 1)].astype(jnp.float32)
-        o_ref[2 * b:2 * b + 2] = jnp.sum(average * weight, axis=0) / jnp.sum(weight, axis=0)
+        at = slice(3 * b, 3 * b + 1)
+        o_ref[2 * b:2 * b + 2] = jnp.sum(average * weight[:, :, at], axis=0) / total[:, at]
 
 
 def merge(parts):
@@ -248,7 +251,7 @@
                     hops.append(((ha_at * 16 + z_at) * 2 + c_at, (ha_at * 16 + there) * 2 + c_at))
         pair = lax.ppermute(pair, ("yh", "x", "z", "c"), hops)
     slot = (ha * sa_count + sa).reshape(1).astype(jnp.int32)
-    context = encoder_attention(slot, span_ids, seg_lengths, enc_query, enc_key, enc_value, enc_resid)
+    context = encoder_attention(slot, span_ids, seg_lengths, enc_query, enc_key, enc_value)
     kv_mine, pair, context = lax.optimization_barrier((kv_mine, pair, context))
     with jax.named_scope("out_weight_over_plane"):
         w_mine = spread(pair, PLANE)
@@ -265,7 +268,7 @@
         w_mine, kvs = lax.optimization_barrier((w_mine, kvs))
         w_other = swap(w_mine)
     place = jnp.stack([z, core, odd]).astype(jnp.int32)
-    keyval = encode(place, norm_gain.reshape(1, D_ENC), context, w_mine, w_other, kvs)
+    keyval = encode(place, norm_gain.reshape(1, D_ENC), context, enc_resid, w_mine, w_other, kvs)
     with jax.named_scope("exchange_keyval"):
         keyval = lax.all_to_all(keyval, HA, 0, 0, tiled=True)
     first = jnp.stack([sa, sa_count]).astype(jnp.int32)

time: 132 us -> 131 us (level)
  no operation moved by 1% of the time
where the time goes in v8:
time: 131 us
  blocking collectives  40.1 us (31%)
  waiting for transfers between devices  35 us (27%)
  starting transfers between devices  33.2 us (25%)
  Pallas kernels  12.6 us (10%)
  local copies, waits for them, and re-layouts  9.38 us (7%)
    all_to_all x1, blocking collectives, local(): parts = lax.all_to_all(parts, SA, 0, 0, tiled=True)  31.7 us
    all_to_all x1, waiting for transfers between devices, local(): keyval = lax.all_to_all(keyval, HA, 0, 0, tiled=True)  17.2 us
    ppermute x4, starting transfers between devices, local(): kvs = kvs + [swap(part) for kv in kvs for part in (kv[:8], kv[8:])]  8.78 us
    all_to_all x2, waiting for transfers between devices, spread(): return lax.all_to_all(copies, axes, 0, 0, tiled=True)  8.49 us
    all_gather x1, blocking collectives, local(): lax.all_gather(out_weight.reshape(16, 8, HEAD).transpose(1, 0, 2), 'c')  8.37 us
    all_to_all x2, starting transfers between devices, spread(): return lax.all_to_all(copies, axes, 0, 0, tiled=True)  8.12 us
    ppermute x1, starting transfers between devices, local(): kv_next = lax.ppermute(kv_mine, ('z', 'c'), pairs)  7.49 us
    all_to_all x1, starting transfers between devices, local(): keyval = lax.all_to_all(keyval, HA, 0, 0, tiled=True)  4.64 us
  transfers between devices with their start and end apart: 10, of which 7 were waited for; matrix products, arithmetic and copies ran while one was open for 4% of the time, Pallas kernels for 2%

profile of v8, /device:TPU:1, one launch (start us, length us, event | category | flops | bytes accessed | tf_op | source)
XLA Modules:
  0.0 130.7 jit_solution(1738607949546743331)
XLA Ops:
  0.8 8.4 %all-gather = bf16[16,16,128]{2,0,1:T(8,128)(2,1)S(1)} all-gather(bf16[8,16,128]{2,0,1:T(8,128)(2,1)S(1)} %bitcast.24), channel_id=2, replica_groups=mesh['yh'=2,'x'=4,'z'=16,'yl'=2,'c'=2] {'c'}, dimensions={0}, use_global_device_ids=true | all-gather | bytes 98304 | tf_op jit(solution)/shard_map/pair_out_weight/all_gather | solution.py:239
  10.4 4.5 %all-to-all-start = ((bf16[16,256,128]{2,1,0:T(8,128)(2,1)}), bf16[16,256,128]{2,1,0:T(8,128)(2,1)}, u32[]{:S(2)}, u32[]{:S(2)}) async-start(bf16[16,256,128]{2,1,0:T(8,128)(2,1)} %broadcast_in_dim.4), calls=%async_computation | async-start | bytes 2097152 | tf_op jit(solution)/shard_map/gather_kv_weight/all_to_all | solution.py:223
  14.9 1.9 %collective-permute-start = (bf16[2,8,16,128]{3,2,1,0:T(8,128)(2,1)S(1)}, bf16[2,8,16,128]{3,2,1,0:T(8,128)(2,1)S(1)}, u32[]{:S(2)}, u32[]{:S(2)}) collective-permute-start(bf16[2,8,16,128]{3,2,1,0:T(8,128)(2,1)S(1)} %bitcast.26), channel_id=1, source_target_pairs={{0,0},{1,5},{4,4},{5,9},{8,8},{9,13},{12,12},{13,17},{16,16},{17,2... | collective-permute-start | bytes 196616 | tf_op jit(solution)/shard_map/out_weight_over_z/ppermute | solution.py:252
  17.6 3.1 %encoder_attention.1.ctx_ref = bf16[256,1024]{1,0:T(8,128)(2,1)S(1)} custom-call(s32[1]{0:T(128)} %bitcast.10.slot_ref, s32[512]{0:T(512)S(1)} %copy-done.7, s32[512]{0:T(512)S(1)} %copy-done.8, bf16[256,1024]{1,0:T(8,128)(2,1)S(1)} %copy-done.1, bf16[256,1024]{1,0:T(8,128)(2,1)S(1)} %copy-done.2, bf16[256,1024]{1,0:T(8,128)(2,1)S(1)} %copy-done.3), custom_call_target="tpu_custom_call" | custom-call | flops 536870912 | bytes 2097152 | tf_op jit(solution)/shard_map/encoder_attention/pallas_call | solution.py:62
  20.7 4.5 %collective-permute-done = bf16[2,8,16,128]{3,2,1,0:T(8,128)(2,1)S(1)} collective-permute-done((bf16[2,8,16,128]{3,2,1,0:T(8,128)(2,1)S(1)}, bf16[2,8,16,128]{3,2,1,0:T(8,128)(2,1)S(1)}, u32[]{:S(2)}, u32[]{:S(2)}) %collective-permute-start) | collective-permute-done | bytes 65568 | tf_op jit(solution)/shard_map/out_weight_over_z/ppermute | solution.py:252
  25.2 8.0 %all-to-all-done.refs_0_ = bf16[16,256,128]{2,1,0:T(8,128)(2,1)} async-done(((bf16[16,256,128]{2,1,0:T(8,128)(2,1)}), bf16[16,256,128]{2,1,0:T(8,128)(2,1)}, u32[]{:S(2)}, u32[]{:S(2)}) %all-to-all-start) | async-done | bytes 1048608 | tf_op jit(solution)/shard_map/gather_kv_weight/all_to_all | solution.py:223
  33.2 7.5 %collective-permute-start.1 = (bf16[16,256,128]{2,1,0:T(8,128)(2,1)}, bf16[16,256,128]{2,1,0:T(8,128)(2,1)}, u32[]{:S(2)}, u32[]{:S(2)}) collective-permute-start(bf16[16,256,128]{2,1,0:T(8,128)(2,1)} %all-to-all-done.refs_0_), channel_id=1, source_target_pairs={{0,4},{1,61},{4,0},{5,9},{8,12},{9,5},{12,8},{13,17},{16,20},{17,1... | collective-permute-start | bytes 3145736 | tf_op jit(solution)/shard_map/kv_weight_over_z/ppermute | solution.py:264
  40.7 1.2 broadcast_in_dim.5
  41.9 3.7 %all-to-all-start.1 = ((bf16[16,2,8,16,128]{4,3,2,1,0:T(8,128)(2,1)}), bf16[16,2,8,16,128]{4,3,2,1,0:T(8,128)(2,1)S(1)}, u32[]{:S(2)}, u32[]{:S(2)}) async-start(bf16[16,2,8,16,128]{4,3,2,1,0:T(8,128)(2,1)} %broadcast_in_dim.5), calls=%async_computation.1 | async-start | bytes 2097152 | tf_op jit(solution)/shard_map/out_weight_over_plane/all_to_all | solution.py:223
  45.6 1.3 fusion.1
  46.9 1.9 %collective-permute-start.2 = (bf16[8,256,128]{2,1,0:T(8,128)(2,1)S(1)}, bf16[8,256,128]{2,1,0:T(8,128)(2,1)S(1)}, u32[]{:S(2)}, u32[]{:S(2)}) collective-permute-start(bf16[8,256,128]{2,1,0:T(8,128)(2,1)S(1)} %get-tuple-element.32), channel_id=1, source_target_pairs={{0,1},{1,0},{2,3},{3,2},{4,5},{5,4},{6,7},{7,6},{8,9},{9,8},{10,11... | collective-permute-start | bytes 1572872 | tf_op jit(solution)/shard_map/swap_weights/ppermute | solution.py:267
  48.8 2.5 %collective-permute-start.3 = (bf16[8,256,128]{2,1,0:T(8,128)(2,1)S(1)}, bf16[8,256,128]{2,1,0:T(8,128)(2,1)S(1)}, u32[]{:S(2)}, u32[]{:S(2)}) collective-permute-start(bf16[8,256,128]{2,1,0:T(8,128)(2,1)S(1)} %get-tuple-element.31), channel_id=1, source_target_pairs={{0,1},{1,0},{2,3},{3,2},{4,5},{5,4},{6,7},{7,6},{8,9},{9,8},{10,11... | collective-permute-start | bytes 1572872 | tf_op jit(solution)/shard_map/swap_weights/ppermute | solution.py:267
  51.4 2.0 %collective-permute-done.1.refs_1_ = bf16[16,256,128]{2,1,0:T(8,128)(2,1)} collective-permute-done((bf16[16,256,128]{2,1,0:T(8,128)(2,1)}, bf16[16,256,128]{2,1,0:T(8,128)(2,1)}, u32[]{:S(2)}, u32[]{:S(2)}) %collective-permute-start.1) | collective-permute-done | bytes 1048608 | tf_op jit(solution)/shard_map/kv_weight_over_z/ppermute | solution.py:264
  53.4 2.3 %fusion = (bf16[8,256,128]{2,1,0:T(8,128)(2,1)}, bf16[8,256,128]{2,1,0:T(8,128)(2,1)}) fusion(bf16[16,256,128]{2,1,0:T(8,128)(2,1)} %collective-permute-done.1.refs_1_), kind=kLoop, calls=%fused_computation.4 | loop fusion | bytes 2097152 | tf_op jit(solution)/shard_map/swap_weights/slice | solution.py:267
  55.7 1.9 %collective-permute-start.4 = (bf16[8,256,128]{2,1,0:T(8,128)(2,1)}, bf16[8,256,128]{2,1,0:T(8,128)(2,1)}, u32[]{:S(2)}, u32[]{:S(2)}) collective-permute-start(bf16[8,256,128]{2,1,0:T(8,128)(2,1)} %get-tuple-element.30), channel_id=1, source_target_pairs={{0,1},{1,0},{2,3},{3,2},{4,5},{5,4},{6,7},{7,6},{8,9},{9,8},{10,11... | collective-permute-start | bytes 1572872 | tf_op jit(solution)/shard_map/swap_weights/ppermute | solution.py:267
  57.6 2.4 %collective-permute-start.5 = (bf16[8,256,128]{2,1,0:T(8,128)(2,1)}, bf16[8,256,128]{2,1,0:T(8,128)(2,1)}, u32[]{:S(2)}, u32[]{:S(2)}) collective-permute-start(bf16[8,256,128]{2,1,0:T(8,128)(2,1)} %get-tuple-element.29), channel_id=1, source_target_pairs={{0,1},{1,0},{2,3},{3,2},{4,5},{5,4},{6,7},{7,6},{8,9},{9,8},{10,11... | collective-permute-start | bytes 1572872 | tf_op jit(solution)/shard_map/swap_weights/ppermute | solution.py:267
  61.9 2.3 %collective-permute-start.6 = (bf16[16,2,8,16,128]{4,3,2,1,0:T(8,128)(2,1)S(1)}, bf16[16,2,8,16,128]{4,3,2,1,0:T(8,128)(2,1)S(1)}, u32[]{:S(2)}, u32[]{:S(2)}) collective-permute-start(bf16[16,2,8,16,128]{4,3,2,1,0:T(8,128)(2,1)S(1)} %all-to-all-done.1.mine_ref), channel_id=1, source_target_pairs={{0,1},{1,0},{2,3},{3,2},{4,5},{5,4},{6,7},{7,6},{8,9},{9,8},{10,11... | collective-permute-start | bytes 3145736 | tf_op jit(solution)/shard_map/swap_weights/ppermute | solution.py:269
  64.3 2.2 %collective-permute-done.6.other_ref = bf16[16,2,8,16,128]{4,3,2,1,0:T(8,128)(2,1)S(1)} collective-permute-done((bf16[16,2,8,16,128]{4,3,2,1,0:T(8,128)(2,1)S(1)}, bf16[16,2,8,16,128]{4,3,2,1,0:T(8,128)(2,1)S(1)}, u32[]{:S(2)}, u32[]{:S(2)}) %collective-permute-start.6) | collective-permute-done | bytes 1048608 | tf_op jit(solution)/shard_map/swap_weights/ppermute | solution.py:269
  67.5 4.3 %encode_keyval.1 = bf16[8,512,128]{2,1,0:T(8,128)(2,1)} custom-call(s32[3]{0:T(128)S(1)} %pad_add_fusion.1.place_ref, f32[1,1024]{1,0:T(1,128)S(1)} %bitcast.22, bf16[256,1024]{1,0:T(8,128)(2,1)S(1)} %encoder_attention.1.ctx_ref, bf16[256,1024]{1,0:T(8,128)(2,1)S(1)} %copy-done.4, bf16[16,2,8,16,128]{4,3,2,1,0:T(8,128)(2,1)S(1)} %all-to-all-done.1.mine_ref, ...), custom_call_target="tpu_custom_call" | custom-call | flops 1610612736 | bytes 8388608 | tf_op jit(solution)/shard_map/encode_keyval/pallas_call | solution.py:133
  71.8 4.6 %all-to-all-start.2 = ((bf16[8,512,128]{2,1,0:T(8,128)(2,1)}), bf16[8,512,128]{2,1,0:T(8,128)(2,1)S(1)}, u32[]{:S(2)}, u32[]{:S(2)}) async-start(bf16[8,512,128]{2,1,0:T(8,128)(2,1)} %encode_keyval.1), calls=%async_computation.2 | async-start | bytes 2097152 | tf_op jit(solution)/shard_map/exchange_keyval/all_to_all | solution.py:273
  76.6 17.2 %all-to-all-done.2.kv_ref = bf16[8,512,128]{2,1,0:T(8,128)(2,1)S(1)} async-done(((bf16[8,512,128]{2,1,0:T(8,128)(2,1)}), bf16[8,512,128]{2,1,0:T(8,128)(2,1)S(1)}, u32[]{:S(2)}, u32[]{:S(2)}) %all-to-all-start.2) | async-done | bytes 1048608 | tf_op jit(solution)/shard_map/exchange_keyval/all_to_all | solution.py:273
  93.8 3.2 %cross_attention.1 = bf16[64,2,640]{2,1,0:T(2,128)(2,1)S(1)} custom-call(s32[2]{0:T(128)S(1)} %pad_add_fusion.first_ref, s32[512]{0:T(512)S(1)} %copy-done.7, s32[512]{0:T(512)S(1)} %copy-done.8, bf16[512,128]{1,0:T(8,128)(2,1)S(1)} %bitcast.21, bf16[8,512,128]{2,1,0:T(8,128)(2,1)S(1)} %all-to-all-done.2.kv_ref), custom_call_target="tpu_custom_call" | custom-call | tf_op jit(solution)/shard_map/cross_attention/pallas_call | solution.py:188
  97.0 31.7 %all_to_all.20.part_ref = bf16[64,2,640]{2,1,0:T(2,128)(2,1)} all-to-all(bf16[64,2,640]{2,1,0:T(2,128)(2,1)S(1)} %cross_attention.1), channel_id=1, replica_groups=mesh['yh'=2,'x'=4,'z'=16,'yl'=2,'c'=2] {'z','yl','c'}, dimensions={0} | all-to-all | bytes 327680 | tf_op jit(solution)/shard_map/exchange_partials/all_to_all | solution.py:278
  128.7 2.0 %merge_partials.1 = f32[8,128]{1,0:T(8,128)} custom-call(bf16[64,2,640]{2,1,0:T(2,128)(2,1)} %all_to_all.20.part_ref), custom_call_target="tpu_custom_call" | custom-call | tf_op jit(solution)/shard_map/merge_partials/pallas_call | solution.py:211
  (39 shorter events, 5.8 us)
Async XLA Ops:
  0.0 9.2 %copy-start = (bf16[1024,1,256]{2,0,1:T(8,128)(2,1)S(1)}, bf16[1024,1,256]{2,0,1:T(8,128)(2,1)}, u32[]{:S(2)}) copy-start(bf16[1024,1,256]{2,0,1:T(8,128)(2,1)} %param.16) | copy-start | bytes 1572868
  0.0 0.8 copy-start.11
  10.4 6.5 %copy-start.1 = (bf16[256,1024]{1,0:T(8,128)(2,1)S(1)}, bf16[256,1024]{1,0:T(8,128)(2,1)}, u32[]{:S(2)}) copy-start(bf16[256,1024]{1,0:T(8,128)(2,1)} %q_ref.1) | copy-start | bytes 1572868
  10.4 6.5 %copy-start.2 = (bf16[256,1024]{1,0:T(8,128)(2,1)S(1)}, bf16[256,1024]{1,0:T(8,128)(2,1)}, u32[]{:S(2)}) copy-start(bf16[256,1024]{1,0:T(8,128)(2,1)} %k_ref.1) | copy-start | bytes 1572868
  10.4 6.5 %copy-start.3 = (bf16[256,1024]{1,0:T(8,128)(2,1)S(1)}, bf16[256,1024]{1,0:T(8,128)(2,1)}, u32[]{:S(2)}) copy-start(bf16[256,1024]{1,0:T(8,128)(2,1)} %v_ref.1) | copy-start | bytes 1572868
  10.4 22.8 %all-to-all-start = ((bf16[16,256,128]{2,1,0:T(8,128)(2,1)}), bf16[16,256,128]{2,1,0:T(8,128)(2,1)}, u32[]{:S(2)}, u32[]{:S(2)}) async-start(bf16[16,256,128]{2,1,0:T(8,128)(2,1)} %broadcast_in_dim.4), calls=%async_computation | async-start | bytes 2097152 | tf_op jit(solution)/shard_map/gather_kv_weight/all_to_all | solution.py:223
  14.9 10.3 %collective-permute-start = (bf16[2,8,16,128]{3,2,1,0:T(8,128)(2,1)S(1)}, bf16[2,8,16,128]{3,2,1,0:T(8,128)(2,1)S(1)}, u32[]{:S(2)}, u32[]{:S(2)}) collective-permute-start(bf16[2,8,16,128]{3,2,1,0:T(8,128)(2,1)S(1)} %bitcast.26), channel_id=1, source_target_pairs={{0,0},{1,5},{4,4},{5,9},{8,8},{9,13},{12,12},{13,17},{16,16},{17,2... | collective-permute-start | bytes 196616 | tf_op jit(solution)/shard_map/out_weight_over_z/ppermute | solution.py:252
  16.9 0.7 copy-start.8
  16.9 0.7 copy-start.7
  33.2 20.2 %collective-permute-start.1 = (bf16[16,256,128]{2,1,0:T(8,128)(2,1)}, bf16[16,256,128]{2,1,0:T(8,128)(2,1)}, u32[]{:S(2)}, u32[]{:S(2)}) collective-permute-start(bf16[16,256,128]{2,1,0:T(8,128)(2,1)} %all-to-all-done.refs_0_), channel_id=1, source_target_pairs={{0,4},{1,61},{4,0},{5,9},{8,12},{9,5},{12,8},{13,17},{16,20},{17,1... | collective-permute-start | bytes 3145736 | tf_op jit(solution)/shard_map/kv_weight_over_z/ppermute | solution.py:264
  41.9 19.4 %all-to-all-start.1 = ((bf16[16,2,8,16,128]{4,3,2,1,0:T(8,128)(2,1)}), bf16[16,2,8,16,128]{4,3,2,1,0:T(8,128)(2,1)S(1)}, u32[]{:S(2)}, u32[]{:S(2)}) async-start(bf16[16,2,8,16,128]{4,3,2,1,0:T(8,128)(2,1)} %broadcast_in_dim.5), calls=%async_computation.1 | async-start | bytes 2097152 | tf_op jit(solution)/shard_map/out_weight_over_plane/all_to_all | solution.py:223
  46.9 13.1 %collective-permute-start.2 = (bf16[8,256,128]{2,1,0:T(8,128)(2,1)S(1)}, bf16[8,256,128]{2,1,0:T(8,128)(2,1)S(1)}, u32[]{:S(2)}, u32[]{:S(2)}) collective-permute-start(bf16[8,256,128]{2,1,0:T(8,128)(2,1)S(1)} %get-tuple-element.32), channel_id=1, source_target_pairs={{0,1},{1,0},{2,3},{3,2},{4,5},{5,4},{6,7},{7,6},{8,9},{9,8},{10,11... | collective-permute-start | bytes 1572872 | tf_op jit(solution)/shard_map/swap_weights/ppermute | solution.py:267
  48.8 17.6 %copy-start.4 = (bf16[256,1024]{1,0:T(8,128)(2,1)S(1)}, bf16[256,1024]{1,0:T(8,128)(2,1)}, u32[]{:S(2)}) copy-start(bf16[256,1024]{1,0:T(8,128)(2,1)} %resid_ref.1) | copy-start | bytes 1572868
  48.8 11.2 %collective-permute-start.3 = (bf16[8,256,128]{2,1,0:T(8,128)(2,1)S(1)}, bf16[8,256,128]{2,1,0:T(8,128)(2,1)S(1)}, u32[]{:S(2)}, u32[]{:S(2)}) collective-permute-start(bf16[8,256,128]{2,1,0:T(8,128)(2,1)S(1)} %get-tuple-element.31), channel_id=1, source_target_pairs={{0,1},{1,0},{2,3},{3,2},{4,5},{5,4},{6,7},{7,6},{8,9},{9,8},{10,11... | collective-permute-start | bytes 1572872 | tf_op jit(solution)/shard_map/swap_weights/ppermute | solution.py:267
  55.7 5.6 %collective-permute-start.4 = (bf16[8,256,128]{2,1,0:T(8,128)(2,1)}, bf16[8,256,128]{2,1,0:T(8,128)(2,1)}, u32[]{:S(2)}, u32[]{:S(2)}) collective-permute-start(bf16[8,256,128]{2,1,0:T(8,128)(2,1)} %get-tuple-element.30), channel_id=1, source_target_pairs={{0,1},{1,0},{2,3},{3,2},{4,5},{5,4},{6,7},{7,6},{8,9},{9,8},{10,11... | collective-permute-start | bytes 1572872 | tf_op jit(solution)/shard_map/swap_weights/ppermute | solution.py:267
  57.6 4.3 %collective-permute-start.5 = (bf16[8,256,128]{2,1,0:T(8,128)(2,1)}, bf16[8,256,128]{2,1,0:T(8,128)(2,1)}, u32[]{:S(2)}, u32[]{:S(2)}) collective-permute-start(bf16[8,256,128]{2,1,0:T(8,128)(2,1)} %get-tuple-element.29), channel_id=1, source_target_pairs={{0,1},{1,0},{2,3},{3,2},{4,5},{5,4},{6,7},{7,6},{8,9},{9,8},{10,11... | collective-permute-start | bytes 1572872 | tf_op jit(solution)/shard_map/swap_weights/ppermute | solution.py:267
  60.0 0.8 copy-start.5
  61.9 4.5 %collective-permute-start.6 = (bf16[16,2,8,16,128]{4,3,2,1,0:T(8,128)(2,1)S(1)}, bf16[16,2,8,16,128]{4,3,2,1,0:T(8,128)(2,1)S(1)}, u32[]{:S(2)}, u32[]{:S(2)}) collective-permute-start(bf16[16,2,8,16,128]{4,3,2,1,0:T(8,128)(2,1)S(1)} %all-to-all-done.1.mine_ref), channel_id=1, source_target_pairs={{0,1},{1,0},{2,3},{3,2},{4,5},{5,4},{6,7},{7,6},{8,9},{9,8},{10,11... | collective-permute-start | bytes 3145736 | tf_op jit(solution)/shard_map/swap_weights/ppermute | solution.py:269
  64.2 2.3 %copy-start.9 = (f32[1024]{0:T(1024)S(1)}, f32[1024]{0:T(1024)}, u32[]{:S(2)}) copy-start(f32[1024]{0:T(1024)} %param.15) | copy-start | bytes 12292
  66.4 1.0 copy-start.6
  71.8 4.7 %copy-start.10 = (bf16[64,1,1024]{2,0,1:T(8,128)(2,1)S(1)}, bf16[64,1,1024]{2,0,1:T(8,128)(2,1)}, u32[]{:S(2)}) copy-start(bf16[64,1,1024]{2,0,1:T(8,128)(2,1)} %param.17) | copy-start | bytes 393220
  71.8 22.0 %all-to-all-start.2 = ((bf16[8,512,128]{2,1,0:T(8,128)(2,1)}), bf16[8,512,128]{2,1,0:T(8,128)(2,1)S(1)}, u32[]{:S(2)}, u32[]{:S(2)}) async-start(bf16[8,512,128]{2,1,0:T(8,128)(2,1)} %encode_keyval.1), calls=%async_computation.2 | async-start | bytes 2097152 | tf_op jit(solution)/shard_map/exchange_keyval/all_to_all | solution.py:273

commit v9 on v8

--- a/solution.py
+++ b/solution.py
@@ -140,7 +140,7 @@
                         pltpu.VMEM(shape.shape, shape.dtype)]
         + [pltpu.VMEM(kvs[0].shape, kvs[0].dtype)] * 4
         + [pltpu.SemaphoreType.DMA((8,)), pltpu.SemaphoreType.DMA((KV_HEADS,))],
-        compiler_params=params(47),
+        compiler_params=params(48),
         cost_estimate=pl.CostEstimate(
             flops=6 * SEG_LEN * D_ENC * D_ENC, bytes_accessed=8 * D_ENC * D_ENC, transcendentals=SEG_LEN),
         name="encode_keyval",
@@ -252,7 +252,7 @@
         pair = lax.ppermute(pair, ("yh", "x", "z", "c"), hops)
     slot = (ha * sa_count + sa).reshape(1).astype(jnp.int32)
     context = encoder_attention(slot, span_ids, seg_lengths, enc_query, enc_key, enc_value)
-    kv_mine, pair, context = lax.optimization_barrier((kv_mine, pair, context))
+    kv_mine, pair = lax.optimization_barrier((kv_mine, pair))
     with jax.named_scope("out_weight_over_plane"):
         w_mine = spread(pair, PLANE)
     with jax.named_scope("kv_weight_over_z"):

time: 131 us -> 133 us (1.015)
    ppermute x1, waiting for transfers between devices: 4.51 us -> 8.34 us  [local(): pair = lax.ppermute(pair, ('yh', 'x', 'z', 'c'), hops)]
    ppermute x1, waiting for transfers between devices: 2.17 us -> 0.01 us  [local(): w_other = swap(w_mine)]
    unnamed x26 -> x30, local copies, waits for them, and re-layouts: 3.36 us -> 3.7 us
  transfers between devices with their start and end apart: 10 -> 10, of which waited for: 7 -> 5; matrix products, arithmetic and copies ran while one was open for 4% -> 4% of each run, Pallas kernels for 2% -> 2%
where the time goes in v9:
time: 133 us; the launch traced here: 132 us
  blocking collectives  40.1 us (30%)
  waiting for transfers between devices  35.9 us (27%)
  starting transfers between devices  33.1 us (25%)
  Pallas kernels  13.2 us (10%)
  local copies, waits for them, and re-layouts  9.69 us (7%)
    all_to_all x1, blocking collectives, local(): parts = lax.all_to_all(parts, SA, 0, 0, tiled=True)  31.7 us
    all_to_all x1, waiting for transfers between devices, local(): keyval = lax.all_to_all(keyval, HA, 0, 0, tiled=True)  17.2 us
    ppermute x4, starting transfers between devices, local(): kvs = kvs + [swap(part) for kv in kvs for part in (kv[:8], kv[8:])]  8.78 us
    all_gather x1, blocking collectives, local(): lax.all_gather(out_weight.reshape(16, 8, HEAD).transpose(1, 0, 2), 'c')  8.37 us
    ppermute x1, waiting for transfers between devices, local(): pair = lax.ppermute(pair, ('yh', 'x', 'z', 'c'), hops)  8.34 us
    all_to_all x2, waiting for transfers between devices, spread(): return lax.all_to_all(copies, axes, 0, 0, tiled=True)  8.03 us
    all_to_all x2, starting transfers between devices, spread(): return lax.all_to_all(copies, axes, 0, 0, tiled=True)  7.98 us
    ppermute x1, starting transfers between devices, local(): kv_next = lax.ppermute(kv_mine, ('z', 'c'), pairs)  7.49 us
  transfers between devices with their start and end apart: 10, of which 5 were waited for; matrix products, arithmetic and copies ran while one was open for 4% of the time, Pallas kernels for 2%

profile of v9, /device:TPU:1, one launch (start us, length us, event | category | flops | bytes accessed | tf_op | source)
XLA Modules:
  0.0 132.4 jit_solution(15590933392904264588)
XLA Ops:
  0.8 8.4 %all-gather = bf16[16,16,128]{2,0,1:T(8,128)(2,1)S(1)} all-gather(bf16[8,16,128]{2,0,1:T(8,128)(2,1)S(1)} %bitcast.24), channel_id=2, replica_groups=mesh['yh'=2,'x'=4,'z'=16,'yl'=2,'c'=2] {'c'}, dimensions={0}, use_global_device_ids=true | all-gather | bytes 98304 | tf_op jit(solution)/shard_map/pair_out_weight/all_gather | solution.py:239
  9.3 1.2 broadcast_in_dim.4
  10.4 4.3 %all-to-all-start = ((bf16[16,256,128]{2,1,0:T(8,128)(2,1)}), bf16[16,256,128]{2,1,0:T(8,128)(2,1)}, u32[]{:S(2)}, u32[]{:S(2)}) async-start(bf16[16,256,128]{2,1,0:T(8,128)(2,1)} %broadcast_in_dim.4), calls=%async_computation | async-start | bytes 2097152 | tf_op jit(solution)/shard_map/gather_kv_weight/all_to_all | solution.py:223
  14.8 1.9 %collective-permute-start = (bf16[2,8,16,128]{3,2,1,0:T(8,128)(2,1)S(1)}, bf16[2,8,16,128]{3,2,1,0:T(8,128)(2,1)S(1)}, u32[]{:S(2)}, u32[]{:S(2)}) collective-permute-start(bf16[2,8,16,128]{3,2,1,0:T(8,128)(2,1)S(1)} %bitcast.26), channel_id=1, source_target_pairs={{0,0},{1,5},{4,4},{5,9},{8,8},{9,13},{12,12},{13,17},{16,16},{17,2... | collective-permute-start | bytes 196616 | tf_op jit(solution)/shard_map/out_weight_over_z/ppermute | solution.py:252
  16.7 8.3 %collective-permute-done = bf16[2,8,16,128]{3,2,1,0:T(8,128)(2,1)S(1)} collective-permute-done((bf16[2,8,16,128]{3,2,1,0:T(8,128)(2,1)S(1)}, bf16[2,8,16,128]{3,2,1,0:T(8,128)(2,1)S(1)}, u32[]{:S(2)}, u32[]{:S(2)}) %collective-permute-start) | collective-permute-done | bytes 65568 | tf_op jit(solution)/shard_map/out_weight_over_z/ppermute | solution.py:252
  25.1 8.0 %all-to-all-done.refs_0_ = bf16[16,256,128]{2,1,0:T(8,128)(2,1)} async-done(((bf16[16,256,128]{2,1,0:T(8,128)(2,1)}), bf16[16,256,128]{2,1,0:T(8,128)(2,1)}, u32[]{:S(2)}, u32[]{:S(2)}) %all-to-all-start) | async-done | bytes 1048608 | tf_op jit(solution)/shard_map/gather_kv_weight/all_to_all | solution.py:223
  33.1 7.5 %collective-permute-start.1 = (bf16[16,256,128]{2,1,0:T(8,128)(2,1)}, bf16[16,256,128]{2,1,0:T(8,128)(2,1)}, u32[]{:S(2)}, u32[]{:S(2)}) collective-permute-start(bf16[16,256,128]{2,1,0:T(8,128)(2,1)} %all-to-all-done.refs_0_), channel_id=1, source_target_pairs={{0,4},{1,61},{4,0},{5,9},{8,12},{9,5},{12,8},{13,17},{16,20},{17,1... | collective-permute-start | bytes 3145736 | tf_op jit(solution)/shard_map/kv_weight_over_z/ppermute | solution.py:264
  40.6 1.2 broadcast_in_dim.5
  41.8 3.7 %all-to-all-start.1 = ((bf16[16,2,8,16,128]{4,3,2,1,0:T(8,128)(2,1)}), bf16[16,2,8,16,128]{4,3,2,1,0:T(8,128)(2,1)S(1)}, u32[]{:S(2)}, u32[]{:S(2)}) async-start(bf16[16,2,8,16,128]{4,3,2,1,0:T(8,128)(2,1)} %broadcast_in_dim.5), calls=%async_computation.1 | async-start | bytes 2097152 | tf_op jit(solution)/shard_map/out_weight_over_plane/all_to_all | solution.py:223
  45.5 1.3 fusion.1
  46.7 1.9 %collective-permute-start.2 = (bf16[8,256,128]{2,1,0:T(8,128)(2,1)S(1)}, bf16[8,256,128]{2,1,0:T(8,128)(2,1)S(1)}, u32[]{:S(2)}, u32[]{:S(2)}) collective-permute-start(bf16[8,256,128]{2,1,0:T(8,128)(2,1)S(1)} %get-tuple-element.30), channel_id=1, source_target_pairs={{0,1},{1,0},{2,3},{3,2},{4,5},{5,4},{6,7},{7,6},{8,9},{9,8},{10,11... | collective-permute-start | bytes 1572872 | tf_op jit(solution)/shard_map/swap_weights/ppermute | solution.py:267
  48.7 2.5 %collective-permute-start.3 = (bf16[8,256,128]{2,1,0:T(8,128)(2,1)S(1)}, bf16[8,256,128]{2,1,0:T(8,128)(2,1)S(1)}, u32[]{:S(2)}, u32[]{:S(2)}) collective-permute-start(bf16[8,256,128]{2,1,0:T(8,128)(2,1)S(1)} %get-tuple-element.29), channel_id=1, source_target_pairs={{0,1},{1,0},{2,3},{3,2},{4,5},{5,4},{6,7},{7,6},{8,9},{9,8},{10,11... | collective-permute-start | bytes 1572872 | tf_op jit(solution)/shard_map/swap_weights/ppermute | solution.py:267
  51.3 2.0 %collective-permute-done.1.refs_1_ = bf16[16,256,128]{2,1,0:T(8,128)(2,1)} collective-permute-done((bf16[16,256,128]{2,1,0:T(8,128)(2,1)}, bf16[16,256,128]{2,1,0:T(8,128)(2,1)}, u32[]{:S(2)}, u32[]{:S(2)}) %collective-permute-start.1) | collective-permute-done | bytes 1048608 | tf_op jit(solution)/shard_map/kv_weight_over_z/ppermute | solution.py:264
  53.3 2.3 %fusion = (bf16[8,256,128]{2,1,0:T(8,128)(2,1)}, bf16[8,256,128]{2,1,0:T(8,128)(2,1)}) fusion(bf16[16,256,128]{2,1,0:T(8,128)(2,1)} %collective-permute-done.1.refs_1_), kind=kLoop, calls=%fused_computation.4 | loop fusion | bytes 2097152 | tf_op jit(solution)/shard_map/swap_weights/slice | solution.py:267
  55.5 1.9 %collective-permute-start.4 = (bf16[8,256,128]{2,1,0:T(8,128)(2,1)}, bf16[8,256,128]{2,1,0:T(8,128)(2,1)}, u32[]{:S(2)}, u32[]{:S(2)}) collective-permute-start(bf16[8,256,128]{2,1,0:T(8,128)(2,1)} %get-tuple-element.28), channel_id=1, source_target_pairs={{0,1},{1,0},{2,3},{3,2},{4,5},{5,4},{6,7},{7,6},{8,9},{9,8},{10,11... | collective-permute-start | bytes 1572872 | tf_op jit(solution)/shard_map/swap_weights/ppermute | solution.py:267
  57.5 2.4 %collective-permute-start.5 = (bf16[8,256,128]{2,1,0:T(8,128)(2,1)}, bf16[8,256,128]{2,1,0:T(8,128)(2,1)}, u32[]{:S(2)}, u32[]{:S(2)}) collective-permute-start(bf16[8,256,128]{2,1,0:T(8,128)(2,1)} %get-tuple-element.27), channel_id=1, source_target_pairs={{0,1},{1,0},{2,3},{3,2},{4,5},{5,4},{6,7},{7,6},{8,9},{9,8},{10,11... | collective-permute-start | bytes 1572872 | tf_op jit(solution)/shard_map/swap_weights/ppermute | solution.py:267
  61.7 2.3 %collective-permute-start.6 = (bf16[16,2,8,16,128]{4,3,2,1,0:T(8,128)(2,1)S(1)}, bf16[16,2,8,16,128]{4,3,2,1,0:T(8,128)(2,1)}, u32[]{:S(2)}, u32[]{:S(2)}) collective-permute-start(bf16[16,2,8,16,128]{4,3,2,1,0:T(8,128)(2,1)S(1)} %all-to-all-done.1.mine_ref), channel_id=1, source_target_pairs={{0,1},{1,0},{2,3},{3,2},{4,5},{5,4},{6,7},{7,6},{8,9},{9,8},{10,11... | collective-permute-start | bytes 3145736 | tf_op jit(solution)/shard_map/swap_weights/ppermute | solution.py:269
  64.7 3.1 %encoder_attention.1.ctx_ref = bf16[256,1024]{1,0:T(8,128)(2,1)S(1)} custom-call(s32[1]{0:T(128)} %bitcast.7.slot_ref, s32[512]{0:T(512)S(1)} %copy-done.9, s32[512]{0:T(512)S(1)} %copy-done.10, bf16[256,1024]{1,0:T(8,128)(2,1)S(1)} %copy-done.1, bf16[256,1024]{1,0:T(8,128)(2,1)S(1)} %copy-done.2, bf16[256,1024]{1,0:T(8,128)(2,1)S(1)} %copy-done.3), custom_call_target="tpu_custom_call" | custom-call | flops 536870912 | bytes 2097152 | tf_op jit(solution)/shard_map/encoder_attention/pallas_call | solution.py:62
  68.5 5.0 %encode_keyval.1 = bf16[8,512,128]{2,1,0:T(8,128)(2,1)} custom-call(s32[3]{0:T(128)S(1)} %pad_add_fusion.1.place_ref, f32[1,1024]{1,0:T(1,128)S(1)} %bitcast.22, bf16[256,1024]{1,0:T(8,128)(2,1)S(1)} %encoder_attention.1.ctx_ref, bf16[256,1024]{1,0:T(8,128)(2,1)S(1)} %copy-done.4, bf16[16,2,8,16,128]{4,3,2,1,0:T(8,128)(2,1)S(1)} %all-to-all-done.1.mine_ref, ...), custom_call_target="tpu_custom_call" | custom-call | flops 1610612736 | bytes 8388608 | tf_op jit(solution)/shard_map/encode_keyval/pallas_call | solution.py:133
  73.5 4.7 %all-to-all-start.2 = ((bf16[8,512,128]{2,1,0:T(8,128)(2,1)}), bf16[8,512,128]{2,1,0:T(8,128)(2,1)S(1)}, u32[]{:S(2)}, u32[]{:S(2)}) async-start(bf16[8,512,128]{2,1,0:T(8,128)(2,1)} %encode_keyval.1), calls=%async_computation.2 | async-start | bytes 2097152 | tf_op jit(solution)/shard_map/exchange_keyval/all_to_all | solution.py:273
  78.3 17.2 %all-to-all-done.2.kv_ref = bf16[8,512,128]{2,1,0:T(8,128)(2,1)S(1)} async-done(((bf16[8,512,128]{2,1,0:T(8,128)(2,1)}), bf16[8,512,128]{2,1,0:T(8,128)(2,1)S(1)}, u32[]{:S(2)}, u32[]{:S(2)}) %all-to-all-start.2) | async-done | bytes 1048608 | tf_op jit(solution)/shard_map/exchange_keyval/all_to_all | solution.py:273
  95.6 3.1 %cross_attention.1 = bf16[64,2,640]{2,1,0:T(2,128)(2,1)S(1)} custom-call(s32[2]{0:T(128)S(1)} %pad_add_fusion.first_ref, s32[512]{0:T(512)S(1)} %copy-done.9, s32[512]{0:T(512)S(1)} %copy-done.10, bf16[512,128]{1,0:T(8,128)(2,1)S(1)} %bitcast.21, bf16[8,512,128]{2,1,0:T(8,128)(2,1)S(1)} %all-to-all-done.2.kv_ref), custom_call_target="tpu_custom_call" | custom-call | tf_op jit(solution)/shard_map/cross_attention/pallas_call | solution.py:188
  98.7 31.7 %all_to_all.20.part_ref = bf16[64,2,640]{2,1,0:T(2,128)(2,1)} all-to-all(bf16[64,2,640]{2,1,0:T(2,128)(2,1)S(1)} %cross_attention.1), channel_id=1, replica_groups=mesh['yh'=2,'x'=4,'z'=16,'yl'=2,'c'=2] {'z','yl','c'}, dimensions={0} | all-to-all | bytes 327680 | tf_op jit(solution)/shard_map/exchange_partials/all_to_all | solution.py:278
  130.4 2.0 %merge_partials.1 = f32[8,128]{1,0:T(8,128)} custom-call(bf16[64,2,640]{2,1,0:T(2,128)(2,1)} %all_to_all.20.part_ref), custom_call_target="tpu_custom_call" | custom-call | tf_op jit(solution)/shard_map/merge_partials/pallas_call | solution.py:211
  (43 shorter events, 4.2 us)
Async XLA Ops:
  0.0 9.2 %copy-start = (bf16[1024,1,256]{2,0,1:T(8,128)(2,1)S(1)}, bf16[1024,1,256]{2,0,1:T(8,128)(2,1)}, u32[]{:S(2)}) copy-start(bf16[1024,1,256]{2,0,1:T(8,128)(2,1)} %param.16) | copy-start | bytes 1572868
  0.0 0.8 copy-start.13
  10.4 22.6 %all-to-all-start = ((bf16[16,256,128]{2,1,0:T(8,128)(2,1)}), bf16[16,256,128]{2,1,0:T(8,128)(2,1)}, u32[]{:S(2)}, u32[]{:S(2)}) async-start(bf16[16,256,128]{2,1,0:T(8,128)(2,1)} %broadcast_in_dim.4), calls=%async_computation | async-start | bytes 2097152 | tf_op jit(solution)/shard_map/gather_kv_weight/all_to_all | solution.py:223
  14.8 10.3 %collective-permute-start = (bf16[2,8,16,128]{3,2,1,0:T(8,128)(2,1)S(1)}, bf16[2,8,16,128]{3,2,1,0:T(8,128)(2,1)S(1)}, u32[]{:S(2)}, u32[]{:S(2)}) collective-permute-start(bf16[2,8,16,128]{3,2,1,0:T(8,128)(2,1)S(1)} %bitcast.26), channel_id=1, source_target_pairs={{0,0},{1,5},{4,4},{5,9},{8,8},{9,13},{12,12},{13,17},{16,16},{17,2... | collective-permute-start | bytes 196616 | tf_op jit(solution)/shard_map/out_weight_over_z/ppermute | solution.py:252
  33.1 20.2 %collective-permute-start.1 = (bf16[16,256,128]{2,1,0:T(8,128)(2,1)}, bf16[16,256,128]{2,1,0:T(8,128)(2,1)}, u32[]{:S(2)}, u32[]{:S(2)}) collective-permute-start(bf16[16,256,128]{2,1,0:T(8,128)(2,1)} %all-to-all-done.refs_0_), channel_id=1, source_target_pairs={{0,4},{1,61},{4,0},{5,9},{8,12},{9,5},{12,8},{13,17},{16,20},{17,1... | collective-permute-start | bytes 3145736 | tf_op jit(solution)/shard_map/kv_weight_over_z/ppermute | solution.py:264
  41.8 19.7 %all-to-all-start.1 = ((bf16[16,2,8,16,128]{4,3,2,1,0:T(8,128)(2,1)}), bf16[16,2,8,16,128]{4,3,2,1,0:T(8,128)(2,1)S(1)}, u32[]{:S(2)}, u32[]{:S(2)}) async-start(bf16[16,2,8,16,128]{4,3,2,1,0:T(8,128)(2,1)} %broadcast_in_dim.5), calls=%async_computation.1 | async-start | bytes 2097152 | tf_op jit(solution)/shard_map/out_weight_over_plane/all_to_all | solution.py:223
  46.7 13.1 %collective-permute-start.2 = (bf16[8,256,128]{2,1,0:T(8,128)(2,1)S(1)}, bf16[8,256,128]{2,1,0:T(8,128)(2,1)S(1)}, u32[]{:S(2)}, u32[]{:S(2)}) collective-permute-start(bf16[8,256,128]{2,1,0:T(8,128)(2,1)S(1)} %get-tuple-element.30), channel_id=1, source_target_pairs={{0,1},{1,0},{2,3},{3,2},{4,5},{5,4},{6,7},{7,6},{8,9},{9,8},{10,11... | collective-permute-start | bytes 1572872 | tf_op jit(solution)/shard_map/swap_weights/ppermute | solution.py:267
  48.7 15.4 %copy-start.1 = (bf16[256,1024]{1,0:T(8,128)(2,1)S(1)}, bf16[256,1024]{1,0:T(8,128)(2,1)}, u32[]{:S(2)}) copy-start(bf16[256,1024]{1,0:T(8,128)(2,1)} %q_ref.1) | copy-start | bytes 1572868
  48.7 15.4 %copy-start.2 = (bf16[256,1024]{1,0:T(8,128)(2,1)S(1)}, bf16[256,1024]{1,0:T(8,128)(2,1)}, u32[]{:S(2)}) copy-start(bf16[256,1024]{1,0:T(8,128)(2,1)} %k_ref.1) | copy-start | bytes 1572868
  48.7 15.4 %copy-start.3 = (bf16[256,1024]{1,0:T(8,128)(2,1)S(1)}, bf16[256,1024]{1,0:T(8,128)(2,1)}, u32[]{:S(2)}) copy-start(bf16[256,1024]{1,0:T(8,128)(2,1)} %v_ref.1) | copy-start | bytes 1572868
  48.7 12.0 %collective-permute-start.3 = (bf16[8,256,128]{2,1,0:T(8,128)(2,1)S(1)}, bf16[8,256,128]{2,1,0:T(8,128)(2,1)S(1)}, u32[]{:S(2)}, u32[]{:S(2)}) collective-permute-start(bf16[8,256,128]{2,1,0:T(8,128)(2,1)S(1)} %get-tuple-element.29), channel_id=1, source_target_pairs={{0,1},{1,0},{2,3},{3,2},{4,5},{5,4},{6,7},{7,6},{8,9},{9,8},{10,11... | collective-permute-start | bytes 1572872 | tf_op jit(solution)/shard_map/swap_weights/ppermute | solution.py:267
  55.5 5.9 %collective-permute-start.4 = (bf16[8,256,128]{2,1,0:T(8,128)(2,1)}, bf16[8,256,128]{2,1,0:T(8,128)(2,1)}, u32[]{:S(2)}, u32[]{:S(2)}) collective-permute-start(bf16[8,256,128]{2,1,0:T(8,128)(2,1)} %get-tuple-element.28), channel_id=1, source_target_pairs={{0,1},{1,0},{2,3},{3,2},{4,5},{5,4},{6,7},{7,6},{8,9},{9,8},{10,11... | collective-permute-start | bytes 1572872 | tf_op jit(solution)/shard_map/swap_weights/ppermute | solution.py:267
  57.5 4.3 %collective-permute-start.5 = (bf16[8,256,128]{2,1,0:T(8,128)(2,1)}, bf16[8,256,128]{2,1,0:T(8,128)(2,1)}, u32[]{:S(2)}, u32[]{:S(2)}) collective-permute-start(bf16[8,256,128]{2,1,0:T(8,128)(2,1)} %get-tuple-element.27), channel_id=1, source_target_pairs={{0,1},{1,0},{2,3},{3,2},{4,5},{5,4},{6,7},{7,6},{8,9},{9,8},{10,11... | collective-permute-start | bytes 1572872 | tf_op jit(solution)/shard_map/swap_weights/ppermute | solution.py:267
  59.9 0.8 copy-start.5
  60.7 0.8 copy-start.7
  61.7 6.2 %collective-permute-start.6 = (bf16[16,2,8,16,128]{4,3,2,1,0:T(8,128)(2,1)S(1)}, bf16[16,2,8,16,128]{4,3,2,1,0:T(8,128)(2,1)}, u32[]{:S(2)}, u32[]{:S(2)}) collective-permute-start(bf16[16,2,8,16,128]{4,3,2,1,0:T(8,128)(2,1)S(1)} %all-to-all-done.1.mine_ref), channel_id=1, source_target_pairs={{0,1},{1,0},{2,3},{3,2},{4,5},{5,4},{6,7},{7,6},{8,9},{9,8},{10,11... | collective-permute-start | bytes 3145736 | tf_op jit(solution)/shard_map/swap_weights/ppermute | solution.py:269
  64.0 0.7 copy-start.10
  64.0 0.7 copy-start.9
  64.7 3.2 %copy-start.4 = (bf16[256,1024]{1,0:T(8,128)(2,1)S(1)}, bf16[256,1024]{1,0:T(8,128)(2,1)}, u32[]{:S(2)}) copy-start(bf16[256,1024]{1,0:T(8,128)(2,1)} %resid_ref.1) | copy-start | bytes 1572868
  64.7 3.2 %copy-start.6 = (bf16[8,256,128]{2,1,0:T(8,128)(2,1)S(1)}, bf16[8,256,128]{2,1,0:T(8,128)(2,1)}, u32[]{:S(2)}) copy-start(bf16[8,256,128]{2,1,0:T(8,128)(2,1)} %copy-done.5) | copy-start | bytes 1572868
  64.7 3.2 %copy-start.8 = (bf16[8,256,128]{2,1,0:T(8,128)(2,1)S(1)}, bf16[8,256,128]{2,1,0:T(8,128)(2,1)}, u32[]{:S(2)}) copy-start(bf16[8,256,128]{2,1,0:T(8,128)(2,1)} %copy-done.7) | copy-start | bytes 1572868
  67.8 0.7 copy-start.11
  73.5 4.7 %copy-start.12 = (bf16[64,1,1024]{2,0,1:T(8,128)(2,1)S(1)}, bf16[64,1,1024]{2,0,1:T(8,128)(2,1)}, u32[]{:S(2)}) copy-start(bf16[64,1,1024]{2,0,1:T(8,128)(2,1)} %param.17) | copy-start | bytes 393220
  73.5 22.0 %all-to-all-start.2 = ((bf16[8,512,128]{2,1,0:T(8,128)(2,1)}), bf16[8,512,128]{2,1,0:T(8,128)(2,1)S(1)}, u32[]{:S(2)}, u32[]{:S(2)}) async-start(bf16[8,512,128]{2,1,0:T(8,128)(2,1)} %encode_keyval.1), calls=%async_computation.2 | async-start | bytes 2097152 | tf_op jit(solution)/shard_map/exchange_keyval/all_to_all | solution.py:273

commit v10 on v8

--- a/solution.py
+++ b/solution.py
@@ -89,7 +89,7 @@
 
     for part_ref, at in ((mine_ref, core), (other_ref, 1 - core)):
         for ha in range(KV_HEADS):
-            plane = lax.rem(z + 32 - 2 * ha - at, 16)
+            plane = lax.rem(z + 32 - ha - 8 * at, 16)
             for yl in range(2):
                 for c in range(2):
                     row = pl.multiple_of(64 * plane + 32 * yl + 16 * c, 16)
@@ -247,7 +247,7 @@
         for ha_at in range(8):
             for z_at in range(16):
                 for c_at in range(2):
-                    there = (z_at + 2 * ha_at + c_at) % 16
+                    there = (z_at + ha_at + 8 * c_at) % 16
                     hops.append(((ha_at * 16 + z_at) * 2 + c_at, (ha_at * 16 + there) * 2 + c_at))
         pair = lax.ppermute(pair, ("yh", "x", "z", "c"), hops)
     slot = (ha * sa_count + sa).reshape(1).astype(jnp.int32)

time: 131 us -> 129 us (0.985)
  waiting for transfers between devices: 35 us -> 24.4 us
  starting transfers between devices: 33.2 us -> 43.8 us
  blocking collectives: 40.1 us -> 37.8 us
    ppermute x1, starting transfers between devices: 1.92 us -> 12.5 us  [local(): pair = lax.ppermute(pair, ('yh', 'x', 'z', 'c'), hops)]
    all_to_all x2, waiting for transfers between devices: 8.49 us -> 2.33 us  [spread(): return lax.all_to_all(copies, axes, 0, 0, tiled=True)]
    ppermute x1, waiting for transfers between devices: 4.51 us -> 0.01 us  [local(): pair = lax.ppermute(pair, ('yh', 'x', 'z', 'c'), hops)]
    all_to_all x1, blocking collectives: 31.7 us -> 29.4 us  [local(): parts = lax.all_to_all(parts, SA, 0, 0, tiled=True)]
  transfers between devices with their start and end apart: 10 -> 10, of which waited for: 7 -> 6; matrix products, arithmetic and copies ran while one was open for 4% -> 4% of each run, Pallas kernels for 2% -> 2%
where the time goes in v10:
time: 129 us; the launch traced here: 128 us
  starting transfers between devices  43.8 us (34%)
  blocking collectives  37.8 us (29%)
  waiting for transfers between devices  24.4 us (19%)
  Pallas kernels  12.6 us (10%)
  local copies, waits for them, and re-layouts  9.38 us (7%)
    all_to_all x1, blocking collectives, local(): parts = lax.all_to_all(parts, SA, 0, 0, tiled=True)  29.4 us
    all_to_all x1, waiting for transfers between devices, local(): keyval = lax.all_to_all(keyval, HA, 0, 0, tiled=True)  17.2 us
    ppermute x1, starting transfers between devices, local(): pair = lax.ppermute(pair, ('yh', 'x', 'z', 'c'), hops)  12.5 us
    ppermute x4, starting transfers between devices, local(): kvs = kvs + [swap(part) for kv in kvs for part in (kv[:8], kv[8:])]  8.78 us
    all_gather x1, blocking collectives, local(): lax.all_gather(out_weight.reshape(16, 8, HEAD).transpose(1, 0, 2), 'c')  8.37 us
    all_to_all x2, starting transfers between devices, spread(): return lax.all_to_all(copies, axes, 0, 0, tiled=True)  8.12 us
    ppermute x1, starting transfers between devices, local(): kv_next = lax.ppermute(kv_mine, ('z', 'c'), pairs)  7.49 us
    all_to_all x1, starting transfers between devices, local(): keyval = lax.all_to_all(keyval, HA, 0, 0, tiled=True)  4.64 us
  transfers between devices with their start and end apart: 10, of which 6 were waited for; matrix products, arithmetic and copies ran while one was open for 4% of the time, Pallas kernels for 2%

profile of v10, /device:TPU:1, one launch (start us, length us, event | category | flops | bytes accessed | tf_op | source)
XLA Modules:
  0.0 128.4 jit_solution(989248160041459792)
XLA Ops:
  0.8 8.4 %all-gather = bf16[16,16,128]{2,0,1:T(8,128)(2,1)S(1)} all-gather(bf16[8,16,128]{2,0,1:T(8,128)(2,1)S(1)} %bitcast.24), channel_id=2, replica_groups=mesh['yh'=2,'x'=4,'z'=16,'yl'=2,'c'=2] {'c'}, dimensions={0}, use_global_device_ids=true | all-gather | bytes 98304 | tf_op jit(solution)/shard_map/pair_out_weight/all_gather | solution.py:239
  9.3 1.2 broadcast_in_dim.4
  10.4 4.5 %all-to-all-start = ((bf16[16,256,128]{2,1,0:T(8,128)(2,1)}), bf16[16,256,128]{2,1,0:T(8,128)(2,1)}, u32[]{:S(2)}, u32[]{:S(2)}) async-start(bf16[16,256,128]{2,1,0:T(8,128)(2,1)} %broadcast_in_dim.4), calls=%async_computation | async-start | bytes 2097152 | tf_op jit(solution)/shard_map/gather_kv_weight/all_to_all | solution.py:223
  14.9 12.5 %collective-permute-start = (bf16[2,8,16,128]{3,2,1,0:T(8,128)(2,1)S(1)}, bf16[2,8,16,128]{3,2,1,0:T(8,128)(2,1)S(1)}, u32[]{:S(2)}, u32[]{:S(2)}) collective-permute-start(bf16[2,8,16,128]{3,2,1,0:T(8,128)(2,1)S(1)} %bitcast.26), channel_id=1, source_target_pairs={{0,0},{1,33},{4,4},{5,37},{8,8},{9,41},{12,12},{13,45},{16,16},{17... | collective-permute-start | bytes 196616 | tf_op jit(solution)/shard_map/out_weight_over_z/ppermute | solution.py:252
  28.2 3.1 %encoder_attention.1.ctx_ref = bf16[256,1024]{1,0:T(8,128)(2,1)S(1)} custom-call(s32[1]{0:T(128)} %bitcast.10.slot_ref, s32[512]{0:T(512)S(1)} %copy-done.7, s32[512]{0:T(512)S(1)} %copy-done.8, bf16[256,1024]{1,0:T(8,128)(2,1)S(1)} %copy-done.1, bf16[256,1024]{1,0:T(8,128)(2,1)S(1)} %copy-done.2, bf16[256,1024]{1,0:T(8,128)(2,1)S(1)} %copy-done.3), custom_call_target="tpu_custom_call" | custom-call | flops 536870912 | bytes 2097152 | tf_op jit(solution)/shard_map/encoder_attention/pallas_call | solution.py:62
  31.3 1.9 %all-to-all-done.refs_0_ = bf16[16,256,128]{2,1,0:T(8,128)(2,1)} async-done(((bf16[16,256,128]{2,1,0:T(8,128)(2,1)}), bf16[16,256,128]{2,1,0:T(8,128)(2,1)}, u32[]{:S(2)}, u32[]{:S(2)}) %all-to-all-start) | async-done | bytes 1048608 | tf_op jit(solution)/shard_map/gather_kv_weight/all_to_all | solution.py:223
  33.2 7.5 %collective-permute-start.1 = (bf16[16,256,128]{2,1,0:T(8,128)(2,1)}, bf16[16,256,128]{2,1,0:T(8,128)(2,1)}, u32[]{:S(2)}, u32[]{:S(2)}) collective-permute-start(bf16[16,256,128]{2,1,0:T(8,128)(2,1)} %all-to-all-done.refs_0_), channel_id=1, source_target_pairs={{0,4},{1,61},{4,0},{5,9},{8,12},{9,5},{12,8},{13,17},{16,20},{17,1... | collective-permute-start | bytes 3145736 | tf_op jit(solution)/shard_map/kv_weight_over_z/ppermute | solution.py:264
  40.7 1.2 broadcast_in_dim.5
  41.9 3.7 %all-to-all-start.1 = ((bf16[16,2,8,16,128]{4,3,2,1,0:T(8,128)(2,1)}), bf16[16,2,8,16,128]{4,3,2,1,0:T(8,128)(2,1)S(1)}, u32[]{:S(2)}, u32[]{:S(2)}) async-start(bf16[16,2,8,16,128]{4,3,2,1,0:T(8,128)(2,1)} %broadcast_in_dim.5), calls=%async_computation.1 | async-start | bytes 2097152 | tf_op jit(solution)/shard_map/out_weight_over_plane/all_to_all | solution.py:223
  45.6 1.3 fusion.1
  46.9 1.9 %collective-permute-start.2 = (bf16[8,256,128]{2,1,0:T(8,128)(2,1)S(1)}, bf16[8,256,128]{2,1,0:T(8,128)(2,1)S(1)}, u32[]{:S(2)}, u32[]{:S(2)}) collective-permute-start(bf16[8,256,128]{2,1,0:T(8,128)(2,1)S(1)} %get-tuple-element.32), channel_id=1, source_target_pairs={{0,1},{1,0},{2,3},{3,2},{4,5},{5,4},{6,7},{7,6},{8,9},{9,8},{10,11... | collective-permute-start | bytes 1572872 | tf_op jit(solution)/shard_map/swap_weights/ppermute | solution.py:267
  48.8 2.5 %collective-permute-start.3 = (bf16[8,256,128]{2,1,0:T(8,128)(2,1)S(1)}, bf16[8,256,128]{2,1,0:T(8,128)(2,1)S(1)}, u32[]{:S(2)}, u32[]{:S(2)}) collective-permute-start(bf16[8,256,128]{2,1,0:T(8,128)(2,1)S(1)} %get-tuple-element.31), channel_id=1, source_target_pairs={{0,1},{1,0},{2,3},{3,2},{4,5},{5,4},{6,7},{7,6},{8,9},{9,8},{10,11... | collective-permute-start | bytes 1572872 | tf_op jit(solution)/shard_map/swap_weights/ppermute | solution.py:267
  51.4 2.0 %collective-permute-done.1.refs_1_ = bf16[16,256,128]{2,1,0:T(8,128)(2,1)} collective-permute-done((bf16[16,256,128]{2,1,0:T(8,128)(2,1)}, bf16[16,256,128]{2,1,0:T(8,128)(2,1)}, u32[]{:S(2)}, u32[]{:S(2)}) %collective-permute-start.1) | collective-permute-done | bytes 1048608 | tf_op jit(solution)/shard_map/kv_weight_over_z/ppermute | solution.py:264
  53.4 2.3 %fusion = (bf16[8,256,128]{2,1,0:T(8,128)(2,1)}, bf16[8,256,128]{2,1,0:T(8,128)(2,1)}) fusion(bf16[16,256,128]{2,1,0:T(8,128)(2,1)} %collective-permute-done.1.refs_1_), kind=kLoop, calls=%fused_computation.4 | loop fusion | bytes 2097152 | tf_op jit(solution)/shard_map/swap_weights/slice | solution.py:267
  55.7 1.9 %collective-permute-start.4 = (bf16[8,256,128]{2,1,0:T(8,128)(2,1)}, bf16[8,256,128]{2,1,0:T(8,128)(2,1)}, u32[]{:S(2)}, u32[]{:S(2)}) collective-permute-start(bf16[8,256,128]{2,1,0:T(8,128)(2,1)} %get-tuple-element.30), channel_id=1, source_target_pairs={{0,1},{1,0},{2,3},{3,2},{4,5},{5,4},{6,7},{7,6},{8,9},{9,8},{10,11... | collective-permute-start | bytes 1572872 | tf_op jit(solution)/shard_map/swap_weights/ppermute | solution.py:267
  57.6 2.4 %collective-permute-start.5 = (bf16[8,256,128]{2,1,0:T(8,128)(2,1)}, bf16[8,256,128]{2,1,0:T(8,128)(2,1)}, u32[]{:S(2)}, u32[]{:S(2)}) collective-permute-start(bf16[8,256,128]{2,1,0:T(8,128)(2,1)} %get-tuple-element.29), channel_id=1, source_target_pairs={{0,1},{1,0},{2,3},{3,2},{4,5},{5,4},{6,7},{7,6},{8,9},{9,8},{10,11... | collective-permute-start | bytes 1572872 | tf_op jit(solution)/shard_map/swap_weights/ppermute | solution.py:267
  61.9 2.3 %collective-permute-start.6 = (bf16[16,2,8,16,128]{4,3,2,1,0:T(8,128)(2,1)S(1)}, bf16[16,2,8,16,128]{4,3,2,1,0:T(8,128)(2,1)S(1)}, u32[]{:S(2)}, u32[]{:S(2)}) collective-permute-start(bf16[16,2,8,16,128]{4,3,2,1,0:T(8,128)(2,1)S(1)} %all-to-all-done.1.mine_ref), channel_id=1, source_target_pairs={{0,1},{1,0},{2,3},{3,2},{4,5},{5,4},{6,7},{7,6},{8,9},{9,8},{10,11... | collective-permute-start | bytes 3145736 | tf_op jit(solution)/shard_map/swap_weights/ppermute | solution.py:269
  64.3 2.2 %collective-permute-done.6.other_ref = bf16[16,2,8,16,128]{4,3,2,1,0:T(8,128)(2,1)S(1)} collective-permute-done((bf16[16,2,8,16,128]{4,3,2,1,0:T(8,128)(2,1)S(1)}, bf16[16,2,8,16,128]{4,3,2,1,0:T(8,128)(2,1)S(1)}, u32[]{:S(2)}, u32[]{:S(2)}) %collective-permute-start.6) | collective-permute-done | bytes 1048608 | tf_op jit(solution)/shard_map/swap_weights/ppermute | solution.py:269
  67.5 4.3 %encode_keyval.1 = bf16[8,512,128]{2,1,0:T(8,128)(2,1)} custom-call(s32[3]{0:T(128)S(1)} %pad_add_fusion.1.place_ref, f32[1,1024]{1,0:T(1,128)S(1)} %bitcast.22, bf16[256,1024]{1,0:T(8,128)(2,1)S(1)} %encoder_attention.1.ctx_ref, bf16[256,1024]{1,0:T(8,128)(2,1)S(1)} %copy-done.4, bf16[16,2,8,16,128]{4,3,2,1,0:T(8,128)(2,1)S(1)} %all-to-all-done.1.mine_ref, ...), custom_call_target="tpu_custom_call" | custom-call | flops 1610612736 | bytes 8388608 | tf_op jit(solution)/shard_map/encode_keyval/pallas_call | solution.py:133
  71.8 4.6 %all-to-all-start.2 = ((bf16[8,512,128]{2,1,0:T(8,128)(2,1)}), bf16[8,512,128]{2,1,0:T(8,128)(2,1)S(1)}, u32[]{:S(2)}, u32[]{:S(2)}) async-start(bf16[8,512,128]{2,1,0:T(8,128)(2,1)} %encode_keyval.1), calls=%async_computation.2 | async-start | bytes 2097152 | tf_op jit(solution)/shard_map/exchange_keyval/all_to_all | solution.py:273
  76.6 17.2 %all-to-all-done.2.kv_ref = bf16[8,512,128]{2,1,0:T(8,128)(2,1)S(1)} async-done(((bf16[8,512,128]{2,1,0:T(8,128)(2,1)}), bf16[8,512,128]{2,1,0:T(8,128)(2,1)S(1)}, u32[]{:S(2)}, u32[]{:S(2)}) %all-to-all-start.2) | async-done | bytes 1048608 | tf_op jit(solution)/shard_map/exchange_keyval/all_to_all | solution.py:273
  93.8 3.2 %cross_attention.1 = bf16[64,2,640]{2,1,0:T(2,128)(2,1)S(1)} custom-call(s32[2]{0:T(128)S(1)} %pad_add_fusion.first_ref, s32[512]{0:T(512)S(1)} %copy-done.7, s32[512]{0:T(512)S(1)} %copy-done.8, bf16[512,128]{1,0:T(8,128)(2,1)S(1)} %bitcast.21, bf16[8,512,128]{2,1,0:T(8,128)(2,1)S(1)} %all-to-all-done.2.kv_ref), custom_call_target="tpu_custom_call" | custom-call | tf_op jit(solution)/shard_map/cross_attention/pallas_call | solution.py:188
  97.0 29.4 %all_to_all.20.part_ref = bf16[64,2,640]{2,1,0:T(2,128)(2,1)} all-to-all(bf16[64,2,640]{2,1,0:T(2,128)(2,1)S(1)} %cross_attention.1), channel_id=1, replica_groups=mesh['yh'=2,'x'=4,'z'=16,'yl'=2,'c'=2] {'z','yl','c'}, dimensions={0} | all-to-all | bytes 327680 | tf_op jit(solution)/shard_map/exchange_partials/all_to_all | solution.py:278
  126.4 2.0 %merge_partials.1 = f32[8,128]{1,0:T(8,128)} custom-call(bf16[64,2,640]{2,1,0:T(2,128)(2,1)} %all_to_all.20.part_ref), custom_call_target="tpu_custom_call" | custom-call | tf_op jit(solution)/shard_map/merge_partials/pallas_call | solution.py:211
  (39 shorter events, 4.6 us)
Async XLA Ops:
  0.0 9.2 %copy-start = (bf16[1024,1,256]{2,0,1:T(8,128)(2,1)S(1)}, bf16[1024,1,256]{2,0,1:T(8,128)(2,1)}, u32[]{:S(2)}) copy-start(bf16[1024,1,256]{2,0,1:T(8,128)(2,1)} %param.16) | copy-start | bytes 1572868
  0.0 0.8 copy-start.11
  10.4 17.1 %copy-start.1 = (bf16[256,1024]{1,0:T(8,128)(2,1)S(1)}, bf16[256,1024]{1,0:T(8,128)(2,1)}, u32[]{:S(2)}) copy-start(bf16[256,1024]{1,0:T(8,128)(2,1)} %q_ref.1) | copy-start | bytes 1572868
  10.4 17.1 %copy-start.2 = (bf16[256,1024]{1,0:T(8,128)(2,1)S(1)}, bf16[256,1024]{1,0:T(8,128)(2,1)}, u32[]{:S(2)}) copy-start(bf16[256,1024]{1,0:T(8,128)(2,1)} %k_ref.1) | copy-start | bytes 1572868
  10.4 17.1 %copy-start.3 = (bf16[256,1024]{1,0:T(8,128)(2,1)S(1)}, bf16[256,1024]{1,0:T(8,128)(2,1)}, u32[]{:S(2)}) copy-start(bf16[256,1024]{1,0:T(8,128)(2,1)} %v_ref.1) | copy-start | bytes 1572868
  10.4 22.8 %all-to-all-start = ((bf16[16,256,128]{2,1,0:T(8,128)(2,1)}), bf16[16,256,128]{2,1,0:T(8,128)(2,1)}, u32[]{:S(2)}, u32[]{:S(2)}) async-start(bf16[16,256,128]{2,1,0:T(8,128)(2,1)} %broadcast_in_dim.4), calls=%async_computation | async-start | bytes 2097152 | tf_op jit(solution)/shard_map/gather_kv_weight/all_to_all | solution.py:223
  14.9 16.4 %collective-permute-start = (bf16[2,8,16,128]{3,2,1,0:T(8,128)(2,1)S(1)}, bf16[2,8,16,128]{3,2,1,0:T(8,128)(2,1)S(1)}, u32[]{:S(2)}, u32[]{:S(2)}) collective-permute-start(bf16[2,8,16,128]{3,2,1,0:T(8,128)(2,1)S(1)} %bitcast.26), channel_id=1, source_target_pairs={{0,0},{1,33},{4,4},{5,37},{8,8},{9,41},{12,12},{13,45},{16,16},{17... | collective-permute-start | bytes 196616 | tf_op jit(solution)/shard_map/out_weight_over_z/ppermute | solution.py:252
  27.5 0.7 copy-start.8
  27.5 0.7 copy-start.7
  33.2 20.2 %collective-permute-start.1 = (bf16[16,256,128]{2,1,0:T(8,128)(2,1)}, bf16[16,256,128]{2,1,0:T(8,128)(2,1)}, u32[]{:S(2)}, u32[]{:S(2)}) collective-permute-start(bf16[16,256,128]{2,1,0:T(8,128)(2,1)} %all-to-all-done.refs_0_), channel_id=1, source_target_pairs={{0,4},{1,61},{4,0},{5,9},{8,12},{9,5},{12,8},{13,17},{16,20},{17,1... | collective-permute-start | bytes 3145736 | tf_op jit(solution)/shard_map/kv_weight_over_z/ppermute | solution.py:264
  41.9 19.3 %all-to-all-start.1 = ((bf16[16,2,8,16,128]{4,3,2,1,0:T(8,128)(2,1)}), bf16[16,2,8,16,128]{4,3,2,1,0:T(8,128)(2,1)S(1)}, u32[]{:S(2)}, u32[]{:S(2)}) async-start(bf16[16,2,8,16,128]{4,3,2,1,0:T(8,128)(2,1)} %broadcast_in_dim.5), calls=%async_computation.1 | async-start | bytes 2097152 | tf_op jit(solution)/shard_map/out_weight_over_plane/all_to_all | solution.py:223
  46.9 13.1 %collective-permute-start.2 = (bf16[8,256,128]{2,1,0:T(8,128)(2,1)S(1)}, bf16[8,256,128]{2,1,0:T(8,128)(2,1)S(1)}, u32[]{:S(2)}, u32[]{:S(2)}) collective-permute-start(bf16[8,256,128]{2,1,0:T(8,128)(2,1)S(1)} %get-tuple-element.32), channel_id=1, source_target_pairs={{0,1},{1,0},{2,3},{3,2},{4,5},{5,4},{6,7},{7,6},{8,9},{9,8},{10,11... | collective-permute-start | bytes 1572872 | tf_op jit(solution)/shard_map/swap_weights/ppermute | solution.py:267
  48.8 17.6 %copy-start.4 = (bf16[256,1024]{1,0:T(8,128)(2,1)S(1)}, bf16[256,1024]{1,0:T(8,128)(2,1)}, u32[]{:S(2)}) copy-start(bf16[256,1024]{1,0:T(8,128)(2,1)} %resid_ref.1) | copy-start | bytes 1572868
  48.8 11.2 %collective-permute-start.3 = (bf16[8,256,128]{2,1,0:T(8,128)(2,1)S(1)}, bf16[8,256,128]{2,1,0:T(8,128)(2,1)S(1)}, u32[]{:S(2)}, u32[]{:S(2)}) collective-permute-start(bf16[8,256,128]{2,1,0:T(8,128)(2,1)S(1)} %get-tuple-element.31), channel_id=1, source_target_pairs={{0,1},{1,0},{2,3},{3,2},{4,5},{5,4},{6,7},{7,6},{8,9},{9,8},{10,11... | collective-permute-start | bytes 1572872 | tf_op jit(solution)/shard_map/swap_weights/ppermute | solution.py:267
  55.7 5.6 %collective-permute-start.4 = (bf16[8,256,128]{2,1,0:T(8,128)(2,1)}, bf16[8,256,128]{2,1,0:T(8,128)(2,1)}, u32[]{:S(2)}, u32[]{:S(2)}) collective-permute-start(bf16[8,256,128]{2,1,0:T(8,128)(2,1)} %get-tuple-element.30), channel_id=1, source_target_pairs={{0,1},{1,0},{2,3},{3,2},{4,5},{5,4},{6,7},{7,6},{8,9},{9,8},{10,11... | collective-permute-start | bytes 1572872 | tf_op jit(solution)/shard_map/swap_weights/ppermute | solution.py:267
  57.6 4.3 %collective-permute-start.5 = (bf16[8,256,128]{2,1,0:T(8,128)(2,1)}, bf16[8,256,128]{2,1,0:T(8,128)(2,1)}, u32[]{:S(2)}, u32[]{:S(2)}) collective-permute-start(bf16[8,256,128]{2,1,0:T(8,128)(2,1)} %get-tuple-element.29), channel_id=1, source_target_pairs={{0,1},{1,0},{2,3},{3,2},{4,5},{5,4},{6,7},{7,6},{8,9},{9,8},{10,11... | collective-permute-start | bytes 1572872 | tf_op jit(solution)/shard_map/swap_weights/ppermute | solution.py:267
  60.0 0.8 copy-start.5
  61.9 4.5 %collective-permute-start.6 = (bf16[16,2,8,16,128]{4,3,2,1,0:T(8,128)(2,1)S(1)}, bf16[16,2,8,16,128]{4,3,2,1,0:T(8,128)(2,1)S(1)}, u32[]{:S(2)}, u32[]{:S(2)}) collective-permute-start(bf16[16,2,8,16,128]{4,3,2,1,0:T(8,128)(2,1)S(1)} %all-to-all-done.1.mine_ref), channel_id=1, source_target_pairs={{0,1},{1,0},{2,3},{3,2},{4,5},{5,4},{6,7},{7,6},{8,9},{9,8},{10,11... | collective-permute-start | bytes 3145736 | tf_op jit(solution)/shard_map/swap_weights/ppermute | solution.py:269
  64.2 2.3 %copy-start.9 = (f32[1024]{0:T(1024)S(1)}, f32[1024]{0:T(1024)}, u32[]{:S(2)}) copy-start(f32[1024]{0:T(1024)} %param.15) | copy-start | bytes 12292
  66.4 1.0 copy-start.6
  71.8 4.7 %copy-start.10 = (bf16[64,1,1024]{2,0,1:T(8,128)(2,1)S(1)}, bf16[64,1,1024]{2,0,1:T(8,128)(2,1)}, u32[]{:S(2)}) copy-start(bf16[64,1,1024]{2,0,1:T(8,128)(2,1)} %param.17) | copy-start | bytes 393220
  71.8 22.0 %all-to-all-start.2 = ((bf16[8,512,128]{2,1,0:T(8,128)(2,1)}), bf16[8,512,128]{2,1,0:T(8,128)(2,1)S(1)}, u32[]{:S(2)}, u32[]{:S(2)}) async-start(bf16[8,512,128]{2,1,0:T(8,128)(2,1)} %encode_keyval.1), calls=%async_computation.2 | async-start | bytes 2097152 | tf_op jit(solution)/shard_map/exchange_keyval/all_to_all | solution.py:273

commit v11 on v10

--- a/solution.py
+++ b/solution.py
@@ -18,6 +18,7 @@
 SEG_LEN = 256
 QTAIL = 64
 MASKED = -1e30
+CUT = 14
 
 PARTS = ("yh", "x", "z", "yl", "c")
 HA = ("yh", "x")
@@ -80,9 +81,16 @@
     copies = []
     for side in range(2):
         some = pl.ds(8 * side, 8)
-        sources = [kv_refs[0].at[some], kv_refs[1].at[some], kv_refs[2 + side], kv_refs[4 + side]]
-        copies.append([pltpu.make_async_copy(source, kv_bufs[i].at[some], in_sems.at[4 * side + i])
-                       for i, source in enumerate(sources)])
+        moves = [(kv_refs[i].at[some], kv_bufs[i].at[some]) for i in range(2)]
+        for i in range(2):
+            first, last = kv_refs[2 + 2 * i], kv_refs[3 + 2 * i]
+            if side == 0:
+                moves.append((first.at[some], kv_bufs[2 + i].at[some]))
+            else:
+                moves.append((first.at[pl.ds(8, CUT - 8)], kv_bufs[2 + i].at[pl.ds(8, CUT - 8)]))
+                moves.append((last, kv_bufs[2 + i].at[pl.ds(CUT, 16 - CUT)]))
+        copies.append([pltpu.make_async_copy(source, target, in_sems.at[4 * side + i])
+                       for i, (source, target) in enumerate(moves)])
     for side in range(2):
         for copy in copies[side]:
             copy.start()
@@ -139,7 +147,7 @@
                         pltpu.VMEM((4, SEG_LEN, 256), jnp.bfloat16),
                         pltpu.VMEM(shape.shape, shape.dtype)]
         + [pltpu.VMEM(kvs[0].shape, kvs[0].dtype)] * 4
-        + [pltpu.SemaphoreType.DMA((8,)), pltpu.SemaphoreType.DMA((KV_HEADS,))],
+        + [pltpu.SemaphoreType.DMA((10,)), pltpu.SemaphoreType.DMA((KV_HEADS,))],
         compiler_params=params(47),
         cost_estimate=pl.CostEstimate(
             flops=6 * SEG_LEN * D_ENC * D_ENC, bytes_accessed=8 * D_ENC * D_ENC, transcendentals=SEG_LEN),
@@ -240,7 +248,6 @@
     with jax.named_scope("gather_kv_weight"):
         eighth = lax.dynamic_slice_in_dim(
             kv_weight.reshape(D_ENC, 2 * HEAD), core * 512 + odd * 256 + yl * 128, 128, 0)
-        pair, eighth = lax.optimization_barrier((pair, eighth))
         kv_mine = spread(jnp.concatenate([eighth[:, :HEAD], eighth[:, HEAD:]], axis=0), PLANE)
     with jax.named_scope("out_weight_over_z"):
         hops = []
@@ -264,7 +271,7 @@
         kv_next = lax.ppermute(kv_mine, ("z", "c"), pairs)
     with jax.named_scope("swap_weights"):
         kvs = [kv_mine, kv_next]
-        kvs = kvs + [swap(part) for kv in kvs for part in (kv[:8], kv[8:])]
+        kvs = kvs + [swap(part) for kv in kvs for part in (kv[:CUT], kv[CUT:])]
         w_mine, kvs = lax.optimization_barrier((w_mine, kvs))
         w_other = swap(w_mine)
     place = jnp.stack([z, core, odd]).astype(jnp.int32)

time: 129 us -> 134 us (1.039)
  local copies, waits for them, and re-layouts: 9.38 us -> 11.7 us
  starting transfers between devices: 43.8 us -> 46.1 us
    all_to_all x2, starting transfers between devices: 8.12 us -> 11.6 us  [spread(): return lax.all_to_all(copies, axes, 0, 0, tiled=True)]
    all_gather x1, blocking collectives: 8.37 us -> 5.08 us  [local(): lax.all_gather(out_weight.reshape(16, 8, HEAD).transpose(1, 0, 2), 'c')]
    all_to_all x1, blocking collectives: 29.4 us -> 32.6 us  [local(): parts = lax.all_to_all(parts, SA, 0, 0, tiled=True)]
    slice x2 -> x4, local copies, waits for them, and re-layouts: 3.57 us -> 5.9 us  [local(): kvs = kvs + [swap(part) for kv in kvs for part in (kv[:CUT], kv[CUT:])]]
    all_to_all x2, waiting for transfers between devices: 2.33 us -> 0.01 us  [spread(): return lax.all_to_all(copies, axes, 0, 0, tiled=True)]
    ppermute x1, starting transfers between devices: 7.49 us -> 5.66 us  [local(): kv_next = lax.ppermute(kv_mine, ('z', 'c'), pairs)]
    ppermute x1, waiting for transfers between devices: 2.02 us -> 3.41 us  [local(): kv_next = lax.ppermute(kv_mine, ('z', 'c'), pairs)]
  transfers between devices with their start and end apart: 10 -> 10, of which waited for: 6 -> 4; matrix products, arithmetic and copies ran while one was open for 4% -> 6% of each run, Pallas kernels for 2% -> 2%
where the time goes in v11:
time: 134 us; the launch traced here: 133 us
  starting transfers between devices  46.1 us (34%)
  blocking collectives  37.7 us (28%)
  waiting for transfers between devices  24 us (18%)
  Pallas kernels  12.9 us (10%)
  local copies, waits for them, and re-layouts  11.7 us (9%)
    all_to_all x1, blocking collectives, local(): parts = lax.all_to_all(parts, SA, 0, 0, tiled=True)  32.6 us
    all_to_all x1, waiting for transfers between devices, local(): keyval = lax.all_to_all(keyval, HA, 0, 0, tiled=True)  17.2 us
    ppermute x1, starting transfers between devices, local(): pair = lax.ppermute(pair, ('yh', 'x', 'z', 'c'), hops)  12.8 us
    all_to_all x2, starting transfers between devices, spread(): return lax.all_to_all(copies, axes, 0, 0, tiled=True)  11.6 us
    ppermute x4, starting transfers between devices, local(): kvs = kvs + [swap(part) for kv in kvs for part in (kv[:CUT], kv[CUT:])]  9.33 us
    slice x4, local copies, waits for them, and re-layouts, local(): kvs = kvs + [swap(part) for kv in kvs for part in (kv[:CUT], kv[CUT:])]  5.9 us
    ppermute x1, starting transfers between devices, local(): kv_next = lax.ppermute(kv_mine, ('z', 'c'), pairs)  5.66 us
    all_gather x1, blocking collectives, local(): lax.all_gather(out_weight.reshape(16, 8, HEAD).transpose(1, 0, 2), 'c')  5.08 us
  transfers between devices with their start and end apart: 10, of which 4 were waited for; matrix products, arithmetic and copies ran while one was open for 6% of the time, Pallas kernels for 2%

profile of v11, /device:TPU:1, one launch (start us, length us, event | category | flops | bytes accessed | tf_op | source)
XLA Modules:
  0.0 132.8 jit_solution(6371751870215730572)
XLA Ops:
  1.1 1.2 broadcast_in_dim.4
  2.3 7.8 %all-to-all-start = ((bf16[16,256,128]{2,1,0:T(8,128)(2,1)}), bf16[16,256,128]{2,1,0:T(8,128)(2,1)}, u32[]{:S(2)}, u32[]{:S(2)}) async-start(bf16[16,256,128]{2,1,0:T(8,128)(2,1)} %broadcast_in_dim.4), calls=%async_computation | async-start | bytes 2097152 | tf_op jit(solution)/shard_map/gather_kv_weight/all_to_all | solution.py:231
  10.1 5.1 %all-gather = bf16[16,16,128]{2,0,1:T(8,128)(2,1)S(1)} all-gather(bf16[8,16,128]{2,0,1:T(8,128)(2,1)S(1)} %bitcast.24), channel_id=2, replica_groups=mesh['yh'=2,'x'=4,'z'=16,'yl'=2,'c'=2] {'c'}, dimensions={0}, use_global_device_ids=true | all-gather | bytes 98304 | tf_op jit(solution)/shard_map/pair_out_weight/all_gather | solution.py:247
  15.2 12.8 %collective-permute-start = (bf16[2,8,16,128]{3,2,1,0:T(8,128)(2,1)S(1)}, bf16[2,8,16,128]{3,2,1,0:T(8,128)(2,1)S(1)}, u32[]{:S(2)}, u32[]{:S(2)}) collective-permute-start(bf16[2,8,16,128]{3,2,1,0:T(8,128)(2,1)S(1)} %bitcast.26), channel_id=1, source_target_pairs={{0,0},{1,33},{4,4},{5,37},{8,8},{9,41},{12,12},{13,45},{16,16},{17... | collective-permute-start | bytes 196616 | tf_op jit(solution)/shard_map/out_weight_over_z/ppermute | solution.py:259
  28.7 3.1 %encoder_attention.1.ctx_ref = bf16[256,1024]{1,0:T(8,128)(2,1)S(1)} custom-call(s32[1]{0:T(128)} %bitcast.10.slot_ref, s32[512]{0:T(512)S(1)} %copy-done.7, s32[512]{0:T(512)S(1)} %copy-done.8, bf16[256,1024]{1,0:T(8,128)(2,1)S(1)} %copy-done.1, bf16[256,1024]{1,0:T(8,128)(2,1)S(1)} %copy-done.2, bf16[256,1024]{1,0:T(8,128)(2,1)S(1)} %copy-done.3), custom_call_target="tpu_custom_call" | custom-call | flops 536870912 | bytes 2097152 | tf_op jit(solution)/shard_map/encoder_attention/pallas_call | solution.py:63
  31.9 5.7 %collective-permute-start.1 = (bf16[16,256,128]{2,1,0:T(8,128)(2,1)}, bf16[16,256,128]{2,1,0:T(8,128)(2,1)}, u32[]{:S(2)}, u32[]{:S(2)}) collective-permute-start(bf16[16,256,128]{2,1,0:T(8,128)(2,1)} %all-to-all-done.refs_0_), channel_id=1, source_target_pairs={{0,4},{1,61},{4,0},{5,9},{8,12},{9,5},{12,8},{13,17},{16,20},{17,1... | collective-permute-start | bytes 3145736 | tf_op jit(solution)/shard_map/kv_weight_over_z/ppermute | solution.py:271
  37.5 1.2 broadcast_in_dim.5
  38.7 3.8 %all-to-all-start.1 = ((bf16[16,2,8,16,128]{4,3,2,1,0:T(8,128)(2,1)}), bf16[16,2,8,16,128]{4,3,2,1,0:T(8,128)(2,1)S(1)}, u32[]{:S(2)}, u32[]{:S(2)}) async-start(bf16[16,2,8,16,128]{4,3,2,1,0:T(8,128)(2,1)} %broadcast_in_dim.5), calls=%async_computation.1 | async-start | bytes 2097152 | tf_op jit(solution)/shard_map/out_weight_over_plane/all_to_all | solution.py:231
  42.6 1.2 slice.20
  43.8 3.0 %collective-permute-start.2 = (bf16[14,256,128]{2,1,0:T(8,128)(2,1)S(1)}, bf16[14,256,128]{2,1,0:T(8,128)(2,1)S(1)}, u32[]{:S(2)}, u32[]{:S(2)}) collective-permute-start(bf16[14,256,128]{2,1,0:T(8,128)(2,1)S(1)} %slice.20), channel_id=1, source_target_pairs={{0,1},{1,0},{2,3},{3,2},{4,5},{5,4},{6,7},{7,6},{8,9},{9,8},{10,11... | collective-permute-start | bytes 2752520 | tf_op jit(solution)/shard_map/swap_weights/ppermute | solution.py:274
  46.8 3.4 %collective-permute-done.1.refs_1_ = bf16[16,256,128]{2,1,0:T(8,128)(2,1)} collective-permute-done((bf16[16,256,128]{2,1,0:T(8,128)(2,1)}, bf16[16,256,128]{2,1,0:T(8,128)(2,1)}, u32[]{:S(2)}, u32[]{:S(2)}) %collective-permute-start.1) | collective-permute-done | bytes 1048608 | tf_op jit(solution)/shard_map/kv_weight_over_z/ppermute | solution.py:271
  50.2 2.2 %slice.26 = bf16[14,256,128]{2,1,0:T(8,128)(2,1)} slice(bf16[16,256,128]{2,1,0:T(8,128)(2,1)} %collective-permute-done.1.refs_1_), slice={[0:14], [0:256], [0:128]} | slice | bytes 1835008 | tf_op jit(solution)/shard_map/swap_weights/slice | solution.py:274
  52.4 2.0 %collective-permute-start.4 = (bf16[14,256,128]{2,1,0:T(8,128)(2,1)}, bf16[14,256,128]{2,1,0:T(8,128)(2,1)}, u32[]{:S(2)}, u32[]{:S(2)}) collective-permute-start(bf16[14,256,128]{2,1,0:T(8,128)(2,1)} %slice.26), channel_id=1, source_target_pairs={{0,1},{1,0},{2,3},{3,2},{4,5},{5,4},{6,7},{7,6},{8,9},{9,8},{10,11... | collective-permute-start | bytes 2752520 | tf_op jit(solution)/shard_map/swap_weights/ppermute | solution.py:274
  55.3 2.4 %collective-permute-start.3 = (bf16[2,256,128]{2,1,0:T(8,128)(2,1)S(1)}, bf16[2,256,128]{2,1,0:T(8,128)(2,1)S(1)}, u32[]{:S(2)}, u32[]{:S(2)}) collective-permute-start(bf16[2,256,128]{2,1,0:T(8,128)(2,1)S(1)} %slice.21), channel_id=1, source_target_pairs={{0,1},{1,0},{2,3},{3,2},{4,5},{5,4},{6,7},{7,6},{8,9},{9,8},{10,11... | collective-permute-start | bytes 393224 | tf_op jit(solution)/shard_map/swap_weights/ppermute | solution.py:274
  57.8 1.6 %slice.27 = bf16[2,256,128]{2,1,0:T(8,128)(2,1)} slice(bf16[16,256,128]{2,1,0:T(8,128)(2,1)} %collective-permute-done.1.refs_1_), slice={[14:16], [0:256], [0:128]} | slice | bytes 262144 | tf_op jit(solution)/shard_map/swap_weights/slice | solution.py:274
  59.3 1.9 %collective-permute-start.5 = (bf16[2,256,128]{2,1,0:T(8,128)(2,1)}, bf16[2,256,128]{2,1,0:T(8,128)(2,1)}, u32[]{:S(2)}, u32[]{:S(2)}) collective-permute-start(bf16[2,256,128]{2,1,0:T(8,128)(2,1)} %slice.27), channel_id=1, source_target_pairs={{0,1},{1,0},{2,3},{3,2},{4,5},{5,4},{6,7},{7,6},{8,9},{9,8},{10,11... | collective-permute-start | bytes 393224 | tf_op jit(solution)/shard_map/swap_weights/ppermute | solution.py:274
  62.9 2.0 %collective-permute-start.6 = (bf16[16,2,8,16,128]{4,3,2,1,0:T(8,128)(2,1)S(1)}, bf16[16,2,8,16,128]{4,3,2,1,0:T(8,128)(2,1)S(1)}, u32[]{:S(2)}, u32[]{:S(2)}) collective-permute-start(bf16[16,2,8,16,128]{4,3,2,1,0:T(8,128)(2,1)S(1)} %all-to-all-done.1.mine_ref), channel_id=1, source_target_pairs={{0,1},{1,0},{2,3},{3,2},{4,5},{5,4},{6,7},{7,6},{8,9},{9,8},{10,11... | collective-permute-start | bytes 3145736 | tf_op jit(solution)/shard_map/swap_weights/ppermute | solution.py:276
  65.1 2.4 %collective-permute-done.6.other_ref = bf16[16,2,8,16,128]{4,3,2,1,0:T(8,128)(2,1)S(1)} collective-permute-done((bf16[16,2,8,16,128]{4,3,2,1,0:T(8,128)(2,1)S(1)}, bf16[16,2,8,16,128]{4,3,2,1,0:T(8,128)(2,1)S(1)}, u32[]{:S(2)}, u32[]{:S(2)}) %collective-permute-start.6) | collective-permute-done | bytes 1048608 | tf_op jit(solution)/shard_map/swap_weights/ppermute | solution.py:276
  68.4 4.6 %encode_keyval.1 = bf16[8,512,128]{2,1,0:T(8,128)(2,1)} custom-call(s32[3]{0:T(128)S(1)} %pad_add_fusion.1.place_ref, f32[1,1024]{1,0:T(1,128)S(1)} %bitcast.22, bf16[256,1024]{1,0:T(8,128)(2,1)S(1)} %encoder_attention.1.ctx_ref, bf16[256,1024]{1,0:T(8,128)(2,1)S(1)} %copy-done.4, bf16[16,2,8,16,128]{4,3,2,1,0:T(8,128)(2,1)S(1)} %all-to-all-done.1.mine_ref, ...), custom_call_target="tpu_custom_call" | custom-call | flops 1610612736 | bytes 8388608 | tf_op jit(solution)/shard_map/encode_keyval/pallas_call | solution.py:141
  73.0 4.7 %all-to-all-start.2 = ((bf16[8,512,128]{2,1,0:T(8,128)(2,1)}), bf16[8,512,128]{2,1,0:T(8,128)(2,1)S(1)}, u32[]{:S(2)}, u32[]{:S(2)}) async-start(bf16[8,512,128]{2,1,0:T(8,128)(2,1)} %encode_keyval.1), calls=%async_computation.2 | async-start | bytes 2097152 | tf_op jit(solution)/shard_map/exchange_keyval/all_to_all | solution.py:280
  77.8 17.2 %all-to-all-done.2.kv_ref = bf16[8,512,128]{2,1,0:T(8,128)(2,1)S(1)} async-done(((bf16[8,512,128]{2,1,0:T(8,128)(2,1)}), bf16[8,512,128]{2,1,0:T(8,128)(2,1)S(1)}, u32[]{:S(2)}, u32[]{:S(2)}) %all-to-all-start.2) | async-done | bytes 1048608 | tf_op jit(solution)/shard_map/exchange_keyval/all_to_all | solution.py:280
  95.0 3.2 %cross_attention.1 = bf16[64,2,640]{2,1,0:T(2,128)(2,1)S(1)} custom-call(s32[2]{0:T(128)S(1)} %pad_add_fusion.first_ref, s32[512]{0:T(512)S(1)} %copy-done.7, s32[512]{0:T(512)S(1)} %copy-done.8, bf16[512,128]{1,0:T(8,128)(2,1)S(1)} %bitcast.21, bf16[8,512,128]{2,1,0:T(8,128)(2,1)S(1)} %all-to-all-done.2.kv_ref), custom_call_target="tpu_custom_call" | custom-call | tf_op jit(solution)/shard_map/cross_attention/pallas_call | solution.py:196
  98.2 32.6 %all_to_all.20.part_ref = bf16[64,2,640]{2,1,0:T(2,128)(2,1)} all-to-all(bf16[64,2,640]{2,1,0:T(2,128)(2,1)S(1)} %cross_attention.1), channel_id=1, replica_groups=mesh['yh'=2,'x'=4,'z'=16,'yl'=2,'c'=2] {'z','yl','c'}, dimensions={0} | all-to-all | bytes 327680 | tf_op jit(solution)/shard_map/exchange_partials/all_to_all | solution.py:285
  130.8 2.0 %merge_partials.1 = f32[8,128]{1,0:T(8,128)} custom-call(bf16[64,2,640]{2,1,0:T(2,128)(2,1)} %all_to_all.20.part_ref), custom_call_target="tpu_custom_call" | custom-call | tf_op jit(solution)/shard_map/merge_partials/pallas_call | solution.py:219
  (41 shorter events, 5.4 us)
Async XLA Ops:
  0.0 1.0 copy-start
  2.2 7.8 %copy-start.11 = (bf16[16,1024]{1,0:T(8,128)(2,1)S(1)}, bf16[16,1024]{1,0:T(8,128)(2,1)}, u32[]{:S(2)}) copy-start(bf16[16,1024]{1,0:T(8,128)(2,1)} %param.14) | copy-start | bytes 98308
  2.2 25.8 %copy-start.1 = (bf16[256,1024]{1,0:T(8,128)(2,1)S(1)}, bf16[256,1024]{1,0:T(8,128)(2,1)}, u32[]{:S(2)}) copy-start(bf16[256,1024]{1,0:T(8,128)(2,1)} %q_ref.1) | copy-start | bytes 1572868
  2.2 25.8 %copy-start.2 = (bf16[256,1024]{1,0:T(8,128)(2,1)S(1)}, bf16[256,1024]{1,0:T(8,128)(2,1)}, u32[]{:S(2)}) copy-start(bf16[256,1024]{1,0:T(8,128)(2,1)} %k_ref.1) | copy-start | bytes 1572868
  2.2 25.8 %copy-start.3 = (bf16[256,1024]{1,0:T(8,128)(2,1)S(1)}, bf16[256,1024]{1,0:T(8,128)(2,1)}, u32[]{:S(2)}) copy-start(bf16[256,1024]{1,0:T(8,128)(2,1)} %v_ref.1) | copy-start | bytes 1572868
  2.3 29.6 %all-to-all-start = ((bf16[16,256,128]{2,1,0:T(8,128)(2,1)}), bf16[16,256,128]{2,1,0:T(8,128)(2,1)}, u32[]{:S(2)}, u32[]{:S(2)}) async-start(bf16[16,256,128]{2,1,0:T(8,128)(2,1)} %broadcast_in_dim.4), calls=%async_computation | async-start | bytes 2097152 | tf_op jit(solution)/shard_map/gather_kv_weight/all_to_all | solution.py:231
  15.2 16.7 %collective-permute-start = (bf16[2,8,16,128]{3,2,1,0:T(8,128)(2,1)S(1)}, bf16[2,8,16,128]{3,2,1,0:T(8,128)(2,1)S(1)}, u32[]{:S(2)}, u32[]{:S(2)}) collective-permute-start(bf16[2,8,16,128]{3,2,1,0:T(8,128)(2,1)S(1)} %bitcast.26), channel_id=1, source_target_pairs={{0,0},{1,33},{4,4},{5,37},{8,8},{9,41},{12,12},{13,45},{16,16},{17... | collective-permute-start | bytes 196616 | tf_op jit(solution)/shard_map/out_weight_over_z/ppermute | solution.py:259
  28.0 0.7 copy-start.8
  28.0 0.7 copy-start.7
  31.9 18.3 %collective-permute-start.1 = (bf16[16,256,128]{2,1,0:T(8,128)(2,1)}, bf16[16,256,128]{2,1,0:T(8,128)(2,1)}, u32[]{:S(2)}, u32[]{:S(2)}) collective-permute-start(bf16[16,256,128]{2,1,0:T(8,128)(2,1)} %all-to-all-done.refs_0_), channel_id=1, source_target_pairs={{0,4},{1,61},{4,0},{5,9},{8,12},{9,5},{12,8},{13,17},{16,20},{17,1... | collective-permute-start | bytes 3145736 | tf_op jit(solution)/shard_map/kv_weight_over_z/ppermute | solution.py:271
  38.7 23.2 %all-to-all-start.1 = ((bf16[16,2,8,16,128]{4,3,2,1,0:T(8,128)(2,1)}), bf16[16,2,8,16,128]{4,3,2,1,0:T(8,128)(2,1)S(1)}, u32[]{:S(2)}, u32[]{:S(2)}) async-start(bf16[16,2,8,16,128]{4,3,2,1,0:T(8,128)(2,1)} %broadcast_in_dim.5), calls=%async_computation.1 | async-start | bytes 2097152 | tf_op jit(solution)/shard_map/out_weight_over_plane/all_to_all | solution.py:231
  43.8 18.1 %collective-permute-start.2 = (bf16[14,256,128]{2,1,0:T(8,128)(2,1)S(1)}, bf16[14,256,128]{2,1,0:T(8,128)(2,1)S(1)}, u32[]{:S(2)}, u32[]{:S(2)}) collective-permute-start(bf16[14,256,128]{2,1,0:T(8,128)(2,1)S(1)} %slice.20), channel_id=1, source_target_pairs={{0,1},{1,0},{2,3},{3,2},{4,5},{5,4},{6,7},{7,6},{8,9},{9,8},{10,11... | collective-permute-start | bytes 2752520 | tf_op jit(solution)/shard_map/swap_weights/ppermute | solution.py:274
  52.4 15.1 %copy-start.4 = (bf16[256,1024]{1,0:T(8,128)(2,1)S(1)}, bf16[256,1024]{1,0:T(8,128)(2,1)}, u32[]{:S(2)}) copy-start(bf16[256,1024]{1,0:T(8,128)(2,1)} %resid_ref.1) | copy-start | bytes 1572868
  52.4 10.5 %collective-permute-start.4 = (bf16[14,256,128]{2,1,0:T(8,128)(2,1)}, bf16[14,256,128]{2,1,0:T(8,128)(2,1)}, u32[]{:S(2)}, u32[]{:S(2)}) collective-permute-start(bf16[14,256,128]{2,1,0:T(8,128)(2,1)} %slice.26), channel_id=1, source_target_pairs={{0,1},{1,0},{2,3},{3,2},{4,5},{5,4},{6,7},{7,6},{8,9},{9,8},{10,11... | collective-permute-start | bytes 2752520 | tf_op jit(solution)/shard_map/swap_weights/ppermute | solution.py:274
  55.3 5.9 %collective-permute-start.3 = (bf16[2,256,128]{2,1,0:T(8,128)(2,1)S(1)}, bf16[2,256,128]{2,1,0:T(8,128)(2,1)S(1)}, u32[]{:S(2)}, u32[]{:S(2)}) collective-permute-start(bf16[2,256,128]{2,1,0:T(8,128)(2,1)S(1)} %slice.21), channel_id=1, source_target_pairs={{0,1},{1,0},{2,3},{3,2},{4,5},{5,4},{6,7},{7,6},{8,9},{9,8},{10,11... | collective-permute-start | bytes 393224 | tf_op jit(solution)/shard_map/swap_weights/ppermute | solution.py:274
  59.3 3.6 %collective-permute-start.5 = (bf16[2,256,128]{2,1,0:T(8,128)(2,1)}, bf16[2,256,128]{2,1,0:T(8,128)(2,1)}, u32[]{:S(2)}, u32[]{:S(2)}) collective-permute-start(bf16[2,256,128]{2,1,0:T(8,128)(2,1)} %slice.27), channel_id=1, source_target_pairs={{0,1},{1,0},{2,3},{3,2},{4,5},{5,4},{6,7},{7,6},{8,9},{9,8},{10,11... | collective-permute-start | bytes 393224 | tf_op jit(solution)/shard_map/swap_weights/ppermute | solution.py:274
  61.3 0.7 copy-start.5
  62.9 4.5 %collective-permute-start.6 = (bf16[16,2,8,16,128]{4,3,2,1,0:T(8,128)(2,1)S(1)}, bf16[16,2,8,16,128]{4,3,2,1,0:T(8,128)(2,1)S(1)}, u32[]{:S(2)}, u32[]{:S(2)}) collective-permute-start(bf16[16,2,8,16,128]{4,3,2,1,0:T(8,128)(2,1)S(1)} %all-to-all-done.1.mine_ref), channel_id=1, source_target_pairs={{0,1},{1,0},{2,3},{3,2},{4,5},{5,4},{6,7},{7,6},{8,9},{9,8},{10,11... | collective-permute-start | bytes 3145736 | tf_op jit(solution)/shard_map/swap_weights/ppermute | solution.py:276
  65.0 2.5 %copy-start.9 = (f32[1024]{0:T(1024)S(1)}, f32[1024]{0:T(1024)}, u32[]{:S(2)}) copy-start(f32[1024]{0:T(1024)} %param.15) | copy-start | bytes 12292
  67.5 0.9 copy-start.6
  73.0 4.7 %copy-start.10 = (bf16[64,1,1024]{2,0,1:T(8,128)(2,1)S(1)}, bf16[64,1,1024]{2,0,1:T(8,128)(2,1)}, u32[]{:S(2)}) copy-start(bf16[64,1,1024]{2,0,1:T(8,128)(2,1)} %param.17) | copy-start | bytes 393220
  73.0 22.0 %all-to-all-start.2 = ((bf16[8,512,128]{2,1,0:T(8,128)(2,1)}), bf16[8,512,128]{2,1,0:T(8,128)(2,1)S(1)}, u32[]{:S(2)}, u32[]{:S(2)}) async-start(bf16[8,512,128]{2,1,0:T(8,128)(2,1)} %encode_keyval.1), calls=%async_computation.2 | async-start | bytes 2097152 | tf_op jit(solution)/shard_map/exchange_keyval/all_to_all | solution.py:280

commit v12 on v10

--- a/solution.py
+++ b/solution.py
@@ -73,14 +73,14 @@
 
 
 def encode_kernel(place_ref, gain_ref, ctx_ref, resid_ref, mine_ref, other_ref, *refs):
-    kv_refs, o_ref = refs[:6], refs[6]
-    w_ref, enc_ref, done_ref = refs[7:10]
-    kv_bufs, in_sems, out_sems = refs[10:14], refs[14], refs[15]
+    kv_refs, o_ref = refs[:5], refs[5]
+    w_ref, enc_ref, done_ref = refs[6:9]
+    kv_bufs, in_sems, out_sems = refs[9:13], refs[13], refs[14]
     z, core, odd = place_ref[0], place_ref[1], place_ref[2]
     copies = []
     for side in range(2):
         some = pl.ds(8 * side, 8)
-        sources = [kv_refs[0].at[some], kv_refs[1].at[some], kv_refs[2 + side], kv_refs[4 + side]]
+        sources = [kv_refs[0].at[some], kv_refs[1].at[some], kv_refs[2].at[some], kv_refs[3 + side]]
         copies.append([pltpu.make_async_copy(source, kv_bufs[i].at[some], in_sems.at[4 * side + i])
                        for i, source in enumerate(sources)])
     for side in range(2):
@@ -133,14 +133,14 @@
     return pl.pallas_call(
         encode_kernel,
         out_shape=shape,
-        in_specs=[smem] + [vmem] * 5 + [hbm] * 6,
+        in_specs=[smem] + [vmem] * 5 + [hbm] * 5,
         out_specs=hbm,
         scratch_shapes=[pltpu.VMEM((8, D_ENC, HEAD), jnp.bfloat16),
                         pltpu.VMEM((4, SEG_LEN, 256), jnp.bfloat16),
                         pltpu.VMEM(shape.shape, shape.dtype)]
         + [pltpu.VMEM(kvs[0].shape, kvs[0].dtype)] * 4
         + [pltpu.SemaphoreType.DMA((8,)), pltpu.SemaphoreType.DMA((KV_HEADS,))],
-        compiler_params=params(47),
+        compiler_params=params(48),
         cost_estimate=pl.CostEstimate(
             flops=6 * SEG_LEN * D_ENC * D_ENC, bytes_accessed=8 * D_ENC * D_ENC, transcendentals=SEG_LEN),
         name="encode_keyval",
@@ -263,10 +263,10 @@
                 pairs.append((2 * z_at + c_at, 2 * there + c_at))
         kv_next = lax.ppermute(kv_mine, ("z", "c"), pairs)
     with jax.named_scope("swap_weights"):
-        kvs = [kv_mine, kv_next]
-        kvs = kvs + [swap(part) for kv in kvs for part in (kv[:8], kv[8:])]
-        w_mine, kvs = lax.optimization_barrier((w_mine, kvs))
+        far = [swap(kv_next[:8]), swap(kv_next[8:])]
+        w_mine, far = lax.optimization_barrier((w_mine, far))
         w_other = swap(w_mine)
+        kvs = [kv_mine, kv_next, swap(kv_mine)] + far
     place = jnp.stack([z, core, odd]).astype(jnp.int32)
     keyval = encode(place, norm_gain.reshape(1, D_ENC), context, enc_resid, w_mine, w_other, kvs)
     with jax.named_scope("exchange_keyval"):

time: 129 us -> 128 us (level)
  waiting for transfers between devices: 24.4 us -> 29.1 us
  starting transfers between devices: 43.8 us -> 40.5 us
  local copies, waits for them, and re-layouts: 9.38 us -> 6.24 us
    ppermute x1, waiting for transfers between devices: 2.02 us -> 7.81 us  [local(): kv_next = lax.ppermute(kv_mine, ('z', 'c'), pairs)]
    ppermute x4 -> x3, starting transfers between devices: 8.78 us -> 6.24 us  [the longest x2 4.32 us: local(): far = [swap(kv_next[:8]), swap(kv_next[8:])]]
    unnamed x26 -> x22, local copies, waits for them, and re-layouts: 3.36 us -> 1.53 us
    slice x2 -> x1, local copies, waits for them, and re-layouts: 3.57 us -> 2.29 us  [local(): far = [swap(kv_next[:8]), swap(kv_next[8:])]]
  transfers between devices with their start and end apart: 10 -> 9, of which waited for: 6 -> 5; matrix products, arithmetic and copies ran while one was open for 4% -> 3% of each run, Pallas kernels for 2% -> 2%
where the time goes in v12:
time: 128 us
  starting transfers between devices  40.5 us (32%)
  blocking collectives  38.6 us (30%)
  waiting for transfers between devices  29.1 us (23%)
  Pallas kernels  13 us (10%)
  local copies, waits for them, and re-layouts  6.24 us (5%)
    all_to_all x1, blocking collectives, local(): parts = lax.all_to_all(parts, SA, 0, 0, tiled=True)  30.2 us
    all_to_all x1, waiting for transfers between devices, local(): keyval = lax.all_to_all(keyval, HA, 0, 0, tiled=True)  17.2 us
    ppermute x1, starting transfers between devices, local(): pair = lax.ppermute(pair, ('yh', 'x', 'z', 'c'), hops)  12.5 us
    all_gather x1, blocking collectives, local(): lax.all_gather(out_weight.reshape(16, 8, HEAD).transpose(1, 0, 2), 'c')  8.37 us
    all_to_all x2, starting transfers between devices, spread(): return lax.all_to_all(copies, axes, 0, 0, tiled=True)  8.12 us
    ppermute x1, waiting for transfers between devices, local(): kv_next = lax.ppermute(kv_mine, ('z', 'c'), pairs)  7.81 us
    ppermute x1, starting transfers between devices, local(): kv_next = lax.ppermute(kv_mine, ('z', 'c'), pairs)  7.49 us
    pallas_call x1, Pallas kernels, encode(): pl.pallas_call(encode_kernel, out_shape=shape, in_specs=[smem] + [vmem] *...  4.7 us
  transfers between devices with their start and end apart: 9, of which 5 were waited for; matrix products, arithmetic and copies ran while one was open for 3% of the time, Pallas kernels for 2%

profile of v12, /device:TPU:1, one launch (start us, length us, event | category | flops | bytes accessed | tf_op | source)
XLA Modules:
  0.0 127.8 jit_solution(16150543512798324900)
XLA Ops:
  0.0 0.8 copy-done.9
  0.8 8.4 %all-gather = bf16[16,16,128]{2,0,1:T(8,128)(2,1)S(1)} all-gather(bf16[8,16,128]{2,0,1:T(8,128)(2,1)S(1)} %bitcast.24), channel_id=2, replica_groups=mesh['yh'=2,'x'=4,'z'=16,'yl'=2,'c'=2] {'c'}, dimensions={0}, use_global_device_ids=true | all-gather | bytes 98304 | tf_op jit(solution)/shard_map/pair_out_weight/all_gather | solution.py:239
  9.3 1.2 broadcast_in_dim.4
  10.5 4.5 %all-to-all-start = ((bf16[16,256,128]{2,1,0:T(8,128)(2,1)}), bf16[16,256,128]{2,1,0:T(8,128)(2,1)}, u32[]{:S(2)}, u32[]{:S(2)}) async-start(bf16[16,256,128]{2,1,0:T(8,128)(2,1)} %broadcast_in_dim.4), calls=%async_computation | async-start | bytes 2097152 | tf_op jit(solution)/shard_map/gather_kv_weight/all_to_all | solution.py:223
  14.9 12.5 %collective-permute-start = (bf16[2,8,16,128]{3,2,1,0:T(8,128)(2,1)S(1)}, bf16[2,8,16,128]{3,2,1,0:T(8,128)(2,1)S(1)}, u32[]{:S(2)}, u32[]{:S(2)}) collective-permute-start(bf16[2,8,16,128]{3,2,1,0:T(8,128)(2,1)S(1)} %bitcast.26), channel_id=1, source_target_pairs={{0,0},{1,33},{4,4},{5,37},{8,8},{9,41},{12,12},{13,45},{16,16},{17... | collective-permute-start | bytes 196616 | tf_op jit(solution)/shard_map/out_weight_over_z/ppermute | solution.py:252
  27.6 0.6 copy-done.6
  28.2 3.1 %encoder_attention.1.ctx_ref = bf16[256,1024]{1,0:T(8,128)(2,1)S(1)} custom-call(s32[1]{0:T(128)} %bitcast.10.slot_ref, s32[512]{0:T(512)S(1)} %copy-done.5, s32[512]{0:T(512)S(1)} %copy-done.6, bf16[256,1024]{1,0:T(8,128)(2,1)S(1)} %copy-done.1, bf16[256,1024]{1,0:T(8,128)(2,1)S(1)} %copy-done.2, bf16[256,1024]{1,0:T(8,128)(2,1)S(1)} %copy-done.3), custom_call_target="tpu_custom_call" | custom-call | flops 536870912 | bytes 2097152 | tf_op jit(solution)/shard_map/encoder_attention/pallas_call | solution.py:62
  31.3 1.9 %all-to-all-done.refs_0_ = bf16[16,256,128]{2,1,0:T(8,128)(2,1)} async-done(((bf16[16,256,128]{2,1,0:T(8,128)(2,1)}), bf16[16,256,128]{2,1,0:T(8,128)(2,1)}, u32[]{:S(2)}, u32[]{:S(2)}) %all-to-all-start) | async-done | bytes 1048608 | tf_op jit(solution)/shard_map/gather_kv_weight/all_to_all | solution.py:223
  33.2 7.5 %collective-permute-start.1 = (bf16[16,256,128]{2,1,0:T(8,128)(2,1)}, bf16[16,256,128]{2,1,0:T(8,128)(2,1)}, u32[]{:S(2)}, u32[]{:S(2)}) collective-permute-start(bf16[16,256,128]{2,1,0:T(8,128)(2,1)} %all-to-all-done.refs_0_), channel_id=1, source_target_pairs={{0,4},{1,61},{4,0},{5,9},{8,12},{9,5},{12,8},{13,17},{16,20},{17,1... | collective-permute-start | bytes 3145736 | tf_op jit(solution)/shard_map/kv_weight_over_z/ppermute | solution.py:264
  40.7 1.2 broadcast_in_dim.5
  41.9 3.7 %all-to-all-start.1 = ((bf16[16,2,8,16,128]{4,3,2,1,0:T(8,128)(2,1)}), bf16[16,2,8,16,128]{4,3,2,1,0:T(8,128)(2,1)S(1)}, u32[]{:S(2)}, u32[]{:S(2)}) async-start(bf16[16,2,8,16,128]{4,3,2,1,0:T(8,128)(2,1)} %broadcast_in_dim.5), calls=%async_computation.1 | async-start | bytes 2097152 | tf_op jit(solution)/shard_map/out_weight_over_plane/all_to_all | solution.py:223
  45.6 7.8 %collective-permute-done.1.refs_1_ = bf16[16,256,128]{2,1,0:T(8,128)(2,1)} collective-permute-done((bf16[16,256,128]{2,1,0:T(8,128)(2,1)}, bf16[16,256,128]{2,1,0:T(8,128)(2,1)}, u32[]{:S(2)}, u32[]{:S(2)}) %collective-permute-start.1) | collective-permute-done | bytes 1048608 | tf_op jit(solution)/shard_map/kv_weight_over_z/ppermute | solution.py:264
  53.4 2.3 %fusion = (bf16[8,256,128]{2,1,0:T(8,128)(2,1)}, bf16[8,256,128]{2,1,0:T(8,128)(2,1)}) fusion(bf16[16,256,128]{2,1,0:T(8,128)(2,1)} %collective-permute-done.1.refs_1_), kind=kLoop, calls=%fused_computation.4 | loop fusion | bytes 2097152 | tf_op jit(solution)/shard_map/swap_weights/slice | solution.py:266
  55.7 1.9 %collective-permute-start.2 = (bf16[8,256,128]{2,1,0:T(8,128)(2,1)}, bf16[8,256,128]{2,1,0:T(8,128)(2,1)S(1)}, u32[]{:S(2)}, u32[]{:S(2)}) collective-permute-start(bf16[8,256,128]{2,1,0:T(8,128)(2,1)} %get-tuple-element.22), channel_id=1, source_target_pairs={{0,1},{1,0},{2,3},{3,2},{4,5},{5,4},{6,7},{7,6},{8,9},{9,8},{10,11... | collective-permute-start | bytes 1572872 | tf_op jit(solution)/shard_map/swap_weights/ppermute | solution.py:266
  57.6 2.4 %collective-permute-start.3 = (bf16[8,256,128]{2,1,0:T(8,128)(2,1)}, bf16[8,256,128]{2,1,0:T(8,128)(2,1)}, u32[]{:S(2)}, u32[]{:S(2)}) collective-permute-start(bf16[8,256,128]{2,1,0:T(8,128)(2,1)} %get-tuple-element.21), channel_id=1, source_target_pairs={{0,1},{1,0},{2,3},{3,2},{4,5},{5,4},{6,7},{7,6},{8,9},{9,8},{10,11... | collective-permute-start | bytes 1572872 | tf_op jit(solution)/shard_map/swap_weights/ppermute | solution.py:266
  60.0 1.9 %collective-permute-start.5 = (bf16[16,256,128]{2,1,0:T(8,128)(2,1)}, bf16[16,256,128]{2,1,0:T(8,128)(2,1)}, u32[]{:S(2)}, u32[]{:S(2)}) collective-permute-start(bf16[16,256,128]{2,1,0:T(8,128)(2,1)} %all-to-all-done.refs_0_), channel_id=1, source_target_pairs={{0,1},{1,0},{2,3},{3,2},{4,5},{5,4},{6,7},{7,6},{8,9},{9,8},{10,11... | collective-permute-start | bytes 3145736 | tf_op jit(solution)/shard_map/swap_weights/ppermute | solution.py:269
  62.0 2.4 %collective-permute-start.4 = (bf16[16,2,8,16,128]{4,3,2,1,0:T(8,128)(2,1)S(1)}, bf16[16,2,8,16,128]{4,3,2,1,0:T(8,128)(2,1)S(1)}, u32[]{:S(2)}, u32[]{:S(2)}) collective-permute-start(bf16[16,2,8,16,128]{4,3,2,1,0:T(8,128)(2,1)S(1)} %all-to-all-done.1.mine_ref), channel_id=1, source_target_pairs={{0,1},{1,0},{2,3},{3,2},{4,5},{5,4},{6,7},{7,6},{8,9},{9,8},{10,11... | collective-permute-start | bytes 3145736 | tf_op jit(solution)/shard_map/swap_weights/ppermute | solution.py:268
  64.9 1.7 %collective-permute-done.4.other_ref = bf16[16,2,8,16,128]{4,3,2,1,0:T(8,128)(2,1)S(1)} collective-permute-done((bf16[16,2,8,16,128]{4,3,2,1,0:T(8,128)(2,1)S(1)}, bf16[16,2,8,16,128]{4,3,2,1,0:T(8,128)(2,1)S(1)}, u32[]{:S(2)}, u32[]{:S(2)}) %collective-permute-start.4) | collective-permute-done | bytes 1048608 | tf_op jit(solution)/shard_map/swap_weights/ppermute | solution.py:268
  66.7 4.7 %encode_keyval.1 = bf16[8,512,128]{2,1,0:T(8,128)(2,1)} custom-call(s32[3]{0:T(128)S(1)} %pad_add_fusion.1.place_ref, f32[1,1024]{1,0:T(1,128)S(1)} %bitcast.22, bf16[256,1024]{1,0:T(8,128)(2,1)S(1)} %encoder_attention.1.ctx_ref, bf16[256,1024]{1,0:T(8,128)(2,1)S(1)} %copy-done.4, bf16[16,2,8,16,128]{4,3,2,1,0:T(8,128)(2,1)S(1)} %all-to-all-done.1.mine_ref, ...), custom_call_target="tpu_custom_call" | custom-call | flops 1610612736 | bytes 8388608 | tf_op jit(solution)/shard_map/encode_keyval/pallas_call | solution.py:133
  71.4 3.7 %all-to-all-start.2 = ((bf16[8,512,128]{2,1,0:T(8,128)(2,1)}), bf16[8,512,128]{2,1,0:T(8,128)(2,1)S(1)}, u32[]{:S(2)}, u32[]{:S(2)}) async-start(bf16[8,512,128]{2,1,0:T(8,128)(2,1)} %encode_keyval.1), calls=%async_computation.2 | async-start | bytes 2097152 | tf_op jit(solution)/shard_map/exchange_keyval/all_to_all | solution.py:273
  75.2 17.2 %all-to-all-done.2.kv_ref = bf16[8,512,128]{2,1,0:T(8,128)(2,1)S(1)} async-done(((bf16[8,512,128]{2,1,0:T(8,128)(2,1)}), bf16[8,512,128]{2,1,0:T(8,128)(2,1)S(1)}, u32[]{:S(2)}, u32[]{:S(2)}) %all-to-all-start.2) | async-done | bytes 1048608 | tf_op jit(solution)/shard_map/exchange_keyval/all_to_all | solution.py:273
  92.4 3.1 %cross_attention.1 = bf16[64,2,640]{2,1,0:T(2,128)(2,1)S(1)} custom-call(s32[2]{0:T(128)S(1)} %pad_add_fusion.first_ref, s32[512]{0:T(512)S(1)} %copy-done.5, s32[512]{0:T(512)S(1)} %copy-done.6, bf16[512,128]{1,0:T(8,128)(2,1)S(1)} %bitcast.21, bf16[8,512,128]{2,1,0:T(8,128)(2,1)S(1)} %all-to-all-done.2.kv_ref), custom_call_target="tpu_custom_call" | custom-call | tf_op jit(solution)/shard_map/cross_attention/pallas_call | solution.py:188
  95.6 30.2 %all_to_all.20.part_ref = bf16[64,2,640]{2,1,0:T(2,128)(2,1)} all-to-all(bf16[64,2,640]{2,1,0:T(2,128)(2,1)S(1)} %cross_attention.1), channel_id=1, replica_groups=mesh['yh'=2,'x'=4,'z'=16,'yl'=2,'c'=2] {'z','yl','c'}, dimensions={0} | all-to-all | bytes 327680 | tf_op jit(solution)/shard_map/exchange_partials/all_to_all | solution.py:278
  125.8 2.0 %merge_partials.1 = f32[8,128]{1,0:T(8,128)} custom-call(bf16[64,2,640]{2,1,0:T(2,128)(2,1)} %all_to_all.20.part_ref), custom_call_target="tpu_custom_call" | custom-call | tf_op jit(solution)/shard_map/merge_partials/pallas_call | solution.py:211
  (32 shorter events, 0.7 us)
Async XLA Ops:
  0.0 9.2 %copy-start = (bf16[1024,1,256]{2,0,1:T(8,128)(2,1)S(1)}, bf16[1024,1,256]{2,0,1:T(8,128)(2,1)}, u32[]{:S(2)}) copy-start(bf16[1024,1,256]{2,0,1:T(8,128)(2,1)} %param.16) | copy-start | bytes 1572868
  0.0 0.8 copy-start.9
  10.5 17.1 %copy-start.1 = (bf16[256,1024]{1,0:T(8,128)(2,1)S(1)}, bf16[256,1024]{1,0:T(8,128)(2,1)}, u32[]{:S(2)}) copy-start(bf16[256,1024]{1,0:T(8,128)(2,1)} %q_ref.1) | copy-start | bytes 1572868
  10.5 17.1 %copy-start.2 = (bf16[256,1024]{1,0:T(8,128)(2,1)S(1)}, bf16[256,1024]{1,0:T(8,128)(2,1)}, u32[]{:S(2)}) copy-start(bf16[256,1024]{1,0:T(8,128)(2,1)} %k_ref.1) | copy-start | bytes 1572868
  10.5 17.1 %copy-start.3 = (bf16[256,1024]{1,0:T(8,128)(2,1)S(1)}, bf16[256,1024]{1,0:T(8,128)(2,1)}, u32[]{:S(2)}) copy-start(bf16[256,1024]{1,0:T(8,128)(2,1)} %v_ref.1) | copy-start | bytes 1572868
  10.5 22.8 %all-to-all-start = ((bf16[16,256,128]{2,1,0:T(8,128)(2,1)}), bf16[16,256,128]{2,1,0:T(8,128)(2,1)}, u32[]{:S(2)}, u32[]{:S(2)}) async-start(bf16[16,256,128]{2,1,0:T(8,128)(2,1)} %broadcast_in_dim.4), calls=%async_computation | async-start | bytes 2097152 | tf_op jit(solution)/shard_map/gather_kv_weight/all_to_all | solution.py:223
  14.9 16.4 %collective-permute-start = (bf16[2,8,16,128]{3,2,1,0:T(8,128)(2,1)S(1)}, bf16[2,8,16,128]{3,2,1,0:T(8,128)(2,1)S(1)}, u32[]{:S(2)}, u32[]{:S(2)}) collective-permute-start(bf16[2,8,16,128]{3,2,1,0:T(8,128)(2,1)S(1)} %bitcast.26), channel_id=1, source_target_pairs={{0,0},{1,33},{4,4},{5,37},{8,8},{9,41},{12,12},{13,45},{16,16},{17... | collective-permute-start | bytes 196616 | tf_op jit(solution)/shard_map/out_weight_over_z/ppermute | solution.py:252
  27.5 0.7 copy-start.6
  27.5 0.7 copy-start.5
  33.2 20.2 %collective-permute-start.1 = (bf16[16,256,128]{2,1,0:T(8,128)(2,1)}, bf16[16,256,128]{2,1,0:T(8,128)(2,1)}, u32[]{:S(2)}, u32[]{:S(2)}) collective-permute-start(bf16[16,256,128]{2,1,0:T(8,128)(2,1)} %all-to-all-done.refs_0_), channel_id=1, source_target_pairs={{0,4},{1,61},{4,0},{5,9},{8,12},{9,5},{12,8},{13,17},{16,20},{17,1... | collective-permute-start | bytes 3145736 | tf_op jit(solution)/shard_map/kv_weight_over_z/ppermute | solution.py:264
  41.9 20.0 %all-to-all-start.1 = ((bf16[16,2,8,16,128]{4,3,2,1,0:T(8,128)(2,1)}), bf16[16,2,8,16,128]{4,3,2,1,0:T(8,128)(2,1)S(1)}, u32[]{:S(2)}, u32[]{:S(2)}) async-start(bf16[16,2,8,16,128]{4,3,2,1,0:T(8,128)(2,1)} %broadcast_in_dim.5), calls=%async_computation.1 | async-start | bytes 2097152 | tf_op jit(solution)/shard_map/out_weight_over_plane/all_to_all | solution.py:223
  45.6 21.1 %copy-start.4 = (bf16[256,1024]{1,0:T(8,128)(2,1)S(1)}, bf16[256,1024]{1,0:T(8,128)(2,1)}, u32[]{:S(2)}) copy-start(bf16[256,1024]{1,0:T(8,128)(2,1)} %resid_ref.1) | copy-start | bytes 1572868
  55.7 6.3 %collective-permute-start.2 = (bf16[8,256,128]{2,1,0:T(8,128)(2,1)}, bf16[8,256,128]{2,1,0:T(8,128)(2,1)S(1)}, u32[]{:S(2)}, u32[]{:S(2)}) collective-permute-start(bf16[8,256,128]{2,1,0:T(8,128)(2,1)} %get-tuple-element.22), channel_id=1, source_target_pairs={{0,1},{1,0},{2,3},{3,2},{4,5},{5,4},{6,7},{7,6},{8,9},{9,8},{10,11... | collective-permute-start | bytes 1572872 | tf_op jit(solution)/shard_map/swap_weights/ppermute | solution.py:266
  57.6 4.4 %collective-permute-start.3 = (bf16[8,256,128]{2,1,0:T(8,128)(2,1)}, bf16[8,256,128]{2,1,0:T(8,128)(2,1)}, u32[]{:S(2)}, u32[]{:S(2)}) collective-permute-start(bf16[8,256,128]{2,1,0:T(8,128)(2,1)} %get-tuple-element.21), channel_id=1, source_target_pairs={{0,1},{1,0},{2,3},{3,2},{4,5},{5,4},{6,7},{7,6},{8,9},{9,8},{10,11... | collective-permute-start | bytes 1572872 | tf_op jit(solution)/shard_map/swap_weights/ppermute | solution.py:266
  60.0 4.9 %collective-permute-start.5 = (bf16[16,256,128]{2,1,0:T(8,128)(2,1)}, bf16[16,256,128]{2,1,0:T(8,128)(2,1)}, u32[]{:S(2)}, u32[]{:S(2)}) collective-permute-start(bf16[16,256,128]{2,1,0:T(8,128)(2,1)} %all-to-all-done.refs_0_), channel_id=1, source_target_pairs={{0,1},{1,0},{2,3},{3,2},{4,5},{5,4},{6,7},{7,6},{8,9},{9,8},{10,11... | collective-permute-start | bytes 3145736 | tf_op jit(solution)/shard_map/swap_weights/ppermute | solution.py:269
  62.0 4.7 %collective-permute-start.4 = (bf16[16,2,8,16,128]{4,3,2,1,0:T(8,128)(2,1)S(1)}, bf16[16,2,8,16,128]{4,3,2,1,0:T(8,128)(2,1)S(1)}, u32[]{:S(2)}, u32[]{:S(2)}) collective-permute-start(bf16[16,2,8,16,128]{4,3,2,1,0:T(8,128)(2,1)S(1)} %all-to-all-done.1.mine_ref), channel_id=1, source_target_pairs={{0,1},{1,0},{2,3},{3,2},{4,5},{5,4},{6,7},{7,6},{8,9},{9,8},{10,11... | collective-permute-start | bytes 3145736 | tf_op jit(solution)/shard_map/swap_weights/ppermute | solution.py:268
  64.4 2.3 %copy-start.7 = (f32[1024]{0:T(1024)S(1)}, f32[1024]{0:T(1024)}, u32[]{:S(2)}) copy-start(f32[1024]{0:T(1024)} %param.15) | copy-start | bytes 12292
  71.4 3.7 %copy-start.8 = (bf16[64,1,1024]{2,0,1:T(8,128)(2,1)S(1)}, bf16[64,1,1024]{2,0,1:T(8,128)(2,1)}, u32[]{:S(2)}) copy-start(bf16[64,1,1024]{2,0,1:T(8,128)(2,1)} %param.17) | copy-start | bytes 393220
  71.4 21.0 %all-to-all-start.2 = ((bf16[8,512,128]{2,1,0:T(8,128)(2,1)}), bf16[8,512,128]{2,1,0:T(8,128)(2,1)S(1)}, u32[]{:S(2)}, u32[]{:S(2)}) async-start(bf16[8,512,128]{2,1,0:T(8,128)(2,1)} %encode_keyval.1), calls=%async_computation.2 | async-start | bytes 2097152 | tf_op jit(solution)/shard_map/exchange_keyval/all_to_all | solution.py:273

commit v13 on v12

--- a/solution.py
+++ b/solution.py
@@ -240,7 +240,6 @@
     with jax.named_scope("gather_kv_weight"):
         eighth = lax.dynamic_slice_in_dim(
             kv_weight.reshape(D_ENC, 2 * HEAD), core * 512 + odd * 256 + yl * 128, 128, 0)
-        pair, eighth = lax.optimization_barrier((pair, eighth))
         kv_mine = spread(jnp.concatenate([eighth[:, :HEAD], eighth[:, HEAD:]], axis=0), PLANE)
     with jax.named_scope("out_weight_over_z"):
         hops = []

time: 128 us -> 129 us (level)
  starting transfers between devices: 40.5 us -> 44.4 us
  waiting for transfers between devices: 29.1 us -> 27 us
  blocking collectives: 38.6 us -> 36.9 us
    all_to_all x2, starting transfers between devices: 8.12 us -> 11.6 us  [spread(): return lax.all_to_all(copies, axes, 0, 0, tiled=True)]
    all_gather x1, blocking collectives: 8.37 us -> 5.09 us  [local(): lax.all_gather(out_weight.reshape(16, 8, HEAD).transpose(1, 0, 2), 'c')]
    ppermute x1, starting transfers between devices: 2.41 us -> 4.42 us  [local(): w_other = swap(w_mine)]
    all_to_all x2, waiting for transfers between devices: 1.91 us -> 0.01 us  [spread(): return lax.all_to_all(copies, axes, 0, 0, tiled=True)]
    ppermute x1, starting transfers between devices: 7.49 us -> 5.65 us  [local(): kv_next = lax.ppermute(kv_mine, ('z', 'c'), pairs)]
    all_to_all x1, blocking collectives: 30.2 us -> 31.8 us  [local(): parts = lax.all_to_all(parts, SA, 0, 0, tiled=True)]
  transfers between devices with their start and end apart: 9 -> 9, of which waited for: 5 -> 3; matrix products, arithmetic and copies ran while one was open for 3% -> 3% of each run, Pallas kernels for 2% -> 2%
where the time goes in v13:
time: 129 us; the launch traced here: 128 us
  starting transfers between devices  44.4 us (34%)
  blocking collectives  36.9 us (29%)
  waiting for transfers between devices  27 us (21%)
  Pallas kernels  13 us (10%)
  local copies, waits for them, and re-layouts  6.46 us (5%)
    all_to_all x1, blocking collectives, local(): parts = lax.all_to_all(parts, SA, 0, 0, tiled=True)  31.8 us
    all_to_all x1, waiting for transfers between devices, local(): keyval = lax.all_to_all(keyval, HA, 0, 0, tiled=True)  17.2 us
    ppermute x1, starting transfers between devices, local(): pair = lax.ppermute(pair, ('yh', 'x', 'z', 'c'), hops)  12.8 us
    all_to_all x2, starting transfers between devices, spread(): return lax.all_to_all(copies, axes, 0, 0, tiled=True)  11.6 us
    ppermute x1, waiting for transfers between devices, local(): kv_next = lax.ppermute(kv_mine, ('z', 'c'), pairs)  7.66 us
    ppermute x1, starting transfers between devices, local(): kv_next = lax.ppermute(kv_mine, ('z', 'c'), pairs)  5.65 us
    all_gather x1, blocking collectives, local(): lax.all_gather(out_weight.reshape(16, 8, HEAD).transpose(1, 0, 2), 'c')  5.09 us
    pallas_call x1, Pallas kernels, encode(): pl.pallas_call(encode_kernel, out_shape=shape, in_specs=[smem] + [vmem] *...  4.7 us
  transfers between devices with their start and end apart: 9, of which 3 were waited for; matrix products, arithmetic and copies ran while one was open for 3% of the time, Pallas kernels for 2%

profile of v13, /device:TPU:1, one launch (start us, length us, event | category | flops | bytes accessed | tf_op | source)
XLA Modules:
  0.0 128.2 jit_solution(1136691844493777037)
XLA Ops:
  0.0 1.0 copy-done
  1.1 1.2 broadcast_in_dim.4
  2.3 7.8 %all-to-all-start = ((bf16[16,256,128]{2,1,0:T(8,128)(2,1)}), bf16[16,256,128]{2,1,0:T(8,128)(2,1)}, u32[]{:S(2)}, u32[]{:S(2)}) async-start(bf16[16,256,128]{2,1,0:T(8,128)(2,1)} %broadcast_in_dim.4), calls=%async_computation | async-start | bytes 2097152 | tf_op jit(solution)/shard_map/gather_kv_weight/all_to_all | solution.py:223
  10.1 5.1 %all-gather = bf16[16,16,128]{2,0,1:T(8,128)(2,1)S(1)} all-gather(bf16[8,16,128]{2,0,1:T(8,128)(2,1)S(1)} %bitcast.24), channel_id=2, replica_groups=mesh['yh'=2,'x'=4,'z'=16,'yl'=2,'c'=2] {'c'}, dimensions={0}, use_global_device_ids=true | all-gather | bytes 98304 | tf_op jit(solution)/shard_map/pair_out_weight/all_gather | solution.py:239
  15.2 12.8 %collective-permute-start = (bf16[2,8,16,128]{3,2,1,0:T(8,128)(2,1)S(1)}, bf16[2,8,16,128]{3,2,1,0:T(8,128)(2,1)S(1)}, u32[]{:S(2)}, u32[]{:S(2)}) collective-permute-start(bf16[2,8,16,128]{3,2,1,0:T(8,128)(2,1)S(1)} %bitcast.26), channel_id=1, source_target_pairs={{0,0},{1,33},{4,4},{5,37},{8,8},{9,41},{12,12},{13,45},{16,16},{17... | collective-permute-start | bytes 196616 | tf_op jit(solution)/shard_map/out_weight_over_z/ppermute | solution.py:251
  28.1 0.6 copy-done.6
  28.7 3.1 %encoder_attention.1.ctx_ref = bf16[256,1024]{1,0:T(8,128)(2,1)S(1)} custom-call(s32[1]{0:T(128)} %bitcast.10.slot_ref, s32[512]{0:T(512)S(1)} %copy-done.5, s32[512]{0:T(512)S(1)} %copy-done.6, bf16[256,1024]{1,0:T(8,128)(2,1)S(1)} %copy-done.1, bf16[256,1024]{1,0:T(8,128)(2,1)S(1)} %copy-done.2, bf16[256,1024]{1,0:T(8,128)(2,1)S(1)} %copy-done.3), custom_call_target="tpu_custom_call" | custom-call | flops 536870912 | bytes 2097152 | tf_op jit(solution)/shard_map/encoder_attention/pallas_call | solution.py:62
  31.9 5.7 %collective-permute-start.1 = (bf16[16,256,128]{2,1,0:T(8,128)(2,1)}, bf16[16,256,128]{2,1,0:T(8,128)(2,1)}, u32[]{:S(2)}, u32[]{:S(2)}) collective-permute-start(bf16[16,256,128]{2,1,0:T(8,128)(2,1)} %all-to-all-done.refs_0_), channel_id=1, source_target_pairs={{0,4},{1,61},{4,0},{5,9},{8,12},{9,5},{12,8},{13,17},{16,20},{17,1... | collective-permute-start | bytes 3145736 | tf_op jit(solution)/shard_map/kv_weight_over_z/ppermute | solution.py:263
  37.5 1.2 broadcast_in_dim.5
  38.7 3.8 %all-to-all-start.1 = ((bf16[16,2,8,16,128]{4,3,2,1,0:T(8,128)(2,1)}), bf16[16,2,8,16,128]{4,3,2,1,0:T(8,128)(2,1)S(1)}, u32[]{:S(2)}, u32[]{:S(2)}) async-start(bf16[16,2,8,16,128]{4,3,2,1,0:T(8,128)(2,1)} %broadcast_in_dim.5), calls=%async_computation.1 | async-start | bytes 2097152 | tf_op jit(solution)/shard_map/out_weight_over_plane/all_to_all | solution.py:223
  42.5 7.7 %collective-permute-done.1.refs_1_ = bf16[16,256,128]{2,1,0:T(8,128)(2,1)} collective-permute-done((bf16[16,256,128]{2,1,0:T(8,128)(2,1)}, bf16[16,256,128]{2,1,0:T(8,128)(2,1)}, u32[]{:S(2)}, u32[]{:S(2)}) %collective-permute-start.1) | collective-permute-done | bytes 1048608 | tf_op jit(solution)/shard_map/kv_weight_over_z/ppermute | solution.py:263
  50.2 2.3 %fusion = (bf16[8,256,128]{2,1,0:T(8,128)(2,1)}, bf16[8,256,128]{2,1,0:T(8,128)(2,1)}) fusion(bf16[16,256,128]{2,1,0:T(8,128)(2,1)} %collective-permute-done.1.refs_1_), kind=kLoop, calls=%fused_computation.4 | loop fusion | bytes 2097152 | tf_op jit(solution)/shard_map/swap_weights/slice | solution.py:265
  52.5 1.9 %collective-permute-start.2 = (bf16[8,256,128]{2,1,0:T(8,128)(2,1)}, bf16[8,256,128]{2,1,0:T(8,128)(2,1)S(1)}, u32[]{:S(2)}, u32[]{:S(2)}) collective-permute-start(bf16[8,256,128]{2,1,0:T(8,128)(2,1)} %get-tuple-element.18), channel_id=1, source_target_pairs={{0,1},{1,0},{2,3},{3,2},{4,5},{5,4},{6,7},{7,6},{8,9},{9,8},{10,11... | collective-permute-start | bytes 1572872 | tf_op jit(solution)/shard_map/swap_weights/ppermute | solution.py:265
  54.4 2.4 %collective-permute-start.3 = (bf16[8,256,128]{2,1,0:T(8,128)(2,1)}, bf16[8,256,128]{2,1,0:T(8,128)(2,1)}, u32[]{:S(2)}, u32[]{:S(2)}) collective-permute-start(bf16[8,256,128]{2,1,0:T(8,128)(2,1)} %get-tuple-element.17), channel_id=1, source_target_pairs={{0,1},{1,0},{2,3},{3,2},{4,5},{5,4},{6,7},{7,6},{8,9},{9,8},{10,11... | collective-permute-start | bytes 1572872 | tf_op jit(solution)/shard_map/swap_weights/ppermute | solution.py:265
  56.8 1.9 %collective-permute-start.5 = (bf16[16,256,128]{2,1,0:T(8,128)(2,1)}, bf16[16,256,128]{2,1,0:T(8,128)(2,1)}, u32[]{:S(2)}, u32[]{:S(2)}) collective-permute-start(bf16[16,256,128]{2,1,0:T(8,128)(2,1)} %all-to-all-done.refs_0_), channel_id=1, source_target_pairs={{0,1},{1,0},{2,3},{3,2},{4,5},{5,4},{6,7},{7,6},{8,9},{9,8},{10,11... | collective-permute-start | bytes 3145736 | tf_op jit(solution)/shard_map/swap_weights/ppermute | solution.py:268
  58.8 4.4 %collective-permute-start.4 = (bf16[16,2,8,16,128]{4,3,2,1,0:T(8,128)(2,1)S(1)}, bf16[16,2,8,16,128]{4,3,2,1,0:T(8,128)(2,1)S(1)}, u32[]{:S(2)}, u32[]{:S(2)}) collective-permute-start(bf16[16,2,8,16,128]{4,3,2,1,0:T(8,128)(2,1)S(1)} %all-to-all-done.1.mine_ref), channel_id=1, source_target_pairs={{0,1},{1,0},{2,3},{3,2},{4,5},{5,4},{6,7},{7,6},{8,9},{9,8},{10,11... | collective-permute-start | bytes 3145736 | tf_op jit(solution)/shard_map/swap_weights/ppermute | solution.py:267
  63.2 0.1 pad_add_fusion.1.place_ref
  63.3 2.2 %collective-permute-done.4.other_ref = bf16[16,2,8,16,128]{4,3,2,1,0:T(8,128)(2,1)S(1)} collective-permute-done((bf16[16,2,8,16,128]{4,3,2,1,0:T(8,128)(2,1)S(1)}, bf16[16,2,8,16,128]{4,3,2,1,0:T(8,128)(2,1)S(1)}, u32[]{:S(2)}, u32[]{:S(2)}) %collective-permute-start.4) | collective-permute-done | bytes 1048608 | tf_op jit(solution)/shard_map/swap_weights/ppermute | solution.py:267
  65.5 4.7 %encode_keyval.1 = bf16[8,512,128]{2,1,0:T(8,128)(2,1)} custom-call(s32[3]{0:T(128)S(1)} %pad_add_fusion.1.place_ref, f32[1,1024]{1,0:T(1,128)S(1)} %bitcast.22, bf16[256,1024]{1,0:T(8,128)(2,1)S(1)} %encoder_attention.1.ctx_ref, bf16[256,1024]{1,0:T(8,128)(2,1)S(1)} %copy-done.4, bf16[16,2,8,16,128]{4,3,2,1,0:T(8,128)(2,1)S(1)} %all-to-all-done.1.mine_ref, ...), custom_call_target="tpu_custom_call" | custom-call | flops 1610612736 | bytes 8388608 | tf_op jit(solution)/shard_map/encode_keyval/pallas_call | solution.py:133
  70.2 3.7 %all-to-all-start.2 = ((bf16[8,512,128]{2,1,0:T(8,128)(2,1)}), bf16[8,512,128]{2,1,0:T(8,128)(2,1)S(1)}, u32[]{:S(2)}, u32[]{:S(2)}) async-start(bf16[8,512,128]{2,1,0:T(8,128)(2,1)} %encode_keyval.1), calls=%async_computation.2 | async-start | bytes 2097152 | tf_op jit(solution)/shard_map/exchange_keyval/all_to_all | solution.py:272
  74.0 17.2 %all-to-all-done.2.kv_ref = bf16[8,512,128]{2,1,0:T(8,128)(2,1)S(1)} async-done(((bf16[8,512,128]{2,1,0:T(8,128)(2,1)}), bf16[8,512,128]{2,1,0:T(8,128)(2,1)S(1)}, u32[]{:S(2)}, u32[]{:S(2)}) %all-to-all-start.2) | async-done | bytes 1048608 | tf_op jit(solution)/shard_map/exchange_keyval/all_to_all | solution.py:272
  91.2 3.2 %cross_attention.1 = bf16[64,2,640]{2,1,0:T(2,128)(2,1)S(1)} custom-call(s32[2]{0:T(128)S(1)} %pad_add_fusion.first_ref, s32[512]{0:T(512)S(1)} %copy-done.5, s32[512]{0:T(512)S(1)} %copy-done.6, bf16[512,128]{1,0:T(8,128)(2,1)S(1)} %bitcast.21, bf16[8,512,128]{2,1,0:T(8,128)(2,1)S(1)} %all-to-all-done.2.kv_ref), custom_call_target="tpu_custom_call" | custom-call | tf_op jit(solution)/shard_map/cross_attention/pallas_call | solution.py:188
  94.4 31.8 %all_to_all.20.part_ref = bf16[64,2,640]{2,1,0:T(2,128)(2,1)} all-to-all(bf16[64,2,640]{2,1,0:T(2,128)(2,1)S(1)} %cross_attention.1), channel_id=1, replica_groups=mesh['yh'=2,'x'=4,'z'=16,'yl'=2,'c'=2] {'z','yl','c'}, dimensions={0} | all-to-all | bytes 327680 | tf_op jit(solution)/shard_map/exchange_partials/all_to_all | solution.py:277
  126.2 2.0 %merge_partials.1 = f32[8,128]{1,0:T(8,128)} custom-call(bf16[64,2,640]{2,1,0:T(2,128)(2,1)} %all_to_all.20.part_ref), custom_call_target="tpu_custom_call" | custom-call | tf_op jit(solution)/shard_map/merge_partials/pallas_call | solution.py:211
  (32 shorter events, 0.2 us)
Async XLA Ops:
  0.0 1.0 copy-start
  2.2 7.8 %copy-start.9 = (bf16[16,1024]{1,0:T(8,128)(2,1)S(1)}, bf16[16,1024]{1,0:T(8,128)(2,1)}, u32[]{:S(2)}) copy-start(bf16[16,1024]{1,0:T(8,128)(2,1)} %param.14) | copy-start | bytes 98308
  2.2 25.8 %copy-start.1 = (bf16[256,1024]{1,0:T(8,128)(2,1)S(1)}, bf16[256,1024]{1,0:T(8,128)(2,1)}, u32[]{:S(2)}) copy-start(bf16[256,1024]{1,0:T(8,128)(2,1)} %q_ref.1) | copy-start | bytes 1572868
  2.2 25.8 %copy-start.2 = (bf16[256,1024]{1,0:T(8,128)(2,1)S(1)}, bf16[256,1024]{1,0:T(8,128)(2,1)}, u32[]{:S(2)}) copy-start(bf16[256,1024]{1,0:T(8,128)(2,1)} %k_ref.1) | copy-start | bytes 1572868
  2.2 25.8 %copy-start.3 = (bf16[256,1024]{1,0:T(8,128)(2,1)S(1)}, bf16[256,1024]{1,0:T(8,128)(2,1)}, u32[]{:S(2)}) copy-start(bf16[256,1024]{1,0:T(8,128)(2,1)} %v_ref.1) | copy-start | bytes 1572868
  2.3 29.6 %all-to-all-start = ((bf16[16,256,128]{2,1,0:T(8,128)(2,1)}), bf16[16,256,128]{2,1,0:T(8,128)(2,1)}, u32[]{:S(2)}, u32[]{:S(2)}) async-start(bf16[16,256,128]{2,1,0:T(8,128)(2,1)} %broadcast_in_dim.4), calls=%async_computation | async-start | bytes 2097152 | tf_op jit(solution)/shard_map/gather_kv_weight/all_to_all | solution.py:223
  15.2 16.7 %collective-permute-start = (bf16[2,8,16,128]{3,2,1,0:T(8,128)(2,1)S(1)}, bf16[2,8,16,128]{3,2,1,0:T(8,128)(2,1)S(1)}, u32[]{:S(2)}, u32[]{:S(2)}) collective-permute-start(bf16[2,8,16,128]{3,2,1,0:T(8,128)(2,1)S(1)} %bitcast.26), channel_id=1, source_target_pairs={{0,0},{1,33},{4,4},{5,37},{8,8},{9,41},{12,12},{13,45},{16,16},{17... | collective-permute-start | bytes 196616 | tf_op jit(solution)/shard_map/out_weight_over_z/ppermute | solution.py:251
  28.0 0.7 copy-start.6
  28.0 0.7 copy-start.5
  31.9 18.3 %collective-permute-start.1 = (bf16[16,256,128]{2,1,0:T(8,128)(2,1)}, bf16[16,256,128]{2,1,0:T(8,128)(2,1)}, u32[]{:S(2)}, u32[]{:S(2)}) collective-permute-start(bf16[16,256,128]{2,1,0:T(8,128)(2,1)} %all-to-all-done.refs_0_), channel_id=1, source_target_pairs={{0,4},{1,61},{4,0},{5,9},{8,12},{9,5},{12,8},{13,17},{16,20},{17,1... | collective-permute-start | bytes 3145736 | tf_op jit(solution)/shard_map/kv_weight_over_z/ppermute | solution.py:263
  38.7 20.0 %all-to-all-start.1 = ((bf16[16,2,8,16,128]{4,3,2,1,0:T(8,128)(2,1)}), bf16[16,2,8,16,128]{4,3,2,1,0:T(8,128)(2,1)S(1)}, u32[]{:S(2)}, u32[]{:S(2)}) async-start(bf16[16,2,8,16,128]{4,3,2,1,0:T(8,128)(2,1)} %broadcast_in_dim.5), calls=%async_computation.1 | async-start | bytes 2097152 | tf_op jit(solution)/shard_map/out_weight_over_plane/all_to_all | solution.py:223
  42.5 22.9 %copy-start.4 = (bf16[256,1024]{1,0:T(8,128)(2,1)S(1)}, bf16[256,1024]{1,0:T(8,128)(2,1)}, u32[]{:S(2)}) copy-start(bf16[256,1024]{1,0:T(8,128)(2,1)} %resid_ref.1) | copy-start | bytes 1572868
  52.5 6.3 %collective-permute-start.2 = (bf16[8,256,128]{2,1,0:T(8,128)(2,1)}, bf16[8,256,128]{2,1,0:T(8,128)(2,1)S(1)}, u32[]{:S(2)}, u32[]{:S(2)}) collective-permute-start(bf16[8,256,128]{2,1,0:T(8,128)(2,1)} %get-tuple-element.18), channel_id=1, source_target_pairs={{0,1},{1,0},{2,3},{3,2},{4,5},{5,4},{6,7},{7,6},{8,9},{9,8},{10,11... | collective-permute-start | bytes 1572872 | tf_op jit(solution)/shard_map/swap_weights/ppermute | solution.py:265
  54.4 4.4 %collective-permute-start.3 = (bf16[8,256,128]{2,1,0:T(8,128)(2,1)}, bf16[8,256,128]{2,1,0:T(8,128)(2,1)}, u32[]{:S(2)}, u32[]{:S(2)}) collective-permute-start(bf16[8,256,128]{2,1,0:T(8,128)(2,1)} %get-tuple-element.17), channel_id=1, source_target_pairs={{0,1},{1,0},{2,3},{3,2},{4,5},{5,4},{6,7},{7,6},{8,9},{9,8},{10,11... | collective-permute-start | bytes 1572872 | tf_op jit(solution)/shard_map/swap_weights/ppermute | solution.py:265
  56.8 6.5 %collective-permute-start.5 = (bf16[16,256,128]{2,1,0:T(8,128)(2,1)}, bf16[16,256,128]{2,1,0:T(8,128)(2,1)}, u32[]{:S(2)}, u32[]{:S(2)}) collective-permute-start(bf16[16,256,128]{2,1,0:T(8,128)(2,1)} %all-to-all-done.refs_0_), channel_id=1, source_target_pairs={{0,1},{1,0},{2,3},{3,2},{4,5},{5,4},{6,7},{7,6},{8,9},{9,8},{10,11... | collective-permute-start | bytes 3145736 | tf_op jit(solution)/shard_map/swap_weights/ppermute | solution.py:268
  58.8 6.7 %collective-permute-start.4 = (bf16[16,2,8,16,128]{4,3,2,1,0:T(8,128)(2,1)S(1)}, bf16[16,2,8,16,128]{4,3,2,1,0:T(8,128)(2,1)S(1)}, u32[]{:S(2)}, u32[]{:S(2)}) collective-permute-start(bf16[16,2,8,16,128]{4,3,2,1,0:T(8,128)(2,1)S(1)} %all-to-all-done.1.mine_ref), channel_id=1, source_target_pairs={{0,1},{1,0},{2,3},{3,2},{4,5},{5,4},{6,7},{7,6},{8,9},{9,8},{10,11... | collective-permute-start | bytes 3145736 | tf_op jit(solution)/shard_map/swap_weights/ppermute | solution.py:267
  63.2 2.3 %copy-start.7 = (f32[1024]{0:T(1024)S(1)}, f32[1024]{0:T(1024)}, u32[]{:S(2)}) copy-start(f32[1024]{0:T(1024)} %param.15) | copy-start | bytes 12292
  70.2 3.7 %copy-start.8 = (bf16[64,1,1024]{2,0,1:T(8,128)(2,1)S(1)}, bf16[64,1,1024]{2,0,1:T(8,128)(2,1)}, u32[]{:S(2)}) copy-start(bf16[64,1,1024]{2,0,1:T(8,128)(2,1)} %param.17) | copy-start | bytes 393220
  70.2 21.0 %all-to-all-start.2 = ((bf16[8,512,128]{2,1,0:T(8,128)(2,1)}), bf16[8,512,128]{2,1,0:T(8,128)(2,1)S(1)}, u32[]{:S(2)}, u32[]{:S(2)}) async-start(bf16[8,512,128]{2,1,0:T(8,128)(2,1)} %encode_keyval.1), calls=%async_computation.2 | async-start | bytes 2097152 | tf_op jit(solution)/shard_map/exchange_keyval/all_to_all | solution.py:272

commit v14 on v12

--- a/solution.py
+++ b/solution.py
@@ -18,6 +18,7 @@
 SEG_LEN = 256
 QTAIL = 64
 MASKED = -1e30
+SHIFTS = (0, 1, 15, 2, 14, 3, 13, 4)
 
 PARTS = ("yh", "x", "z", "yl", "c")
 HA = ("yh", "x")
@@ -89,7 +90,7 @@
 
     for part_ref, at in ((mine_ref, core), (other_ref, 1 - core)):
         for ha in range(KV_HEADS):
-            plane = lax.rem(z + 32 - ha - 8 * at, 16)
+            plane = lax.rem(z + 32 - SHIFTS[ha] - 8 * at, 16)
             for yl in range(2):
                 for c in range(2):
                     row = pl.multiple_of(64 * plane + 32 * yl + 16 * c, 16)
@@ -247,7 +248,7 @@
         for ha_at in range(8):
             for z_at in range(16):
                 for c_at in range(2):
-                    there = (z_at + ha_at + 8 * c_at) % 16
+                    there = (z_at + SHIFTS[ha_at] + 8 * c_at) % 16
                     hops.append(((ha_at * 16 + z_at) * 2 + c_at, (ha_at * 16 + there) * 2 + c_at))
         pair = lax.ppermute(pair, ("yh", "x", "z", "c"), hops)
     slot = (ha * sa_count + sa).reshape(1).astype(jnp.int32)

time: 128 us -> 127 us (level)
  no operation moved by 1% of the time
where the time goes in v14:
time: 127 us
  starting transfers between devices  40.5 us (32%)
  blocking collectives  37.5 us (30%)
  waiting for transfers between devices  29.1 us (23%)
  Pallas kernels  13 us (10%)
  local copies, waits for them, and re-layouts  6.24 us (5%)
    all_to_all x1, blocking collectives, local(): parts = lax.all_to_all(parts, SA, 0, 0, tiled=True)  29.1 us
    all_to_all x1, waiting for transfers between devices, local(): keyval = lax.all_to_all(keyval, HA, 0, 0, tiled=True)  17.2 us
    ppermute x1, starting transfers between devices, local(): pair = lax.ppermute(pair, ('yh', 'x', 'z', 'c'), hops)  12.5 us
    all_gather x1, blocking collectives, local(): lax.all_gather(out_weight.reshape(16, 8, HEAD).transpose(1, 0, 2), 'c')  8.37 us
    all_to_all x2, starting transfers between devices, spread(): return lax.all_to_all(copies, axes, 0, 0, tiled=True)  8.12 us
    ppermute x1, waiting for transfers between devices, local(): kv_next = lax.ppermute(kv_mine, ('z', 'c'), pairs)  7.81 us
    ppermute x1, starting transfers between devices, local(): kv_next = lax.ppermute(kv_mine, ('z', 'c'), pairs)  7.49 us
    pallas_call x1, Pallas kernels, encode(): pl.pallas_call(encode_kernel, out_shape=shape, in_specs=[smem] + [vmem] *...  4.7 us
  transfers between devices with their start and end apart: 9, of which 5 were waited for; matrix products, arithmetic and copies ran while one was open for 3% of the time, Pallas kernels for 2%

profile of v14, /device:TPU:1, one launch (start us, length us, event | category | flops | bytes accessed | tf_op | source)
XLA Modules:
  0.0 126.7 jit_solution(5479570271994421032)
XLA Ops:
  0.0 0.8 copy-done.9
  0.8 8.4 %all-gather = bf16[16,16,128]{2,0,1:T(8,128)(2,1)S(1)} all-gather(bf16[8,16,128]{2,0,1:T(8,128)(2,1)S(1)} %bitcast.24), channel_id=2, replica_groups=mesh['yh'=2,'x'=4,'z'=16,'yl'=2,'c'=2] {'c'}, dimensions={0}, use_global_device_ids=true | all-gather | bytes 98304 | tf_op jit(solution)/shard_map/pair_out_weight/all_gather | solution.py:240
  9.3 1.2 broadcast_in_dim.4
  10.5 4.5 %all-to-all-start = ((bf16[16,256,128]{2,1,0:T(8,128)(2,1)}), bf16[16,256,128]{2,1,0:T(8,128)(2,1)}, u32[]{:S(2)}, u32[]{:S(2)}) async-start(bf16[16,256,128]{2,1,0:T(8,128)(2,1)} %broadcast_in_dim.4), calls=%async_computation | async-start | bytes 2097152 | tf_op jit(solution)/shard_map/gather_kv_weight/all_to_all | solution.py:224
  14.9 12.5 %collective-permute-start = (bf16[2,8,16,128]{3,2,1,0:T(8,128)(2,1)S(1)}, bf16[2,8,16,128]{3,2,1,0:T(8,128)(2,1)S(1)}, u32[]{:S(2)}, u32[]{:S(2)}) collective-permute-start(bf16[2,8,16,128]{3,2,1,0:T(8,128)(2,1)S(1)} %bitcast.26), channel_id=1, source_target_pairs={{0,0},{1,33},{4,4},{5,37},{8,8},{9,41},{12,12},{13,45},{16,16},{17... | collective-permute-start | bytes 196616 | tf_op jit(solution)/shard_map/out_weight_over_z/ppermute | solution.py:253
  27.6 0.6 copy-done.6
  28.2 3.1 %encoder_attention.1.ctx_ref = bf16[256,1024]{1,0:T(8,128)(2,1)S(1)} custom-call(s32[1]{0:T(128)} %bitcast.10.slot_ref, s32[512]{0:T(512)S(1)} %copy-done.5, s32[512]{0:T(512)S(1)} %copy-done.6, bf16[256,1024]{1,0:T(8,128)(2,1)S(1)} %copy-done.1, bf16[256,1024]{1,0:T(8,128)(2,1)S(1)} %copy-done.2, bf16[256,1024]{1,0:T(8,128)(2,1)S(1)} %copy-done.3), custom_call_target="tpu_custom_call" | custom-call | flops 536870912 | bytes 2097152 | tf_op jit(solution)/shard_map/encoder_attention/pallas_call | solution.py:63
  31.3 1.9 %all-to-all-done.refs_0_ = bf16[16,256,128]{2,1,0:T(8,128)(2,1)} async-done(((bf16[16,256,128]{2,1,0:T(8,128)(2,1)}), bf16[16,256,128]{2,1,0:T(8,128)(2,1)}, u32[]{:S(2)}, u32[]{:S(2)}) %all-to-all-start) | async-done | bytes 1048608 | tf_op jit(solution)/shard_map/gather_kv_weight/all_to_all | solution.py:224
  33.2 7.5 %collective-permute-start.1 = (bf16[16,256,128]{2,1,0:T(8,128)(2,1)}, bf16[16,256,128]{2,1,0:T(8,128)(2,1)}, u32[]{:S(2)}, u32[]{:S(2)}) collective-permute-start(bf16[16,256,128]{2,1,0:T(8,128)(2,1)} %all-to-all-done.refs_0_), channel_id=1, source_target_pairs={{0,4},{1,61},{4,0},{5,9},{8,12},{9,5},{12,8},{13,17},{16,20},{17,1... | collective-permute-start | bytes 3145736 | tf_op jit(solution)/shard_map/kv_weight_over_z/ppermute | solution.py:265
  40.7 1.2 broadcast_in_dim.5
  41.9 3.7 %all-to-all-start.1 = ((bf16[16,2,8,16,128]{4,3,2,1,0:T(8,128)(2,1)}), bf16[16,2,8,16,128]{4,3,2,1,0:T(8,128)(2,1)S(1)}, u32[]{:S(2)}, u32[]{:S(2)}) async-start(bf16[16,2,8,16,128]{4,3,2,1,0:T(8,128)(2,1)} %broadcast_in_dim.5), calls=%async_computation.1 | async-start | bytes 2097152 | tf_op jit(solution)/shard_map/out_weight_over_plane/all_to_all | solution.py:224
  45.6 7.8 %collective-permute-done.1.refs_1_ = bf16[16,256,128]{2,1,0:T(8,128)(2,1)} collective-permute-done((bf16[16,256,128]{2,1,0:T(8,128)(2,1)}, bf16[16,256,128]{2,1,0:T(8,128)(2,1)}, u32[]{:S(2)}, u32[]{:S(2)}) %collective-permute-start.1) | collective-permute-done | bytes 1048608 | tf_op jit(solution)/shard_map/kv_weight_over_z/ppermute | solution.py:265
  53.4 2.3 %fusion = (bf16[8,256,128]{2,1,0:T(8,128)(2,1)}, bf16[8,256,128]{2,1,0:T(8,128)(2,1)}) fusion(bf16[16,256,128]{2,1,0:T(8,128)(2,1)} %collective-permute-done.1.refs_1_), kind=kLoop, calls=%fused_computation.4 | loop fusion | bytes 2097152 | tf_op jit(solution)/shard_map/swap_weights/slice | solution.py:267
  55.7 1.9 %collective-permute-start.2 = (bf16[8,256,128]{2,1,0:T(8,128)(2,1)}, bf16[8,256,128]{2,1,0:T(8,128)(2,1)S(1)}, u32[]{:S(2)}, u32[]{:S(2)}) collective-permute-start(bf16[8,256,128]{2,1,0:T(8,128)(2,1)} %get-tuple-element.22), channel_id=1, source_target_pairs={{0,1},{1,0},{2,3},{3,2},{4,5},{5,4},{6,7},{7,6},{8,9},{9,8},{10,11... | collective-permute-start | bytes 1572872 | tf_op jit(solution)/shard_map/swap_weights/ppermute | solution.py:267
  57.6 2.4 %collective-permute-start.3 = (bf16[8,256,128]{2,1,0:T(8,128)(2,1)}, bf16[8,256,128]{2,1,0:T(8,128)(2,1)}, u32[]{:S(2)}, u32[]{:S(2)}) collective-permute-start(bf16[8,256,128]{2,1,0:T(8,128)(2,1)} %get-tuple-element.21), channel_id=1, source_target_pairs={{0,1},{1,0},{2,3},{3,2},{4,5},{5,4},{6,7},{7,6},{8,9},{9,8},{10,11... | collective-permute-start | bytes 1572872 | tf_op jit(solution)/shard_map/swap_weights/ppermute | solution.py:267
  60.0 1.9 %collective-permute-start.5 = (bf16[16,256,128]{2,1,0:T(8,128)(2,1)}, bf16[16,256,128]{2,1,0:T(8,128)(2,1)}, u32[]{:S(2)}, u32[]{:S(2)}) collective-permute-start(bf16[16,256,128]{2,1,0:T(8,128)(2,1)} %all-to-all-done.refs_0_), channel_id=1, source_target_pairs={{0,1},{1,0},{2,3},{3,2},{4,5},{5,4},{6,7},{7,6},{8,9},{9,8},{10,11... | collective-permute-start | bytes 3145736 | tf_op jit(solution)/shard_map/swap_weights/ppermute | solution.py:270
  62.0 2.4 %collective-permute-start.4 = (bf16[16,2,8,16,128]{4,3,2,1,0:T(8,128)(2,1)S(1)}, bf16[16,2,8,16,128]{4,3,2,1,0:T(8,128)(2,1)S(1)}, u32[]{:S(2)}, u32[]{:S(2)}) collective-permute-start(bf16[16,2,8,16,128]{4,3,2,1,0:T(8,128)(2,1)S(1)} %all-to-all-done.1.mine_ref), channel_id=1, source_target_pairs={{0,1},{1,0},{2,3},{3,2},{4,5},{5,4},{6,7},{7,6},{8,9},{9,8},{10,11... | collective-permute-start | bytes 3145736 | tf_op jit(solution)/shard_map/swap_weights/ppermute | solution.py:269
  64.9 1.7 %collective-permute-done.4.other_ref = bf16[16,2,8,16,128]{4,3,2,1,0:T(8,128)(2,1)S(1)} collective-permute-done((bf16[16,2,8,16,128]{4,3,2,1,0:T(8,128)(2,1)S(1)}, bf16[16,2,8,16,128]{4,3,2,1,0:T(8,128)(2,1)S(1)}, u32[]{:S(2)}, u32[]{:S(2)}) %collective-permute-start.4) | collective-permute-done | bytes 1048608 | tf_op jit(solution)/shard_map/swap_weights/ppermute | solution.py:269
  66.7 4.7 %encode_keyval.1 = bf16[8,512,128]{2,1,0:T(8,128)(2,1)} custom-call(s32[3]{0:T(128)S(1)} %pad_add_fusion.1.place_ref, f32[1,1024]{1,0:T(1,128)S(1)} %bitcast.22, bf16[256,1024]{1,0:T(8,128)(2,1)S(1)} %encoder_attention.1.ctx_ref, bf16[256,1024]{1,0:T(8,128)(2,1)S(1)} %copy-done.4, bf16[16,2,8,16,128]{4,3,2,1,0:T(8,128)(2,1)S(1)} %all-to-all-done.1.mine_ref, ...), custom_call_target="tpu_custom_call" | custom-call | flops 1610612736 | bytes 8388608 | tf_op jit(solution)/shard_map/encode_keyval/pallas_call | solution.py:134
  71.4 3.7 %all-to-all-start.2 = ((bf16[8,512,128]{2,1,0:T(8,128)(2,1)}), bf16[8,512,128]{2,1,0:T(8,128)(2,1)S(1)}, u32[]{:S(2)}, u32[]{:S(2)}) async-start(bf16[8,512,128]{2,1,0:T(8,128)(2,1)} %encode_keyval.1), calls=%async_computation.2 | async-start | bytes 2097152 | tf_op jit(solution)/shard_map/exchange_keyval/all_to_all | solution.py:274
  75.2 17.2 %all-to-all-done.2.kv_ref = bf16[8,512,128]{2,1,0:T(8,128)(2,1)S(1)} async-done(((bf16[8,512,128]{2,1,0:T(8,128)(2,1)}), bf16[8,512,128]{2,1,0:T(8,128)(2,1)S(1)}, u32[]{:S(2)}, u32[]{:S(2)}) %all-to-all-start.2) | async-done | bytes 1048608 | tf_op jit(solution)/shard_map/exchange_keyval/all_to_all | solution.py:274
  92.4 3.1 %cross_attention.1 = bf16[64,2,640]{2,1,0:T(2,128)(2,1)S(1)} custom-call(s32[2]{0:T(128)S(1)} %pad_add_fusion.first_ref, s32[512]{0:T(512)S(1)} %copy-done.5, s32[512]{0:T(512)S(1)} %copy-done.6, bf16[512,128]{1,0:T(8,128)(2,1)S(1)} %bitcast.21, bf16[8,512,128]{2,1,0:T(8,128)(2,1)S(1)} %all-to-all-done.2.kv_ref), custom_call_target="tpu_custom_call" | custom-call | tf_op jit(solution)/shard_map/cross_attention/pallas_call | solution.py:189
  95.6 29.1 %all_to_all.20.part_ref = bf16[64,2,640]{2,1,0:T(2,128)(2,1)} all-to-all(bf16[64,2,640]{2,1,0:T(2,128)(2,1)S(1)} %cross_attention.1), channel_id=1, replica_groups=mesh['yh'=2,'x'=4,'z'=16,'yl'=2,'c'=2] {'z','yl','c'}, dimensions={0} | all-to-all | bytes 327680 | tf_op jit(solution)/shard_map/exchange_partials/all_to_all | solution.py:279
  124.7 2.0 %merge_partials.1 = f32[8,128]{1,0:T(8,128)} custom-call(bf16[64,2,640]{2,1,0:T(2,128)(2,1)} %all_to_all.20.part_ref), custom_call_target="tpu_custom_call" | custom-call | tf_op jit(solution)/shard_map/merge_partials/pallas_call | solution.py:212
  (32 shorter events, 0.7 us)
Async XLA Ops:
  0.0 9.2 %copy-start = (bf16[1024,1,256]{2,0,1:T(8,128)(2,1)S(1)}, bf16[1024,1,256]{2,0,1:T(8,128)(2,1)}, u32[]{:S(2)}) copy-start(bf16[1024,1,256]{2,0,1:T(8,128)(2,1)} %param.16) | copy-start | bytes 1572868
  0.0 0.8 copy-start.9
  10.5 17.1 %copy-start.1 = (bf16[256,1024]{1,0:T(8,128)(2,1)S(1)}, bf16[256,1024]{1,0:T(8,128)(2,1)}, u32[]{:S(2)}) copy-start(bf16[256,1024]{1,0:T(8,128)(2,1)} %q_ref.1) | copy-start | bytes 1572868
  10.5 17.1 %copy-start.2 = (bf16[256,1024]{1,0:T(8,128)(2,1)S(1)}, bf16[256,1024]{1,0:T(8,128)(2,1)}, u32[]{:S(2)}) copy-start(bf16[256,1024]{1,0:T(8,128)(2,1)} %k_ref.1) | copy-start | bytes 1572868
  10.5 17.1 %copy-start.3 = (bf16[256,1024]{1,0:T(8,128)(2,1)S(1)}, bf16[256,1024]{1,0:T(8,128)(2,1)}, u32[]{:S(2)}) copy-start(bf16[256,1024]{1,0:T(8,128)(2,1)} %v_ref.1) | copy-start | bytes 1572868
  10.5 22.8 %all-to-all-start = ((bf16[16,256,128]{2,1,0:T(8,128)(2,1)}), bf16[16,256,128]{2,1,0:T(8,128)(2,1)}, u32[]{:S(2)}, u32[]{:S(2)}) async-start(bf16[16,256,128]{2,1,0:T(8,128)(2,1)} %broadcast_in_dim.4), calls=%async_computation | async-start | bytes 2097152 | tf_op jit(solution)/shard_map/gather_kv_weight/all_to_all | solution.py:224
  14.9 16.4 %collective-permute-start = (bf16[2,8,16,128]{3,2,1,0:T(8,128)(2,1)S(1)}, bf16[2,8,16,128]{3,2,1,0:T(8,128)(2,1)S(1)}, u32[]{:S(2)}, u32[]{:S(2)}) collective-permute-start(bf16[2,8,16,128]{3,2,1,0:T(8,128)(2,1)S(1)} %bitcast.26), channel_id=1, source_target_pairs={{0,0},{1,33},{4,4},{5,37},{8,8},{9,41},{12,12},{13,45},{16,16},{17... | collective-permute-start | bytes 196616 | tf_op jit(solution)/shard_map/out_weight_over_z/ppermute | solution.py:253
  27.5 0.7 copy-start.6
  27.5 0.7 copy-start.5
  33.2 20.2 %collective-permute-start.1 = (bf16[16,256,128]{2,1,0:T(8,128)(2,1)}, bf16[16,256,128]{2,1,0:T(8,128)(2,1)}, u32[]{:S(2)}, u32[]{:S(2)}) collective-permute-start(bf16[16,256,128]{2,1,0:T(8,128)(2,1)} %all-to-all-done.refs_0_), channel_id=1, source_target_pairs={{0,4},{1,61},{4,0},{5,9},{8,12},{9,5},{12,8},{13,17},{16,20},{17,1... | collective-permute-start | bytes 3145736 | tf_op jit(solution)/shard_map/kv_weight_over_z/ppermute | solution.py:265
  41.9 20.0 %all-to-all-start.1 = ((bf16[16,2,8,16,128]{4,3,2,1,0:T(8,128)(2,1)}), bf16[16,2,8,16,128]{4,3,2,1,0:T(8,128)(2,1)S(1)}, u32[]{:S(2)}, u32[]{:S(2)}) async-start(bf16[16,2,8,16,128]{4,3,2,1,0:T(8,128)(2,1)} %broadcast_in_dim.5), calls=%async_computation.1 | async-start | bytes 2097152 | tf_op jit(solution)/shard_map/out_weight_over_plane/all_to_all | solution.py:224
  45.6 21.1 %copy-start.4 = (bf16[256,1024]{1,0:T(8,128)(2,1)S(1)}, bf16[256,1024]{1,0:T(8,128)(2,1)}, u32[]{:S(2)}) copy-start(bf16[256,1024]{1,0:T(8,128)(2,1)} %resid_ref.1) | copy-start | bytes 1572868
  55.7 6.3 %collective-permute-start.2 = (bf16[8,256,128]{2,1,0:T(8,128)(2,1)}, bf16[8,256,128]{2,1,0:T(8,128)(2,1)S(1)}, u32[]{:S(2)}, u32[]{:S(2)}) collective-permute-start(bf16[8,256,128]{2,1,0:T(8,128)(2,1)} %get-tuple-element.22), channel_id=1, source_target_pairs={{0,1},{1,0},{2,3},{3,2},{4,5},{5,4},{6,7},{7,6},{8,9},{9,8},{10,11... | collective-permute-start | bytes 1572872 | tf_op jit(solution)/shard_map/swap_weights/ppermute | solution.py:267
  57.6 4.4 %collective-permute-start.3 = (bf16[8,256,128]{2,1,0:T(8,128)(2,1)}, bf16[8,256,128]{2,1,0:T(8,128)(2,1)}, u32[]{:S(2)}, u32[]{:S(2)}) collective-permute-start(bf16[8,256,128]{2,1,0:T(8,128)(2,1)} %get-tuple-element.21), channel_id=1, source_target_pairs={{0,1},{1,0},{2,3},{3,2},{4,5},{5,4},{6,7},{7,6},{8,9},{9,8},{10,11... | collective-permute-start | bytes 1572872 | tf_op jit(solution)/shard_map/swap_weights/ppermute | solution.py:267
  60.0 4.9 %collective-permute-start.5 = (bf16[16,256,128]{2,1,0:T(8,128)(2,1)}, bf16[16,256,128]{2,1,0:T(8,128)(2,1)}, u32[]{:S(2)}, u32[]{:S(2)}) collective-permute-start(bf16[16,256,128]{2,1,0:T(8,128)(2,1)} %all-to-all-done.refs_0_), channel_id=1, source_target_pairs={{0,1},{1,0},{2,3},{3,2},{4,5},{5,4},{6,7},{7,6},{8,9},{9,8},{10,11... | collective-permute-start | bytes 3145736 | tf_op jit(solution)/shard_map/swap_weights/ppermute | solution.py:270
  62.0 4.7 %collective-permute-start.4 = (bf16[16,2,8,16,128]{4,3,2,1,0:T(8,128)(2,1)S(1)}, bf16[16,2,8,16,128]{4,3,2,1,0:T(8,128)(2,1)S(1)}, u32[]{:S(2)}, u32[]{:S(2)}) collective-permute-start(bf16[16,2,8,16,128]{4,3,2,1,0:T(8,128)(2,1)S(1)} %all-to-all-done.1.mine_ref), channel_id=1, source_target_pairs={{0,1},{1,0},{2,3},{3,2},{4,5},{5,4},{6,7},{7,6},{8,9},{9,8},{10,11... | collective-permute-start | bytes 3145736 | tf_op jit(solution)/shard_map/swap_weights/ppermute | solution.py:269
  64.4 2.3 %copy-start.7 = (f32[1024]{0:T(1024)S(1)}, f32[1024]{0:T(1024)}, u32[]{:S(2)}) copy-start(f32[1024]{0:T(1024)} %param.15) | copy-start | bytes 12292
  71.4 3.7 %copy-start.8 = (bf16[64,1,1024]{2,0,1:T(8,128)(2,1)S(1)}, bf16[64,1,1024]{2,0,1:T(8,128)(2,1)}, u32[]{:S(2)}) copy-start(bf16[64,1,1024]{2,0,1:T(8,128)(2,1)} %param.17) | copy-start | bytes 393220
  71.4 21.0 %all-to-all-start.2 = ((bf16[8,512,128]{2,1,0:T(8,128)(2,1)}), bf16[8,512,128]{2,1,0:T(8,128)(2,1)S(1)}, u32[]{:S(2)}, u32[]{:S(2)}) async-start(bf16[8,512,128]{2,1,0:T(8,128)(2,1)} %encode_keyval.1), calls=%async_computation.2 | async-start | bytes 2097152 | tf_op jit(solution)/shard_map/exchange_keyval/all_to_all | solution.py:274
